TPU v7x, 32 devices: a whole 2x2x4 slice. The times are simulated.
32 devices in a mesh: ctx: 16 (over z, x, core), head: 2 (over y).
Axes of the slice: x: 2, y: 2, z: 4, core: 2. Of those that a mesh axis runs over, the one named last changes fastest.
Arguments:
- queries: bfloat16 [6144, 2048], P('ctx', 'head')
- keys: bfloat16 [6144, 512], P('ctx', 'head')
- values: bfloat16 [6144, 512], P('ctx', 'head'), may hold values from -6 to 6
- block_start: int32 [48], P('ctx'), may hold values from 0 to 6016, as said below
- out_weight: bfloat16 [2048, 4096], P('head'), may hold values from -0.125 to 0.125
Outputs:
- attended: bfloat16 [6144, 4096], P('ctx', 'head')
Inputs may be any that keep to these rules, and one draw needn't show every extreme that they name: block_start never falls; every document is a whole number of blocks and at most 3072 tokens long, and one document is exactly 3072 tokens long; the first and the last block each begin a document.
All inputs are finite; a program needn't handle non-finite values.
Results may differ from a plain program's by a relative error of at most 0.012.
Values may be sent and summed in bfloat16 or wider, within the bound.
No kernel may reach another device: no remote copies, remote signals or barrier semaphores. Data moves between devices by JAX's collectives and lax.ppermute only.
A program may use at most 64 MiB of HBM per device.

v0:
```python
import functools

import jax
import jax.numpy as jnp
from jax import lax
from jax.experimental import pallas as pl
from jax.experimental.pallas import tpu as pltpu
from jax.sharding import PartitionSpec as P

HEAD_SIZE = 128
BLOCK = 128
LOG2E = 1.4426950408889634
MASKED = -1e30
TILE = 256


def shift(x, distance):
    n = lax.axis_size("ctx")
    return lax.ppermute(x, "ctx", [(i, i + distance) for i in range(n - distance)])


def swap(x, mask):
    return lax.ppermute(x, "ctx", [(i, i ^ mask) for i in range(lax.axis_size("ctx"))])


def attention_kernel(first, last, distances, n_head, starts_ref, recv_starts_ref, *refs):
    refs = list(refs)
    me = lax.axis_index("ctx")
    pair, core, col = me // 2, me % 2, (me // 2) % 2
    if first:
        queries_ref, q_recv_ref, own_ref = refs[:3]
        refs = refs[3:]
    else:
        q_ref, top_in, acc_in = refs[:3]
        refs = refs[3:]
    pieces = refs[: len(distances)]
    refs = refs[len(distances) :]
    if first:
        q_ref, top_ref, acc_ref, held_ref = refs
    elif last:
        out_own, out_other, held_ref, top_ref, acc_ref = refs
    else:
        top_ref, acc_ref, held_ref = refs
    tok = starts_ref.shape[0] * BLOCK
    half = tok // BLOCK
    blocks = 2 * half
    rows = n_head * BLOCK

    def start_of(b):
        mine = b // half == core
        return jnp.where(mine, starts_ref[b % half], recv_starts_ref[b % half])

    def rows_of(ref, j, lane0):
        t = slice(j * BLOCK, (j + 1) * BLOCK)
        return jnp.concatenate(
            [ref[t, pl.ds(lane0 + h * HEAD_SIZE, HEAD_SIZE)] for h in range(n_head)], axis=0
        )

    def value_ones(piece_ref, width):
        v = piece_ref[:width, HEAD_SIZE:]
        return jnp.concatenate([v, jnp.ones_like(v)], axis=1)

    def dot_t(a, b):
        return lax.dot_general(a, b, (((1,), (1,)), ((), ())), preferred_element_type=jnp.float32)

    factor = HEAD_SIZE**-0.5 * LOG2E
    tiles = [(b, slice(r, r + TILE)) for b in range(blocks) for r in range(0, rows, TILE)]

    def keep(s, since):
        k_id = lax.broadcasted_iota(jnp.int32, (1, s.shape[1]), 1)
        return jnp.where(k_id >= since, s, MASKED)

    if first:
        for j in range(half):
            mine = rows_of(queries_ref, j, pl.multiple_of(core * rows, rows))
            q_ref[core * half + j] = mine
            q_ref[(1 - core) * half + j] = rows_of(q_recv_ref, j, 0)
        t_id = lax.broadcasted_iota(jnp.int32, (TILE, BLOCK), 0) % BLOCK
        causal = lax.broadcasted_iota(jnp.int32, (TILE, BLOCK), 1) <= t_id
        for b, r in tiles:
            width = (b + 1) * BLOCK
            s = dot_t(q_ref[b, r], own_ref[:width, :HEAD_SIZE])
            since = start_of(b) - pair * 2 * tok
            diag = jnp.where(causal, s[:, b * BLOCK :], MASKED)
            s = jnp.concatenate([keep(s[:, : b * BLOCK], since), diag], 1) if b else diag
            top = jnp.max(s, axis=1, keepdims=True)
            p = jnp.exp2(s * factor - top * factor).astype(jnp.bfloat16)
            top_ref[b, r] = jnp.broadcast_to(top, (TILE, HEAD_SIZE))
            acc_ref[b, r] = jnp.dot(p, value_ones(own_ref, width), preferred_element_type=jnp.float32)
    else:
        top_ref[...] = top_in[...]
        acc_ref[...] = acc_in[...]

    for i, piece_ref in enumerate(pieces):
        held_ref[i] = piece_ref[...]

    @pl.loop(0, 2 * len(pieces))
    def _(step):
        i, first_block = step // 2, step % 2 * half
        behind = sum(
            jnp.where(i == n, jnp.where(col == 0, *d), 0) for n, d in enumerate(distances)
        )
        base = (pair - behind) * 2 * tok

        @pl.when(start_of(first_block) < base + 2 * tok)
        def _():
            for b, r in tiles[: len(tiles) // 2]:
                b = first_block + b
                s = keep(dot_t(q_ref[b, r], held_ref[i, :, :HEAD_SIZE]), start_of(b) - base)
                old = top_ref[b, r][:, :1]
                top = jnp.maximum(old, jnp.max(s, axis=1, keepdims=True))
                p = jnp.exp2(s * factor - top * factor).astype(jnp.bfloat16)
                top_ref[b, r] = jnp.broadcast_to(top, (TILE, HEAD_SIZE))
                acc_ref[b, r] = acc_ref[b, r] * jnp.exp2((old - top) * factor) + jnp.dot(
                    p, value_ones(held_ref.at[i], 2 * tok), preferred_element_type=jnp.float32
                )

    if last:
        for j in range(half):
            for out, shard in ((out_own, core), (out_other, 1 - core)):
                acc = acc_ref[shard * half + j]
                o = (acc[:, :HEAD_SIZE] / acc[:, HEAD_SIZE:]).astype(jnp.bfloat16)
                for h in range(n_head):
                    out[j * BLOCK : (j + 1) * BLOCK, h * HEAD_SIZE : (h + 1) * HEAD_SIZE] = o[
                        h * BLOCK : (h + 1) * BLOCK
                    ]


def attention_call(first, last, distances, n_head, starts, recv_starts, operands):
    tok = starts.shape[0] * BLOCK
    blocks, rows = 2 * starts.shape[0], n_head * BLOCK
    state = [
        jax.ShapeDtypeStruct((blocks, rows, HEAD_SIZE), jnp.float32),
        jax.ShapeDtypeStruct((blocks, rows, 2 * HEAD_SIZE), jnp.float32),
    ]
    scratch = [pltpu.VMEM((len(distances), 2 * tok, 2 * HEAD_SIZE), jnp.bfloat16)]
    if first:
        outs = [jax.ShapeDtypeStruct((blocks, rows, HEAD_SIZE), jnp.bfloat16)] + state
    elif last:
        outs = [jax.ShapeDtypeStruct((tok, rows), jnp.bfloat16)] * 2
        scratch += [pltpu.VMEM(s.shape, s.dtype) for s in state]
    else:
        outs = state
    n_pieces = len(distances) + 0.5 * first
    vmem, smem = pl.BlockSpec(memory_space=pltpu.VMEM), pl.BlockSpec(memory_space=pltpu.SMEM)
    return pl.pallas_call(
        functools.partial(attention_kernel, first, last, distances, n_head),
        out_shape=outs,
        in_specs=[smem, smem] + [vmem] * len(operands),
        out_specs=[vmem] * len(outs),
        scratch_shapes=scratch,
        compiler_params=pltpu.CompilerParams(vmem_limit_bytes=40 * 2**20),
        cost_estimate=pl.CostEstimate(
            flops=int(n_pieces * blocks * rows * 2 * tok * HEAD_SIZE * 8),
            bytes_accessed=8 * 2**20,
            transcendentals=int(n_pieces * blocks * rows * 2 * tok),
        ),
    )(starts, recv_starts, *operands)


def per_device(queries, keys, values, block_start, out_weight):
    tok = queries.shape[0]
    group = queries.shape[1] // 2
    n_head = group // HEAD_SIZE
    me = lax.axis_index("ctx")
    core, col = me % 2, (me // 2) % 2
    head = lax.axis_index("head")

    def part(x, index, size):
        return lax.dynamic_slice_in_dim(x, index * size, size, 1)

    mine = jnp.concatenate([part(keys, core, HEAD_SIZE), part(values, core, HEAD_SIZE)], 1)
    theirs = jnp.concatenate([part(keys, 1 - core, HEAD_SIZE), part(values, 1 - core, HEAD_SIZE)], 1)
    recv = swap(theirs, 1)
    own = jnp.where(core == 0, jnp.concatenate([mine, recv]), jnp.concatenate([recv, mine]))
    one_behind = shift(own, 4)
    q_recv = swap(part(queries, 1 - core, group), 1)
    recv_starts = swap(block_start, 1)
    two_behind = shift(one_behind, 4)
    across = swap(one_behind, 2)
    q, top, acc = attention_call(
        True, False, ((2, 2),), n_head, block_start, recv_starts, (queries, q_recv, own, one_behind)
    )
    third = swap(jnp.where(col == 1, two_behind, own), 2)
    top, acc = attention_call(
        False, False, ((1, 3), (4, 4)), n_head, block_start, recv_starts,
        (q, top, acc, across, two_behind),
    )
    o_own, o_other = attention_call(
        False, True, ((3, 1),), n_head, block_start, recv_starts, (q, top, acc, third)
    )
    o_recv = swap(o_other, 1)
    heads_out = jnp.where(
        core == 0, jnp.concatenate([o_own, o_recv], 1), jnp.concatenate([o_recv, o_own], 1)
    )
    cols = out_weight.shape[1] // 2
    away = jnp.dot(heads_out, part(out_weight, 1 - head, cols), preferred_element_type=jnp.float32)
    away = lax.ppermute(away.astype(jnp.bfloat16), "head", [(0, 1), (1, 0)])
    here = jnp.dot(heads_out, part(out_weight, head, cols), preferred_element_type=jnp.float32)
    here = here.astype(jnp.bfloat16).astype(jnp.float32)
    return (here + away.astype(jnp.float32)).astype(jnp.bfloat16)


def solution(mesh):
    in_specs = (P("ctx", "head"), P("ctx", "head"), P("ctx", "head"), P("ctx"), P("head", None))
    out_specs = P("ctx", "head")
    return jax.shard_map(
        per_device, mesh=mesh, in_specs=in_specs, out_specs=out_specs, check_vma=False
    )
```

profile of v0, /device:TPU:2, one launch (start us, length us, event | category | flops | bytes accessed | tf_op | source)
XLA Modules:
  0.0 90.4 jit_solution(9387414799908159494)
XLA Ops:
  0.0 0.0 copy-start
  0.0 0.0 copy-start.1
  0.0 1.1 %constant_dynamic-slice_fusion.2 = (bf16[384,128]{1,0:T(8,128)(2,1)S(1)}, bf16[384,128]{1,0:T(8,128)(2,1)S(1)}, bf16[384,128]{1,0:T(8,128)(2,1)S(1)}, bf16[384,128]{1,0:T(8,128)(2,1)S(1)}) fusion(bf16[384,256]{1,0:T(8,128)(2,1)} %param.7, s32[]{:T(128)S(6)} %select_n.58, s32[]{:T(128)S(6)} %select_n.59, bf16[384,256]{1,0:T(8,128)(2,1)} %param.6), kind=kLoop, calls=%fused_computation.15 | loop fusion | bytes 786440 | tf_op jit(solution)/shard_map/dynamic_slice | solution.py:170
  1.2 0.1 collective-permute-start.2
  1.3 1.4 %collective-permute-done.2 = bf16[384,256]{1,0:T(8,128)(2,1)S(1)} collective-permute-done((bf16[384,256]{1,0:T(8,128)(2,1)S(1)}, bf16[384,256]{1,0:T(8,128)(2,1)S(1)}, u32[]{:S(2)}, u32[]{:S(2)}) %collective-permute-start.2) | collective-permute-done | bytes 196640 | tf_op jit(solution)/shard_map/ppermute | solution.py:23
  2.7 0.2 maximum_select_fusion.1.refs_2_
  2.9 3.5 %collective-permute-start.3 = (bf16[768,256]{1,0:T(8,128)(2,1)S(1)}, bf16[768,256]{1,0:T(8,128)(2,1)S(1)}, u32[]{:S(2)}, u32[]{:S(2)}) collective-permute-start(bf16[768,256]{1,0:T(8,128)(2,1)S(1)} %maximum_select_fusion.1.refs_2_), channel_id=1, source_target_pairs={{0,8},{2,10},{4,12},{6,14},{8,16},{10,18},{12,20},{14,22},{16,24},... | collective-permute-start | bytes 1179656 | tf_op jit(solution)/shard_map/ppermute | solution.py:19
  6.4 0.0 copy-done
  6.4 0.1 collective-permute-start.1
  6.5 8.5 %collective-permute-done.3.refs_3_ = bf16[768,256]{1,0:T(8,128)(2,1)S(1)} collective-permute-done((bf16[768,256]{1,0:T(8,128)(2,1)S(1)}, bf16[768,256]{1,0:T(8,128)(2,1)S(1)}, u32[]{:S(2)}, u32[]{:S(2)}) %collective-permute-start.3) | collective-permute-done | bytes 393248 | tf_op jit(solution)/shard_map/ppermute | solution.py:19
  15.0 4.4 %collective-permute-start.5 = (bf16[768,256]{1,0:T(8,128)(2,1)S(1)}, bf16[768,256]{1,0:T(8,128)(2,1)S(1)}, u32[]{:S(2)}, u32[]{:S(2)}) collective-permute-start(bf16[768,256]{1,0:T(8,128)(2,1)S(1)} %collective-permute-done.3.refs_3_), channel_id=1, source_target_pairs={{0,8},{2,10},{4,12},{6,14},{8,16},{10,18},{12,20},{14,22},{16,24},... | collective-permute-start | bytes 1179656 | tf_op jit(solution)/shard_map/ppermute | solution.py:19
  19.4 0.0 copy-done.1
  19.4 0.1 collective-permute-start
  19.5 0.6 collective-permute-start.4
  20.1 0.5 collective-permute-done.recv_starts_ref
  20.6 0.0 collective-permute-done.1.refs_1_
  20.6 4.0 %shard_map.55 = (bf16[6,512,128]{2,1,0:T(8,128)(2,1)S(1)}, f32[6,512,128]{2,1,0:T(8,128)S(1)}, f32[6,512,256]{2,1,0:T(8,128)S(1)}) custom-call(s32[3]{0:T(128)S(1)} %copy-done.1, s32[3]{0:T(128)S(1)} %collective-permute-done.recv_starts_ref, bf16[384,1024]{1,0:T(8,128)(2,1)S(1)} %copy-done, bf16[384,512]{1,0:T(8,128)(2,1)S(1)} %collective-permute-done.1.refs_1_, ...), custom_call_target="tpu_custom_call" | custom-call | flops 3623878656 | bytes 8388608 | tf_op jit(solution)/shard_map/pallas_call | solution.py:146
  24.6 2.6 %collective-permute-done.5.refs_4_ = bf16[768,256]{1,0:T(8,128)(2,1)S(1)} collective-permute-done((bf16[768,256]{1,0:T(8,128)(2,1)S(1)}, bf16[768,256]{1,0:T(8,128)(2,1)S(1)}, u32[]{:S(2)}, u32[]{:S(2)}) %collective-permute-start.5) | collective-permute-done | bytes 393248 | tf_op jit(solution)/shard_map/ppermute | solution.py:19
  27.3 0.6 collective-permute-start.6
  27.9 3.7 %collective-permute-done.4.refs_3_ = bf16[768,256]{1,0:T(8,128)(2,1)S(1)} collective-permute-done((bf16[768,256]{1,0:T(8,128)(2,1)S(1)}, bf16[768,256]{1,0:T(8,128)(2,1)S(1)}, u32[]{:S(2)}, u32[]{:S(2)}) %collective-permute-start.4) | collective-permute-done | bytes 393248 | tf_op jit(solution)/shard_map/ppermute | solution.py:23
  31.5 1.0 %shard_map.56 = (f32[6,512,128]{2,1,0:T(8,128)S(1)}, f32[6,512,256]{2,1,0:T(8,128)S(1)}) custom-call(s32[3]{0:T(128)S(1)} %copy-done.1, s32[3]{0:T(128)S(1)} %collective-permute-done.recv_starts_ref, bf16[6,512,128]{2,1,0:T(8,128)(2,1)S(1)} %get-tuple-element.12.refs_0_, f32[6,512,128]{2,1,0:T(8,128)S(1)} %get-tuple-element.13.refs_1_, ...), custom_call_target="tpu_custom_call" | custom-call | flops 4831838208 | bytes 8388608 | tf_op jit(solution)/shard_map/pallas_call | solution.py:146
  32.5 6.9 %collective-permute-done.6.refs_3_ = bf16[768,256]{1,0:T(8,128)(2,1)S(1)} collective-permute-done((bf16[768,256]{1,0:T(8,128)(2,1)S(1)}, bf16[768,256]{1,0:T(8,128)(2,1)S(1)}, u32[]{:S(2)}, u32[]{:S(2)}) %collective-permute-start.6) | collective-permute-done | bytes 393248 | tf_op jit(solution)/shard_map/ppermute | solution.py:23
  39.5 5.6 %shard_map.57 = (bf16[384,512]{1,0:T(8,128)(2,1)S(1)}, bf16[384,512]{1,0:T(8,128)(2,1)S(1)}) custom-call(s32[3]{0:T(128)S(1)} %copy-done.1, s32[3]{0:T(128)S(1)} %collective-permute-done.recv_starts_ref, bf16[6,512,128]{2,1,0:T(8,128)(2,1)S(1)} %get-tuple-element.12.refs_0_, f32[6,512,128]{2,1,0:T(8,128)S(1)} %get-tuple-element.15.refs_1_, ...), custom_call_target="tpu_custom_call" | custom-call | flops 2415919104 | bytes 8388608 | tf_op jit(solution)/shard_map/pallas_call | solution.py:146
  45.0 0.1 collective-permute-start.7
  45.1 1.7 %collective-permute-done.7 = bf16[384,512]{1,0:T(8,128)(2,1)S(1)} collective-permute-done((bf16[384,512]{1,0:T(8,128)(2,1)S(1)}, bf16[384,512]{1,0:T(8,128)(2,1)S(1)}, u32[]{:S(2)}, u32[]{:S(2)}) %collective-permute-start.7) | collective-permute-done | bytes 393248 | tf_op jit(solution)/shard_map/ppermute | solution.py:23
  46.8 5.2 %fusion.7 = bf16[384,2048]{1,0:T(8,128)(2,1)} fusion(bf16[1024,4096]{1,0:T(8,128)(2,1)} %param.9, s32[]{:T(128)S(6)} %select_n.67, bf16[384,512]{1,0:T(8,128)(2,1)S(1)} %collective-permute-done.7, bf16[384,512]{1,0:T(8,128)(2,1)S(1)} %get-tuple-element.17, pred[]{:T(512)S(6)} %eq.10), kind=kOutput, calls=%fused_computation.6 | convolution fusion | flops 1614938112 | bytes 6553605 | tf_op jit(solution)/shard_map/dot_general | solution.py:197
  52.0 1.5 %collective-permute-start.8 = (bf16[384,2048]{1,0:T(8,128)(2,1)}, bf16[384,2048]{1,0:T(8,128)(2,1)S(1)}, u32[]{:S(2)}, u32[]{:S(2)}) collective-permute-start(bf16[384,2048]{1,0:T(8,128)(2,1)} %fusion.7), channel_id=1, source_target_pairs={{0,1},{1,0},{2,3},{3,2},{4,5},{5,4},{6,7},{7,6},{8,9},{9,8},{10,11... | collective-permute-start | bytes 4718600 | tf_op jit(solution)/shard_map/ppermute | solution.py:198
  53.5 4.0 %fusion.4 = bf16[384,2048]{1,0:T(8,128)(2,1)S(1)} fusion(bf16[1024,4096]{1,0:T(8,128)(2,1)} %param.9, s32[]{:T(128)S(6)} %select_n.66, bf16[384,512]{1,0:T(8,128)(2,1)S(1)} %collective-permute-done.7, bf16[384,512]{1,0:T(8,128)(2,1)S(1)} %get-tuple-element.17, pred[]{:T(512)S(6)} %eq.10), kind=kOutput, calls=%fused_computation.5 | convolution fusion | flops 1614938112 | bytes 6553605 | tf_op jit(solution)/shard_map/dot_general | solution.py:199
  57.5 31.1 %collective-permute-done.8 = bf16[384,2048]{1,0:T(8,128)(2,1)S(1)} collective-permute-done((bf16[384,2048]{1,0:T(8,128)(2,1)}, bf16[384,2048]{1,0:T(8,128)(2,1)S(1)}, u32[]{:S(2)}, u32[]{:S(2)}) %collective-permute-start.8) | collective-permute-done | bytes 1572896 | tf_op jit(solution)/shard_map/ppermute | solution.py:198
  88.6 1.8 %add_convert_fusion = bf16[384,2048]{1,0:T(8,128)(2,1)} fusion(bf16[384,2048]{1,0:T(8,128)(2,1)S(1)} %collective-permute-done.8, bf16[384,2048]{1,0:T(8,128)(2,1)S(1)} %fusion.4), kind=kLoop, calls=%fused_computation.4 | loop fusion | flops 3145728 | bytes 4718592 | tf_op jit(solution)/shard_map/convert_element_type | solution.py:201
  (3 shorter events, 0.1 us)
Async XLA Ops:
  0.0 6.4 %copy-start = (bf16[384,1024]{1,0:T(8,128)(2,1)S(1)}, bf16[384,1024]{1,0:T(8,128)(2,1)}, u32[]{:S(2)}) copy-start(bf16[384,1024]{1,0:T(8,128)(2,1)} %refs_0_.1) | copy-start | bytes 2359300
  0.0 19.4 %copy-start.1 = (s32[3]{0:T(128)S(1)}, s32[3]{0:T(128)}, u32[]{:S(2)}) copy-start(s32[3]{0:T(128)} %starts_ref.5) | copy-start | bytes 40
  1.2 1.5 %collective-permute-start.2 = (bf16[384,256]{1,0:T(8,128)(2,1)S(1)}, bf16[384,256]{1,0:T(8,128)(2,1)S(1)}, u32[]{:S(2)}, u32[]{:S(2)}) collective-permute-start(bf16[384,256]{1,0:T(8,128)(2,1)S(1)} %pad_maximum_fusion), channel_id=1, source_target_pairs={{0,2},{2,0},{4,6},{6,4},{8,10},{10,8},{12,14},{14,12},{16,18},{18,... | collective-permute-start | bytes 589832 | tf_op jit(solution)/shard_map/ppermute | solution.py:23
  2.9 12.1 %collective-permute-start.3 = (bf16[768,256]{1,0:T(8,128)(2,1)S(1)}, bf16[768,256]{1,0:T(8,128)(2,1)S(1)}, u32[]{:S(2)}, u32[]{:S(2)}) collective-permute-start(bf16[768,256]{1,0:T(8,128)(2,1)S(1)} %maximum_select_fusion.1.refs_2_), channel_id=1, source_target_pairs={{0,8},{2,10},{4,12},{6,14},{8,16},{10,18},{12,20},{14,22},{16,24},... | collective-permute-start | bytes 1179656 | tf_op jit(solution)/shard_map/ppermute | solution.py:19
  6.4 14.2 %collective-permute-start.1 = (bf16[384,512]{1,0:T(8,128)(2,1)S(1)}, bf16[384,512]{1,0:T(8,128)(2,1)S(1)}, u32[]{:S(2)}, u32[]{:S(2)}) collective-permute-start(bf16[384,512]{1,0:T(8,128)(2,1)S(1)} %constant_dynamic-slice_fusion.4), channel_id=1, source_target_pairs={{0,2},{2,0},{4,6},{6,4},{8,10},{10,8},{12,14},{14,12},{16,18},{18,... | collective-permute-start | bytes 1179656 | tf_op jit(solution)/shard_map/ppermute | solution.py:23
  15.0 12.2 %collective-permute-start.5 = (bf16[768,256]{1,0:T(8,128)(2,1)S(1)}, bf16[768,256]{1,0:T(8,128)(2,1)S(1)}, u32[]{:S(2)}, u32[]{:S(2)}) collective-permute-start(bf16[768,256]{1,0:T(8,128)(2,1)S(1)} %collective-permute-done.3.refs_3_), channel_id=1, source_target_pairs={{0,8},{2,10},{4,12},{6,14},{8,16},{10,18},{12,20},{14,22},{16,24},... | collective-permute-start | bytes 1179656 | tf_op jit(solution)/shard_map/ppermute | solution.py:19
  19.4 1.2 %collective-permute-start = (s32[3]{0:T(128)S(1)}, s32[3]{0:T(128)S(1)}, u32[]{:S(2)}, u32[]{:S(2)}) collective-permute-start(s32[3]{0:T(128)S(1)} %copy-done.1), channel_id=1, source_target_pairs={{0,2},{2,0},{4,6},{6,4},{8,10},{10,8},{12,14},{14,12},{16,18},{18,... | collective-permute-start | bytes 44 | tf_op jit(solution)/shard_map/ppermute | solution.py:23
  19.5 12.0 %collective-permute-start.4 = (bf16[768,256]{1,0:T(8,128)(2,1)S(1)}, bf16[768,256]{1,0:T(8,128)(2,1)S(1)}, u32[]{:S(2)}, u32[]{:S(2)}) collective-permute-start(bf16[768,256]{1,0:T(8,128)(2,1)S(1)} %collective-permute-done.3.refs_3_), channel_id=1, source_target_pairs={{0,4},{2,6},{4,0},{6,2},{8,12},{10,14},{12,8},{14,10},{16,20},{18,... | collective-permute-start | bytes 1179656 | tf_op jit(solution)/shard_map/ppermute | solution.py:23
  27.3 12.2 %collective-permute-start.6 = (bf16[768,256]{1,0:T(8,128)(2,1)S(1)}, bf16[768,256]{1,0:T(8,128)(2,1)S(1)}, u32[]{:S(2)}, u32[]{:S(2)}) collective-permute-start(bf16[768,256]{1,0:T(8,128)(2,1)S(1)} %broadcast_select_fusion), channel_id=1, source_target_pairs={{0,4},{2,6},{4,0},{6,2},{8,12},{10,14},{12,8},{14,10},{16,20},{18,... | collective-permute-start | bytes 1179656 | tf_op jit(solution)/shard_map/ppermute | solution.py:23
  45.0 1.8 %collective-permute-start.7 = (bf16[384,512]{1,0:T(8,128)(2,1)S(1)}, bf16[384,512]{1,0:T(8,128)(2,1)S(1)}, u32[]{:S(2)}, u32[]{:S(2)}) collective-permute-start(bf16[384,512]{1,0:T(8,128)(2,1)S(1)} %get-tuple-element.18), channel_id=1, source_target_pairs={{0,2},{2,0},{4,6},{6,4},{8,10},{10,8},{12,14},{14,12},{16,18},{18,... | collective-permute-start | bytes 1179656 | tf_op jit(solution)/shard_map/ppermute | solution.py:23
  52.0 36.7 %collective-permute-start.8 = (bf16[384,2048]{1,0:T(8,128)(2,1)}, bf16[384,2048]{1,0:T(8,128)(2,1)S(1)}, u32[]{:S(2)}, u32[]{:S(2)}) collective-permute-start(bf16[384,2048]{1,0:T(8,128)(2,1)} %fusion.7), channel_id=1, source_target_pairs={{0,1},{1,0},{2,3},{3,2},{4,5},{5,4},{6,7},{7,6},{8,9},{9,8},{10,11... | collective-permute-start | bytes 4718600 | tf_op jit(solution)/shard_map/ppermute | solution.py:198
where the time goes:
time: 91.6 us; the launch traced here: 90.4 us
  waiting for transfers between devices  56.4 us (62%)
  starting transfers between devices  10.9 us (12%)
  Pallas kernels  10.6 us (12%)
  matrix products  9.16 us (10%)
  other arithmetic  1.98 us (2%)
  local copies, waits for them, and re-layouts  1.18 us (1%)
    ppermute x1, waiting for transfers between devices, per_device(): away = lax.ppermute(away.astype(jnp.bfloat16), 'head', [(0, 1), (1, 0)])  31.1 us
    ppermute x6, waiting for transfers between devices, swap(): lax.ppermute(x, 'ctx', [(i, i ^ mask) for i in range(lax.axis_size('ctx'))])  14.2 us
    ppermute x2, waiting for transfers between devices, shift(): lax.ppermute(x, 'ctx', [(i, i + distance) for i in range(n - distance)])  11.1 us
    pallas_call x3, Pallas kernels, attention_call(): pl.pallas_call(functools.partial(attention_kernel, first, last, distances...  10.6 us
    ppermute x2, starting transfers between devices, shift(): lax.ppermute(x, 'ctx', [(i, i + distance) for i in range(n - distance)])  7.9 us
    dot_general x1, matrix products, per_device(): jnp.dot(heads_out, part(out_weight, 1 - head, cols), preferred_element_ty...  5.15 us
    dot_general x1, matrix products, per_device(): jnp.dot(heads_out, part(out_weight, head, cols), preferred_element_type=j...  4 us
  transfers between devices with their start and end apart: 9, of which 8 were waited for; matrix products, arithmetic and copies ran while one was open for 5% of the time, Pallas kernels for 6%

commit v1 on v0

--- a/solution.py
+++ b/solution.py
@@ -11,6 +11,7 @@
 BLOCK = 128
 LOG2E = 1.4426950408889634
 MASKED = -1e30
+W_CHUNKS = 2
 TILE = 256
 
 
@@ -21,6 +22,45 @@
 
 def swap(x, mask):
     return lax.ppermute(x, "ctx", [(i, i ^ mask) for i in range(lax.axis_size("ctx"))])
+
+
+def cross(x, mask):
+    n = lax.axis_size("ctx")
+    route = [(2 * i + h, 2 * (i ^ mask) + 1 - h) for i in range(n) for h in range(2)]
+    return lax.ppermute(x, ("ctx", "head"), route)
+
+
+def project_kernel(*refs):
+    given_ref, heads_ref, *chunk_refs, out_ref = refs
+    chunk = chunk_refs[0].shape[0]
+
+    @pl.loop(0, out_ref.shape[1] // 512)
+    def _(n):
+        cols = pl.ds(pl.multiple_of(n * 512, 512), 512)
+        total = given_ref[:, cols]
+        for m, ref in enumerate(chunk_refs):
+            total += jnp.dot(
+                heads_ref[:, m * chunk : (m + 1) * chunk],
+                ref[:, cols],
+                preferred_element_type=jnp.float32,
+            )
+        out_ref[:, cols] = total.astype(out_ref.dtype)
+
+
+def project(given, heads, chunks, dtype):
+    vmem = pl.BlockSpec(memory_space=pltpu.VMEM)
+    return pl.pallas_call(
+        project_kernel,
+        out_shape=jax.ShapeDtypeStruct(given.shape, dtype),
+        in_specs=[vmem] * (2 + len(chunks)),
+        out_specs=vmem,
+        compiler_params=pltpu.CompilerParams(vmem_limit_bytes=40 * 2**20),
+        cost_estimate=pl.CostEstimate(
+            flops=2 * heads.shape[0] * heads.shape[1] * given.shape[1],
+            bytes_accessed=8 * 2**20,
+            transcendentals=0,
+        ),
+    )(given, heads, *chunks)
 
 
 def attention_kernel(first, last, distances, n_head, starts_ref, recv_starts_ref, *refs):
@@ -38,7 +78,7 @@
     if first:
         q_ref, top_ref, acc_ref, held_ref = refs
     elif last:
-        out_own, out_other, held_ref, top_ref, acc_ref = refs
+        out_ref, acc_ref = refs
     else:
         top_ref, acc_ref, held_ref = refs
     tok = starts_ref.shape[0] * BLOCK
@@ -69,6 +109,37 @@
     def keep(s, since):
         k_id = lax.broadcasted_iota(jnp.int32, (1, s.shape[1]), 1)
         return jnp.where(k_id >= since, s, MASKED)
+
+    def update(piece_ref, base, b, r, top_from, acc_from, to):
+        s = keep(dot_t(q_ref[b, r], piece_ref[:, :HEAD_SIZE]), start_of(b) - base)
+        old = top_from[b, r][:, :1]
+        top = jnp.maximum(old, jnp.max(s, axis=1, keepdims=True))
+        p = jnp.exp2(s * factor - top * factor).astype(jnp.bfloat16)
+        if not last:
+            top_ref[to, r] = jnp.broadcast_to(top, (TILE, HEAD_SIZE))
+        acc_ref[to, r] = acc_from[b, r] * jnp.exp2((old - top) * factor) + jnp.dot(
+            p, value_ones(piece_ref, 2 * tok), preferred_element_type=jnp.float32
+        )
+
+    def attend_last(first_block):
+        base = (pair - jnp.where(col == 0, *distances[0])) * 2 * tok
+        needed = start_of(first_block) < base + 2 * tok
+
+        @pl.when(needed)
+        def _():
+            for b, r in tiles[: len(tiles) // 2]:
+                update(pieces[0], base, first_block + b, r, top_in, acc_in, b)
+
+        @pl.when(jnp.logical_not(needed))
+        def _():
+            acc_ref[...] = acc_in[pl.ds(first_block, half)]
+
+        for j in range(half):
+            o = (acc_ref[j, :, :HEAD_SIZE] / acc_ref[j, :, HEAD_SIZE:]).astype(jnp.bfloat16)
+            for h in range(n_head):
+                out_ref[j * BLOCK : (j + 1) * BLOCK, h * HEAD_SIZE : (h + 1) * HEAD_SIZE] = o[
+                    h * BLOCK : (h + 1) * BLOCK
+                ]
 
     if first:
         for j in range(half):
@@ -87,6 +158,10 @@
             p = jnp.exp2(s * factor - top * factor).astype(jnp.bfloat16)
             top_ref[b, r] = jnp.broadcast_to(top, (TILE, HEAD_SIZE))
             acc_ref[b, r] = jnp.dot(p, value_ones(own_ref, width), preferred_element_type=jnp.float32)
+    elif last:
+        shard = core if last == "own" else 1 - core
+        attend_last(shard * half)
+        return
     else:
         top_ref[...] = top_in[...]
         acc_ref[...] = acc_in[...]
@@ -106,24 +181,7 @@
         def _():
             for b, r in tiles[: len(tiles) // 2]:
                 b = first_block + b
-                s = keep(dot_t(q_ref[b, r], held_ref[i, :, :HEAD_SIZE]), start_of(b) - base)
-                old = top_ref[b, r][:, :1]
-                top = jnp.maximum(old, jnp.max(s, axis=1, keepdims=True))
-                p = jnp.exp2(s * factor - top * factor).astype(jnp.bfloat16)
-                top_ref[b, r] = jnp.broadcast_to(top, (TILE, HEAD_SIZE))
-                acc_ref[b, r] = acc_ref[b, r] * jnp.exp2((old - top) * factor) + jnp.dot(
-                    p, value_ones(held_ref.at[i], 2 * tok), preferred_element_type=jnp.float32
-                )
-
-    if last:
-        for j in range(half):
-            for out, shard in ((out_own, core), (out_other, 1 - core)):
-                acc = acc_ref[shard * half + j]
-                o = (acc[:, :HEAD_SIZE] / acc[:, HEAD_SIZE:]).astype(jnp.bfloat16)
-                for h in range(n_head):
-                    out[j * BLOCK : (j + 1) * BLOCK, h * HEAD_SIZE : (h + 1) * HEAD_SIZE] = o[
-                        h * BLOCK : (h + 1) * BLOCK
-                    ]
+                update(held_ref.at[i], base, b, r, top_ref, acc_ref, b)
 
 
 def attention_call(first, last, distances, n_head, starts, recv_starts, operands):
@@ -137,11 +195,11 @@
     if first:
         outs = [jax.ShapeDtypeStruct((blocks, rows, HEAD_SIZE), jnp.bfloat16)] + state
     elif last:
-        outs = [jax.ShapeDtypeStruct((tok, rows), jnp.bfloat16)] * 2
-        scratch += [pltpu.VMEM(s.shape, s.dtype) for s in state]
+        outs = [jax.ShapeDtypeStruct((tok, rows), jnp.bfloat16)]
+        scratch = [pltpu.VMEM((blocks // 2, rows, 2 * HEAD_SIZE), jnp.float32)]
     else:
         outs = state
-    n_pieces = len(distances) + 0.5 * first
+    n_pieces = (len(distances) + 0.5 * first) / (2 if last else 1)
     vmem, smem = pl.BlockSpec(memory_space=pltpu.VMEM), pl.BlockSpec(memory_space=pltpu.SMEM)
     return pl.pallas_call(
         functools.partial(attention_kernel, first, last, distances, n_head),
@@ -169,6 +227,11 @@
     def part(x, index, size):
         return lax.dynamic_slice_in_dim(x, index * size, size, 1)
 
+    def rows_at(index, size=group):
+        return lax.dynamic_slice_in_dim(out_weight, index * size, size, 0)
+
+    cols = out_weight.shape[1] // 2
+    chunk = group // W_CHUNKS
     mine = jnp.concatenate([part(keys, core, HEAD_SIZE), part(values, core, HEAD_SIZE)], 1)
     theirs = jnp.concatenate([part(keys, 1 - core, HEAD_SIZE), part(values, 1 - core, HEAD_SIZE)], 1)
     recv = swap(theirs, 1)
@@ -176,6 +239,11 @@
     one_behind = shift(own, 4)
     q_recv = swap(part(queries, 1 - core, group), 1)
     recv_starts = swap(block_start, 1)
+    sent = part(rows_at(core), 1 - head, cols)
+    over = [
+        cross(sent[n * chunk : (n + 1) * chunk], 0) for n in range(W_CHUNKS)
+    ]
+    weights = [over, [swap(w, 1) for w in over]]
     two_behind = shift(one_behind, 4)
     across = swap(one_behind, 2)
     q, top, acc = attention_call(
@@ -186,19 +254,20 @@
         False, False, ((1, 3), (4, 4)), n_head, block_start, recv_starts,
         (q, top, acc, across, two_behind),
     )
-    o_own, o_other = attention_call(
-        False, True, ((3, 1),), n_head, block_start, recv_starts, (q, top, acc, third)
-    )
-    o_recv = swap(o_other, 1)
-    heads_out = jnp.where(
-        core == 0, jnp.concatenate([o_own, o_recv], 1), jnp.concatenate([o_recv, o_own], 1)
-    )
-    cols = out_weight.shape[1] // 2
-    away = jnp.dot(heads_out, part(out_weight, 1 - head, cols), preferred_element_type=jnp.float32)
-    away = lax.ppermute(away.astype(jnp.bfloat16), "head", [(0, 1), (1, 0)])
-    here = jnp.dot(heads_out, part(out_weight, head, cols), preferred_element_type=jnp.float32)
-    here = here.astype(jnp.bfloat16).astype(jnp.float32)
-    return (here + away.astype(jnp.float32)).astype(jnp.bfloat16)
+    last = [
+        attention_call(
+            False, which, ((3, 1),), n_head, block_start, recv_starts, (q, top, acc, third)
+        )[0]
+        for which in ("own", "other")
+    ]
+    o_across = [cross(last[0], 0), cross(last[1], 1)]
+    o_swapped = swap(last[1], 1)
+    here = sum(
+        jnp.dot(o, part(rows_at(c), head, cols), preferred_element_type=jnp.float32)
+        for o, c in ((last[0], core), (o_swapped, 1 - core))
+    )
+    here = project(here, o_across[0], weights[0], jnp.float32)
+    return project(here, o_across[1], weights[1], jnp.bfloat16)
 
 
 def solution(mesh):

time: 91.6 us -> 99.9 us (1.091)
  local copies, waits for them, and re-layouts: 1.18 us -> 9.62 us
  Pallas kernels: 10.6 us -> 19 us
  waiting for transfers between devices: 56.4 us -> 48.2 us
  starting transfers between devices: 10.9 us -> 14.9 us
  matrix products: 9.16 us -> 5.87 us
  other arithmetic: 1.98 us -> 0.23 us
    pallas_call x0 -> x2, Pallas kernels: none -> 7.21 us  [project(): pl.pallas_call(project_kernel, out_shape=jax.ShapeDtypeStruct(given.shape...]
    ppermute x2, waiting for transfers between devices: 11.1 us -> 7.02 us  [shift(): lax.ppermute(x, 'ctx', [(i, i + distance) for i in range(n - distance)])]
    slice x0 -> x1, local copies, waits for them, and re-layouts: none -> 3.97 us  [per_device(): over = [cross(sent[n * chunk:(n + 1) * chunk], 0) for n in range(W_CHUNKS)]]
    unnamed x4 -> x16, local copies, waits for them, and re-layouts: 0.01 us -> 3.57 us
    dot_general x2, matrix products: 9.16 us -> 5.87 us  [per_device(): jnp.dot(o, part(rows_at(c), head, cols), preferred_element_type=jnp.float32)]
    ppermute x6 -> x8, waiting for transfers between devices: 14.2 us -> 11.3 us  [swap(): lax.ppermute(x, 'ctx', [(i, i ^ mask) for i in range(lax.axis_size('ctx'))])]
    ppermute x1 -> x4, starting transfers between devices: 1.52 us -> 3.72 us  [cross(): return lax.ppermute(x, ('ctx', 'head'), route)]
    ppermute x6 -> x8, starting transfers between devices: 1.48 us -> 3.24 us  [swap(): lax.ppermute(x, 'ctx', [(i, i ^ mask) for i in range(lax.axis_size('ctx'))])]
  transfers between devices with their start and end apart: 9 -> 14, of which waited for: 8 -> 6; matrix products, arithmetic and copies ran while one was open for 5% -> 11% of each run, Pallas kernels for 6% -> 15%
where the time goes in v1:
time: 99.9 us; the launch traced here: 98 us
  waiting for transfers between devices  48.2 us (48%)
  Pallas kernels  19 us (19%)
  starting transfers between devices  14.9 us (15%)
  local copies, waits for them, and re-layouts  9.62 us (10%)
  matrix products  5.87 us (6%)
    ppermute x4, waiting for transfers between devices, cross(): return lax.ppermute(x, ('ctx', 'head'), route)  29.9 us
    pallas_call x4, Pallas kernels, attention_call(): pl.pallas_call(functools.partial(attention_kernel, first, last, distances...  11.8 us
    ppermute x8, waiting for transfers between devices, swap(): lax.ppermute(x, 'ctx', [(i, i ^ mask) for i in range(lax.axis_size('ctx'))])  11.3 us
    ppermute x2, starting transfers between devices, shift(): lax.ppermute(x, 'ctx', [(i, i + distance) for i in range(n - distance)])  7.9 us
    pallas_call x2, Pallas kernels, project(): pl.pallas_call(project_kernel, out_shape=jax.ShapeDtypeStruct(given.shape...  7.21 us
    ppermute x2, waiting for transfers between devices, shift(): lax.ppermute(x, 'ctx', [(i, i + distance) for i in range(n - distance)])  7.02 us
    dot_general x2, matrix products, per_device(): jnp.dot(o, part(rows_at(c), head, cols), preferred_element_type=jnp.float32)  5.87 us
    slice x1, local copies, waits for them, and re-layouts, per_device(): over = [cross(sent[n * chunk:(n + 1) * chunk], 0) for n in range(W_CHUNKS)]  3.97 us
  transfers between devices with their start and end apart: 14, of which 6 were waited for; matrix products, arithmetic and copies ran while one was open for 11% of the time, Pallas kernels for 15%

profile of v1, /device:TPU:2, one launch (start us, length us, event | category | flops | bytes accessed | tf_op | source)
XLA Modules:
  0.0 98.0 jit_solution(17834688427830105729)
XLA Ops:
  0.0 1.1 %constant_dynamic-slice_fusion.2 = (bf16[384,128]{1,0:T(8,128)(2,1)S(1)}, bf16[384,128]{1,0:T(8,128)(2,1)S(1)}, bf16[384,128]{1,0:T(8,128)(2,1)S(1)}, bf16[384,128]{1,0:T(8,128)(2,1)S(1)}) fusion(bf16[384,256]{1,0:T(8,128)(2,1)} %param.7, s32[]{:T(128)S(6)} %select_n.63, s32[]{:T(128)S(6)} %select_n.64, bf16[384,256]{1,0:T(8,128)(2,1)} %param.6), kind=kLoop, calls=%fused_computation.9 | loop fusion | bytes 786440 | tf_op jit(solution)/shard_map/dynamic_slice | solution.py:228
  1.1 0.0 copy-start.6
  1.1 0.0 copy-start.7
  1.1 0.1 collective-permute-start.2
  1.2 1.4 %collective-permute-done.2 = bf16[384,256]{1,0:T(8,128)(2,1)S(1)} collective-permute-done((bf16[384,256]{1,0:T(8,128)(2,1)S(1)}, bf16[384,256]{1,0:T(8,128)(2,1)S(1)}, u32[]{:S(2)}, u32[]{:S(2)}) %collective-permute-start.2) | collective-permute-done | bytes 196640 | tf_op jit(solution)/shard_map/ppermute | solution.py:24
  2.6 0.2 maximum_select_fusion.refs_2_
  2.8 3.5 %collective-permute-start.3 = (bf16[768,256]{1,0:T(8,128)(2,1)S(1)}, bf16[768,256]{1,0:T(8,128)(2,1)S(1)}, u32[]{:S(2)}, u32[]{:S(2)}) collective-permute-start(bf16[768,256]{1,0:T(8,128)(2,1)S(1)} %maximum_select_fusion.refs_2_), channel_id=1, source_target_pairs={{0,8},{2,10},{4,12},{6,14},{8,16},{10,18},{12,20},{14,22},{16,24},... | collective-permute-start | bytes 1179656 | tf_op jit(solution)/shard_map/ppermute | solution.py:20
  6.3 1.0 %constant_dynamic-slice_fusion.4 = bf16[384,512]{1,0:T(8,128)(2,1)S(1)} fusion(bf16[384,1024]{1,0:T(8,128)(2,1)} %refs_0_.1, s32[]{:T(128)S(6)} %select_n.61), kind=kLoop, calls=%fused_computation.11 | loop fusion | bytes 786436 | tf_op jit(solution)/shard_map/dynamic_slice | solution.py:228
  7.3 0.1 collective-permute-start.1
  7.4 0.5 collective-permute-start
  7.9 7.0 %collective-permute-done.3.refs_3_ = bf16[768,256]{1,0:T(8,128)(2,1)S(1)} collective-permute-done((bf16[768,256]{1,0:T(8,128)(2,1)S(1)}, bf16[768,256]{1,0:T(8,128)(2,1)S(1)}, u32[]{:S(2)}, u32[]{:S(2)}) %collective-permute-start.3) | collective-permute-done | bytes 393248 | tf_op jit(solution)/shard_map/ppermute | solution.py:20
  14.9 4.4 %collective-permute-start.5 = (bf16[768,256]{1,0:T(8,128)(2,1)S(1)}, bf16[768,256]{1,0:T(8,128)(2,1)S(1)}, u32[]{:S(2)}, u32[]{:S(2)}) collective-permute-start(bf16[768,256]{1,0:T(8,128)(2,1)S(1)} %collective-permute-done.3.refs_3_), channel_id=1, source_target_pairs={{0,8},{2,10},{4,12},{6,14},{8,16},{10,18},{12,20},{14,22},{16,24},... | collective-permute-start | bytes 1179656 | tf_op jit(solution)/shard_map/ppermute | solution.py:20
  19.4 4.0 %fusion.3 = (bf16[256,2048]{1,0:T(8,128)(2,1)}, bf16[256,2048]{1,0:T(8,128)(2,1)}) fusion(bf16[1024,4096]{1,0:T(8,128)(2,1)} %param.9, s32[]{:T(128)S(6)} %add.49, s32[]{:T(128)S(6)} %select_n.76, s32[]{:T(128)S(6)} %select_n.71), kind=kLoop, calls=%fused_computation.12 | loop fusion | bytes 4194316 | tf_op jit(solution)/shard_map/slice | solution.py:244
  23.3 1.6 %collective-permute-start.10 = (bf16[256,2048]{1,0:T(8,128)(2,1)}, bf16[256,2048]{1,0:T(8,128)(2,1)}, u32[]{:S(2)}, u32[]{:S(2)}) collective-permute-start(bf16[256,2048]{1,0:T(8,128)(2,1)} %get-tuple-element.15), channel_id=1, source_target_pairs={{0,1},{1,0},{2,3},{3,2},{4,5},{5,4},{6,7},{7,6},{8,9},{9,8},{10,11... | collective-permute-start | bytes 3145736 | tf_op jit(solution)/shard_map/ppermute | solution.py:30
  24.9 0.5 collective-permute-start.9
  25.3 0.0 collective-permute-done.recv_starts_ref
  25.3 0.5 collective-permute-start.4
  25.9 0.0 collective-permute-done.1.refs_1_
  25.9 0.0 copy-done.6
  25.9 0.0 copy-done.7
  25.9 3.8 %shard_map.55 = (bf16[6,512,128]{2,1,0:T(8,128)(2,1)S(1)}, f32[6,512,128]{2,1,0:T(8,128)S(1)}, f32[6,512,256]{2,1,0:T(8,128)S(1)}) custom-call(s32[3]{0:T(128)S(1)} %copy-done.7, s32[3]{0:T(128)S(1)} %collective-permute-done.recv_starts_ref, bf16[384,1024]{1,0:T(8,128)(2,1)S(1)} %copy-done.6, bf16[384,512]{1,0:T(8,128)(2,1)S(1)} %collective-permute-done.1.refs_1_, ...), custom_call_target="tpu_custom_call" | custom-call | flops 3623878656 | bytes 8388608 | tf_op jit(solution)/shard_map/pallas_call | solution.py:204
  29.7 0.0 copy-start.2
  29.7 0.0 collective-permute-done.5.refs_4_
  29.7 0.0 copy-start.4
  29.8 1.6 %collective-permute-start.6 = (bf16[768,256]{1,0:T(8,128)(2,1)S(1)}, bf16[768,256]{1,0:T(8,128)(2,1)S(1)}, u32[]{:S(2)}, u32[]{:S(2)}) collective-permute-start(bf16[768,256]{1,0:T(8,128)(2,1)S(1)} %broadcast_select_fusion), channel_id=1, source_target_pairs={{0,4},{2,6},{4,0},{6,2},{8,12},{10,14},{12,8},{14,10},{16,20},{18,... | collective-permute-start | bytes 1179656 | tf_op jit(solution)/shard_map/ppermute | solution.py:24
  31.4 6.0 %collective-permute-done.4.refs_3_ = bf16[768,256]{1,0:T(8,128)(2,1)S(1)} collective-permute-done((bf16[768,256]{1,0:T(8,128)(2,1)S(1)}, bf16[768,256]{1,0:T(8,128)(2,1)S(1)}, u32[]{:S(2)}, u32[]{:S(2)}) %collective-permute-start.4) | collective-permute-done | bytes 393248 | tf_op jit(solution)/shard_map/ppermute | solution.py:24
  37.4 0.0 copy-done.4
  37.4 0.0 copy-start.5
  37.4 1.0 %copy-done.5 = bf16[768,256]{1,0:T(8,128)(2,1)S(1)} copy-done((bf16[768,256]{1,0:T(8,128)(2,1)S(1)}, bf16[768,256]{1,0:T(8,128)(2,1)}, u32[]{:S(2)}) %copy-start.5) | copy-done | bytes 393240
  38.4 1.0 %shard_map.56 = (f32[6,512,128]{2,1,0:T(8,128)S(1)}, f32[6,512,256]{2,1,0:T(8,128)S(1)}) custom-call(s32[3]{0:T(128)S(1)} %copy-done.7, s32[3]{0:T(128)S(1)} %collective-permute-done.recv_starts_ref, bf16[6,512,128]{2,1,0:T(8,128)(2,1)S(1)} %get-tuple-element.10.refs_0_, f32[6,512,128]{2,1,0:T(8,128)S(1)} %get-tuple-element.11.refs_1_, ...), custom_call_target="tpu_custom_call" | custom-call | flops 4831838208 | bytes 8388608 | tf_op jit(solution)/shard_map/pallas_call | solution.py:204
  39.4 0.0 copy-start
  39.4 3.8 %collective-permute-done.6.refs_3_ = bf16[768,256]{1,0:T(8,128)(2,1)S(1)} collective-permute-done((bf16[768,256]{1,0:T(8,128)(2,1)S(1)}, bf16[768,256]{1,0:T(8,128)(2,1)S(1)}, u32[]{:S(2)}, u32[]{:S(2)}) %collective-permute-start.6) | collective-permute-done | bytes 393248 | tf_op jit(solution)/shard_map/ppermute | solution.py:24
  43.3 0.0 copy-done.2
  43.3 4.0 %shard_map.58 = bf16[384,512]{1,0:T(8,128)(2,1)} custom-call(s32[3]{0:T(128)S(1)} %copy-done.7, s32[3]{0:T(128)S(1)} %collective-permute-done.recv_starts_ref, bf16[6,512,128]{2,1,0:T(8,128)(2,1)S(1)} %get-tuple-element.10.refs_0_, f32[6,512,128]{2,1,0:T(8,128)S(1)} %get-tuple-element.13.refs_1_, f32[6,512,256]{2,1,0:T(8,128)S(1)} %get-tuple-element.14.refs_2_, ...), custom_call_target="tpu_custom_call" | custom-call | flops 1207959552 | bytes 8388608 | tf_op jit(solution)/shard_map/pallas_call | solution.py:204
  47.2 0.0 copy-done
  47.2 0.0 collective-permute-start.7
  47.2 23.0 %collective-permute-done.9.refs_2_ = bf16[256,2048]{1,0:T(8,128)(2,1)} collective-permute-done((bf16[256,2048]{1,0:T(8,128)(2,1)}, bf16[256,2048]{1,0:T(8,128)(2,1)}, u32[]{:S(2)}, u32[]{:S(2)}) %collective-permute-start.9) | collective-permute-done | bytes 1048608 | tf_op jit(solution)/shard_map/ppermute | solution.py:30
  70.2 0.0 collective-permute-start.12
  70.2 0.0 collective-permute-done.10.refs_3_
  70.2 0.5 collective-permute-start.13
  70.7 1.2 %collective-permute-start.11 = (bf16[384,512]{1,0:T(8,128)(2,1)}, bf16[384,512]{1,0:T(8,128)(2,1)S(1)}, u32[]{:S(2)}, u32[]{:S(2)}) collective-permute-start(bf16[384,512]{1,0:T(8,128)(2,1)} %shard_map.58), channel_id=1, source_target_pairs={{0,3},{1,2},{2,1},{3,0},{4,7},{5,6},{6,5},{7,4},{8,11},{9,10},{10,... | collective-permute-start | bytes 1179656 | tf_op jit(solution)/shard_map/ppermute | solution.py:30
  71.9 0.0 copy-start.1
  71.9 1.4 %copy-done.1 = f32[6,512,128]{2,1,0:T(8,128)S(1)} copy-done((f32[6,512,128]{2,1,0:T(8,128)S(1)}, f32[6,512,128]{2,1,0:T(8,128)}, u32[]{:S(2)}) %copy-start.1) | copy-done | bytes 1572888
  73.3 0.0 copy-start.3
  73.3 1.1 %copy-done.3 = bf16[6,512,128]{2,1,0:T(8,128)(2,1)S(1)} copy-done((bf16[6,512,128]{2,1,0:T(8,128)(2,1)S(1)}, bf16[6,512,128]{2,1,0:T(8,128)(2,1)}, u32[]{:S(2)}) %copy-start.3) | copy-done | bytes 786456
  74.4 3.0 %shard_map.57 = bf16[384,512]{1,0:T(8,128)(2,1)S(1)} custom-call(s32[3]{0:T(128)S(1)} %copy-done.7, s32[3]{0:T(128)S(1)} %collective-permute-done.recv_starts_ref, bf16[6,512,128]{2,1,0:T(8,128)(2,1)S(1)} %copy-done.3, f32[6,512,128]{2,1,0:T(8,128)S(1)} %copy-done.1, f32[6,512,256]{2,1,0:T(8,128)S(1)} %get-tuple-element.14.refs_2_, ...), custom_call_target="tpu_custom_call" | custom-call | flops 1207959552 | bytes 8388608 | tf_op jit(solution)/shard_map/pallas_call | solution.py:204
  77.4 0.5 collective-permute-start.8
  78.0 0.0 collective-permute-done.7
  78.0 2.9 %fusion = f32[384,2048]{1,0:T(8,128)S(1)} fusion(bf16[384,512]{1,0:T(8,128)(2,1)} %collective-permute-done.7, bf16[1024,4096]{1,0:T(8,128)(2,1)} %param.9, s32[]{:T(128)S(6)} %select_n.74, s32[]{:T(128)S(6)} %select_n.73), kind=kOutput, calls=%fused_computation.1 | convolution fusion | flops 805306368 | bytes 5636104 | tf_op jit(solution)/shard_map/dot_general | solution.py:266
  80.9 2.9 %convolution_add_fusion.refs_0_ = f32[384,2048]{1,0:T(8,128)S(1)} fusion(f32[384,2048]{1,0:T(8,128)S(1)} %fusion, bf16[384,512]{1,0:T(8,128)(2,1)S(1)} %shard_map.57, bf16[1024,4096]{1,0:T(8,128)(2,1)} %param.9, s32[]{:T(128)S(6)} %select_n.71, s32[]{:T(128)S(6)} %select_n.73), kind=kOutput, calls=%fused_computation | convolution fusion | flops 806092800 | bytes 8781832 | tf_op jit(solution)/shard_map/dot_general | solution.py:266
  83.8 6.9 %collective-permute-done.8.refs_1_ = bf16[384,512]{1,0:T(8,128)(2,1)S(1)} collective-permute-done((bf16[384,512]{1,0:T(8,128)(2,1)S(1)}, bf16[384,512]{1,0:T(8,128)(2,1)S(1)}, u32[]{:S(2)}, u32[]{:S(2)}) %collective-permute-start.8) | collective-permute-done | bytes 393248 | tf_op jit(solution)/shard_map/ppermute | solution.py:30
  90.8 3.0 %shard_map.59.refs_0_ = f32[384,2048]{1,0:T(8,128)S(1)} custom-call(f32[384,2048]{1,0:T(8,128)S(1)} %convolution_add_fusion.refs_0_, bf16[384,512]{1,0:T(8,128)(2,1)S(1)} %collective-permute-done.8.refs_1_, bf16[256,2048]{1,0:T(8,128)(2,1)} %collective-permute-done.9.refs_2_, bf16[256,2048]{1,0:T(8,128)(2,1)} %collective-permute-done.10.refs_3_), custom_call_target="tpu_custom_call" | custom-call | flops 805306368 | bytes 8388608 | tf_op jit(solution)/shard_map/pallas_call | solution.py:52
  93.8 0.0 collective-permute-done.11.refs_1_
  93.8 0.0 collective-permute-done.12.refs_2_
  93.8 0.0 collective-permute-done.13.refs_3_
  93.8 4.2 %shard_map.60 = bf16[384,2048]{1,0:T(8,128)(2,1)} custom-call(f32[384,2048]{1,0:T(8,128)S(1)} %shard_map.59.refs_0_, bf16[384,512]{1,0:T(8,128)(2,1)S(1)} %collective-permute-done.11.refs_1_, bf16[256,2048]{1,0:T(8,128)(2,1)} %collective-permute-done.12.refs_2_, bf16[256,2048]{1,0:T(8,128)(2,1)} %collective-permute-done.13.refs_3_), custom_call_target="tpu_custom_call" | custom-call | flops 805306368 | bytes 8388608 | tf_op jit(solution)/shard_map/pallas_call | solution.py:52
  (2 shorter events, 0.1 us)
Async XLA Ops:
  1.1 24.8 %copy-start.6 = (bf16[384,1024]{1,0:T(8,128)(2,1)S(1)}, bf16[384,1024]{1,0:T(8,128)(2,1)}, u32[]{:S(2)}) copy-start(bf16[384,1024]{1,0:T(8,128)(2,1)} %refs_0_.1) | copy-start | bytes 2359300
  1.1 24.8 %copy-start.7 = (s32[3]{0:T(128)S(1)}, s32[3]{0:T(128)}, u32[]{:S(2)}) copy-start(s32[3]{0:T(128)} %starts_ref.7) | copy-start | bytes 40
  1.1 1.5 %collective-permute-start.2 = (bf16[384,256]{1,0:T(8,128)(2,1)S(1)}, bf16[384,256]{1,0:T(8,128)(2,1)S(1)}, u32[]{:S(2)}, u32[]{:S(2)}) collective-permute-start(bf16[384,256]{1,0:T(8,128)(2,1)S(1)} %pad_maximum_fusion), channel_id=1, source_target_pairs={{0,2},{2,0},{4,6},{6,4},{8,10},{10,8},{12,14},{14,12},{16,18},{18,... | collective-permute-start | bytes 589832 | tf_op jit(solution)/shard_map/ppermute | solution.py:24
  2.8 12.1 %collective-permute-start.3 = (bf16[768,256]{1,0:T(8,128)(2,1)S(1)}, bf16[768,256]{1,0:T(8,128)(2,1)S(1)}, u32[]{:S(2)}, u32[]{:S(2)}) collective-permute-start(bf16[768,256]{1,0:T(8,128)(2,1)S(1)} %maximum_select_fusion.refs_2_), channel_id=1, source_target_pairs={{0,8},{2,10},{4,12},{6,14},{8,16},{10,18},{12,20},{14,22},{16,24},... | collective-permute-start | bytes 1179656 | tf_op jit(solution)/shard_map/ppermute | solution.py:20
  7.3 18.5 %collective-permute-start.1 = (bf16[384,512]{1,0:T(8,128)(2,1)S(1)}, bf16[384,512]{1,0:T(8,128)(2,1)S(1)}, u32[]{:S(2)}, u32[]{:S(2)}) collective-permute-start(bf16[384,512]{1,0:T(8,128)(2,1)S(1)} %constant_dynamic-slice_fusion.4), channel_id=1, source_target_pairs={{0,2},{2,0},{4,6},{6,4},{8,10},{10,8},{12,14},{14,12},{16,18},{18,... | collective-permute-start | bytes 1179656 | tf_op jit(solution)/shard_map/ppermute | solution.py:24
  7.4 17.9 %collective-permute-start = (s32[3]{0:T(128)}, s32[3]{0:T(128)S(1)}, u32[]{:S(2)}, u32[]{:S(2)}) collective-permute-start(s32[3]{0:T(128)} %starts_ref.7), channel_id=1, source_target_pairs={{0,2},{2,0},{4,6},{6,4},{8,10},{10,8},{12,14},{14,12},{16,18},{18,... | collective-permute-start | bytes 44 | tf_op jit(solution)/shard_map/ppermute | solution.py:24
  14.9 14.8 %collective-permute-start.5 = (bf16[768,256]{1,0:T(8,128)(2,1)S(1)}, bf16[768,256]{1,0:T(8,128)(2,1)S(1)}, u32[]{:S(2)}, u32[]{:S(2)}) collective-permute-start(bf16[768,256]{1,0:T(8,128)(2,1)S(1)} %collective-permute-done.3.refs_3_), channel_id=1, source_target_pairs={{0,8},{2,10},{4,12},{6,14},{8,16},{10,18},{12,20},{14,22},{16,24},... | collective-permute-start | bytes 1179656 | tf_op jit(solution)/shard_map/ppermute | solution.py:20
  23.3 46.9 %collective-permute-start.10 = (bf16[256,2048]{1,0:T(8,128)(2,1)}, bf16[256,2048]{1,0:T(8,128)(2,1)}, u32[]{:S(2)}, u32[]{:S(2)}) collective-permute-start(bf16[256,2048]{1,0:T(8,128)(2,1)} %get-tuple-element.15), channel_id=1, source_target_pairs={{0,1},{1,0},{2,3},{3,2},{4,5},{5,4},{6,7},{7,6},{8,9},{9,8},{10,11... | collective-permute-start | bytes 3145736 | tf_op jit(solution)/shard_map/ppermute | solution.py:30
  24.9 45.3 %collective-permute-start.9 = (bf16[256,2048]{1,0:T(8,128)(2,1)}, bf16[256,2048]{1,0:T(8,128)(2,1)}, u32[]{:S(2)}, u32[]{:S(2)}) collective-permute-start(bf16[256,2048]{1,0:T(8,128)(2,1)} %get-tuple-element.16), channel_id=1, source_target_pairs={{0,1},{1,0},{2,3},{3,2},{4,5},{5,4},{6,7},{7,6},{8,9},{9,8},{10,11... | collective-permute-start | bytes 3145736 | tf_op jit(solution)/shard_map/ppermute | solution.py:30
  25.3 12.1 %collective-permute-start.4 = (bf16[768,256]{1,0:T(8,128)(2,1)S(1)}, bf16[768,256]{1,0:T(8,128)(2,1)S(1)}, u32[]{:S(2)}, u32[]{:S(2)}) collective-permute-start(bf16[768,256]{1,0:T(8,128)(2,1)S(1)} %collective-permute-done.3.refs_3_), channel_id=1, source_target_pairs={{0,4},{2,6},{4,0},{6,2},{8,12},{10,14},{12,8},{14,10},{16,20},{18,... | collective-permute-start | bytes 1179656 | tf_op jit(solution)/shard_map/ppermute | solution.py:24
  29.7 13.5 %copy-start.2 = (bf16[6,512,128]{2,1,0:T(8,128)(2,1)}, bf16[6,512,128]{2,1,0:T(8,128)(2,1)S(1)}, u32[]{:S(2)}) copy-start(bf16[6,512,128]{2,1,0:T(8,128)(2,1)S(1)} %get-tuple-element.10.refs_0_) | copy-start | bytes 2359300
  29.7 7.7 %copy-start.4 = (bf16[768,256]{1,0:T(8,128)(2,1)}, bf16[768,256]{1,0:T(8,128)(2,1)S(1)}, u32[]{:S(2)}) copy-start(bf16[768,256]{1,0:T(8,128)(2,1)S(1)} %collective-permute-done.5.refs_4_) | copy-start | bytes 1179652
  29.8 13.5 %collective-permute-start.6 = (bf16[768,256]{1,0:T(8,128)(2,1)S(1)}, bf16[768,256]{1,0:T(8,128)(2,1)S(1)}, u32[]{:S(2)}, u32[]{:S(2)}) collective-permute-start(bf16[768,256]{1,0:T(8,128)(2,1)S(1)} %broadcast_select_fusion), channel_id=1, source_target_pairs={{0,4},{2,6},{4,0},{6,2},{8,12},{10,14},{12,8},{14,10},{16,20},{18,... | collective-permute-start | bytes 1179656 | tf_op jit(solution)/shard_map/ppermute | solution.py:24
  37.4 1.0 %copy-start.5 = (bf16[768,256]{1,0:T(8,128)(2,1)S(1)}, bf16[768,256]{1,0:T(8,128)(2,1)}, u32[]{:S(2)}) copy-start(bf16[768,256]{1,0:T(8,128)(2,1)} %copy-done.4) | copy-start | bytes 1179652
  39.4 7.8 %copy-start = (f32[6,512,128]{2,1,0:T(8,128)}, f32[6,512,128]{2,1,0:T(8,128)S(1)}, u32[]{:S(2)}) copy-start(f32[6,512,128]{2,1,0:T(8,128)S(1)} %get-tuple-element.13.refs_1_) | copy-start | bytes 4718596
  47.2 30.7 %collective-permute-start.7 = (bf16[384,512]{1,0:T(8,128)(2,1)}, bf16[384,512]{1,0:T(8,128)(2,1)}, u32[]{:S(2)}, u32[]{:S(2)}) collective-permute-start(bf16[384,512]{1,0:T(8,128)(2,1)} %shard_map.58), channel_id=1, source_target_pairs={{0,2},{2,0},{4,6},{6,4},{8,10},{10,8},{12,14},{14,12},{16,18},{18,... | collective-permute-start | bytes 1179656 | tf_op jit(solution)/shard_map/ppermute | solution.py:24
  70.2 23.6 %collective-permute-start.12 = (bf16[256,2048]{1,0:T(8,128)(2,1)}, bf16[256,2048]{1,0:T(8,128)(2,1)}, u32[]{:S(2)}, u32[]{:S(2)}) collective-permute-start(bf16[256,2048]{1,0:T(8,128)(2,1)} %collective-permute-done.9.refs_2_), channel_id=1, source_target_pairs={{0,2},{2,0},{4,6},{6,4},{8,10},{10,8},{12,14},{14,12},{16,18},{18,... | collective-permute-start | bytes 3145736 | tf_op jit(solution)/shard_map/ppermute | solution.py:24
  70.2 23.6 %collective-permute-start.13 = (bf16[256,2048]{1,0:T(8,128)(2,1)}, bf16[256,2048]{1,0:T(8,128)(2,1)}, u32[]{:S(2)}, u32[]{:S(2)}) collective-permute-start(bf16[256,2048]{1,0:T(8,128)(2,1)} %collective-permute-done.10.refs_3_), channel_id=1, source_target_pairs={{0,2},{2,0},{4,6},{6,4},{8,10},{10,8},{12,14},{14,12},{16,18},{18,... | collective-permute-start | bytes 3145736 | tf_op jit(solution)/shard_map/ppermute | solution.py:24
  70.7 23.1 %collective-permute-start.11 = (bf16[384,512]{1,0:T(8,128)(2,1)}, bf16[384,512]{1,0:T(8,128)(2,1)S(1)}, u32[]{:S(2)}, u32[]{:S(2)}) collective-permute-start(bf16[384,512]{1,0:T(8,128)(2,1)} %shard_map.58), channel_id=1, source_target_pairs={{0,3},{1,2},{2,1},{3,0},{4,7},{5,6},{6,5},{7,4},{8,11},{9,10},{10,... | collective-permute-start | bytes 1179656 | tf_op jit(solution)/shard_map/ppermute | solution.py:30
  71.9 1.4 %copy-start.1 = (f32[6,512,128]{2,1,0:T(8,128)S(1)}, f32[6,512,128]{2,1,0:T(8,128)}, u32[]{:S(2)}) copy-start(f32[6,512,128]{2,1,0:T(8,128)} %copy-done) | copy-start | bytes 4718596
  73.3 1.1 %copy-start.3 = (bf16[6,512,128]{2,1,0:T(8,128)(2,1)S(1)}, bf16[6,512,128]{2,1,0:T(8,128)(2,1)}, u32[]{:S(2)}) copy-start(bf16[6,512,128]{2,1,0:T(8,128)(2,1)} %copy-done.2) | copy-start | bytes 2359300
  77.4 13.3 %collective-permute-start.8 = (bf16[384,512]{1,0:T(8,128)(2,1)S(1)}, bf16[384,512]{1,0:T(8,128)(2,1)S(1)}, u32[]{:S(2)}, u32[]{:S(2)}) collective-permute-start(bf16[384,512]{1,0:T(8,128)(2,1)S(1)} %shard_map.57), channel_id=1, source_target_pairs={{0,1},{1,0},{2,3},{3,2},{4,5},{5,4},{6,7},{7,6},{8,9},{9,8},{10,11... | collective-permute-start | bytes 1179656 | tf_op jit(solution)/shard_map/ppermute | solution.py:30

commit v2 on v1

--- a/solution.py
+++ b/solution.py
@@ -11,7 +11,6 @@
 BLOCK = 128
 LOG2E = 1.4426950408889634
 MASKED = -1e30
-W_CHUNKS = 2
 TILE = 256
 
 
@@ -30,40 +29,32 @@
     return lax.ppermute(x, ("ctx", "head"), route)
 
 
-def project_kernel(*refs):
-    given_ref, heads_ref, *chunk_refs, out_ref = refs
-    chunk = chunk_refs[0].shape[0]
-
-    @pl.loop(0, out_ref.shape[1] // 512)
-    def _(n):
-        cols = pl.ds(pl.multiple_of(n * 512, 512), 512)
-        total = given_ref[:, cols]
-        for m, ref in enumerate(chunk_refs):
-            total += jnp.dot(
-                heads_ref[:, m * chunk : (m + 1) * chunk],
-                ref[:, cols],
-                preferred_element_type=jnp.float32,
-            )
-        out_ref[:, cols] = total.astype(out_ref.dtype)
-
-
-def project(given, heads, chunks, dtype):
+def project_kernel(given_ref, heads_a, rows_a, heads_b, rows_b, out_ref):
+    width = out_ref.shape[1]
+    cols = pl.ds(pl.multiple_of(pl.program_id(0) * width, width), width)
+    total = given_ref[:, cols].astype(jnp.float32)
+    for heads, rows in ((heads_a, rows_a), (heads_b, rows_b)):
+        total += jnp.dot(heads[...], rows[:, cols], preferred_element_type=jnp.float32)
+    out_ref[...] = total.astype(out_ref.dtype)
+
+
+def project(given, *terms):
+    tok, cols = given.shape
     vmem = pl.BlockSpec(memory_space=pltpu.VMEM)
     return pl.pallas_call(
         project_kernel,
-        out_shape=jax.ShapeDtypeStruct(given.shape, dtype),
-        in_specs=[vmem] * (2 + len(chunks)),
-        out_specs=vmem,
-        compiler_params=pltpu.CompilerParams(vmem_limit_bytes=40 * 2**20),
+        grid=(cols // 512,),
+        out_shape=jax.ShapeDtypeStruct(given.shape, jnp.bfloat16),
+        in_specs=[vmem] * 5,
+        out_specs=pl.BlockSpec((tok, 512), lambda n: (0, n)),
+        compiler_params=pltpu.CompilerParams(vmem_limit_bytes=16 * 2**20),
         cost_estimate=pl.CostEstimate(
-            flops=2 * heads.shape[0] * heads.shape[1] * given.shape[1],
-            bytes_accessed=8 * 2**20,
-            transcendentals=0,
+            flops=4 * tok * terms[0].shape[1] * cols, bytes_accessed=8 * 2**20, transcendentals=0
         ),
-    )(given, heads, *chunks)
-
-
-def attention_kernel(first, last, distances, n_head, starts_ref, recv_starts_ref, *refs):
+    )(given, *terms)
+
+
+def attention_kernel(first, last, distances, n_head, n_after, starts_ref, recv_starts_ref, *refs):
     refs = list(refs)
     me = lax.axis_index("ctx")
     pair, core, col = me // 2, me % 2, (me // 2) % 2
@@ -74,11 +65,11 @@
         q_ref, top_in, acc_in = refs[:3]
         refs = refs[3:]
     pieces = refs[: len(distances)]
-    refs = refs[len(distances) :]
+    refs = refs[len(distances) + n_after :]
     if first:
         q_ref, top_ref, acc_ref, held_ref = refs
     elif last:
-        out_ref, acc_ref = refs
+        out_ref, acc_ref = refs[0], refs[-1]
     else:
         top_ref, acc_ref, held_ref = refs
     tok = starts_ref.shape[0] * BLOCK
@@ -184,7 +175,7 @@
                 update(held_ref.at[i], base, b, r, top_ref, acc_ref, b)
 
 
-def attention_call(first, last, distances, n_head, starts, recv_starts, operands):
+def attention_call(first, last, distances, n_head, starts, recv_starts, operands, held=(), after=()):
     tok = starts.shape[0] * BLOCK
     blocks, rows = 2 * starts.shape[0], n_head * BLOCK
     state = [
@@ -202,18 +193,19 @@
     n_pieces = (len(distances) + 0.5 * first) / (2 if last else 1)
     vmem, smem = pl.BlockSpec(memory_space=pltpu.VMEM), pl.BlockSpec(memory_space=pltpu.SMEM)
     return pl.pallas_call(
-        functools.partial(attention_kernel, first, last, distances, n_head),
-        out_shape=outs,
-        in_specs=[smem, smem] + [vmem] * len(operands),
-        out_specs=[vmem] * len(outs),
+        functools.partial(attention_kernel, first, last, distances, n_head, len(held + after)),
+        out_shape=outs + [jax.ShapeDtypeStruct(x.shape, x.dtype) for x in held],
+        in_specs=[smem, smem] + [vmem] * len(operands) + [pl.BlockSpec(memory_space=pl.ANY)] * len(held + after),
+        out_specs=[vmem] * len(outs) + [pl.BlockSpec(memory_space=pl.ANY)] * len(held),
         scratch_shapes=scratch,
-        compiler_params=pltpu.CompilerParams(vmem_limit_bytes=40 * 2**20),
+        input_output_aliases={2 + len(operands) + n: len(outs) + n for n in range(len(held))},
+        compiler_params=pltpu.CompilerParams(vmem_limit_bytes=24 * 2**20),
         cost_estimate=pl.CostEstimate(
             flops=int(n_pieces * blocks * rows * 2 * tok * HEAD_SIZE * 8),
             bytes_accessed=8 * 2**20,
             transcendentals=int(n_pieces * blocks * rows * 2 * tok),
         ),
-    )(starts, recv_starts, *operands)
+    )(starts, recv_starts, *operands, *held, *after)
 
 
 def per_device(queries, keys, values, block_start, out_weight):
@@ -227,11 +219,10 @@
     def part(x, index, size):
         return lax.dynamic_slice_in_dim(x, index * size, size, 1)
 
-    def rows_at(index, size=group):
-        return lax.dynamic_slice_in_dim(out_weight, index * size, size, 0)
+    def rows_at(index):
+        return lax.dynamic_slice_in_dim(out_weight, index * group, group, 0)
 
     cols = out_weight.shape[1] // 2
-    chunk = group // W_CHUNKS
     mine = jnp.concatenate([part(keys, core, HEAD_SIZE), part(values, core, HEAD_SIZE)], 1)
     theirs = jnp.concatenate([part(keys, 1 - core, HEAD_SIZE), part(values, 1 - core, HEAD_SIZE)], 1)
     recv = swap(theirs, 1)
@@ -239,11 +230,7 @@
     one_behind = shift(own, 4)
     q_recv = swap(part(queries, 1 - core, group), 1)
     recv_starts = swap(block_start, 1)
-    sent = part(rows_at(core), 1 - head, cols)
-    over = [
-        cross(sent[n * chunk : (n + 1) * chunk], 0) for n in range(W_CHUNKS)
-    ]
-    weights = [over, [swap(w, 1) for w in over]]
+    rows_own = cross(part(rows_at(core), 1 - head, cols), 0)
     two_behind = shift(one_behind, 4)
     across = swap(one_behind, 2)
     q, top, acc = attention_call(
@@ -254,20 +241,18 @@
         False, False, ((1, 3), (4, 4)), n_head, block_start, recv_starts,
         (q, top, acc, across, two_behind),
     )
-    last = [
-        attention_call(
-            False, which, ((3, 1),), n_head, block_start, recv_starts, (q, top, acc, third)
-        )[0]
-        for which in ("own", "other")
-    ]
-    o_across = [cross(last[0], 0), cross(last[1], 1)]
-    o_swapped = swap(last[1], 1)
-    here = sum(
-        jnp.dot(o, part(rows_at(c), head, cols), preferred_element_type=jnp.float32)
-        for o, c in ((last[0], core), (o_swapped, 1 - core))
-    )
-    here = project(here, o_across[0], weights[0], jnp.float32)
-    return project(here, o_across[1], weights[1], jnp.bfloat16)
+    args = (((3, 1),), n_head, block_start, recv_starts, (q, top, acc, third))
+    (o_other,) = attention_call(False, "other", *args)
+    across_other = cross(o_other, 1)
+    swapped_other = swap(o_other, 1)
+    o_own, rows_own = attention_call(False, "own", *args, (rows_own,), (o_other,))
+    across_own = cross(o_own, 0)
+    rows_other = swap(rows_own, 1)
+    here = jnp.dot(o_own, part(rows_at(core), head, cols), preferred_element_type=jnp.float32)
+    here += jnp.dot(
+        swapped_other, part(rows_at(1 - core), head, cols), preferred_element_type=jnp.float32
+    )
+    return project(here.astype(jnp.bfloat16), across_own, rows_own, across_other, rows_other)
 
 
 def solution(mesh):

time: 99.9 us -> 80.7 us (0.81); the launches traced: 98 us -> 80.1 us
  waiting for transfers between devices: 48.2 us -> 35.5 us
  Pallas kernels: 19 us -> 16.4 us
  local copies, waits for them, and re-layouts: 9.62 us -> 7.15 us
  starting transfers between devices: 14.9 us -> 13.9 us
    ppermute x4 -> x3, waiting for transfers between devices: 29.9 us -> 12.3 us  [cross(): return lax.ppermute(x, ('ctx', 'head'), route)]
    slice x1 -> x0, local copies, waits for them, and re-layouts: 3.97 us -> none  [per_device(): over = [cross(sent[n * chunk:(n + 1) * chunk], 0) for n in range(W_CHUNKS)]]
    dynamic_slice x2 -> x3, local copies, waits for them, and re-layouts: 2.09 us -> 6 us  [part(): return lax.dynamic_slice_in_dim(x, index * size, size, 1)]
    ppermute x8 -> x7, waiting for transfers between devices: 11.3 us -> 14.6 us  [swap(): lax.ppermute(x, 'ctx', [(i, i ^ mask) for i in range(lax.axis_size('ctx'))])]
    unnamed x16 -> x8, local copies, waits for them, and re-layouts: 3.57 us -> 1.15 us
    pallas_call x2 -> x1, Pallas kernels: 7.21 us -> 4.86 us  [project(): pl.pallas_call(project_kernel, grid=(cols // 512,), out_shape=jax.ShapeDt...]
    ppermute x2, waiting for transfers between devices: 7.02 us -> 8.59 us  [shift(): lax.ppermute(x, 'ctx', [(i, i + distance) for i in range(n - distance)])]
    ppermute x8 -> x7, starting transfers between devices: 3.24 us -> 1.91 us  [swap(): lax.ppermute(x, 'ctx', [(i, i ^ mask) for i in range(lax.axis_size('ctx'))])]
  transfers between devices with their start and end apart: 14 -> 12, of which waited for: 6 -> 10; matrix products, arithmetic and copies ran while one was open for 11% -> 11% of each run, Pallas kernels for 15% -> 11%
where the time goes in v2:
time: 80.7 us; the launch traced here: 80.1 us
  waiting for transfers between devices  35.5 us (44%)
  Pallas kernels  16.4 us (20%)
  starting transfers between devices  13.9 us (17%)
  local copies, waits for them, and re-layouts  7.15 us (9%)
  matrix products  5.8 us (7%)
  other arithmetic  1.22 us (2%)
    ppermute x7, waiting for transfers between devices, swap(): lax.ppermute(x, 'ctx', [(i, i ^ mask) for i in range(lax.axis_size('ctx'))])  14.6 us
    ppermute x3, waiting for transfers between devices, cross(): return lax.ppermute(x, ('ctx', 'head'), route)  12.3 us
    pallas_call x4, Pallas kernels, attention_call(): pl.pallas_call(functools.partial(attention_kernel, first, last, distances...  11.5 us
    ppermute x2, starting transfers between devices, shift(): lax.ppermute(x, 'ctx', [(i, i + distance) for i in range(n - distance)])  8.74 us
    ppermute x2, waiting for transfers between devices, shift(): lax.ppermute(x, 'ctx', [(i, i + distance) for i in range(n - distance)])  8.59 us
    dynamic_slice x3, local copies, waits for them, and re-layouts, part(): return lax.dynamic_slice_in_dim(x, index * size, size, 1)  6 us
    pallas_call x1, Pallas kernels, project(): pl.pallas_call(project_kernel, grid=(cols // 512,), out_shape=jax.ShapeDt...  4.86 us
    ppermute x3, starting transfers between devices, cross(): return lax.ppermute(x, ('ctx', 'head'), route)  3.27 us
  transfers between devices with their start and end apart: 12, of which 10 were waited for; matrix products, arithmetic and copies ran while one was open for 11% of the time, Pallas kernels for 11%

profile of v2, /device:TPU:2, one launch (start us, length us, event | category | flops | bytes accessed | tf_op | source)
XLA Modules:
  0.0 80.1 jit_solution(765876548747028467)
XLA Ops:
  0.0 0.0 copy-start.3
  0.0 0.0 copy-start
  0.0 4.2 %dynamic_slice.32 = bf16[512,2048]{1,0:T(8,128)(2,1)} dynamic-slice(bf16[1024,4096]{1,0:T(8,128)(2,1)} %param.9, s32[]{:T(128)S(6)} %select_n.71, s32[]{:T(128)S(6)} %select_n.73), dynamic_slice_sizes={512,2048} | dynamic-slice | bytes 4194308 | tf_op jit(solution)/shard_map/dynamic_slice | solution.py:220
  4.3 0.0 copy-start.2
  4.3 1.6 %collective-permute-start.7 = (bf16[512,2048]{1,0:T(8,128)(2,1)}, bf16[512,2048]{1,0:T(8,128)(2,1)S(1)}, u32[]{:S(2)}, u32[]{:S(2)}) collective-permute-start(bf16[512,2048]{1,0:T(8,128)(2,1)} %dynamic_slice.32), channel_id=1, source_target_pairs={{0,1},{1,0},{2,3},{3,2},{4,5},{5,4},{6,7},{7,6},{8,9},{9,8},{10,11... | collective-permute-start | bytes 6291464 | tf_op jit(solution)/shard_map/ppermute | solution.py:29
  5.8 0.0 copy-done.3
  5.8 1.0 %constant_dynamic-slice_fusion.2 = (bf16[384,128]{1,0:T(8,128)(2,1)S(1)}, bf16[384,128]{1,0:T(8,128)(2,1)S(1)}, bf16[384,128]{1,0:T(8,128)(2,1)S(1)}, bf16[384,128]{1,0:T(8,128)(2,1)S(1)}) fusion(bf16[384,256]{1,0:T(8,128)(2,1)S(1)} %copy-done.3, s32[]{:T(128)S(6)} %select_n.63, s32[]{:T(128)S(6)} %select_n.64, bf16[384,256]{1,0:T(8,128)(2,1)} %param.6), kind=kLoop, calls=%fused_computation.9 | loop fusion | bytes 786440 | tf_op jit(solution)/shard_map/dynamic_slice | solution.py:220
  6.8 0.1 collective-permute-start.2
  6.9 1.5 %collective-permute-done.2 = bf16[384,256]{1,0:T(8,128)(2,1)} collective-permute-done((bf16[384,256]{1,0:T(8,128)(2,1)S(1)}, bf16[384,256]{1,0:T(8,128)(2,1)}, u32[]{:S(2)}, u32[]{:S(2)}) %collective-permute-start.2) | collective-permute-done | bytes 196640 | tf_op jit(solution)/shard_map/ppermute | solution.py:23
  8.5 1.2 %maximum_select_fusion.refs_2_ = bf16[768,256]{1,0:T(8,128)(2,1)S(1)} fusion(bf16[384,256]{1,0:T(8,128)(2,1)} %collective-permute-done.2, bf16[384,128]{1,0:T(8,128)(2,1)S(1)} %get-tuple-element.21, bf16[384,128]{1,0:T(8,128)(2,1)S(1)} %get-tuple-element.24, pred[]{:T(512)S(6)} %eq.9), kind=kLoop, calls=%fused_computation.4 | loop fusion | flops 2555904 | bytes 786433 | tf_op jit(solution)/shard_map/jit(_where)/select_n | solution.py:229
  9.6 4.2 %collective-permute-start.3 = (bf16[768,256]{1,0:T(8,128)(2,1)S(1)}, bf16[768,256]{1,0:T(8,128)(2,1)}, u32[]{:S(2)}, u32[]{:S(2)}) collective-permute-start(bf16[768,256]{1,0:T(8,128)(2,1)S(1)} %maximum_select_fusion.refs_2_), channel_id=1, source_target_pairs={{0,8},{2,10},{4,12},{6,14},{8,16},{10,18},{12,20},{14,22},{16,24},... | collective-permute-start | bytes 1179656 | tf_op jit(solution)/shard_map/ppermute | solution.py:19
  13.9 0.0 copy-done
  13.9 0.8 constant_dynamic-slice_fusion.4
  14.6 0.0 collective-permute-start.1
  14.6 7.1 %collective-permute-done.3.refs_3_ = bf16[768,256]{1,0:T(8,128)(2,1)} collective-permute-done((bf16[768,256]{1,0:T(8,128)(2,1)S(1)}, bf16[768,256]{1,0:T(8,128)(2,1)}, u32[]{:S(2)}, u32[]{:S(2)}) %collective-permute-start.3) | collective-permute-done | bytes 393248 | tf_op jit(solution)/shard_map/ppermute | solution.py:19
  21.8 4.5 %collective-permute-start.5 = (bf16[768,256]{1,0:T(8,128)(2,1)}, bf16[768,256]{1,0:T(8,128)(2,1)S(1)}, u32[]{:S(2)}, u32[]{:S(2)}) collective-permute-start(bf16[768,256]{1,0:T(8,128)(2,1)} %collective-permute-done.3.refs_3_), channel_id=1, source_target_pairs={{0,8},{2,10},{4,12},{6,14},{8,16},{10,18},{12,20},{14,22},{16,24},... | collective-permute-start | bytes 1179656 | tf_op jit(solution)/shard_map/ppermute | solution.py:19
  26.3 0.0 copy-done.2
  26.3 0.1 collective-permute-start
  26.4 0.6 collective-permute-start.4
  27.0 0.5 collective-permute-done.recv_starts_ref
  27.5 0.0 collective-permute-done.1.refs_1_
  27.5 0.0 copy-start.1
  27.5 1.1 %copy-done.1 = bf16[384,1024]{1,0:T(8,128)(2,1)S(1)} copy-done((bf16[384,1024]{1,0:T(8,128)(2,1)S(1)}, bf16[384,1024]{1,0:T(8,128)(2,1)}, u32[]{:S(2)}) %copy-start.1) | copy-done | bytes 786456
  28.6 4.3 %shard_map.55 = (bf16[6,512,128]{2,1,0:T(8,128)(2,1)S(1)}, f32[6,512,128]{2,1,0:T(8,128)S(1)}, f32[6,512,256]{2,1,0:T(8,128)S(1)}) custom-call(s32[3]{0:T(128)S(1)} %copy-done.2, s32[3]{0:T(128)S(1)} %collective-permute-done.recv_starts_ref, bf16[384,1024]{1,0:T(8,128)(2,1)S(1)} %copy-done.1, bf16[384,512]{1,0:T(8,128)(2,1)} %collective-permute-done.1.refs_1_, ...), custom_call_target="tpu_custom_call" | custom-call | flops 3623878656 | bytes 8388608 | tf_op jit(solution)/shard_map/pallas_call | solution.py:195
  33.0 1.5 %collective-permute-done.5.refs_4_ = bf16[768,256]{1,0:T(8,128)(2,1)S(1)} collective-permute-done((bf16[768,256]{1,0:T(8,128)(2,1)}, bf16[768,256]{1,0:T(8,128)(2,1)S(1)}, u32[]{:S(2)}, u32[]{:S(2)}) %collective-permute-start.5) | collective-permute-done | bytes 393248 | tf_op jit(solution)/shard_map/ppermute | solution.py:19
  34.5 0.6 collective-permute-start.6
  35.1 3.5 %collective-permute-done.4.refs_3_ = bf16[768,256]{1,0:T(8,128)(2,1)S(1)} collective-permute-done((bf16[768,256]{1,0:T(8,128)(2,1)}, bf16[768,256]{1,0:T(8,128)(2,1)S(1)}, u32[]{:S(2)}, u32[]{:S(2)}) %collective-permute-start.4) | collective-permute-done | bytes 393248 | tf_op jit(solution)/shard_map/ppermute | solution.py:23
  38.6 1.0 %shard_map.56 = (f32[6,512,128]{2,1,0:T(8,128)S(1)}, f32[6,512,256]{2,1,0:T(8,128)S(1)}) custom-call(s32[3]{0:T(128)S(1)} %copy-done.2, s32[3]{0:T(128)S(1)} %collective-permute-done.recv_starts_ref, bf16[6,512,128]{2,1,0:T(8,128)(2,1)S(1)} %get-tuple-element.12.refs_0_, f32[6,512,128]{2,1,0:T(8,128)S(1)} %get-tuple-element.13.refs_1_, ...), custom_call_target="tpu_custom_call" | custom-call | flops 4831838208 | bytes 8388608 | tf_op jit(solution)/shard_map/pallas_call | solution.py:195
  39.6 6.9 %collective-permute-done.6.refs_3_ = bf16[768,256]{1,0:T(8,128)(2,1)S(1)} collective-permute-done((bf16[768,256]{1,0:T(8,128)(2,1)S(1)}, bf16[768,256]{1,0:T(8,128)(2,1)S(1)}, u32[]{:S(2)}, u32[]{:S(2)}) %collective-permute-start.6) | collective-permute-done | bytes 393248 | tf_op jit(solution)/shard_map/ppermute | solution.py:23
  46.6 3.2 %shard_map.57.refs_5_ = bf16[384,512]{1,0:T(8,128)(2,1)S(1)} custom-call(s32[3]{0:T(128)S(1)} %copy-done.2, s32[3]{0:T(128)S(1)} %collective-permute-done.recv_starts_ref, bf16[6,512,128]{2,1,0:T(8,128)(2,1)S(1)} %get-tuple-element.12.refs_0_, f32[6,512,128]{2,1,0:T(8,128)S(1)} %get-tuple-element.15.refs_1_, f32[6,512,256]{2,1,0:T(8,128)S(1)} %get-tuple-element.16.refs_2_, ...), custom_call_target="tpu_custom_call" | custom-call | flops 1207959552 | bytes 8388608 | tf_op jit(solution)/shard_map/pallas_call | solution.py:195
  49.8 2.1 %collective-permute-done.7.refs_4_ = bf16[512,2048]{1,0:T(8,128)(2,1)S(1)} collective-permute-done((bf16[512,2048]{1,0:T(8,128)(2,1)}, bf16[512,2048]{1,0:T(8,128)(2,1)S(1)}, u32[]{:S(2)}, u32[]{:S(2)}) %collective-permute-start.7) | collective-permute-done | bytes 2097184 | tf_op jit(solution)/shard_map/ppermute | solution.py:29
  51.8 3.0 %shard_map.58 = (bf16[384,512]{1,0:T(8,128)(2,1)S(1)}, bf16[512,2048]{1,0:T(8,128)(2,1)S(1)}) custom-call(s32[3]{0:T(128)S(1)} %copy-done.2, s32[3]{0:T(128)S(1)} %collective-permute-done.recv_starts_ref, bf16[6,512,128]{2,1,0:T(8,128)(2,1)S(1)} %get-tuple-element.12.refs_0_, ...), custom_call_target="tpu_custom_call", output_to_operand_aliasing={{1}: (6, {})} | custom-call | flops 1207959552 | bytes 8388608 | tf_op jit(solution)/shard_map/pallas_call | solution.py:195
  54.8 0.1 collective-permute-start.11
  54.9 0.5 collective-permute-start.8
  55.4 1.2 %collective-permute-start.10 = (bf16[384,512]{1,0:T(8,128)(2,1)S(1)}, bf16[384,512]{1,0:T(8,128)(2,1)S(1)}, u32[]{:S(2)}, u32[]{:S(2)}) collective-permute-start(bf16[384,512]{1,0:T(8,128)(2,1)S(1)} %shard_map.57.refs_5_), channel_id=1, source_target_pairs={{0,3},{1,2},{2,1},{3,0},{4,7},{5,6},{6,5},{7,4},{8,11},{9,10},{10,... | collective-permute-start | bytes 1179656 | tf_op jit(solution)/shard_map/ppermute | solution.py:29
  56.6 0.5 collective-permute-start.9
  57.1 2.1 %collective-permute-done.8 = bf16[384,512]{1,0:T(8,128)(2,1)S(1)} collective-permute-done((bf16[384,512]{1,0:T(8,128)(2,1)S(1)}, bf16[384,512]{1,0:T(8,128)(2,1)S(1)}, u32[]{:S(2)}, u32[]{:S(2)}) %collective-permute-start.8) | collective-permute-done | bytes 393248 | tf_op jit(solution)/shard_map/ppermute | solution.py:23
  59.3 2.8 %fusion = f32[384,2048]{1,0:T(8,128)S(1)} fusion(bf16[384,512]{1,0:T(8,128)(2,1)S(1)} %collective-permute-done.8, bf16[1024,4096]{1,0:T(8,128)(2,1)} %param.9, s32[]{:T(128)S(6)} %select_n.76, s32[]{:T(128)S(6)} %select_n.75), kind=kOutput, calls=%fused_computation.1 | convolution fusion | flops 805306368 | bytes 5636104 | tf_op jit(solution)/shard_map/dot_general | solution.py:252
  62.1 3.0 %add_convert_fusion.given_ref = bf16[384,2048]{1,0:T(8,128)(2,1)S(1)} fusion(f32[384,2048]{1,0:T(8,128)S(1)} %fusion, bf16[384,512]{1,0:T(8,128)(2,1)S(1)} %get-tuple-element.17, bf16[1024,4096]{1,0:T(8,128)(2,1)} %param.9, s32[]{:T(128)S(6)} %select_n.71, s32[]{:T(128)S(6)} %select_n.75), kind=kOutput, calls=%fused_computation | convolution fusion | flops 806879232 | bytes 7208968 | tf_op jit(solution)/shard_map/dot_general | solution.py:251
  65.1 1.5 %collective-permute-done.10.heads_b = bf16[384,512]{1,0:T(8,128)(2,1)S(1)} collective-permute-done((bf16[384,512]{1,0:T(8,128)(2,1)S(1)}, bf16[384,512]{1,0:T(8,128)(2,1)S(1)}, u32[]{:S(2)}, u32[]{:S(2)}) %collective-permute-start.10) | collective-permute-done | bytes 393248 | tf_op jit(solution)/shard_map/ppermute | solution.py:29
  66.6 8.7 %collective-permute-done.9.heads_a = bf16[384,512]{1,0:T(8,128)(2,1)S(1)} collective-permute-done((bf16[384,512]{1,0:T(8,128)(2,1)S(1)}, bf16[384,512]{1,0:T(8,128)(2,1)S(1)}, u32[]{:S(2)}, u32[]{:S(2)}) %collective-permute-start.9) | collective-permute-done | bytes 393248 | tf_op jit(solution)/shard_map/ppermute | solution.py:29
  75.3 0.0 collective-permute-done.11.rows_b
  75.3 4.9 %shard_map.59 = bf16[384,2048]{1,0:T(8,128)(2,1)} custom-call(bf16[384,2048]{1,0:T(8,128)(2,1)S(1)} %add_convert_fusion.given_ref, bf16[384,512]{1,0:T(8,128)(2,1)S(1)} %collective-permute-done.9.heads_a, bf16[512,2048]{1,0:T(8,128)(2,1)S(1)} %get-tuple-element.18.rows_a, bf16[384,512]{1,0:T(8,128)(2,1)S(1)} %collective-permute-done.10.heads_b, ...), custom_call_target="tpu_custom_call" | custom-call | flops 1610612736 | bytes 8388608 | tf_op jit(solution)/shard_map/pallas_call | solution.py:44
  (2 shorter events, 0.1 us)
Async XLA Ops:
  0.0 5.8 %copy-start.3 = (bf16[384,256]{1,0:T(8,128)(2,1)S(1)}, bf16[384,256]{1,0:T(8,128)(2,1)}, u32[]{:S(2)}) copy-start(bf16[384,256]{1,0:T(8,128)(2,1)} %param.7) | copy-start | bytes 589828
  0.0 13.9 %copy-start = (bf16[384,1024]{1,0:T(8,128)(2,1)S(1)}, bf16[384,1024]{1,0:T(8,128)(2,1)}, u32[]{:S(2)}) copy-start(bf16[384,1024]{1,0:T(8,128)(2,1)} %refs_0_.1) | copy-start | bytes 2359300
  4.3 22.0 %copy-start.2 = (s32[3]{0:T(128)S(1)}, s32[3]{0:T(128)}, u32[]{:S(2)}) copy-start(s32[3]{0:T(128)} %starts_ref.7) | copy-start | bytes 40
  4.3 47.6 %collective-permute-start.7 = (bf16[512,2048]{1,0:T(8,128)(2,1)}, bf16[512,2048]{1,0:T(8,128)(2,1)S(1)}, u32[]{:S(2)}, u32[]{:S(2)}) collective-permute-start(bf16[512,2048]{1,0:T(8,128)(2,1)} %dynamic_slice.32), channel_id=1, source_target_pairs={{0,1},{1,0},{2,3},{3,2},{4,5},{5,4},{6,7},{7,6},{8,9},{9,8},{10,11... | collective-permute-start | bytes 6291464 | tf_op jit(solution)/shard_map/ppermute | solution.py:29
  6.8 1.6 %collective-permute-start.2 = (bf16[384,256]{1,0:T(8,128)(2,1)S(1)}, bf16[384,256]{1,0:T(8,128)(2,1)}, u32[]{:S(2)}, u32[]{:S(2)}) collective-permute-start(bf16[384,256]{1,0:T(8,128)(2,1)S(1)} %pad_maximum_fusion), channel_id=1, source_target_pairs={{0,2},{2,0},{4,6},{6,4},{8,10},{10,8},{12,14},{14,12},{16,18},{18,... | collective-permute-start | bytes 589832 | tf_op jit(solution)/shard_map/ppermute | solution.py:23
  9.6 12.1 %collective-permute-start.3 = (bf16[768,256]{1,0:T(8,128)(2,1)S(1)}, bf16[768,256]{1,0:T(8,128)(2,1)}, u32[]{:S(2)}, u32[]{:S(2)}) collective-permute-start(bf16[768,256]{1,0:T(8,128)(2,1)S(1)} %maximum_select_fusion.refs_2_), channel_id=1, source_target_pairs={{0,8},{2,10},{4,12},{6,14},{8,16},{10,18},{12,20},{14,22},{16,24},... | collective-permute-start | bytes 1179656 | tf_op jit(solution)/shard_map/ppermute | solution.py:19
  14.6 12.8 %collective-permute-start.1 = (bf16[384,512]{1,0:T(8,128)(2,1)}, bf16[384,512]{1,0:T(8,128)(2,1)}, u32[]{:S(2)}, u32[]{:S(2)}) collective-permute-start(bf16[384,512]{1,0:T(8,128)(2,1)} %constant_dynamic-slice_fusion.4), channel_id=1, source_target_pairs={{0,2},{2,0},{4,6},{6,4},{8,10},{10,8},{12,14},{14,12},{16,18},{18,... | collective-permute-start | bytes 1179656 | tf_op jit(solution)/shard_map/ppermute | solution.py:23
  21.8 12.6 %collective-permute-start.5 = (bf16[768,256]{1,0:T(8,128)(2,1)}, bf16[768,256]{1,0:T(8,128)(2,1)S(1)}, u32[]{:S(2)}, u32[]{:S(2)}) collective-permute-start(bf16[768,256]{1,0:T(8,128)(2,1)} %collective-permute-done.3.refs_3_), channel_id=1, source_target_pairs={{0,8},{2,10},{4,12},{6,14},{8,16},{10,18},{12,20},{14,22},{16,24},... | collective-permute-start | bytes 1179656 | tf_op jit(solution)/shard_map/ppermute | solution.py:19
  26.3 1.2 %collective-permute-start = (s32[3]{0:T(128)S(1)}, s32[3]{0:T(128)S(1)}, u32[]{:S(2)}, u32[]{:S(2)}) collective-permute-start(s32[3]{0:T(128)S(1)} %copy-done.2), channel_id=1, source_target_pairs={{0,2},{2,0},{4,6},{6,4},{8,10},{10,8},{12,14},{14,12},{16,18},{18,... | collective-permute-start | bytes 44 | tf_op jit(solution)/shard_map/ppermute | solution.py:23
  26.4 12.2 %collective-permute-start.4 = (bf16[768,256]{1,0:T(8,128)(2,1)}, bf16[768,256]{1,0:T(8,128)(2,1)S(1)}, u32[]{:S(2)}, u32[]{:S(2)}) collective-permute-start(bf16[768,256]{1,0:T(8,128)(2,1)} %collective-permute-done.3.refs_3_), channel_id=1, source_target_pairs={{0,4},{2,6},{4,0},{6,2},{8,12},{10,14},{12,8},{14,10},{16,20},{18,... | collective-permute-start | bytes 1179656 | tf_op jit(solution)/shard_map/ppermute | solution.py:23
  27.5 1.1 %copy-start.1 = (bf16[384,1024]{1,0:T(8,128)(2,1)S(1)}, bf16[384,1024]{1,0:T(8,128)(2,1)}, u32[]{:S(2)}) copy-start(bf16[384,1024]{1,0:T(8,128)(2,1)} %refs_0_.1) | copy-start | bytes 2359300
  34.5 12.1 %collective-permute-start.6 = (bf16[768,256]{1,0:T(8,128)(2,1)S(1)}, bf16[768,256]{1,0:T(8,128)(2,1)S(1)}, u32[]{:S(2)}, u32[]{:S(2)}) collective-permute-start(bf16[768,256]{1,0:T(8,128)(2,1)S(1)} %broadcast_select_fusion), channel_id=1, source_target_pairs={{0,4},{2,6},{4,0},{6,2},{8,12},{10,14},{12,8},{14,10},{16,20},{18,... | collective-permute-start | bytes 1179656 | tf_op jit(solution)/shard_map/ppermute | solution.py:23
  54.8 20.4 %collective-permute-start.11 = (bf16[512,2048]{1,0:T(8,128)(2,1)S(1)}, bf16[512,2048]{1,0:T(8,128)(2,1)}, u32[]{:S(2)}, u32[]{:S(2)}) collective-permute-start(bf16[512,2048]{1,0:T(8,128)(2,1)S(1)} %get-tuple-element.18.rows_a), channel_id=1, source_target_pairs={{0,2},{2,0},{4,6},{6,4},{8,10},{10,8},{12,14},{14,12},{16,18},{18,... | collective-permute-start | bytes 6291464 | tf_op jit(solution)/shard_map/ppermute | solution.py:23
  54.9 4.3 %collective-permute-start.8 = (bf16[384,512]{1,0:T(8,128)(2,1)S(1)}, bf16[384,512]{1,0:T(8,128)(2,1)S(1)}, u32[]{:S(2)}, u32[]{:S(2)}) collective-permute-start(bf16[384,512]{1,0:T(8,128)(2,1)S(1)} %shard_map.57.refs_5_), channel_id=1, source_target_pairs={{0,2},{2,0},{4,6},{6,4},{8,10},{10,8},{12,14},{14,12},{16,18},{18,... | collective-permute-start | bytes 1179656 | tf_op jit(solution)/shard_map/ppermute | solution.py:23
  55.4 11.2 %collective-permute-start.10 = (bf16[384,512]{1,0:T(8,128)(2,1)S(1)}, bf16[384,512]{1,0:T(8,128)(2,1)S(1)}, u32[]{:S(2)}, u32[]{:S(2)}) collective-permute-start(bf16[384,512]{1,0:T(8,128)(2,1)S(1)} %shard_map.57.refs_5_), channel_id=1, source_target_pairs={{0,3},{1,2},{2,1},{3,0},{4,7},{5,6},{6,5},{7,4},{8,11},{9,10},{10,... | collective-permute-start | bytes 1179656 | tf_op jit(solution)/shard_map/ppermute | solution.py:29
  56.6 18.6 %collective-permute-start.9 = (bf16[384,512]{1,0:T(8,128)(2,1)S(1)}, bf16[384,512]{1,0:T(8,128)(2,1)S(1)}, u32[]{:S(2)}, u32[]{:S(2)}) collective-permute-start(bf16[384,512]{1,0:T(8,128)(2,1)S(1)} %get-tuple-element.17), channel_id=1, source_target_pairs={{0,1},{1,0},{2,3},{3,2},{4,5},{5,4},{6,7},{7,6},{8,9},{9,8},{10,11... | collective-permute-start | bytes 1179656 | tf_op jit(solution)/shard_map/ppermute | solution.py:29

commit v3 on v0

v3 whole, which is shorter than its diff:
```python
import functools

import jax
import jax.numpy as jnp
from jax import lax
from jax.experimental import pallas as pl
from jax.experimental.pallas import tpu as pltpu
from jax.sharding import PartitionSpec as P

HEAD_SIZE = 128
BLOCK = 128
LOG2E = 1.4426950408889634
MASKED = -1e30
TILE = 256


def shift(x, distance):
    n = lax.axis_size("ctx")
    return lax.ppermute(x, "ctx", [(i, i + distance) for i in range(n - distance)])


def swap(x, mask):
    return lax.ppermute(x, "ctx", [(i, i ^ mask) for i in range(lax.axis_size("ctx"))])


def cross(x, mask):
    n = lax.axis_size("ctx")
    route = [(2 * i + h, 2 * (i ^ mask) + 1 - h) for i in range(n) for h in range(2)]
    return lax.ppermute(x, ("ctx", "head"), route)


def slice_kernel(weight_ref, _, *refs):
    outs, sems = refs[:2], refs[2]
    core, part = lax.axis_index("ctx") % 2, lax.axis_index("ctx") // 4 % 2
    rows, cols = outs[0].shape
    copies = []
    for n, out in enumerate(outs):
        col = ((1 - lax.axis_index("head")) * 4 + part * 2 + n) * cols
        source = weight_ref.at[pl.ds(core * rows, rows), pl.ds(pl.multiple_of(col, cols), cols)]
        copies.append(pltpu.make_async_copy(source, out, sems.at[n]))
    for copy in copies:
        copy.start()
    for copy in copies:
        copy.wait()


def slice_weight(weight, after):
    anywhere = pl.BlockSpec(memory_space=pl.ANY)
    hbm = pl.BlockSpec(memory_space=pltpu.HBM)
    out = jax.ShapeDtypeStruct((weight.shape[0] // 2, weight.shape[1] // 8), weight.dtype)
    return pl.pallas_call(
        slice_kernel,
        out_shape=[out] * 2,
        in_specs=[hbm, anywhere],
        out_specs=[hbm] * 2,
        scratch_shapes=[pltpu.SemaphoreType.DMA((2,))],
    )(weight, after)


def project_kernel(given_ref, heads_ref, *refs):
    tiles, out_ref, built, sems = refs[:8], refs[8], refs[9], refs[10]
    me = lax.axis_index("ctx")
    core, part = me % 2, me // 4 % 2
    group, width = tiles[0].shape
    copies = []
    for n in range(4):
        first = (part if n < 2 else 1 - part) * 2 + n % 2
        cols = pl.ds(pl.multiple_of(first * width, width), width)
        total = given_ref[:, cols].astype(jnp.float32)
        for index, tile in ((core, tiles[n]), (1 - core, tiles[4 + n])):
            heads = heads_ref[:, pl.ds(pl.multiple_of(index * group, group), group)]
            total += jnp.dot(heads, tile[...], preferred_element_type=jnp.float32)
        built[n] = total.astype(out_ref.dtype)
        copies.append(pltpu.make_async_copy(built.at[n], out_ref.at[:, cols], sems.at[n]))
        copies[-1].start()
    for copy in copies:
        copy.wait()


def project(given, heads, tiles):
    tok, cols = given.shape
    vmem = pl.BlockSpec(memory_space=pltpu.VMEM)
    return pl.pallas_call(
        project_kernel,
        out_shape=jax.ShapeDtypeStruct(given.shape, jnp.bfloat16),
        in_specs=[vmem] * 10,
        out_specs=pl.BlockSpec(memory_space=pltpu.HBM),
        scratch_shapes=[pltpu.VMEM((4, tok, cols // 4), jnp.bfloat16), pltpu.SemaphoreType.DMA((4,))],
        compiler_params=pltpu.CompilerParams(vmem_limit_bytes=16 * 2**20),
        cost_estimate=pl.CostEstimate(
            flops=2 * tok * heads.shape[1] * cols, bytes_accessed=4 * 2**20, transcendentals=0
        ),
    )(given, heads, *tiles)


def attention_kernel(stage, distances, n_head, n_after, starts_ref, recv_starts_ref, *refs):
    refs = list(refs)
    me = lax.axis_index("ctx")
    pair, core, col = me // 2, me % 2, (me // 2) % 2
    if stage == "first":
        queries_ref, q_recv_ref = refs[:2]
        refs = refs[2:]
    else:
        q_ref, top_in, acc_in = refs[:3]
        refs = refs[3:]
    n_pieces = len(distances)
    halves = refs[: 2 * n_pieces]
    refs = refs[2 * n_pieces + n_after :]
    if stage == "first":
        q_ref, top_ref, acc_ref, held_ref = refs
    elif stage == "next":
        top_ref, acc_ref, held_ref = refs
    else:
        if stage == "own":
            swapped_ref, *refs = refs
        out_ref, acc_ref, held_ref = refs
    tok = starts_ref.shape[0] * BLOCK
    half = tok // BLOCK
    blocks = 2 * half
    rows = n_head * BLOCK
    factor = HEAD_SIZE**-0.5 * LOG2E
    tiles = [(b, slice(r, r + TILE)) for b in range(blocks) for r in range(0, rows, TILE)]

    for n, ref in enumerate(halves):
        shard = core if n % 2 == 0 else 1 - core
        held_ref[n // 2, pl.ds(pl.multiple_of(shard * tok, tok), tok)] = ref[...]

    def start_of(b):
        mine = b // half == core
        return jnp.where(mine, starts_ref[b % half], recv_starts_ref[b % half])

    def rows_of(ref, j, lane0):
        t = slice(j * BLOCK, (j + 1) * BLOCK)
        return jnp.concatenate(
            [ref[t, pl.ds(lane0 + h * HEAD_SIZE, HEAD_SIZE)] for h in range(n_head)], axis=0
        )

    def scores(b, r, i, width):
        k = held_ref[i, :width, :HEAD_SIZE]
        return lax.dot_general(
            q_ref[b, r], k, (((1,), (1,)), ((), ())), preferred_element_type=jnp.float32
        )

    def weigh(p, i, width):
        v = held_ref[i, :width, HEAD_SIZE:]
        v = jnp.concatenate([v, jnp.ones_like(v)], axis=1)
        return jnp.dot(p.astype(jnp.bfloat16), v, preferred_element_type=jnp.float32)

    def keep(s, since):
        k_id = lax.broadcasted_iota(jnp.int32, (1, s.shape[1]), 1)
        return jnp.where(k_id >= since, s, MASKED)

    def update(i, base, b, r, top_from, acc_from, to):
        s = keep(scores(b, r, i, 2 * tok), start_of(b) - base)
        old = top_from[b, r][:, :1]
        top = jnp.maximum(old, jnp.max(s, axis=1, keepdims=True))
        p = jnp.exp2(s * factor - top * factor)
        if stage == "next":
            top_ref[to, r] = jnp.broadcast_to(top, (TILE, HEAD_SIZE))
        acc_ref[to, r] = acc_from[b, r] * jnp.exp2((old - top) * factor) + weigh(p, i, 2 * tok)

    def attend_own():
        for j in range(half):
            mine = rows_of(queries_ref, j, pl.multiple_of(core * rows, rows))
            q_ref[core * half + j] = mine
            q_ref[(1 - core) * half + j] = rows_of(q_recv_ref, j, 0)
        t_id = lax.broadcasted_iota(jnp.int32, (TILE, BLOCK), 0) % BLOCK
        causal = lax.broadcasted_iota(jnp.int32, (TILE, BLOCK), 1) <= t_id
        for b, r in tiles:
            width = (b + 1) * BLOCK
            s = scores(b, r, 0, width)
            since = start_of(b) - pair * 2 * tok
            diag = jnp.where(causal, s[:, b * BLOCK :], MASKED)
            s = jnp.concatenate([keep(s[:, : b * BLOCK], since), diag], 1) if b else diag
            top = jnp.max(s, axis=1, keepdims=True)
            p = jnp.exp2(s * factor - top * factor)
            top_ref[b, r] = jnp.broadcast_to(top, (TILE, HEAD_SIZE))
            acc_ref[b, r] = weigh(p, 0, width)

    def attend_next():
        top_ref[...] = top_in[...]
        acc_ref[...] = acc_in[...]

        @pl.loop(0, 2 * n_pieces)
        def _(step):
            i, first_block = step // 2, step % 2 * half
            behind = sum(
                jnp.where(i == n, jnp.where(col == 0, *d), 0) for n, d in enumerate(distances)
            )
            base = (pair - behind) * 2 * tok

            @pl.when(start_of(first_block) < base + 2 * tok)
            def _():
                for b, r in tiles[: len(tiles) // 2]:
                    b = first_block + b
                    update(i, base, b, r, top_ref, acc_ref, b)

    def attend_last(shard):
        first_block = shard * half
        base = (pair - jnp.where(col == 0, *distances[0])) * 2 * tok
        needed = start_of(first_block) < base + 2 * tok

        @pl.when(needed)
        def _():
            for b, r in tiles[: len(tiles) // 2]:
                update(0, base, first_block + b, r, top_in, acc_in, b)

        @pl.when(jnp.logical_not(needed))
        def _():
            acc_ref[...] = acc_in[pl.ds(first_block, half)]

        for j in range(half):
            o = (acc_ref[j, :, :HEAD_SIZE] / acc_ref[j, :, HEAD_SIZE:]).astype(jnp.bfloat16)
            for h in range(n_head):
                first = core * rows + h * HEAD_SIZE if stage == "own" else h * HEAD_SIZE
                lanes = pl.ds(pl.multiple_of(first, HEAD_SIZE), HEAD_SIZE)
                out_ref[j * BLOCK : (j + 1) * BLOCK, lanes] = o[h * BLOCK : (h + 1) * BLOCK]
        if stage == "own":
            out_ref[:, pl.ds(pl.multiple_of((1 - core) * rows, rows), rows)] = swapped_ref[...]

    if stage == "first":
        attend_own()
    elif stage == "next":
        attend_next()
    else:
        attend_last(core if stage == "own" else 1 - core)


def attention_call(stage, distances, starts, recv_starts, operands, after=()):
    tok, half = starts.shape[0] * BLOCK, starts.shape[0]
    rows = operands[1].shape[1]
    blocks, n_head, n_pieces = 2 * half, rows // BLOCK, len(distances)
    state = [
        jax.ShapeDtypeStruct((blocks, rows, HEAD_SIZE), jnp.float32),
        jax.ShapeDtypeStruct((blocks, rows, 2 * HEAD_SIZE), jnp.float32),
    ]
    scratch = [pltpu.VMEM((n_pieces, 2 * tok, 2 * HEAD_SIZE), jnp.bfloat16)]
    share = n_pieces
    if stage == "first":
        outs, share = [jax.ShapeDtypeStruct((blocks, rows, HEAD_SIZE), jnp.bfloat16)] + state, 0.6
    elif stage == "next":
        outs = state
    else:
        width = rows * (2 if stage == "own" else 1)
        outs, share = [jax.ShapeDtypeStruct((tok, width), jnp.bfloat16)], 0.5
        scratch = [pltpu.VMEM((half, rows, 2 * HEAD_SIZE), jnp.float32)] + scratch
    vmem, smem = pl.BlockSpec(memory_space=pltpu.VMEM), pl.BlockSpec(memory_space=pltpu.SMEM)
    return pl.pallas_call(
        functools.partial(attention_kernel, stage, distances, n_head, len(after)),
        out_shape=outs,
        in_specs=[smem, smem]
        + [vmem] * len(operands)
        + [pl.BlockSpec(memory_space=pl.ANY)] * len(after),
        out_specs=[vmem] * len(outs),
        scratch_shapes=scratch,
        compiler_params=pltpu.CompilerParams(vmem_limit_bytes=24 * 2**20),
        cost_estimate=pl.CostEstimate(
            flops=int(share * blocks * rows * 2 * tok * HEAD_SIZE * 8),
            bytes_accessed=8 * 2**20,
            transcendentals=int(share * blocks * rows * 2 * tok),
        ),
    )(starts, recv_starts, *operands, *after)


def per_device(queries, keys, values, block_start, out_weight):
    group = queries.shape[1] // 2
    me = lax.axis_index("ctx")
    core, col = me % 2, (me // 2) % 2
    head = lax.axis_index("head")

    def part(x, index, size):
        return lax.dynamic_slice_in_dim(x, index * size, size, 1)

    cols = out_weight.shape[1] // 2
    mine = jnp.concatenate([part(keys, core, HEAD_SIZE), part(values, core, HEAD_SIZE)], 1)
    theirs = jnp.concatenate([part(keys, 1 - core, HEAD_SIZE), part(values, 1 - core, HEAD_SIZE)], 1)
    own = (mine, swap(theirs, 1))
    q_recv = swap(part(queries, 1 - core, group), 1)
    recv_starts = swap(block_start, 1)
    one_behind = [shift(x, 4) for x in own]
    two_behind = [shift(x, 4) for x in one_behind]
    across = [swap(x, 2) for x in one_behind]
    third = [swap(jnp.where(col == 1, x, y), 2) for x, y in zip(two_behind, own, strict=True)]

    tiles = [cross(x, 0) for x in slice_weight(out_weight, one_behind[0])]
    tiles += [swap(x, 4) for x in tiles]

    starts = (block_start, recv_starts)
    q, *state = attention_call("first", ((0, 0),), *starts, (queries, q_recv, *own))
    state = attention_call("next", ((2, 2),), *starts, (q, *state, *one_behind))
    state = attention_call("next", ((1, 3), (4, 4)), *starts, (q, *state, *across, *two_behind))
    (o_other,) = attention_call("other", ((3, 1),), *starts, (q, *state, *third))
    (heads,) = attention_call("own", ((3, 1),), *starts, (q, *state, *third, swap(o_other, 1)))
    across = cross(heads, 0)
    here = jnp.dot(heads, part(out_weight, head, cols), preferred_element_type=jnp.float32)
    tiles += [swap(x, 1) for x in tiles]
    return project(here.astype(jnp.bfloat16), across, tiles)


def solution(mesh):
    in_specs = (P("ctx", "head"), P("ctx", "head"), P("ctx", "head"), P("ctx"), P("head", None))
    out_specs = P("ctx", "head")
    return jax.shard_map(
        per_device, mesh=mesh, in_specs=in_specs, out_specs=out_specs, check_vma=False
    )
```

time: 91.6 us -> 122 us (1.33)
  Pallas kernels: 10.6 us -> 48.8 us
  waiting for transfers between devices: 56.4 us -> 30.3 us
  starting transfers between devices: 10.9 us -> 34 us
  matrix products: 9.16 us -> 3.98 us
  other arithmetic: 1.98 us -> 0.15 us
  local copies, waits for them, and re-layouts: 1.18 us -> 2.85 us
    pallas_call x3 -> x7, Pallas kernels: 10.6 us -> 48.8 us  [the longest x1 32.9 us: slice_weight(): pl.pallas_call(slice_kernel, out_shape=[out] * 2, in_specs=[hbm, anywhere...]
    ppermute x1 -> x3, waiting for transfers between devices: 31.1 us -> 0.01 us  [cross(): return lax.ppermute(x, ('ctx', 'head'), route)]
    ppermute x6 -> x14, starting transfers between devices: 1.48 us -> 14.6 us  [swap(): lax.ppermute(x, 'ctx', [(i, i ^ mask) for i in range(lax.axis_size('ctx'))])]
    ppermute x6 -> x14, waiting for transfers between devices: 14.2 us -> 24.7 us  [swap(): lax.ppermute(x, 'ctx', [(i, i ^ mask) for i in range(lax.axis_size('ctx'))])]
    ppermute x2 -> x4, starting transfers between devices: 7.9 us -> 15.7 us  [shift(): lax.ppermute(x, 'ctx', [(i, i + distance) for i in range(n - distance)])]
    ppermute x2 -> x4, waiting for transfers between devices: 11.1 us -> 5.61 us  [shift(): lax.ppermute(x, 'ctx', [(i, i + distance) for i in range(n - distance)])]
    dot_general x2 -> x1, matrix products: 9.16 us -> 3.98 us  [per_device(): jnp.dot(heads, part(out_weight, head, cols), preferred_element_type=jnp.f...]
    ppermute x1 -> x3, starting transfers between devices: 1.52 us -> 3.68 us  [cross(): return lax.ppermute(x, ('ctx', 'head'), route)]
  transfers between devices with their start and end apart: 9 -> 21, of which waited for: 8 -> 6; matrix products, arithmetic and copies ran while one was open for 5% -> 5% of each run, Pallas kernels for 6% -> 37%
where the time goes in v3:
time: 122 us; the launch traced here: 120 us
  Pallas kernels  48.8 us (40%)
  starting transfers between devices  34 us (28%)
  waiting for transfers between devices  30.3 us (25%)
  matrix products  3.98 us (3%)
  local copies, waits for them, and re-layouts  2.85 us (2%)
    pallas_call x1, Pallas kernels, slice_weight(): pl.pallas_call(slice_kernel, out_shape=[out] * 2, in_specs=[hbm, anywhere...  32.9 us
    ppermute x14, waiting for transfers between devices, swap(): lax.ppermute(x, 'ctx', [(i, i ^ mask) for i in range(lax.axis_size('ctx'))])  24.7 us
    ppermute x4, starting transfers between devices, shift(): lax.ppermute(x, 'ctx', [(i, i + distance) for i in range(n - distance)])  15.7 us
    ppermute x14, starting transfers between devices, swap(): lax.ppermute(x, 'ctx', [(i, i ^ mask) for i in range(lax.axis_size('ctx'))])  14.6 us
    pallas_call x5, Pallas kernels, attention_call(): pl.pallas_call(functools.partial(attention_kernel, stage, distances, n_he...  11.6 us
    ppermute x4, waiting for transfers between devices, shift(): lax.ppermute(x, 'ctx', [(i, i + distance) for i in range(n - distance)])  5.61 us
    pallas_call x1, Pallas kernels, project(): pl.pallas_call(project_kernel, out_shape=jax.ShapeDtypeStruct(given.shape...  4.29 us
    dot_general x1, matrix products, per_device(): jnp.dot(heads, part(out_weight, head, cols), preferred_element_type=jnp.f...  3.98 us
  transfers between devices with their start and end apart: 21, of which 6 were waited for; matrix products, arithmetic and copies ran while one was open for 5% of the time, Pallas kernels for 37%

profile of v3, /device:TPU:2, one launch (start us, length us, event | category | flops | bytes accessed | tf_op | source)
XLA Modules:
  0.0 120.5 jit_solution(8593424981572020029)
XLA Ops:
  0.0 1.1 constant_dynamic-slice_fusion
  1.1 3.5 %collective-permute-start.3 = (bf16[384,256]{1,0:T(8,128)(2,1)S(1)}, bf16[384,256]{1,0:T(8,128)(2,1)S(1)}, u32[]{:S(2)}, u32[]{:S(2)}) collective-permute-start(bf16[384,256]{1,0:T(8,128)(2,1)S(1)} %pad_maximum_fusion.refs_2_), channel_id=1, source_target_pairs={{0,8},{2,10},{4,12},{6,14},{8,16},{10,18},{12,20},{14,22},{16,24},... | collective-permute-start | bytes 589832 | tf_op jit(solution)/shard_map/ppermute | solution.py:19
  4.6 0.1 collective-permute-start.2
  4.7 4.0 %collective-permute-done.3.refs_3_._ = bf16[384,256]{1,0:T(8,128)(2,1)S(1)} collective-permute-done((bf16[384,256]{1,0:T(8,128)(2,1)S(1)}, bf16[384,256]{1,0:T(8,128)(2,1)S(1)}, u32[]{:S(2)}, u32[]{:S(2)}) %collective-permute-start.3) | collective-permute-done | bytes 196640 | tf_op jit(solution)/shard_map/ppermute | solution.py:19
  8.7 0.0 copy-start.1
  8.7 4.4 %collective-permute-start.7 = (bf16[384,256]{1,0:T(8,128)(2,1)S(1)}, bf16[384,256]{1,0:T(8,128)(2,1)S(1)}, u32[]{:S(2)}, u32[]{:S(2)}) collective-permute-start(bf16[384,256]{1,0:T(8,128)(2,1)S(1)} %collective-permute-done.3.refs_3_._), channel_id=1, source_target_pairs={{0,8},{2,10},{4,12},{6,14},{8,16},{10,18},{12,20},{14,22},{16,24},... | collective-permute-start | bytes 589832 | tf_op jit(solution)/shard_map/ppermute | solution.py:19
  13.1 1.8 %constant_dynamic-slice_fusion.4 = bf16[384,512]{1,0:T(8,128)(2,1)} fusion(bf16[384,1024]{1,0:T(8,128)(2,1)} %refs_0_.1, s32[]{:T(128)S(6)} %select_n.42), kind=kLoop, calls=%fused_computation.12 | loop fusion | bytes 786436 | tf_op jit(solution)/shard_map/dynamic_slice | solution.py:272
  14.9 0.0 collective-permute-start.1
  14.9 0.5 collective-permute-start
  15.4 0.0 copy-done.1
  15.4 0.0 copy-start
  15.4 0.0 copy-start.3
  15.4 32.9 %shard_map.60 = (bf16[512,512]{1,0:T(8,128)(2,1)}, bf16[512,512]{1,0:T(8,128)(2,1)}) custom-call(bf16[1024,4096]{1,0:T(8,128)(2,1)} %weight_ref.1, bf16[384,256]{1,0:T(8,128)(2,1)} %copy-done.1), custom_call_target="tpu_custom_call" | custom-call | tf_op jit(solution)/shard_map/pallas_call | solution.py:51
  48.3 0.0 copy-start.2
  48.3 1.6 %collective-permute-start.13 = (bf16[512,512]{1,0:T(8,128)(2,1)}, bf16[512,512]{1,0:T(8,128)(2,1)S(1)}, u32[]{:S(2)}, u32[]{:S(2)}) collective-permute-start(bf16[512,512]{1,0:T(8,128)(2,1)} %get-tuple-element.21), channel_id=1, source_target_pairs={{0,1},{1,0},{2,3},{3,2},{4,5},{5,4},{6,7},{7,6},{8,9},{9,8},{10,11... | collective-permute-start | bytes 1572872 | tf_op jit(solution)/shard_map/ppermute | solution.py:29
  49.9 0.0 collective-permute-done.2.refs_3_
  49.9 0.5 collective-permute-start.14
  50.4 0.0 collective-permute-done.7.refs_5_
  50.4 3.5 %collective-permute-start.4 = (bf16[384,256]{1,0:T(8,128)(2,1)S(1)}, bf16[384,256]{1,0:T(8,128)(2,1)S(1)}, u32[]{:S(2)}, u32[]{:S(2)}) collective-permute-start(bf16[384,256]{1,0:T(8,128)(2,1)S(1)} %collective-permute-done.2.refs_3_), channel_id=1, source_target_pairs={{0,8},{2,10},{4,12},{6,14},{8,16},{10,18},{12,20},{14,22},{16,24},... | collective-permute-start | bytes 589832 | tf_op jit(solution)/shard_map/ppermute | solution.py:19
  53.9 0.1 broadcast_select_fusion.1
  54.0 0.0 collective-permute-done.recv_starts_ref
  54.0 0.6 collective-permute-start.5
  54.6 0.0 collective-permute-done.1.refs_1_
  54.6 1.5 %collective-permute-start.9 = (bf16[384,256]{1,0:T(8,128)(2,1)S(1)}, bf16[384,256]{1,0:T(8,128)(2,1)S(1)}, u32[]{:S(2)}, u32[]{:S(2)}) collective-permute-start(bf16[384,256]{1,0:T(8,128)(2,1)S(1)} %broadcast_select_fusion.1), channel_id=1, source_target_pairs={{0,4},{2,6},{4,0},{6,2},{8,12},{10,14},{12,8},{14,10},{16,20},{18,... | collective-permute-start | bytes 589832 | tf_op jit(solution)/shard_map/ppermute | solution.py:23
  56.1 1.6 %collective-permute-done.4.refs_4_ = bf16[384,256]{1,0:T(8,128)(2,1)S(1)} collective-permute-done((bf16[384,256]{1,0:T(8,128)(2,1)S(1)}, bf16[384,256]{1,0:T(8,128)(2,1)S(1)}, u32[]{:S(2)}, u32[]{:S(2)}) %collective-permute-start.4) | collective-permute-done | bytes 196640 | tf_op jit(solution)/shard_map/ppermute | solution.py:19
  57.7 4.4 %collective-permute-start.8 = (bf16[384,256]{1,0:T(8,128)(2,1)S(1)}, bf16[384,256]{1,0:T(8,128)(2,1)S(1)}, u32[]{:S(2)}, u32[]{:S(2)}) collective-permute-start(bf16[384,256]{1,0:T(8,128)(2,1)S(1)} %collective-permute-done.4.refs_4_), channel_id=1, source_target_pairs={{0,8},{2,10},{4,12},{6,14},{8,16},{10,18},{12,20},{14,22},{16,24},... | collective-permute-start | bytes 589832 | tf_op jit(solution)/shard_map/ppermute | solution.py:19
  62.1 0.0 copy-done
  62.1 0.0 copy-done.3
  62.1 3.7 %shard_map.55 = (bf16[6,512,128]{2,1,0:T(8,128)(2,1)S(1)}, f32[6,512,128]{2,1,0:T(8,128)S(1)}, f32[6,512,256]{2,1,0:T(8,128)S(1)}) custom-call(s32[3]{0:T(128)S(1)} %copy-done.3, s32[3]{0:T(128)S(1)} %collective-permute-done.recv_starts_ref, bf16[384,1024]{1,0:T(8,128)(2,1)S(1)} %copy-done, bf16[384,512]{1,0:T(8,128)(2,1)S(1)} %collective-permute-done.1.refs_1_, ...), custom_call_target="tpu_custom_call" | custom-call | flops 1449551488 | bytes 8388608 | tf_op jit(solution)/shard_map/pallas_call | solution.py:248
  65.8 0.0 copy-done.2
  65.8 1.0 shard_map.56
  66.8 0.0 collective-permute-done.8.refs_6_
  66.8 0.6 collective-permute-start.6
  67.4 0.0 collective-permute-done.5.refs_3_
  67.4 1.6 %collective-permute-start.10 = (bf16[384,256]{1,0:T(8,128)(2,1)S(1)}, bf16[384,256]{1,0:T(8,128)(2,1)S(1)}, u32[]{:S(2)}, u32[]{:S(2)}) collective-permute-start(bf16[384,256]{1,0:T(8,128)(2,1)S(1)} %broadcast_select_fusion), channel_id=1, source_target_pairs={{0,4},{2,6},{4,0},{6,2},{8,12},{10,14},{12,8},{14,10},{16,20},{18,... | collective-permute-start | bytes 589832 | tf_op jit(solution)/shard_map/ppermute | solution.py:23
  69.0 5.0 %collective-permute-done.6.refs_4_ = bf16[384,256]{1,0:T(8,128)(2,1)S(1)} collective-permute-done((bf16[384,256]{1,0:T(8,128)(2,1)S(1)}, bf16[384,256]{1,0:T(8,128)(2,1)S(1)}, u32[]{:S(2)}, u32[]{:S(2)}) %collective-permute-start.6) | collective-permute-done | bytes 196640 | tf_op jit(solution)/shard_map/ppermute | solution.py:23
  74.0 1.0 shard_map.57
  75.1 0.0 collective-permute-done.9.refs_3_
  75.1 1.0 collective-permute-done.10.refs_4_
  76.1 2.8 %shard_map.58 = bf16[384,512]{1,0:T(8,128)(2,1)S(1)} custom-call(s32[3]{0:T(128)S(1)} %copy-done.3, s32[3]{0:T(128)S(1)} %collective-permute-done.recv_starts_ref, bf16[6,512,128]{2,1,0:T(8,128)(2,1)S(1)} %get-tuple-element.14.refs_0_, f32[6,512,128]{2,1,0:T(8,128)S(1)} %get-tuple-element.19.refs_1_, f32[6,512,256]{2,1,0:T(8,128)S(1)} %get-tuple-element.20.refs_2_, ...), custom_call_target="tpu_custom_call" | custom-call | flops 1207959552 | bytes 8388608 | tf_op jit(solution)/shard_map/pallas_call | solution.py:248
  79.0 0.1 collective-permute-start.11
  79.1 0.0 collective-permute-done.13.refs_0_
  79.1 9.1 %collective-permute-start.15 = (bf16[512,512]{1,0:T(8,128)(2,1)S(1)}, bf16[512,512]{1,0:T(8,128)(2,1)S(1)}, u32[]{:S(2)}, u32[]{:S(2)}) collective-permute-start(bf16[512,512]{1,0:T(8,128)(2,1)S(1)} %collective-permute-done.13.refs_0_), channel_id=1, source_target_pairs={{0,8},{2,10},{4,12},{6,14},{8,0},{10,2},{12,4},{14,6},{16,24},{18,... | collective-permute-start | bytes 1572872 | tf_op jit(solution)/shard_map/ppermute | solution.py:23
  88.1 0.0 collective-permute-done.14.refs_1_
  88.2 0.1 collective-permute-start.16
  88.2 0.0 collective-permute-done.11.refs_5_
  88.2 3.1 %shard_map.59 = bf16[384,1024]{1,0:T(8,128)(2,1)S(1)} custom-call(s32[3]{0:T(128)S(1)} %copy-done.3, s32[3]{0:T(128)S(1)} %collective-permute-done.recv_starts_ref, bf16[6,512,128]{2,1,0:T(8,128)(2,1)S(1)} %get-tuple-element.14.refs_0_, f32[6,512,128]{2,1,0:T(8,128)S(1)} %get-tuple-element.19.refs_1_, f32[6,512,256]{2,1,0:T(8,128)S(1)} %get-tuple-element.20.refs_2_, ...), custom_call_target="tpu_custom_call" | custom-call | flops 1207959552 | bytes 8388608 | tf_op jit(solution)/shard_map/pallas_call | solution.py:248
  91.3 1.6 %collective-permute-start.12 = (bf16[384,1024]{1,0:T(8,128)(2,1)S(1)}, bf16[384,1024]{1,0:T(8,128)(2,1)S(1)}, u32[]{:S(2)}, u32[]{:S(2)}) collective-permute-start(bf16[384,1024]{1,0:T(8,128)(2,1)S(1)} %shard_map.59), channel_id=1, source_target_pairs={{0,1},{1,0},{2,3},{3,2},{4,5},{5,4},{6,7},{7,6},{8,9},{9,8},{10,11... | collective-permute-start | bytes 2359304 | tf_op jit(solution)/shard_map/ppermute | solution.py:29
  92.9 0.0 collective-permute-start.17
  92.9 0.5 collective-permute-start.18
  93.4 7.5 %collective-permute-done.15.refs_2_ = bf16[512,512]{1,0:T(8,128)(2,1)S(1)} collective-permute-done((bf16[512,512]{1,0:T(8,128)(2,1)S(1)}, bf16[512,512]{1,0:T(8,128)(2,1)S(1)}, u32[]{:S(2)}, u32[]{:S(2)}) %collective-permute-start.15) | collective-permute-done | bytes 524320 | tf_op jit(solution)/shard_map/ppermute | solution.py:23
  100.9 0.0 collective-permute-start.19
  100.9 11.1 %collective-permute-done.16.refs_3_ = bf16[512,512]{1,0:T(8,128)(2,1)} collective-permute-done((bf16[512,512]{1,0:T(8,128)(2,1)S(1)}, bf16[512,512]{1,0:T(8,128)(2,1)}, u32[]{:S(2)}, u32[]{:S(2)}) %collective-permute-start.16) | collective-permute-done | bytes 524320 | tf_op jit(solution)/shard_map/ppermute | solution.py:23
  112.0 0.0 collective-permute-start.20
  112.0 4.0 %fusion.2.given_ref = bf16[384,2048]{1,0:T(8,128)(2,1)S(1)} fusion(bf16[384,1024]{1,0:T(8,128)(2,1)S(1)} %shard_map.59, bf16[1024,4096]{1,0:T(8,128)(2,1)} %weight_ref.1, s32[]{:T(128)S(6)} %select_n.50), kind=kOutput, calls=%fused_computation.2 | convolution fusion | flops 1611399168 | bytes 6553604 | tf_op jit(solution)/shard_map/dot_general | solution.py:295
  116.0 0.0 collective-permute-done.17.refs_4_
  116.0 0.0 collective-permute-done.18.refs_5_
  116.0 0.0 collective-permute-done.19.refs_6_
  116.0 0.0 collective-permute-done.20.refs_7_
  116.0 0.0 collective-permute-done.12.heads_ref
  116.0 4.3 %shard_map.61 = bf16[384,2048]{1,0:T(8,128)(2,1)} custom-call(bf16[384,2048]{1,0:T(8,128)(2,1)S(1)} %fusion.2.given_ref, bf16[384,1024]{1,0:T(8,128)(2,1)S(1)} %collective-permute-done.12.heads_ref, bf16[512,512]{1,0:T(8,128)(2,1)S(1)} %collective-permute-done.13.refs_0_, bf16[512,512]{1,0:T(8,128)(2,1)S(1)} %collective-permute-done.14.refs_1_, ...), custom_call_target="tpu_custom_call" | custom-call | flops 1610612736 | bytes 4194304 | tf_op jit(solution)/shard_map/pallas_call | solution.py:83
  (3 shorter events, 0.1 us)
Async XLA Ops:
  1.1 7.6 %collective-permute-start.3 = (bf16[384,256]{1,0:T(8,128)(2,1)S(1)}, bf16[384,256]{1,0:T(8,128)(2,1)S(1)}, u32[]{:S(2)}, u32[]{:S(2)}) collective-permute-start(bf16[384,256]{1,0:T(8,128)(2,1)S(1)} %pad_maximum_fusion.refs_2_), channel_id=1, source_target_pairs={{0,8},{2,10},{4,12},{6,14},{8,16},{10,18},{12,20},{14,22},{16,24},... | collective-permute-start | bytes 589832 | tf_op jit(solution)/shard_map/ppermute | solution.py:19
  4.6 45.3 %collective-permute-start.2 = (bf16[384,256]{1,0:T(8,128)(2,1)S(1)}, bf16[384,256]{1,0:T(8,128)(2,1)S(1)}, u32[]{:S(2)}, u32[]{:S(2)}) collective-permute-start(bf16[384,256]{1,0:T(8,128)(2,1)S(1)} %pad_maximum_fusion.1), channel_id=1, source_target_pairs={{0,2},{2,0},{4,6},{6,4},{8,10},{10,8},{12,14},{14,12},{16,18},{18,... | collective-permute-start | bytes 589832 | tf_op jit(solution)/shard_map/ppermute | solution.py:23
  8.7 6.7 %copy-start.1 = (bf16[384,256]{1,0:T(8,128)(2,1)}, bf16[384,256]{1,0:T(8,128)(2,1)S(1)}, u32[]{:S(2)}) copy-start(bf16[384,256]{1,0:T(8,128)(2,1)S(1)} %collective-permute-done.3.refs_3_._) | copy-start | bytes 589828
  8.7 41.7 %collective-permute-start.7 = (bf16[384,256]{1,0:T(8,128)(2,1)S(1)}, bf16[384,256]{1,0:T(8,128)(2,1)S(1)}, u32[]{:S(2)}, u32[]{:S(2)}) collective-permute-start(bf16[384,256]{1,0:T(8,128)(2,1)S(1)} %collective-permute-done.3.refs_3_._), channel_id=1, source_target_pairs={{0,8},{2,10},{4,12},{6,14},{8,16},{10,18},{12,20},{14,22},{16,24},... | collective-permute-start | bytes 589832 | tf_op jit(solution)/shard_map/ppermute | solution.py:19
  14.9 39.7 %collective-permute-start.1 = (bf16[384,512]{1,0:T(8,128)(2,1)}, bf16[384,512]{1,0:T(8,128)(2,1)S(1)}, u32[]{:S(2)}, u32[]{:S(2)}) collective-permute-start(bf16[384,512]{1,0:T(8,128)(2,1)} %constant_dynamic-slice_fusion.4), channel_id=1, source_target_pairs={{0,2},{2,0},{4,6},{6,4},{8,10},{10,8},{12,14},{14,12},{16,18},{18,... | collective-permute-start | bytes 1179656 | tf_op jit(solution)/shard_map/ppermute | solution.py:23
  14.9 39.1 %collective-permute-start = (s32[3]{0:T(128)}, s32[3]{0:T(128)S(1)}, u32[]{:S(2)}, u32[]{:S(2)}) collective-permute-start(s32[3]{0:T(128)} %starts_ref.9), channel_id=1, source_target_pairs={{0,2},{2,0},{4,6},{6,4},{8,10},{10,8},{12,14},{14,12},{16,18},{18,... | collective-permute-start | bytes 44 | tf_op jit(solution)/shard_map/ppermute | solution.py:23
  15.4 46.6 %copy-start = (bf16[384,1024]{1,0:T(8,128)(2,1)S(1)}, bf16[384,1024]{1,0:T(8,128)(2,1)}, u32[]{:S(2)}) copy-start(bf16[384,1024]{1,0:T(8,128)(2,1)} %refs_0_.1) | copy-start | bytes 2359300
  15.4 46.7 %copy-start.3 = (s32[3]{0:T(128)S(1)}, s32[3]{0:T(128)}, u32[]{:S(2)}) copy-start(s32[3]{0:T(128)} %starts_ref.9) | copy-start | bytes 40
  48.3 17.5 %copy-start.2 = (bf16[384,256]{1,0:T(8,128)(2,1)S(1)}, bf16[384,256]{1,0:T(8,128)(2,1)}, u32[]{:S(2)}) copy-start(bf16[384,256]{1,0:T(8,128)(2,1)} %copy-done.1) | copy-start | bytes 589828
  48.3 30.7 %collective-permute-start.13 = (bf16[512,512]{1,0:T(8,128)(2,1)}, bf16[512,512]{1,0:T(8,128)(2,1)S(1)}, u32[]{:S(2)}, u32[]{:S(2)}) collective-permute-start(bf16[512,512]{1,0:T(8,128)(2,1)} %get-tuple-element.21), channel_id=1, source_target_pairs={{0,1},{1,0},{2,3},{3,2},{4,5},{5,4},{6,7},{7,6},{8,9},{9,8},{10,11... | collective-permute-start | bytes 1572872 | tf_op jit(solution)/shard_map/ppermute | solution.py:29
  49.9 38.2 %collective-permute-start.14 = (bf16[512,512]{1,0:T(8,128)(2,1)}, bf16[512,512]{1,0:T(8,128)(2,1)S(1)}, u32[]{:S(2)}, u32[]{:S(2)}) collective-permute-start(bf16[512,512]{1,0:T(8,128)(2,1)} %get-tuple-element.22), channel_id=1, source_target_pairs={{0,1},{1,0},{2,3},{3,2},{4,5},{5,4},{6,7},{7,6},{8,9},{9,8},{10,11... | collective-permute-start | bytes 1572872 | tf_op jit(solution)/shard_map/ppermute | solution.py:29
  50.4 7.2 %collective-permute-start.4 = (bf16[384,256]{1,0:T(8,128)(2,1)S(1)}, bf16[384,256]{1,0:T(8,128)(2,1)S(1)}, u32[]{:S(2)}, u32[]{:S(2)}) collective-permute-start(bf16[384,256]{1,0:T(8,128)(2,1)S(1)} %collective-permute-done.2.refs_3_), channel_id=1, source_target_pairs={{0,8},{2,10},{4,12},{6,14},{8,16},{10,18},{12,20},{14,22},{16,24},... | collective-permute-start | bytes 589832 | tf_op jit(solution)/shard_map/ppermute | solution.py:19
  54.0 13.4 %collective-permute-start.5 = (bf16[384,256]{1,0:T(8,128)(2,1)}, bf16[384,256]{1,0:T(8,128)(2,1)S(1)}, u32[]{:S(2)}, u32[]{:S(2)}) collective-permute-start(bf16[384,256]{1,0:T(8,128)(2,1)} %copy-done.1), channel_id=1, source_target_pairs={{0,4},{2,6},{4,0},{6,2},{8,12},{10,14},{12,8},{14,10},{16,20},{18,... | collective-permute-start | bytes 589832 | tf_op jit(solution)/shard_map/ppermute | solution.py:23
  54.6 20.5 %collective-permute-start.9 = (bf16[384,256]{1,0:T(8,128)(2,1)S(1)}, bf16[384,256]{1,0:T(8,128)(2,1)S(1)}, u32[]{:S(2)}, u32[]{:S(2)}) collective-permute-start(bf16[384,256]{1,0:T(8,128)(2,1)S(1)} %broadcast_select_fusion.1), channel_id=1, source_target_pairs={{0,4},{2,6},{4,0},{6,2},{8,12},{10,14},{12,8},{14,10},{16,20},{18,... | collective-permute-start | bytes 589832 | tf_op jit(solution)/shard_map/ppermute | solution.py:23
  57.7 9.1 %collective-permute-start.8 = (bf16[384,256]{1,0:T(8,128)(2,1)S(1)}, bf16[384,256]{1,0:T(8,128)(2,1)S(1)}, u32[]{:S(2)}, u32[]{:S(2)}) collective-permute-start(bf16[384,256]{1,0:T(8,128)(2,1)S(1)} %collective-permute-done.4.refs_4_), channel_id=1, source_target_pairs={{0,8},{2,10},{4,12},{6,14},{8,16},{10,18},{12,20},{14,22},{16,24},... | collective-permute-start | bytes 589832 | tf_op jit(solution)/shard_map/ppermute | solution.py:19
  66.8 7.2 %collective-permute-start.6 = (bf16[384,256]{1,0:T(8,128)(2,1)S(1)}, bf16[384,256]{1,0:T(8,128)(2,1)S(1)}, u32[]{:S(2)}, u32[]{:S(2)}) collective-permute-start(bf16[384,256]{1,0:T(8,128)(2,1)S(1)} %collective-permute-done.4.refs_4_), channel_id=1, source_target_pairs={{0,4},{2,6},{4,0},{6,2},{8,12},{10,14},{12,8},{14,10},{16,20},{18,... | collective-permute-start | bytes 589832 | tf_op jit(solution)/shard_map/ppermute | solution.py:23
  67.4 8.7 %collective-permute-start.10 = (bf16[384,256]{1,0:T(8,128)(2,1)S(1)}, bf16[384,256]{1,0:T(8,128)(2,1)S(1)}, u32[]{:S(2)}, u32[]{:S(2)}) collective-permute-start(bf16[384,256]{1,0:T(8,128)(2,1)S(1)} %broadcast_select_fusion), channel_id=1, source_target_pairs={{0,4},{2,6},{4,0},{6,2},{8,12},{10,14},{12,8},{14,10},{16,20},{18,... | collective-permute-start | bytes 589832 | tf_op jit(solution)/shard_map/ppermute | solution.py:23
  79.0 9.3 %collective-permute-start.11 = (bf16[384,512]{1,0:T(8,128)(2,1)S(1)}, bf16[384,512]{1,0:T(8,128)(2,1)S(1)}, u32[]{:S(2)}, u32[]{:S(2)}) collective-permute-start(bf16[384,512]{1,0:T(8,128)(2,1)S(1)} %shard_map.58), channel_id=1, source_target_pairs={{0,2},{2,0},{4,6},{6,4},{8,10},{10,8},{12,14},{14,12},{16,18},{18,... | collective-permute-start | bytes 1179656 | tf_op jit(solution)/shard_map/ppermute | solution.py:23
  79.1 21.9 %collective-permute-start.15 = (bf16[512,512]{1,0:T(8,128)(2,1)S(1)}, bf16[512,512]{1,0:T(8,128)(2,1)S(1)}, u32[]{:S(2)}, u32[]{:S(2)}) collective-permute-start(bf16[512,512]{1,0:T(8,128)(2,1)S(1)} %collective-permute-done.13.refs_0_), channel_id=1, source_target_pairs={{0,8},{2,10},{4,12},{6,14},{8,0},{10,2},{12,4},{14,6},{16,24},{18,... | collective-permute-start | bytes 1572872 | tf_op jit(solution)/shard_map/ppermute | solution.py:23
  88.2 23.8 %collective-permute-start.16 = (bf16[512,512]{1,0:T(8,128)(2,1)S(1)}, bf16[512,512]{1,0:T(8,128)(2,1)}, u32[]{:S(2)}, u32[]{:S(2)}) collective-permute-start(bf16[512,512]{1,0:T(8,128)(2,1)S(1)} %collective-permute-done.14.refs_1_), channel_id=1, source_target_pairs={{0,8},{2,10},{4,12},{6,14},{8,0},{10,2},{12,4},{14,6},{16,24},{18,... | collective-permute-start | bytes 1572872 | tf_op jit(solution)/shard_map/ppermute | solution.py:23
  91.3 24.7 %collective-permute-start.12 = (bf16[384,1024]{1,0:T(8,128)(2,1)S(1)}, bf16[384,1024]{1,0:T(8,128)(2,1)S(1)}, u32[]{:S(2)}, u32[]{:S(2)}) collective-permute-start(bf16[384,1024]{1,0:T(8,128)(2,1)S(1)} %shard_map.59), channel_id=1, source_target_pairs={{0,1},{1,0},{2,3},{3,2},{4,5},{5,4},{6,7},{7,6},{8,9},{9,8},{10,11... | collective-permute-start | bytes 2359304 | tf_op jit(solution)/shard_map/ppermute | solution.py:29
  92.9 23.1 %collective-permute-start.17 = (bf16[512,512]{1,0:T(8,128)(2,1)S(1)}, bf16[512,512]{1,0:T(8,128)(2,1)}, u32[]{:S(2)}, u32[]{:S(2)}) collective-permute-start(bf16[512,512]{1,0:T(8,128)(2,1)S(1)} %collective-permute-done.13.refs_0_), channel_id=1, source_target_pairs={{0,2},{2,0},{4,6},{6,4},{8,10},{10,8},{12,14},{14,12},{16,18},{18,... | collective-permute-start | bytes 1572872 | tf_op jit(solution)/shard_map/ppermute | solution.py:23
  92.9 23.1 %collective-permute-start.18 = (bf16[512,512]{1,0:T(8,128)(2,1)S(1)}, bf16[512,512]{1,0:T(8,128)(2,1)}, u32[]{:S(2)}, u32[]{:S(2)}) collective-permute-start(bf16[512,512]{1,0:T(8,128)(2,1)S(1)} %collective-permute-done.14.refs_1_), channel_id=1, source_target_pairs={{0,2},{2,0},{4,6},{6,4},{8,10},{10,8},{12,14},{14,12},{16,18},{18,... | collective-permute-start | bytes 1572872 | tf_op jit(solution)/shard_map/ppermute | solution.py:23
  100.9 15.1 %collective-permute-start.19 = (bf16[512,512]{1,0:T(8,128)(2,1)S(1)}, bf16[512,512]{1,0:T(8,128)(2,1)}, u32[]{:S(2)}, u32[]{:S(2)}) collective-permute-start(bf16[512,512]{1,0:T(8,128)(2,1)S(1)} %collective-permute-done.15.refs_2_), channel_id=1, source_target_pairs={{0,2},{2,0},{4,6},{6,4},{8,10},{10,8},{12,14},{14,12},{16,18},{18,... | collective-permute-start | bytes 1572872 | tf_op jit(solution)/shard_map/ppermute | solution.py:23
  112.0 4.0 %collective-permute-start.20 = (bf16[512,512]{1,0:T(8,128)(2,1)}, bf16[512,512]{1,0:T(8,128)(2,1)}, u32[]{:S(2)}, u32[]{:S(2)}) collective-permute-start(bf16[512,512]{1,0:T(8,128)(2,1)} %collective-permute-done.16.refs_3_), channel_id=1, source_target_pairs={{0,2},{2,0},{4,6},{6,4},{8,10},{10,8},{12,14},{14,12},{16,18},{18,... | collective-permute-start | bytes 1572872 | tf_op jit(solution)/shard_map/ppermute | solution.py:23

commit v4 on v3

--- a/solution.py
+++ b/solution.py
@@ -46,14 +46,14 @@
 
 def slice_weight(weight, after):
     anywhere = pl.BlockSpec(memory_space=pl.ANY)
-    hbm = pl.BlockSpec(memory_space=pltpu.HBM)
     out = jax.ShapeDtypeStruct((weight.shape[0] // 2, weight.shape[1] // 8), weight.dtype)
     return pl.pallas_call(
         slice_kernel,
         out_shape=[out] * 2,
-        in_specs=[hbm, anywhere],
-        out_specs=[hbm] * 2,
+        in_specs=[pl.BlockSpec(memory_space=pltpu.HBM), anywhere],
+        out_specs=[pl.BlockSpec(memory_space=pltpu.VMEM)] * 2,
         scratch_shapes=[pltpu.SemaphoreType.DMA((2,))],
+        compiler_params=pltpu.CompilerParams(vmem_limit_bytes=57 * 2**20),
     )(weight, after)
 
 

time: 122 us -> 90.8 us (0.74)
  Pallas kernels: 48.8 us -> 18.3 us
    pallas_call x1, Pallas kernels: 32.9 us -> 2.29 us  [slice_weight(): pl.pallas_call(slice_kernel, out_shape=[out] * 2, in_specs=[pl.BlockSpec(...]
  transfers between devices with their start and end apart: 21 -> 21, of which waited for: 6 -> 6; matrix products, arithmetic and copies ran while one was open for 5% -> 6% of each run, Pallas kernels for 37% -> 16%
where the time goes in v4:
time: 90.8 us; the launch traced here: 89.6 us
  starting transfers between devices  34.2 us (38%)
  waiting for transfers between devices  30.4 us (33%)
  Pallas kernels  18.3 us (20%)
  matrix products  3.99 us (4%)
  local copies, waits for them, and re-layouts  2.1 us (2%)
    ppermute x14, waiting for transfers between devices, swap(): lax.ppermute(x, 'ctx', [(i, i ^ mask) for i in range(lax.axis_size('ctx'))])  24.7 us
    ppermute x4, starting transfers between devices, shift(): lax.ppermute(x, 'ctx', [(i, i + distance) for i in range(n - distance)])  15.7 us
    ppermute x14, starting transfers between devices, swap(): lax.ppermute(x, 'ctx', [(i, i ^ mask) for i in range(lax.axis_size('ctx'))])  14.8 us
    pallas_call x5, Pallas kernels, attention_call(): pl.pallas_call(functools.partial(attention_kernel, stage, distances, n_he...  11.7 us
    ppermute x4, waiting for transfers between devices, shift(): lax.ppermute(x, 'ctx', [(i, i + distance) for i in range(n - distance)])  5.66 us
    pallas_call x1, Pallas kernels, project(): pl.pallas_call(project_kernel, out_shape=jax.ShapeDtypeStruct(given.shape...  4.32 us
    dot_general x1, matrix products, per_device(): jnp.dot(heads, part(out_weight, head, cols), preferred_element_type=jnp.f...  3.99 us
    ppermute x3, starting transfers between devices, cross(): return lax.ppermute(x, ('ctx', 'head'), route)  3.68 us
  transfers between devices with their start and end apart: 21, of which 6 were waited for; matrix products, arithmetic and copies ran while one was open for 6% of the time, Pallas kernels for 16%

profile of v4, /device:TPU:2, one launch (start us, length us, event | category | flops | bytes accessed | tf_op | source)
XLA Modules:
  0.0 89.6 jit_solution(8114833177065465230)
XLA Ops:
  0.0 1.1 %constant_dynamic-slice_fusion = (bf16[384,128]{1,0:T(8,128)(2,1)S(1)}, bf16[384,128]{1,0:T(8,128)(2,1)S(1)}, bf16[384,128]{1,0:T(8,128)(2,1)S(1)}, bf16[384,128]{1,0:T(8,128)(2,1)S(1)}) fusion(bf16[384,256]{1,0:T(8,128)(2,1)} %param.7, s32[]{:T(128)S(6)} %select_n.44, s32[]{:T(128)S(6)} %select_n.43, bf16[384,256]{1,0:T(8,128)(2,1)} %param.6), kind=kLoop, calls=%fused_computation.8 | loop fusion | bytes 786440 | tf_op jit(solution)/shard_map/dynamic_slice | solution.py:272
  1.1 3.5 %collective-permute-start.3 = (bf16[384,256]{1,0:T(8,128)(2,1)S(1)}, bf16[384,256]{1,0:T(8,128)(2,1)S(1)}, u32[]{:S(2)}, u32[]{:S(2)}) collective-permute-start(bf16[384,256]{1,0:T(8,128)(2,1)S(1)} %pad_maximum_fusion.refs_2_), channel_id=1, source_target_pairs={{0,8},{2,10},{4,12},{6,14},{8,16},{10,18},{12,20},{14,22},{16,24},... | collective-permute-start | bytes 589832 | tf_op jit(solution)/shard_map/ppermute | solution.py:19
  4.6 0.1 collective-permute-start.2
  4.7 4.0 %collective-permute-done.3.refs_3_._ = bf16[384,256]{1,0:T(8,128)(2,1)S(1)} collective-permute-done((bf16[384,256]{1,0:T(8,128)(2,1)S(1)}, bf16[384,256]{1,0:T(8,128)(2,1)S(1)}, u32[]{:S(2)}, u32[]{:S(2)}) %collective-permute-start.3) | collective-permute-done | bytes 196640 | tf_op jit(solution)/shard_map/ppermute | solution.py:19
  8.7 0.0 copy-start.1
  8.7 4.4 %collective-permute-start.7 = (bf16[384,256]{1,0:T(8,128)(2,1)S(1)}, bf16[384,256]{1,0:T(8,128)(2,1)S(1)}, u32[]{:S(2)}, u32[]{:S(2)}) collective-permute-start(bf16[384,256]{1,0:T(8,128)(2,1)S(1)} %collective-permute-done.3.refs_3_._), channel_id=1, source_target_pairs={{0,8},{2,10},{4,12},{6,14},{8,16},{10,18},{12,20},{14,22},{16,24},... | collective-permute-start | bytes 589832 | tf_op jit(solution)/shard_map/ppermute | solution.py:19
  13.1 1.0 %constant_dynamic-slice_fusion.4 = bf16[384,512]{1,0:T(8,128)(2,1)S(1)} fusion(bf16[384,1024]{1,0:T(8,128)(2,1)} %refs_0_.1, s32[]{:T(128)S(6)} %select_n.42), kind=kLoop, calls=%fused_computation.12 | loop fusion | bytes 786436 | tf_op jit(solution)/shard_map/dynamic_slice | solution.py:272
  14.2 0.1 collective-permute-start.1
  14.2 0.5 collective-permute-start
  14.7 0.0 copy-done.1
  14.7 0.0 copy-start
  14.7 0.0 copy-start.3
  14.7 2.3 %shard_map.60 = (bf16[512,512]{1,0:T(8,128)(2,1)}, bf16[512,512]{1,0:T(8,128)(2,1)}) custom-call(bf16[1024,4096]{1,0:T(8,128)(2,1)} %weight_ref.1, bf16[384,256]{1,0:T(8,128)(2,1)} %copy-done.1), custom_call_target="tpu_custom_call" | custom-call | tf_op jit(solution)/shard_map/pallas_call | solution.py:50
  17.0 0.0 copy-start.2
  17.0 1.6 %collective-permute-start.13 = (bf16[512,512]{1,0:T(8,128)(2,1)}, bf16[512,512]{1,0:T(8,128)(2,1)S(1)}, u32[]{:S(2)}, u32[]{:S(2)}) collective-permute-start(bf16[512,512]{1,0:T(8,128)(2,1)} %get-tuple-element.21), channel_id=1, source_target_pairs={{0,1},{1,0},{2,3},{3,2},{4,5},{5,4},{6,7},{7,6},{8,9},{9,8},{10,11... | collective-permute-start | bytes 1572872 | tf_op jit(solution)/shard_map/ppermute | solution.py:29
  18.6 0.0 collective-permute-done.2.refs_3_
  18.6 0.5 collective-permute-start.14
  19.1 0.0 collective-permute-done.7.refs_5_
  19.1 3.5 %collective-permute-start.4 = (bf16[384,256]{1,0:T(8,128)(2,1)S(1)}, bf16[384,256]{1,0:T(8,128)(2,1)S(1)}, u32[]{:S(2)}, u32[]{:S(2)}) collective-permute-start(bf16[384,256]{1,0:T(8,128)(2,1)S(1)} %collective-permute-done.2.refs_3_), channel_id=1, source_target_pairs={{0,8},{2,10},{4,12},{6,14},{8,16},{10,18},{12,20},{14,22},{16,24},... | collective-permute-start | bytes 589832 | tf_op jit(solution)/shard_map/ppermute | solution.py:19
  22.6 0.1 broadcast_select_fusion.1
  22.7 0.0 collective-permute-done.recv_starts_ref
  22.7 0.6 collective-permute-start.5
  23.3 0.0 collective-permute-done.1.refs_1_
  23.3 1.5 %collective-permute-start.9 = (bf16[384,256]{1,0:T(8,128)(2,1)S(1)}, bf16[384,256]{1,0:T(8,128)(2,1)S(1)}, u32[]{:S(2)}, u32[]{:S(2)}) collective-permute-start(bf16[384,256]{1,0:T(8,128)(2,1)S(1)} %broadcast_select_fusion.1), channel_id=1, source_target_pairs={{0,4},{2,6},{4,0},{6,2},{8,12},{10,14},{12,8},{14,10},{16,20},{18,... | collective-permute-start | bytes 589832 | tf_op jit(solution)/shard_map/ppermute | solution.py:23
  24.8 1.6 %collective-permute-done.4.refs_4_ = bf16[384,256]{1,0:T(8,128)(2,1)S(1)} collective-permute-done((bf16[384,256]{1,0:T(8,128)(2,1)S(1)}, bf16[384,256]{1,0:T(8,128)(2,1)S(1)}, u32[]{:S(2)}, u32[]{:S(2)}) %collective-permute-start.4) | collective-permute-done | bytes 196640 | tf_op jit(solution)/shard_map/ppermute | solution.py:19
  26.4 4.4 %collective-permute-start.8 = (bf16[384,256]{1,0:T(8,128)(2,1)S(1)}, bf16[384,256]{1,0:T(8,128)(2,1)S(1)}, u32[]{:S(2)}, u32[]{:S(2)}) collective-permute-start(bf16[384,256]{1,0:T(8,128)(2,1)S(1)} %collective-permute-done.4.refs_4_), channel_id=1, source_target_pairs={{0,8},{2,10},{4,12},{6,14},{8,16},{10,18},{12,20},{14,22},{16,24},... | collective-permute-start | bytes 589832 | tf_op jit(solution)/shard_map/ppermute | solution.py:19
  30.8 0.0 copy-done
  30.8 0.0 copy-done.3
  30.9 3.7 %shard_map.55 = (bf16[6,512,128]{2,1,0:T(8,128)(2,1)S(1)}, f32[6,512,128]{2,1,0:T(8,128)S(1)}, f32[6,512,256]{2,1,0:T(8,128)S(1)}) custom-call(s32[3]{0:T(128)S(1)} %copy-done.3, s32[3]{0:T(128)S(1)} %collective-permute-done.recv_starts_ref, bf16[384,1024]{1,0:T(8,128)(2,1)S(1)} %copy-done, bf16[384,512]{1,0:T(8,128)(2,1)S(1)} %collective-permute-done.1.refs_1_, ...), custom_call_target="tpu_custom_call" | custom-call | flops 1449551488 | bytes 8388608 | tf_op jit(solution)/shard_map/pallas_call | solution.py:248
  34.6 0.0 copy-done.2
  34.6 1.0 %shard_map.56 = (f32[6,512,128]{2,1,0:T(8,128)S(1)}, f32[6,512,256]{2,1,0:T(8,128)S(1)}) custom-call(s32[3]{0:T(128)S(1)} %copy-done.3, s32[3]{0:T(128)S(1)} %collective-permute-done.recv_starts_ref, bf16[6,512,128]{2,1,0:T(8,128)(2,1)S(1)} %get-tuple-element.14.refs_0_, f32[6,512,128]{2,1,0:T(8,128)S(1)} %get-tuple-element.15.refs_1_, ...), custom_call_target="tpu_custom_call" | custom-call | flops 2415919104 | bytes 8388608 | tf_op jit(solution)/shard_map/pallas_call | solution.py:248
  35.6 0.0 collective-permute-done.8.refs_6_
  35.6 0.6 collective-permute-start.6
  36.2 0.0 collective-permute-done.5.refs_3_
  36.2 1.6 %collective-permute-start.10 = (bf16[384,256]{1,0:T(8,128)(2,1)S(1)}, bf16[384,256]{1,0:T(8,128)(2,1)S(1)}, u32[]{:S(2)}, u32[]{:S(2)}) collective-permute-start(bf16[384,256]{1,0:T(8,128)(2,1)S(1)} %broadcast_select_fusion), channel_id=1, source_target_pairs={{0,4},{2,6},{4,0},{6,2},{8,12},{10,14},{12,8},{14,10},{16,20},{18,... | collective-permute-start | bytes 589832 | tf_op jit(solution)/shard_map/ppermute | solution.py:23
  37.8 5.1 %collective-permute-done.6.refs_4_ = bf16[384,256]{1,0:T(8,128)(2,1)S(1)} collective-permute-done((bf16[384,256]{1,0:T(8,128)(2,1)S(1)}, bf16[384,256]{1,0:T(8,128)(2,1)S(1)}, u32[]{:S(2)}, u32[]{:S(2)}) %collective-permute-start.6) | collective-permute-done | bytes 196640 | tf_op jit(solution)/shard_map/ppermute | solution.py:23
  42.9 1.0 %shard_map.57 = (f32[6,512,128]{2,1,0:T(8,128)S(1)}, f32[6,512,256]{2,1,0:T(8,128)S(1)}) custom-call(s32[3]{0:T(128)S(1)} %copy-done.3, s32[3]{0:T(128)S(1)} %collective-permute-done.recv_starts_ref, bf16[6,512,128]{2,1,0:T(8,128)(2,1)S(1)} %get-tuple-element.14.refs_0_, f32[6,512,128]{2,1,0:T(8,128)S(1)} %get-tuple-element.17.refs_1_, ...), custom_call_target="tpu_custom_call" | custom-call | flops 4831838208 | bytes 8388608 | tf_op jit(solution)/shard_map/pallas_call | solution.py:248
  43.9 0.0 collective-permute-done.9.refs_3_
  43.9 1.0 %collective-permute-done.10.refs_4_ = bf16[384,256]{1,0:T(8,128)(2,1)S(1)} collective-permute-done((bf16[384,256]{1,0:T(8,128)(2,1)S(1)}, bf16[384,256]{1,0:T(8,128)(2,1)S(1)}, u32[]{:S(2)}, u32[]{:S(2)}) %collective-permute-start.10) | collective-permute-done | bytes 196640 | tf_op jit(solution)/shard_map/ppermute | solution.py:23
  45.0 2.9 %shard_map.58 = bf16[384,512]{1,0:T(8,128)(2,1)S(1)} custom-call(s32[3]{0:T(128)S(1)} %copy-done.3, s32[3]{0:T(128)S(1)} %collective-permute-done.recv_starts_ref, bf16[6,512,128]{2,1,0:T(8,128)(2,1)S(1)} %get-tuple-element.14.refs_0_, f32[6,512,128]{2,1,0:T(8,128)S(1)} %get-tuple-element.19.refs_1_, f32[6,512,256]{2,1,0:T(8,128)S(1)} %get-tuple-element.20.refs_2_, ...), custom_call_target="tpu_custom_call" | custom-call | flops 1207959552 | bytes 8388608 | tf_op jit(solution)/shard_map/pallas_call | solution.py:248
  47.8 0.1 collective-permute-start.11
  47.9 0.0 collective-permute-done.13.refs_0_
  47.9 9.2 %collective-permute-start.15 = (bf16[512,512]{1,0:T(8,128)(2,1)S(1)}, bf16[512,512]{1,0:T(8,128)(2,1)S(1)}, u32[]{:S(2)}, u32[]{:S(2)}) collective-permute-start(bf16[512,512]{1,0:T(8,128)(2,1)S(1)} %collective-permute-done.13.refs_0_), channel_id=1, source_target_pairs={{0,8},{2,10},{4,12},{6,14},{8,0},{10,2},{12,4},{14,6},{16,24},{18,... | collective-permute-start | bytes 1572872 | tf_op jit(solution)/shard_map/ppermute | solution.py:23
  57.2 0.0 collective-permute-done.14.refs_1_
  57.2 0.1 collective-permute-start.16
  57.3 0.0 collective-permute-done.11.refs_5_
  57.3 3.1 %shard_map.59 = bf16[384,1024]{1,0:T(8,128)(2,1)S(1)} custom-call(s32[3]{0:T(128)S(1)} %copy-done.3, s32[3]{0:T(128)S(1)} %collective-permute-done.recv_starts_ref, bf16[6,512,128]{2,1,0:T(8,128)(2,1)S(1)} %get-tuple-element.14.refs_0_, f32[6,512,128]{2,1,0:T(8,128)S(1)} %get-tuple-element.19.refs_1_, f32[6,512,256]{2,1,0:T(8,128)S(1)} %get-tuple-element.20.refs_2_, ...), custom_call_target="tpu_custom_call" | custom-call | flops 1207959552 | bytes 8388608 | tf_op jit(solution)/shard_map/pallas_call | solution.py:248
  60.4 1.6 %collective-permute-start.12 = (bf16[384,1024]{1,0:T(8,128)(2,1)S(1)}, bf16[384,1024]{1,0:T(8,128)(2,1)S(1)}, u32[]{:S(2)}, u32[]{:S(2)}) collective-permute-start(bf16[384,1024]{1,0:T(8,128)(2,1)S(1)} %shard_map.59), channel_id=1, source_target_pairs={{0,1},{1,0},{2,3},{3,2},{4,5},{5,4},{6,7},{7,6},{8,9},{9,8},{10,11... | collective-permute-start | bytes 2359304 | tf_op jit(solution)/shard_map/ppermute | solution.py:29
  62.0 0.0 collective-permute-start.17
  62.0 0.5 collective-permute-start.18
  62.5 7.5 %collective-permute-done.15.refs_2_ = bf16[512,512]{1,0:T(8,128)(2,1)S(1)} collective-permute-done((bf16[512,512]{1,0:T(8,128)(2,1)S(1)}, bf16[512,512]{1,0:T(8,128)(2,1)S(1)}, u32[]{:S(2)}, u32[]{:S(2)}) %collective-permute-start.15) | collective-permute-done | bytes 524320 | tf_op jit(solution)/shard_map/ppermute | solution.py:23
  69.9 0.0 collective-permute-start.19
  70.0 11.1 %collective-permute-done.16.refs_3_ = bf16[512,512]{1,0:T(8,128)(2,1)} collective-permute-done((bf16[512,512]{1,0:T(8,128)(2,1)S(1)}, bf16[512,512]{1,0:T(8,128)(2,1)}, u32[]{:S(2)}, u32[]{:S(2)}) %collective-permute-start.16) | collective-permute-done | bytes 524320 | tf_op jit(solution)/shard_map/ppermute | solution.py:23
  81.0 0.0 collective-permute-start.20
  81.0 4.0 %fusion.2.given_ref = bf16[384,2048]{1,0:T(8,128)(2,1)S(1)} fusion(bf16[384,1024]{1,0:T(8,128)(2,1)S(1)} %shard_map.59, bf16[1024,4096]{1,0:T(8,128)(2,1)} %weight_ref.1, s32[]{:T(128)S(6)} %select_n.50), kind=kOutput, calls=%fused_computation.2 | convolution fusion | flops 1611399168 | bytes 6553604 | tf_op jit(solution)/shard_map/dot_general | solution.py:295
  85.0 0.0 collective-permute-done.17.refs_4_
  85.0 0.0 collective-permute-done.18.refs_5_
  85.0 0.0 collective-permute-done.19.refs_6_
  85.1 0.0 collective-permute-done.20.refs_7_
  85.1 0.0 collective-permute-done.12.heads_ref
  85.1 4.3 %shard_map.61 = bf16[384,2048]{1,0:T(8,128)(2,1)} custom-call(bf16[384,2048]{1,0:T(8,128)(2,1)S(1)} %fusion.2.given_ref, bf16[384,1024]{1,0:T(8,128)(2,1)S(1)} %collective-permute-done.12.heads_ref, bf16[512,512]{1,0:T(8,128)(2,1)S(1)} %collective-permute-done.13.refs_0_, bf16[512,512]{1,0:T(8,128)(2,1)S(1)} %collective-permute-done.14.refs_1_, ...), custom_call_target="tpu_custom_call" | custom-call | flops 1610612736 | bytes 4194304 | tf_op jit(solution)/shard_map/pallas_call | solution.py:83
  (3 shorter events, 0.1 us)
Async XLA Ops:
  1.1 7.6 %collective-permute-start.3 = (bf16[384,256]{1,0:T(8,128)(2,1)S(1)}, bf16[384,256]{1,0:T(8,128)(2,1)S(1)}, u32[]{:S(2)}, u32[]{:S(2)}) collective-permute-start(bf16[384,256]{1,0:T(8,128)(2,1)S(1)} %pad_maximum_fusion.refs_2_), channel_id=1, source_target_pairs={{0,8},{2,10},{4,12},{6,14},{8,16},{10,18},{12,20},{14,22},{16,24},... | collective-permute-start | bytes 589832 | tf_op jit(solution)/shard_map/ppermute | solution.py:19
  4.6 14.0 %collective-permute-start.2 = (bf16[384,256]{1,0:T(8,128)(2,1)S(1)}, bf16[384,256]{1,0:T(8,128)(2,1)S(1)}, u32[]{:S(2)}, u32[]{:S(2)}) collective-permute-start(bf16[384,256]{1,0:T(8,128)(2,1)S(1)} %pad_maximum_fusion.1), channel_id=1, source_target_pairs={{0,2},{2,0},{4,6},{6,4},{8,10},{10,8},{12,14},{14,12},{16,18},{18,... | collective-permute-start | bytes 589832 | tf_op jit(solution)/shard_map/ppermute | solution.py:23
  8.7 6.0 %copy-start.1 = (bf16[384,256]{1,0:T(8,128)(2,1)}, bf16[384,256]{1,0:T(8,128)(2,1)S(1)}, u32[]{:S(2)}) copy-start(bf16[384,256]{1,0:T(8,128)(2,1)S(1)} %collective-permute-done.3.refs_3_._) | copy-start | bytes 589828
  8.7 10.4 %collective-permute-start.7 = (bf16[384,256]{1,0:T(8,128)(2,1)S(1)}, bf16[384,256]{1,0:T(8,128)(2,1)S(1)}, u32[]{:S(2)}, u32[]{:S(2)}) collective-permute-start(bf16[384,256]{1,0:T(8,128)(2,1)S(1)} %collective-permute-done.3.refs_3_._), channel_id=1, source_target_pairs={{0,8},{2,10},{4,12},{6,14},{8,16},{10,18},{12,20},{14,22},{16,24},... | collective-permute-start | bytes 589832 | tf_op jit(solution)/shard_map/ppermute | solution.py:19
  14.2 9.1 %collective-permute-start.1 = (bf16[384,512]{1,0:T(8,128)(2,1)S(1)}, bf16[384,512]{1,0:T(8,128)(2,1)S(1)}, u32[]{:S(2)}, u32[]{:S(2)}) collective-permute-start(bf16[384,512]{1,0:T(8,128)(2,1)S(1)} %constant_dynamic-slice_fusion.4), channel_id=1, source_target_pairs={{0,2},{2,0},{4,6},{6,4},{8,10},{10,8},{12,14},{14,12},{16,18},{18,... | collective-permute-start | bytes 1179656 | tf_op jit(solution)/shard_map/ppermute | solution.py:23
  14.2 8.5 %collective-permute-start = (s32[3]{0:T(128)}, s32[3]{0:T(128)S(1)}, u32[]{:S(2)}, u32[]{:S(2)}) collective-permute-start(s32[3]{0:T(128)} %starts_ref.9), channel_id=1, source_target_pairs={{0,2},{2,0},{4,6},{6,4},{8,10},{10,8},{12,14},{14,12},{16,18},{18,... | collective-permute-start | bytes 44 | tf_op jit(solution)/shard_map/ppermute | solution.py:23
  14.7 16.1 %copy-start = (bf16[384,1024]{1,0:T(8,128)(2,1)S(1)}, bf16[384,1024]{1,0:T(8,128)(2,1)}, u32[]{:S(2)}) copy-start(bf16[384,1024]{1,0:T(8,128)(2,1)} %refs_0_.1) | copy-start | bytes 2359300
  14.7 16.1 %copy-start.3 = (s32[3]{0:T(128)S(1)}, s32[3]{0:T(128)}, u32[]{:S(2)}) copy-start(s32[3]{0:T(128)} %starts_ref.9) | copy-start | bytes 40
  17.0 17.5 %copy-start.2 = (bf16[384,256]{1,0:T(8,128)(2,1)S(1)}, bf16[384,256]{1,0:T(8,128)(2,1)}, u32[]{:S(2)}) copy-start(bf16[384,256]{1,0:T(8,128)(2,1)} %copy-done.1) | copy-start | bytes 589828
  17.0 30.9 %collective-permute-start.13 = (bf16[512,512]{1,0:T(8,128)(2,1)}, bf16[512,512]{1,0:T(8,128)(2,1)S(1)}, u32[]{:S(2)}, u32[]{:S(2)}) collective-permute-start(bf16[512,512]{1,0:T(8,128)(2,1)} %get-tuple-element.21), channel_id=1, source_target_pairs={{0,1},{1,0},{2,3},{3,2},{4,5},{5,4},{6,7},{7,6},{8,9},{9,8},{10,11... | collective-permute-start | bytes 1572872 | tf_op jit(solution)/shard_map/ppermute | solution.py:29
  18.6 38.5 %collective-permute-start.14 = (bf16[512,512]{1,0:T(8,128)(2,1)}, bf16[512,512]{1,0:T(8,128)(2,1)S(1)}, u32[]{:S(2)}, u32[]{:S(2)}) collective-permute-start(bf16[512,512]{1,0:T(8,128)(2,1)} %get-tuple-element.22), channel_id=1, source_target_pairs={{0,1},{1,0},{2,3},{3,2},{4,5},{5,4},{6,7},{7,6},{8,9},{9,8},{10,11... | collective-permute-start | bytes 1572872 | tf_op jit(solution)/shard_map/ppermute | solution.py:29
  19.1 7.3 %collective-permute-start.4 = (bf16[384,256]{1,0:T(8,128)(2,1)S(1)}, bf16[384,256]{1,0:T(8,128)(2,1)S(1)}, u32[]{:S(2)}, u32[]{:S(2)}) collective-permute-start(bf16[384,256]{1,0:T(8,128)(2,1)S(1)} %collective-permute-done.2.refs_3_), channel_id=1, source_target_pairs={{0,8},{2,10},{4,12},{6,14},{8,16},{10,18},{12,20},{14,22},{16,24},... | collective-permute-start | bytes 589832 | tf_op jit(solution)/shard_map/ppermute | solution.py:19
  22.7 13.5 %collective-permute-start.5 = (bf16[384,256]{1,0:T(8,128)(2,1)}, bf16[384,256]{1,0:T(8,128)(2,1)S(1)}, u32[]{:S(2)}, u32[]{:S(2)}) collective-permute-start(bf16[384,256]{1,0:T(8,128)(2,1)} %copy-done.1), channel_id=1, source_target_pairs={{0,4},{2,6},{4,0},{6,2},{8,12},{10,14},{12,8},{14,10},{16,20},{18,... | collective-permute-start | bytes 589832 | tf_op jit(solution)/shard_map/ppermute | solution.py:23
  23.3 20.6 %collective-permute-start.9 = (bf16[384,256]{1,0:T(8,128)(2,1)S(1)}, bf16[384,256]{1,0:T(8,128)(2,1)S(1)}, u32[]{:S(2)}, u32[]{:S(2)}) collective-permute-start(bf16[384,256]{1,0:T(8,128)(2,1)S(1)} %broadcast_select_fusion.1), channel_id=1, source_target_pairs={{0,4},{2,6},{4,0},{6,2},{8,12},{10,14},{12,8},{14,10},{16,20},{18,... | collective-permute-start | bytes 589832 | tf_op jit(solution)/shard_map/ppermute | solution.py:23
  26.4 9.1 %collective-permute-start.8 = (bf16[384,256]{1,0:T(8,128)(2,1)S(1)}, bf16[384,256]{1,0:T(8,128)(2,1)S(1)}, u32[]{:S(2)}, u32[]{:S(2)}) collective-permute-start(bf16[384,256]{1,0:T(8,128)(2,1)S(1)} %collective-permute-done.4.refs_4_), channel_id=1, source_target_pairs={{0,8},{2,10},{4,12},{6,14},{8,16},{10,18},{12,20},{14,22},{16,24},... | collective-permute-start | bytes 589832 | tf_op jit(solution)/shard_map/ppermute | solution.py:19
  35.6 7.3 %collective-permute-start.6 = (bf16[384,256]{1,0:T(8,128)(2,1)S(1)}, bf16[384,256]{1,0:T(8,128)(2,1)S(1)}, u32[]{:S(2)}, u32[]{:S(2)}) collective-permute-start(bf16[384,256]{1,0:T(8,128)(2,1)S(1)} %collective-permute-done.4.refs_4_), channel_id=1, source_target_pairs={{0,4},{2,6},{4,0},{6,2},{8,12},{10,14},{12,8},{14,10},{16,20},{18,... | collective-permute-start | bytes 589832 | tf_op jit(solution)/shard_map/ppermute | solution.py:23
  36.2 8.8 %collective-permute-start.10 = (bf16[384,256]{1,0:T(8,128)(2,1)S(1)}, bf16[384,256]{1,0:T(8,128)(2,1)S(1)}, u32[]{:S(2)}, u32[]{:S(2)}) collective-permute-start(bf16[384,256]{1,0:T(8,128)(2,1)S(1)} %broadcast_select_fusion), channel_id=1, source_target_pairs={{0,4},{2,6},{4,0},{6,2},{8,12},{10,14},{12,8},{14,10},{16,20},{18,... | collective-permute-start | bytes 589832 | tf_op jit(solution)/shard_map/ppermute | solution.py:23
  47.8 9.4 %collective-permute-start.11 = (bf16[384,512]{1,0:T(8,128)(2,1)S(1)}, bf16[384,512]{1,0:T(8,128)(2,1)S(1)}, u32[]{:S(2)}, u32[]{:S(2)}) collective-permute-start(bf16[384,512]{1,0:T(8,128)(2,1)S(1)} %shard_map.58), channel_id=1, source_target_pairs={{0,2},{2,0},{4,6},{6,4},{8,10},{10,8},{12,14},{14,12},{16,18},{18,... | collective-permute-start | bytes 1179656 | tf_op jit(solution)/shard_map/ppermute | solution.py:23
  47.9 22.0 %collective-permute-start.15 = (bf16[512,512]{1,0:T(8,128)(2,1)S(1)}, bf16[512,512]{1,0:T(8,128)(2,1)S(1)}, u32[]{:S(2)}, u32[]{:S(2)}) collective-permute-start(bf16[512,512]{1,0:T(8,128)(2,1)S(1)} %collective-permute-done.13.refs_0_), channel_id=1, source_target_pairs={{0,8},{2,10},{4,12},{6,14},{8,0},{10,2},{12,4},{14,6},{16,24},{18,... | collective-permute-start | bytes 1572872 | tf_op jit(solution)/shard_map/ppermute | solution.py:23
  57.2 23.8 %collective-permute-start.16 = (bf16[512,512]{1,0:T(8,128)(2,1)S(1)}, bf16[512,512]{1,0:T(8,128)(2,1)}, u32[]{:S(2)}, u32[]{:S(2)}) collective-permute-start(bf16[512,512]{1,0:T(8,128)(2,1)S(1)} %collective-permute-done.14.refs_1_), channel_id=1, source_target_pairs={{0,8},{2,10},{4,12},{6,14},{8,0},{10,2},{12,4},{14,6},{16,24},{18,... | collective-permute-start | bytes 1572872 | tf_op jit(solution)/shard_map/ppermute | solution.py:23
  60.4 24.7 %collective-permute-start.12 = (bf16[384,1024]{1,0:T(8,128)(2,1)S(1)}, bf16[384,1024]{1,0:T(8,128)(2,1)S(1)}, u32[]{:S(2)}, u32[]{:S(2)}) collective-permute-start(bf16[384,1024]{1,0:T(8,128)(2,1)S(1)} %shard_map.59), channel_id=1, source_target_pairs={{0,1},{1,0},{2,3},{3,2},{4,5},{5,4},{6,7},{7,6},{8,9},{9,8},{10,11... | collective-permute-start | bytes 2359304 | tf_op jit(solution)/shard_map/ppermute | solution.py:29
  62.0 23.1 %collective-permute-start.17 = (bf16[512,512]{1,0:T(8,128)(2,1)S(1)}, bf16[512,512]{1,0:T(8,128)(2,1)}, u32[]{:S(2)}, u32[]{:S(2)}) collective-permute-start(bf16[512,512]{1,0:T(8,128)(2,1)S(1)} %collective-permute-done.13.refs_0_), channel_id=1, source_target_pairs={{0,2},{2,0},{4,6},{6,4},{8,10},{10,8},{12,14},{14,12},{16,18},{18,... | collective-permute-start | bytes 1572872 | tf_op jit(solution)/shard_map/ppermute | solution.py:23
  62.0 23.1 %collective-permute-start.18 = (bf16[512,512]{1,0:T(8,128)(2,1)S(1)}, bf16[512,512]{1,0:T(8,128)(2,1)}, u32[]{:S(2)}, u32[]{:S(2)}) collective-permute-start(bf16[512,512]{1,0:T(8,128)(2,1)S(1)} %collective-permute-done.14.refs_1_), channel_id=1, source_target_pairs={{0,2},{2,0},{4,6},{6,4},{8,10},{10,8},{12,14},{14,12},{16,18},{18,... | collective-permute-start | bytes 1572872 | tf_op jit(solution)/shard_map/ppermute | solution.py:23
  69.9 15.1 %collective-permute-start.19 = (bf16[512,512]{1,0:T(8,128)(2,1)S(1)}, bf16[512,512]{1,0:T(8,128)(2,1)}, u32[]{:S(2)}, u32[]{:S(2)}) collective-permute-start(bf16[512,512]{1,0:T(8,128)(2,1)S(1)} %collective-permute-done.15.refs_2_), channel_id=1, source_target_pairs={{0,2},{2,0},{4,6},{6,4},{8,10},{10,8},{12,14},{14,12},{16,18},{18,... | collective-permute-start | bytes 1572872 | tf_op jit(solution)/shard_map/ppermute | solution.py:23
  81.0 4.0 %collective-permute-start.20 = (bf16[512,512]{1,0:T(8,128)(2,1)}, bf16[512,512]{1,0:T(8,128)(2,1)}, u32[]{:S(2)}, u32[]{:S(2)}) collective-permute-start(bf16[512,512]{1,0:T(8,128)(2,1)} %collective-permute-done.16.refs_3_), channel_id=1, source_target_pairs={{0,2},{2,0},{4,6},{6,4},{8,10},{10,8},{12,14},{14,12},{16,18},{18,... | collective-permute-start | bytes 1572872 | tf_op jit(solution)/shard_map/ppermute | solution.py:23

commit v5 on v4

--- a/solution.py
+++ b/solution.py
@@ -14,9 +14,9 @@
 TILE = 256
 
 
-def shift(x, distance):
+def rotate(x, distance):
     n = lax.axis_size("ctx")
-    return lax.ppermute(x, "ctx", [(i, i + distance) for i in range(n - distance)])
+    return lax.ppermute(x, "ctx", [(i, (i + distance) % n) for i in range(n)])
 
 
 def swap(x, mask):
@@ -29,47 +29,44 @@
     return lax.ppermute(x, ("ctx", "head"), route)
 
 
-def slice_kernel(weight_ref, _, *refs):
-    outs, sems = refs[:2], refs[2]
+def slice_weight(weight_ref, common_ref, single_ref):
     core, part = lax.axis_index("ctx") % 2, lax.axis_index("ctx") // 4 % 2
-    rows, cols = outs[0].shape
-    copies = []
-    for n, out in enumerate(outs):
-        col = ((1 - lax.axis_index("head")) * 4 + part * 2 + n) * cols
-        source = weight_ref.at[pl.ds(core * rows, rows), pl.ds(pl.multiple_of(col, cols), cols)]
-        copies.append(pltpu.make_async_copy(source, out, sems.at[n]))
-    for copy in copies:
-        copy.start()
-    for copy in copies:
-        copy.wait()
-
-
-def slice_weight(weight, after):
-    anywhere = pl.BlockSpec(memory_space=pl.ANY)
-    out = jax.ShapeDtypeStruct((weight.shape[0] // 2, weight.shape[1] // 8), weight.dtype)
+    rows, width = single_ref.shape
+    for out, tile in ((single_ref, 2 + part), (common_ref, 0)):
+        col = pl.multiple_of(((1 - lax.axis_index("head")) * 4 + tile) * width, width)
+        out[...] = weight_ref[pl.ds(pl.multiple_of(core * rows, rows), rows), pl.ds(col, out.shape[1])]
+
+
+def join_kernel(first_ref, second_ref, _, out_ref):
+    tok = first_ref.shape[0]
+    out_ref[:tok] = first_ref[...]
+    out_ref[tok:] = second_ref[...]
+
+
+def join(first, second, after):
+    vmem = pl.BlockSpec(memory_space=pltpu.VMEM)
     return pl.pallas_call(
-        slice_kernel,
-        out_shape=[out] * 2,
-        in_specs=[pl.BlockSpec(memory_space=pltpu.HBM), anywhere],
-        out_specs=[pl.BlockSpec(memory_space=pltpu.VMEM)] * 2,
-        scratch_shapes=[pltpu.SemaphoreType.DMA((2,))],
-        compiler_params=pltpu.CompilerParams(vmem_limit_bytes=57 * 2**20),
-    )(weight, after)
+        join_kernel,
+        out_shape=jax.ShapeDtypeStruct((2 * first.shape[0], first.shape[1]), first.dtype),
+        in_specs=[vmem, vmem, pl.BlockSpec(memory_space=pl.ANY)],
+        out_specs=vmem,
+        compiler_params=pltpu.CompilerParams(vmem_limit_bytes=4 * 2**20),
+    )(first, second, after)
 
 
 def project_kernel(given_ref, heads_ref, *refs):
-    tiles, out_ref, built, sems = refs[:8], refs[8], refs[9], refs[10]
+    parts, out_ref, built, sems = refs[:6], refs[6], refs[7], refs[8]
     me = lax.axis_index("ctx")
     core, part = me % 2, me // 4 % 2
-    group, width = tiles[0].shape
+    group, width = parts[1].shape
     copies = []
-    for n in range(4):
-        first = (part if n < 2 else 1 - part) * 2 + n % 2
+    for n, first in enumerate((0, 1, 2 + part, 3 - part)):
         cols = pl.ds(pl.multiple_of(first * width, width), width)
         total = given_ref[:, cols].astype(jnp.float32)
-        for index, tile in ((core, tiles[n]), (1 - core, tiles[4 + n])):
+        for index, (common, *single) in ((core, parts[:3]), (1 - core, parts[3:])):
             heads = heads_ref[:, pl.ds(pl.multiple_of(index * group, group), group)]
-            total += jnp.dot(heads, tile[...], preferred_element_type=jnp.float32)
+            tile = common[:, n * width : (n + 1) * width] if n < 2 else single[n - 2][...]
+            total += jnp.dot(heads, tile, preferred_element_type=jnp.float32)
         built[n] = total.astype(out_ref.dtype)
         copies.append(pltpu.make_async_copy(built.at[n], out_ref.at[:, cols], sems.at[n]))
         copies[-1].start()
@@ -83,7 +80,7 @@
     return pl.pallas_call(
         project_kernel,
         out_shape=jax.ShapeDtypeStruct(given.shape, jnp.bfloat16),
-        in_specs=[vmem] * 10,
+        in_specs=[vmem] * 8,
         out_specs=pl.BlockSpec(memory_space=pltpu.HBM),
         scratch_shapes=[pltpu.VMEM((4, tok, cols // 4), jnp.bfloat16), pltpu.SemaphoreType.DMA((4,))],
         compiler_params=pltpu.CompilerParams(vmem_limit_bytes=16 * 2**20),
@@ -93,21 +90,21 @@
     )(given, heads, *tiles)
 
 
-def attention_kernel(stage, distances, n_head, n_after, starts_ref, recv_starts_ref, *refs):
+def attention_kernel(stage, distances, n_head, starts_ref, recv_starts_ref, *refs):
     refs = list(refs)
     me = lax.axis_index("ctx")
     pair, core, col = me // 2, me % 2, (me // 2) % 2
     if stage == "first":
-        queries_ref, q_recv_ref = refs[:2]
-        refs = refs[2:]
+        weight_ref, queries_ref, q_recv_ref = refs[:3]
+        refs = refs[3:]
     else:
         q_ref, top_in, acc_in = refs[:3]
         refs = refs[3:]
     n_pieces = len(distances)
-    halves = refs[: 2 * n_pieces]
-    refs = refs[2 * n_pieces + n_after :]
+    pieces = refs[:n_pieces]
+    refs = refs[n_pieces:]
     if stage == "first":
-        q_ref, top_ref, acc_ref, held_ref = refs
+        q_ref, top_ref, acc_ref, common_ref, single_ref, held_ref = refs
     elif stage == "next":
         top_ref, acc_ref, held_ref = refs
     else:
@@ -121,9 +118,9 @@
     factor = HEAD_SIZE**-0.5 * LOG2E
     tiles = [(b, slice(r, r + TILE)) for b in range(blocks) for r in range(0, rows, TILE)]
 
-    for n, ref in enumerate(halves):
-        shard = core if n % 2 == 0 else 1 - core
-        held_ref[n // 2, pl.ds(pl.multiple_of(shard * tok, tok), tok)] = ref[...]
+    for n, ref in enumerate(pieces):
+        held_ref[n, pl.ds(pl.multiple_of(core * tok, tok), tok)] = ref[:tok]
+        held_ref[n, pl.ds(pl.multiple_of((1 - core) * tok, tok), tok)] = ref[tok:]
 
     def start_of(b):
         mine = b // half == core
@@ -219,6 +216,7 @@
             out_ref[:, pl.ds(pl.multiple_of((1 - core) * rows, rows), rows)] = swapped_ref[...]
 
     if stage == "first":
+        slice_weight(weight_ref, common_ref, single_ref)
         attend_own()
     elif stage == "next":
         attend_next()
@@ -226,9 +224,9 @@
         attend_last(core if stage == "own" else 1 - core)
 
 
-def attention_call(stage, distances, starts, recv_starts, operands, after=()):
+def attention_call(stage, distances, starts, recv_starts, operands):
     tok, half = starts.shape[0] * BLOCK, starts.shape[0]
-    rows = operands[1].shape[1]
+    rows = operands[2].shape[1] if stage == "first" else operands[1].shape[1]
     blocks, n_head, n_pieces = 2 * half, rows // BLOCK, len(distances)
     state = [
         jax.ShapeDtypeStruct((blocks, rows, HEAD_SIZE), jnp.float32),
@@ -238,6 +236,9 @@
     share = n_pieces
     if stage == "first":
         outs, share = [jax.ShapeDtypeStruct((blocks, rows, HEAD_SIZE), jnp.bfloat16)] + state, 0.6
+        weight = operands[0]
+        deep, wide = weight.shape[0] // 2, weight.shape[1] // 8
+        outs += [jax.ShapeDtypeStruct((deep, n * wide), weight.dtype) for n in (2, 1)]
     elif stage == "next":
         outs = state
     else:
@@ -246,11 +247,9 @@
         scratch = [pltpu.VMEM((half, rows, 2 * HEAD_SIZE), jnp.float32)] + scratch
     vmem, smem = pl.BlockSpec(memory_space=pltpu.VMEM), pl.BlockSpec(memory_space=pltpu.SMEM)
     return pl.pallas_call(
-        functools.partial(attention_kernel, stage, distances, n_head, len(after)),
+        functools.partial(attention_kernel, stage, distances, n_head),
         out_shape=outs,
-        in_specs=[smem, smem]
-        + [vmem] * len(operands)
-        + [pl.BlockSpec(memory_space=pl.ANY)] * len(after),
+        in_specs=[smem, smem] + [vmem] * len(operands),
         out_specs=[vmem] * len(outs),
         scratch_shapes=scratch,
         compiler_params=pltpu.CompilerParams(vmem_limit_bytes=24 * 2**20),
@@ -259,7 +258,7 @@
             bytes_accessed=8 * 2**20,
             transcendentals=int(share * blocks * rows * 2 * tok),
         ),
-    )(starts, recv_starts, *operands, *after)
+    )(starts, recv_starts, *operands)
 
 
 def per_device(queries, keys, values, block_start, out_weight):
@@ -274,27 +273,29 @@
     cols = out_weight.shape[1] // 2
     mine = jnp.concatenate([part(keys, core, HEAD_SIZE), part(values, core, HEAD_SIZE)], 1)
     theirs = jnp.concatenate([part(keys, 1 - core, HEAD_SIZE), part(values, 1 - core, HEAD_SIZE)], 1)
-    own = (mine, swap(theirs, 1))
+    recv = swap(theirs, 1)
+    one_behind = [rotate(mine, 4), rotate(recv, 4)]
     q_recv = swap(part(queries, 1 - core, group), 1)
     recv_starts = swap(block_start, 1)
-    one_behind = [shift(x, 4) for x in own]
-    two_behind = [shift(x, 4) for x in one_behind]
-    across = [swap(x, 2) for x in one_behind]
-    third = [swap(jnp.where(col == 1, x, y), 2) for x, y in zip(two_behind, own, strict=True)]
-
-    tiles = [cross(x, 0) for x in slice_weight(out_weight, one_behind[0])]
-    tiles += [swap(x, 4) for x in tiles]
-
+    own = jnp.concatenate([mine, recv])
     starts = (block_start, recv_starts)
-    q, *state = attention_call("first", ((0, 0),), *starts, (queries, q_recv, *own))
-    state = attention_call("next", ((2, 2),), *starts, (q, *state, *one_behind))
-    state = attention_call("next", ((1, 3), (4, 4)), *starts, (q, *state, *across, *two_behind))
-    (o_other,) = attention_call("other", ((3, 1),), *starts, (q, *state, *third))
-    (heads,) = attention_call("own", ((3, 1),), *starts, (q, *state, *third, swap(o_other, 1)))
-    across = cross(heads, 0)
+    q, *state, common, single = attention_call(
+        "first", ((0, 0),), *starts, (out_weight, queries, q_recv, own)
+    )
+    single, common = cross(single, 0), cross(common, 0)
+    weights = [common, single, swap(single, 4)]
+    one_behind = join(*one_behind, q)
+    two_behind = rotate(one_behind, 4)
+    across = swap(one_behind, 2)
+    third = swap(jnp.where(col == 1, two_behind, own), 2)
+    state = attention_call("next", ((2, 2),), *starts, (q, *state, one_behind))
+    state = attention_call("next", ((1, 3), (4, 4)), *starts, (q, *state, across, two_behind))
+    (o_other,) = attention_call("other", ((3, 1),), *starts, (q, *state, third))
+    (heads,) = attention_call("own", ((3, 1),), *starts, (q, *state, third, swap(o_other, 1)))
+    heads_across = cross(heads, 0)
     here = jnp.dot(heads, part(out_weight, head, cols), preferred_element_type=jnp.float32)
-    tiles += [swap(x, 1) for x in tiles]
-    return project(here.astype(jnp.bfloat16), across, tiles)
+    weights += [swap(x, 1) for x in weights]
+    return project(here.astype(jnp.bfloat16), heads_across, weights)
 
 
 def solution(mesh):

time: 90.8 us -> 84.8 us (0.934)
  starting transfers between devices: 34.2 us -> 11.7 us
  local copies, waits for them, and re-layouts: 2.1 us -> 13.3 us
  waiting for transfers between devices: 30.4 us -> 37.8 us
  Pallas kernels: 18.3 us -> 16.6 us
    ppermute x3, waiting for transfers between devices: 0.01 us -> 25 us  [cross(): return lax.ppermute(x, ('ctx', 'head'), route)]
    ppermute x14 -> x10, waiting for transfers between devices: 24.7 us -> 8.47 us  [swap(): lax.ppermute(x, 'ctx', [(i, i ^ mask) for i in range(lax.axis_size('ctx'))])]
    ppermute x14 -> x10, starting transfers between devices: 14.8 us -> 3.38 us  [swap(): lax.ppermute(x, 'ctx', [(i, i ^ mask) for i in range(lax.axis_size('ctx'))])]
    unnamed x8 -> x18, local copies, waits for them, and re-layouts: 0.02 us -> 11.2 us
    ppermute x4 -> x3, starting transfers between devices: 15.7 us -> 4.78 us  [rotate(): return lax.ppermute(x, 'ctx', [(i, (i + distance) % n) for i in range(n)])]
    pallas_call x1, Pallas kernels: 2.29 us -> 0.03 us  [join(): pl.pallas_call(join_kernel, out_shape=jax.ShapeDtypeStruct((2 * first.sha...]
    ppermute x4 -> x3, waiting for transfers between devices: 5.66 us -> 4.31 us  [rotate(): return lax.ppermute(x, 'ctx', [(i, (i + distance) % n) for i in range(n)])]
  transfers between devices with their start and end apart: 21 -> 16, of which waited for: 6 -> 4; matrix products, arithmetic and copies ran while one was open for 6% -> 7% of each run, Pallas kernels for 16% -> 15%
where the time goes in v5:
time: 84.8 us; the launch traced here: 84.2 us
  waiting for transfers between devices  37.8 us (45%)
  Pallas kernels  16.6 us (20%)
  local copies, waits for them, and re-layouts  13.3 us (16%)
  starting transfers between devices  11.7 us (14%)
  matrix products  4.22 us (5%)
    ppermute x3, waiting for transfers between devices, cross(): return lax.ppermute(x, ('ctx', 'head'), route)  25 us
    pallas_call x5, Pallas kernels, attention_call(): pl.pallas_call(functools.partial(attention_kernel, stage, distances, n_he...  12.6 us
    unnamed x18, local copies, waits for them, and re-layouts  11.2 us
    ppermute x10, waiting for transfers between devices, swap(): lax.ppermute(x, 'ctx', [(i, i ^ mask) for i in range(lax.axis_size('ctx'))])  8.47 us
    ppermute x3, starting transfers between devices, rotate(): return lax.ppermute(x, 'ctx', [(i, (i + distance) % n) for i in range(n)])  4.78 us
    ppermute x3, waiting for transfers between devices, rotate(): return lax.ppermute(x, 'ctx', [(i, (i + distance) % n) for i in range(n)])  4.31 us
    dot_general x1, matrix products, per_device(): jnp.dot(heads, part(out_weight, head, cols), preferred_element_type=jnp.f...  4.22 us
    pallas_call x1, Pallas kernels, project(): pl.pallas_call(project_kernel, out_shape=jax.ShapeDtypeStruct(given.shape...  3.96 us
  transfers between devices with their start and end apart: 16, of which 4 were waited for; matrix products, arithmetic and copies ran while one was open for 7% of the time, Pallas kernels for 15%

profile of v5, /device:TPU:2, one launch (start us, length us, event | category | flops | bytes accessed | tf_op | source)
XLA Modules:
  0.0 84.2 jit_solution(17338057081319628317)
XLA Ops:
  0.0 0.0 copy-start.1
  0.0 0.0 copy-start.2
  0.0 1.1 %constant_dynamic-slice_fusion.4 = bf16[384,512]{1,0:T(8,128)(2,1)S(1)} fusion(bf16[384,1024]{1,0:T(8,128)(2,1)} %refs_1_.1, s32[]{:T(128)S(6)} %select_n.38), kind=kLoop, calls=%fused_computation.12 | loop fusion | bytes 786436 | tf_op jit(solution)/shard_map/dynamic_slice | solution.py:271
  1.1 0.1 collective-permute-start.1
  1.2 1.1 %constant_dynamic-slice_fusion.2 = (bf16[384,128]{1,0:T(8,128)(2,1)S(1)}, bf16[384,128]{1,0:T(8,128)(2,1)S(1)}, bf16[384,128]{1,0:T(8,128)(2,1)S(1)}, bf16[384,128]{1,0:T(8,128)(2,1)S(1)}) fusion(bf16[384,256]{1,0:T(8,128)(2,1)} %param.7, s32[]{:T(128)S(6)} %select_n.39, s32[]{:T(128)S(6)} %select_n.40, bf16[384,256]{1,0:T(8,128)(2,1)} %param.6), kind=kLoop, calls=%fused_computation.10 | loop fusion | bytes 786440 | tf_op jit(solution)/shard_map/dynamic_slice | solution.py:271
  2.3 0.5 collective-permute-start.2
  2.8 0.1 collective-permute-start
  2.9 1.6 %collective-permute-start.3 = (bf16[384,256]{1,0:T(8,128)(2,1)S(1)}, bf16[384,256]{1,0:T(8,128)(2,1)S(1)}, u32[]{:S(2)}, u32[]{:S(2)}) collective-permute-start(bf16[384,256]{1,0:T(8,128)(2,1)S(1)} %pad_maximum_fusion.1), channel_id=1, source_target_pairs={{0,8},{2,10},{4,12},{6,14},{8,16},{10,18},{12,20},{14,22},{16,24},... | collective-permute-start | bytes 589832 | tf_op jit(solution)/shard_map/ppermute | solution.py:19
  4.6 0.0 collective-permute-done.2
  4.6 1.6 %collective-permute-start.4 = (bf16[384,256]{1,0:T(8,128)(2,1)S(1)}, bf16[384,256]{1,0:T(8,128)(2,1)S(1)}, u32[]{:S(2)}, u32[]{:S(2)}) collective-permute-start(bf16[384,256]{1,0:T(8,128)(2,1)S(1)} %collective-permute-done.2), channel_id=1, source_target_pairs={{0,8},{2,10},{4,12},{6,14},{8,16},{10,18},{12,20},{14,22},{16,24},... | collective-permute-start | bytes 589832 | tf_op jit(solution)/shard_map/ppermute | solution.py:19
  6.2 0.0 collective-permute-done.recv_starts_ref
  6.2 0.0 collective-permute-done.1.refs_2_
  6.2 0.0 copy-done.1
  6.2 0.0 copy-done.2
  6.2 0.0 copy-start
  6.2 3.4 %copy-done = bf16[1024,4096]{1,0:T(8,128)(2,1)S(1)} copy-done((bf16[1024,4096]{1,0:T(8,128)(2,1)S(1)}, bf16[1024,4096]{1,0:T(8,128)(2,1)}, u32[]{:S(2)}) %copy-start) | copy-done | bytes 8388632
  9.6 3.8 %shard_map.55 = (bf16[6,512,128]{2,1,0:T(8,128)(2,1)S(1)}, f32[6,512,128]{2,1,0:T(8,128)S(1)}, f32[6,512,256]{2,1,0:T(8,128)S(1)}, bf16[512,1024]{1,0:T(8,128)(2,1)S(1)}, bf16[512,512]{1,0:T(8,128)(2,1)S(1)}) custom-call(s32[3]{0:T(128)S(1)} %copy-done.2, s32[3]{0:T(128)S(1)} %collective-permute-done.recv_starts_ref, bf16[1024,4096]{1,0:T(8,128)(2,1)S(1)} %copy-done, ...), custom_call_target="tpu_custom_call" | custom-call | flops 1449551488 | bytes 8388608 | tf_op jit(solution)/shard_map/pallas_call | solution.py:249
  13.4 0.0 copy-start.3
  13.4 1.6 %copy-done.3 = f32[6,512,256]{2,1,0:T(8,128)} copy-done((f32[6,512,256]{2,1,0:T(8,128)}, f32[6,512,256]{2,1,0:T(8,128)S(1)}, u32[]{:S(2)}) %copy-start.3) | copy-done | bytes 3145752
  15.0 0.0 copy-start.7
  15.0 1.0 %copy-done.7 = bf16[512,1024]{1,0:T(8,128)(2,1)} copy-done((bf16[512,1024]{1,0:T(8,128)(2,1)}, bf16[512,1024]{1,0:T(8,128)(2,1)S(1)}, u32[]{:S(2)}) %copy-start.7) | copy-done | bytes 1048600
  16.0 0.0 copy-start.8
  16.0 0.8 copy-done.8
  16.8 0.0 copy-start.5
  16.8 0.0 collective-permute-done.3.first_ref
  16.8 0.0 collective-permute-done.4.second_ref
  16.8 1.1 %copy-done.5 = f32[6,512,128]{2,1,0:T(8,128)} copy-done((f32[6,512,128]{2,1,0:T(8,128)}, f32[6,512,128]{2,1,0:T(8,128)S(1)}, u32[]{:S(2)}) %copy-start.5) | copy-done | bytes 1572888
  17.9 1.6 %collective-permute-start.6 = (bf16[768,256]{1,0:T(8,128)(2,1)S(1)}, bf16[768,256]{1,0:T(8,128)(2,1)S(1)}, u32[]{:S(2)}, u32[]{:S(2)}) collective-permute-start(bf16[768,256]{1,0:T(8,128)(2,1)S(1)} %shard_map.56.refs_3_), channel_id=1, source_target_pairs={{0,8},{2,10},{4,12},{6,14},{8,16},{10,18},{12,20},{14,22},{16,24},... | collective-permute-start | bytes 1179656 | tf_op jit(solution)/shard_map/ppermute | solution.py:19
  19.5 0.5 collective-permute-start.5
  20.1 1.5 %collective-permute-start.11 = (bf16[512,512]{1,0:T(8,128)(2,1)}, bf16[512,512]{1,0:T(8,128)(2,1)S(1)}, u32[]{:S(2)}, u32[]{:S(2)}) collective-permute-start(bf16[512,512]{1,0:T(8,128)(2,1)} %copy-done.8), channel_id=1, source_target_pairs={{0,1},{1,0},{2,3},{3,2},{4,5},{5,4},{6,7},{7,6},{8,9},{9,8},{10,11... | collective-permute-start | bytes 1572872 | tf_op jit(solution)/shard_map/ppermute | solution.py:29
  21.6 0.5 collective-permute-start.10
  22.1 0.0 copy-start.4
  22.1 1.9 %copy-done.4 = f32[6,512,256]{2,1,0:T(8,128)S(1)} copy-done((f32[6,512,256]{2,1,0:T(8,128)S(1)}, f32[6,512,256]{2,1,0:T(8,128)}, u32[]{:S(2)}) %copy-start.4) | copy-done | bytes 3145752
  24.0 0.0 copy-start.6
  24.0 1.4 %copy-done.6 = f32[6,512,128]{2,1,0:T(8,128)S(1)} copy-done((f32[6,512,128]{2,1,0:T(8,128)S(1)}, f32[6,512,128]{2,1,0:T(8,128)}, u32[]{:S(2)}) %copy-start.6) | copy-done | bytes 1572888
  25.4 1.0 %shard_map.57 = (f32[6,512,128]{2,1,0:T(8,128)S(1)}, f32[6,512,256]{2,1,0:T(8,128)S(1)}) custom-call(s32[3]{0:T(128)S(1)} %copy-done.2, s32[3]{0:T(128)S(1)} %collective-permute-done.recv_starts_ref, bf16[6,512,128]{2,1,0:T(8,128)(2,1)S(1)} %get-tuple-element.14._.refs_0_, f32[6,512,128]{2,1,0:T(8,128)S(1)} %copy-done.6, f32[6,512,256]{2,1,0:T(8,128)S(1)} %copy-done.4, ...), custom_call_target="tpu_custom_call" | custom-call | flops 2415919104 | bytes 8388608 | tf_op jit(solution)/shard_map/pallas_call | solution.py:249
  26.3 4.3 %collective-permute-done.6.refs_4_ = bf16[768,256]{1,0:T(8,128)(2,1)S(1)} collective-permute-done((bf16[768,256]{1,0:T(8,128)(2,1)S(1)}, bf16[768,256]{1,0:T(8,128)(2,1)S(1)}, u32[]{:S(2)}, u32[]{:S(2)}) %collective-permute-start.6) | collective-permute-done | bytes 393248 | tf_op jit(solution)/shard_map/ppermute | solution.py:19
  30.6 0.1 broadcast_select_fusion
  30.8 0.6 collective-permute-start.7
  31.3 0.0 collective-permute-done.5.refs_3_
  31.4 1.0 %shard_map.58 = (f32[6,512,128]{2,1,0:T(8,128)S(1)}, f32[6,512,256]{2,1,0:T(8,128)S(1)}) custom-call(s32[3]{0:T(128)S(1)} %copy-done.2, s32[3]{0:T(128)S(1)} %collective-permute-done.recv_starts_ref, bf16[6,512,128]{2,1,0:T(8,128)(2,1)S(1)} %get-tuple-element.14._.refs_0_, f32[6,512,128]{2,1,0:T(8,128)S(1)} %get-tuple-element.17.refs_1_, ...), custom_call_target="tpu_custom_call" | custom-call | flops 4831838208 | bytes 8388608 | tf_op jit(solution)/shard_map/pallas_call | solution.py:249
  32.4 8.4 %collective-permute-done.7.refs_3_ = bf16[768,256]{1,0:T(8,128)(2,1)S(1)} collective-permute-done((bf16[768,256]{1,0:T(8,128)(2,1)S(1)}, bf16[768,256]{1,0:T(8,128)(2,1)S(1)}, u32[]{:S(2)}, u32[]{:S(2)}) %collective-permute-start.7) | collective-permute-done | bytes 393248 | tf_op jit(solution)/shard_map/ppermute | solution.py:23
  40.8 2.9 %shard_map.59 = bf16[384,512]{1,0:T(8,128)(2,1)S(1)} custom-call(s32[3]{0:T(128)S(1)} %copy-done.2, s32[3]{0:T(128)S(1)} %collective-permute-done.recv_starts_ref, bf16[6,512,128]{2,1,0:T(8,128)(2,1)S(1)} %get-tuple-element.14._.refs_0_, f32[6,512,128]{2,1,0:T(8,128)S(1)} %get-tuple-element.19.refs_1_, f32[6,512,256]{2,1,0:T(8,128)S(1)} %get-tuple-element.20.refs_2_, ...), custom_call_target="tpu_custom_call" | custom-call | flops 1207959552 | bytes 8388608 | tf_op jit(solution)/shard_map/pallas_call | solution.py:249
  43.7 0.1 collective-permute-start.8
  43.8 0.0 collective-permute-done.11.refs_1_
  43.8 1.0 %collective-permute-start.12 = (bf16[512,512]{1,0:T(8,128)(2,1)S(1)}, bf16[512,512]{1,0:T(8,128)(2,1)}, u32[]{:S(2)}, u32[]{:S(2)}) collective-permute-start(bf16[512,512]{1,0:T(8,128)(2,1)S(1)} %collective-permute-done.11.refs_1_), channel_id=1, source_target_pairs={{0,8},{2,10},{4,12},{6,14},{8,0},{10,2},{12,4},{14,6},{16,24},{18,... | collective-permute-start | bytes 1572872 | tf_op jit(solution)/shard_map/ppermute | solution.py:23
  44.8 11.1 %collective-permute-done.10.refs_0_ = bf16[512,1024]{1,0:T(8,128)(2,1)S(1)} collective-permute-done((bf16[512,1024]{1,0:T(8,128)(2,1)}, bf16[512,1024]{1,0:T(8,128)(2,1)S(1)}, u32[]{:S(2)}, u32[]{:S(2)}) %collective-permute-start.10) | collective-permute-done | bytes 1048608 | tf_op jit(solution)/shard_map/ppermute | solution.py:29
  55.9 0.0 collective-permute-start.13
  55.9 0.0 collective-permute-done.8.refs_4_
  55.9 4.0 %shard_map.60 = bf16[384,1024]{1,0:T(8,128)(2,1)} custom-call(s32[3]{0:T(128)S(1)} %copy-done.2, s32[3]{0:T(128)S(1)} %collective-permute-done.recv_starts_ref, bf16[6,512,128]{2,1,0:T(8,128)(2,1)S(1)} %get-tuple-element.14._.refs_0_, f32[6,512,128]{2,1,0:T(8,128)S(1)} %get-tuple-element.19.refs_1_, f32[6,512,256]{2,1,0:T(8,128)S(1)} %get-tuple-element.20.refs_2_, ...), custom_call_target="tpu_custom_call" | custom-call | flops 1207959552 | bytes 8388608 | tf_op jit(solution)/shard_map/pallas_call | solution.py:249
  59.9 1.5 %collective-permute-start.9 = (bf16[384,1024]{1,0:T(8,128)(2,1)}, bf16[384,1024]{1,0:T(8,128)(2,1)S(1)}, u32[]{:S(2)}, u32[]{:S(2)}) collective-permute-start(bf16[384,1024]{1,0:T(8,128)(2,1)} %shard_map.60), channel_id=1, source_target_pairs={{0,1},{1,0},{2,3},{3,2},{4,5},{5,4},{6,7},{7,6},{8,9},{9,8},{10,11... | collective-permute-start | bytes 2359304 | tf_op jit(solution)/shard_map/ppermute | solution.py:29
  61.4 0.2 collective-permute-start.14
  61.6 0.0 collective-permute-done.12.refs_2_
  61.6 0.3 collective-permute-start.15
  61.9 4.2 %fusion.2.given_ref = bf16[384,2048]{1,0:T(8,128)(2,1)S(1)} fusion(bf16[384,1024]{1,0:T(8,128)(2,1)} %shard_map.60, bf16[1024,4096]{1,0:T(8,128)(2,1)} %refs_0_.1, s32[]{:T(128)S(6)} %select_n.45), kind=kOutput, calls=%fused_computation.2 | convolution fusion | flops 1611399168 | bytes 6553604 | tf_op jit(solution)/shard_map/dot_general | solution.py:296
  66.1 0.0 collective-permute-done.14.refs_4_
  66.1 0.0 collective-permute-done.15.refs_5_
  66.2 13.9 %collective-permute-done.9.heads_ref = bf16[384,1024]{1,0:T(8,128)(2,1)S(1)} collective-permute-done((bf16[384,1024]{1,0:T(8,128)(2,1)}, bf16[384,1024]{1,0:T(8,128)(2,1)S(1)}, u32[]{:S(2)}, u32[]{:S(2)}) %collective-permute-start.9) | collective-permute-done | bytes 786464 | tf_op jit(solution)/shard_map/ppermute | solution.py:29
  80.0 0.0 collective-permute-done.13.refs_3_
  80.0 4.0 %shard_map.61 = bf16[384,2048]{1,0:T(8,128)(2,1)} custom-call(bf16[384,2048]{1,0:T(8,128)(2,1)S(1)} %fusion.2.given_ref, bf16[384,1024]{1,0:T(8,128)(2,1)S(1)} %collective-permute-done.9.heads_ref, bf16[512,1024]{1,0:T(8,128)(2,1)S(1)} %collective-permute-done.10.refs_0_, bf16[512,512]{1,0:T(8,128)(2,1)S(1)} %collective-permute-done.11.refs_1_, ...), custom_call_target="tpu_custom_call" | custom-call | flops 1610612736 | bytes 4194304 | tf_op jit(solution)/shard_map/pallas_call | solution.py:80
  (4 shorter events, 0.1 us)
Async XLA Ops:
  0.0 6.2 %copy-start.1 = (bf16[384,1024]{1,0:T(8,128)(2,1)S(1)}, bf16[384,1024]{1,0:T(8,128)(2,1)}, u32[]{:S(2)}) copy-start(bf16[384,1024]{1,0:T(8,128)(2,1)} %refs_1_.1) | copy-start | bytes 2359300
  0.0 6.2 %copy-start.2 = (s32[3]{0:T(128)S(1)}, s32[3]{0:T(128)}, u32[]{:S(2)}) copy-start(s32[3]{0:T(128)} %starts_ref.9) | copy-start | bytes 40
  1.1 5.1 %collective-permute-start.1 = (bf16[384,512]{1,0:T(8,128)(2,1)S(1)}, bf16[384,512]{1,0:T(8,128)(2,1)S(1)}, u32[]{:S(2)}, u32[]{:S(2)}) collective-permute-start(bf16[384,512]{1,0:T(8,128)(2,1)S(1)} %constant_dynamic-slice_fusion.4), channel_id=1, source_target_pairs={{0,2},{2,0},{4,6},{6,4},{8,10},{10,8},{12,14},{14,12},{16,18},{18,... | collective-permute-start | bytes 1179656 | tf_op jit(solution)/shard_map/ppermute | solution.py:23
  2.3 2.3 %collective-permute-start.2 = (bf16[384,256]{1,0:T(8,128)(2,1)S(1)}, bf16[384,256]{1,0:T(8,128)(2,1)S(1)}, u32[]{:S(2)}, u32[]{:S(2)}) collective-permute-start(bf16[384,256]{1,0:T(8,128)(2,1)S(1)} %pad_maximum_fusion.2), channel_id=1, source_target_pairs={{0,2},{2,0},{4,6},{6,4},{8,10},{10,8},{12,14},{14,12},{16,18},{18,... | collective-permute-start | bytes 589832 | tf_op jit(solution)/shard_map/ppermute | solution.py:23
  2.8 3.4 %collective-permute-start = (s32[3]{0:T(128)}, s32[3]{0:T(128)S(1)}, u32[]{:S(2)}, u32[]{:S(2)}) collective-permute-start(s32[3]{0:T(128)} %starts_ref.9), channel_id=1, source_target_pairs={{0,2},{2,0},{4,6},{6,4},{8,10},{10,8},{12,14},{14,12},{16,18},{18,... | collective-permute-start | bytes 44 | tf_op jit(solution)/shard_map/ppermute | solution.py:23
  2.9 13.9 %collective-permute-start.3 = (bf16[384,256]{1,0:T(8,128)(2,1)S(1)}, bf16[384,256]{1,0:T(8,128)(2,1)S(1)}, u32[]{:S(2)}, u32[]{:S(2)}) collective-permute-start(bf16[384,256]{1,0:T(8,128)(2,1)S(1)} %pad_maximum_fusion.1), channel_id=1, source_target_pairs={{0,8},{2,10},{4,12},{6,14},{8,16},{10,18},{12,20},{14,22},{16,24},... | collective-permute-start | bytes 589832 | tf_op jit(solution)/shard_map/ppermute | solution.py:19
  4.6 12.2 %collective-permute-start.4 = (bf16[384,256]{1,0:T(8,128)(2,1)S(1)}, bf16[384,256]{1,0:T(8,128)(2,1)S(1)}, u32[]{:S(2)}, u32[]{:S(2)}) collective-permute-start(bf16[384,256]{1,0:T(8,128)(2,1)S(1)} %collective-permute-done.2), channel_id=1, source_target_pairs={{0,8},{2,10},{4,12},{6,14},{8,16},{10,18},{12,20},{14,22},{16,24},... | collective-permute-start | bytes 589832 | tf_op jit(solution)/shard_map/ppermute | solution.py:19
  6.2 3.4 %copy-start = (bf16[1024,4096]{1,0:T(8,128)(2,1)S(1)}, bf16[1024,4096]{1,0:T(8,128)(2,1)}, u32[]{:S(2)}) copy-start(bf16[1024,4096]{1,0:T(8,128)(2,1)} %refs_0_.1) | copy-start | bytes 25165828
  13.4 1.6 %copy-start.3 = (f32[6,512,256]{2,1,0:T(8,128)}, f32[6,512,256]{2,1,0:T(8,128)S(1)}, u32[]{:S(2)}) copy-start(f32[6,512,256]{2,1,0:T(8,128)S(1)} %get-tuple-element.16.refs_2_) | copy-start | bytes 9437188
  15.0 1.0 %copy-start.7 = (bf16[512,1024]{1,0:T(8,128)(2,1)}, bf16[512,1024]{1,0:T(8,128)(2,1)S(1)}, u32[]{:S(2)}) copy-start(bf16[512,1024]{1,0:T(8,128)(2,1)S(1)} %get-tuple-element.21) | copy-start | bytes 3145732
  16.0 0.8 copy-start.8
  16.8 1.1 %copy-start.5 = (f32[6,512,128]{2,1,0:T(8,128)}, f32[6,512,128]{2,1,0:T(8,128)S(1)}, u32[]{:S(2)}) copy-start(f32[6,512,128]{2,1,0:T(8,128)S(1)} %get-tuple-element.15.refs_1_) | copy-start | bytes 4718596
  17.9 12.7 %collective-permute-start.6 = (bf16[768,256]{1,0:T(8,128)(2,1)S(1)}, bf16[768,256]{1,0:T(8,128)(2,1)S(1)}, u32[]{:S(2)}, u32[]{:S(2)}) collective-permute-start(bf16[768,256]{1,0:T(8,128)(2,1)S(1)} %shard_map.56.refs_3_), channel_id=1, source_target_pairs={{0,8},{2,10},{4,12},{6,14},{8,16},{10,18},{12,20},{14,22},{16,24},... | collective-permute-start | bytes 1179656 | tf_op jit(solution)/shard_map/ppermute | solution.py:19
  19.5 11.8 %collective-permute-start.5 = (bf16[768,256]{1,0:T(8,128)(2,1)S(1)}, bf16[768,256]{1,0:T(8,128)(2,1)S(1)}, u32[]{:S(2)}, u32[]{:S(2)}) collective-permute-start(bf16[768,256]{1,0:T(8,128)(2,1)S(1)} %shard_map.56.refs_3_), channel_id=1, source_target_pairs={{0,4},{2,6},{4,0},{6,2},{8,12},{10,14},{12,8},{14,10},{16,20},{18,... | collective-permute-start | bytes 1179656 | tf_op jit(solution)/shard_map/ppermute | solution.py:23
  20.1 23.8 %collective-permute-start.11 = (bf16[512,512]{1,0:T(8,128)(2,1)}, bf16[512,512]{1,0:T(8,128)(2,1)S(1)}, u32[]{:S(2)}, u32[]{:S(2)}) collective-permute-start(bf16[512,512]{1,0:T(8,128)(2,1)} %copy-done.8), channel_id=1, source_target_pairs={{0,1},{1,0},{2,3},{3,2},{4,5},{5,4},{6,7},{7,6},{8,9},{9,8},{10,11... | collective-permute-start | bytes 1572872 | tf_op jit(solution)/shard_map/ppermute | solution.py:29
  21.6 34.3 %collective-permute-start.10 = (bf16[512,1024]{1,0:T(8,128)(2,1)}, bf16[512,1024]{1,0:T(8,128)(2,1)S(1)}, u32[]{:S(2)}, u32[]{:S(2)}) collective-permute-start(bf16[512,1024]{1,0:T(8,128)(2,1)} %copy-done.7), channel_id=1, source_target_pairs={{0,1},{1,0},{2,3},{3,2},{4,5},{5,4},{6,7},{7,6},{8,9},{9,8},{10,11... | collective-permute-start | bytes 3145736 | tf_op jit(solution)/shard_map/ppermute | solution.py:29
  22.1 1.9 %copy-start.4 = (f32[6,512,256]{2,1,0:T(8,128)S(1)}, f32[6,512,256]{2,1,0:T(8,128)}, u32[]{:S(2)}) copy-start(f32[6,512,256]{2,1,0:T(8,128)} %copy-done.3) | copy-start | bytes 9437188
  24.0 1.4 %copy-start.6 = (f32[6,512,128]{2,1,0:T(8,128)S(1)}, f32[6,512,128]{2,1,0:T(8,128)}, u32[]{:S(2)}) copy-start(f32[6,512,128]{2,1,0:T(8,128)} %copy-done.5) | copy-start | bytes 4718596
  30.8 10.1 %collective-permute-start.7 = (bf16[768,256]{1,0:T(8,128)(2,1)S(1)}, bf16[768,256]{1,0:T(8,128)(2,1)S(1)}, u32[]{:S(2)}, u32[]{:S(2)}) collective-permute-start(bf16[768,256]{1,0:T(8,128)(2,1)S(1)} %broadcast_select_fusion), channel_id=1, source_target_pairs={{0,4},{2,6},{4,0},{6,2},{8,12},{10,14},{12,8},{14,10},{16,20},{18,... | collective-permute-start | bytes 1179656 | tf_op jit(solution)/shard_map/ppermute | solution.py:23
  43.7 12.2 %collective-permute-start.8 = (bf16[384,512]{1,0:T(8,128)(2,1)S(1)}, bf16[384,512]{1,0:T(8,128)(2,1)S(1)}, u32[]{:S(2)}, u32[]{:S(2)}) collective-permute-start(bf16[384,512]{1,0:T(8,128)(2,1)S(1)} %shard_map.59), channel_id=1, source_target_pairs={{0,2},{2,0},{4,6},{6,4},{8,10},{10,8},{12,14},{14,12},{16,18},{18,... | collective-permute-start | bytes 1179656 | tf_op jit(solution)/shard_map/ppermute | solution.py:23
  43.8 17.8 %collective-permute-start.12 = (bf16[512,512]{1,0:T(8,128)(2,1)S(1)}, bf16[512,512]{1,0:T(8,128)(2,1)}, u32[]{:S(2)}, u32[]{:S(2)}) collective-permute-start(bf16[512,512]{1,0:T(8,128)(2,1)S(1)} %collective-permute-done.11.refs_1_), channel_id=1, source_target_pairs={{0,8},{2,10},{4,12},{6,14},{8,0},{10,2},{12,4},{14,6},{16,24},{18,... | collective-permute-start | bytes 1572872 | tf_op jit(solution)/shard_map/ppermute | solution.py:23
  55.9 24.1 %collective-permute-start.13 = (bf16[512,1024]{1,0:T(8,128)(2,1)S(1)}, bf16[512,1024]{1,0:T(8,128)(2,1)S(1)}, u32[]{:S(2)}, u32[]{:S(2)}) collective-permute-start(bf16[512,1024]{1,0:T(8,128)(2,1)S(1)} %collective-permute-done.10.refs_0_), channel_id=1, source_target_pairs={{0,2},{2,0},{4,6},{6,4},{8,10},{10,8},{12,14},{14,12},{16,18},{18,... | collective-permute-start | bytes 3145736 | tf_op jit(solution)/shard_map/ppermute | solution.py:23
  59.9 20.2 %collective-permute-start.9 = (bf16[384,1024]{1,0:T(8,128)(2,1)}, bf16[384,1024]{1,0:T(8,128)(2,1)S(1)}, u32[]{:S(2)}, u32[]{:S(2)}) collective-permute-start(bf16[384,1024]{1,0:T(8,128)(2,1)} %shard_map.60), channel_id=1, source_target_pairs={{0,1},{1,0},{2,3},{3,2},{4,5},{5,4},{6,7},{7,6},{8,9},{9,8},{10,11... | collective-permute-start | bytes 2359304 | tf_op jit(solution)/shard_map/ppermute | solution.py:29
  61.4 4.7 %collective-permute-start.14 = (bf16[512,512]{1,0:T(8,128)(2,1)S(1)}, bf16[512,512]{1,0:T(8,128)(2,1)}, u32[]{:S(2)}, u32[]{:S(2)}) collective-permute-start(bf16[512,512]{1,0:T(8,128)(2,1)S(1)} %collective-permute-done.11.refs_1_), channel_id=1, source_target_pairs={{0,2},{2,0},{4,6},{6,4},{8,10},{10,8},{12,14},{14,12},{16,18},{18,... | collective-permute-start | bytes 1572872 | tf_op jit(solution)/shard_map/ppermute | solution.py:23
  61.6 4.5 %collective-permute-start.15 = (bf16[512,512]{1,0:T(8,128)(2,1)}, bf16[512,512]{1,0:T(8,128)(2,1)}, u32[]{:S(2)}, u32[]{:S(2)}) collective-permute-start(bf16[512,512]{1,0:T(8,128)(2,1)} %collective-permute-done.12.refs_2_), channel_id=1, source_target_pairs={{0,2},{2,0},{4,6},{6,4},{8,10},{10,8},{12,14},{14,12},{16,18},{18,... | collective-permute-start | bytes 1572872 | tf_op jit(solution)/shard_map/ppermute | solution.py:23

commit v6 on v5

--- a/solution.py
+++ b/solution.py
@@ -29,43 +29,18 @@
     return lax.ppermute(x, ("ctx", "head"), route)
 
 
-def slice_weight(weight_ref, common_ref, single_ref):
-    core, part = lax.axis_index("ctx") % 2, lax.axis_index("ctx") // 4 % 2
-    rows, width = single_ref.shape
-    for out, tile in ((single_ref, 2 + part), (common_ref, 0)):
-        col = pl.multiple_of(((1 - lax.axis_index("head")) * 4 + tile) * width, width)
-        out[...] = weight_ref[pl.ds(pl.multiple_of(core * rows, rows), rows), pl.ds(col, out.shape[1])]
-
-
-def join_kernel(first_ref, second_ref, _, out_ref):
-    tok = first_ref.shape[0]
-    out_ref[:tok] = first_ref[...]
-    out_ref[tok:] = second_ref[...]
-
-
-def join(first, second, after):
-    vmem = pl.BlockSpec(memory_space=pltpu.VMEM)
-    return pl.pallas_call(
-        join_kernel,
-        out_shape=jax.ShapeDtypeStruct((2 * first.shape[0], first.shape[1]), first.dtype),
-        in_specs=[vmem, vmem, pl.BlockSpec(memory_space=pl.ANY)],
-        out_specs=vmem,
-        compiler_params=pltpu.CompilerParams(vmem_limit_bytes=4 * 2**20),
-    )(first, second, after)
-
-
 def project_kernel(given_ref, heads_ref, *refs):
-    parts, out_ref, built, sems = refs[:6], refs[6], refs[7], refs[8]
+    parts, out_ref, built, sems = refs[:4], refs[4], refs[5], refs[6]
     me = lax.axis_index("ctx")
     core, part = me % 2, me // 4 % 2
     group, width = parts[1].shape
     copies = []
-    for n, first in enumerate((0, 1, 2 + part, 3 - part)):
+    for n, first in enumerate((part, part + 1, part + 2, 3 - 3 * part)):
         cols = pl.ds(pl.multiple_of(first * width, width), width)
         total = given_ref[:, cols].astype(jnp.float32)
-        for index, (common, *single) in ((core, parts[:3]), (1 - core, parts[3:])):
+        for index, (fetched, single) in ((core, parts[:2]), (1 - core, parts[2:])):
             heads = heads_ref[:, pl.ds(pl.multiple_of(index * group, group), group)]
-            tile = common[:, n * width : (n + 1) * width] if n < 2 else single[n - 2][...]
+            tile = fetched[:, n * width : (n + 1) * width] if n < 3 else single[...]
             total += jnp.dot(heads, tile, preferred_element_type=jnp.float32)
         built[n] = total.astype(out_ref.dtype)
         copies.append(pltpu.make_async_copy(built.at[n], out_ref.at[:, cols], sems.at[n]))
@@ -80,7 +55,7 @@
     return pl.pallas_call(
         project_kernel,
         out_shape=jax.ShapeDtypeStruct(given.shape, jnp.bfloat16),
-        in_specs=[vmem] * 8,
+        in_specs=[vmem] * 6,
         out_specs=pl.BlockSpec(memory_space=pltpu.HBM),
         scratch_shapes=[pltpu.VMEM((4, tok, cols // 4), jnp.bfloat16), pltpu.SemaphoreType.DMA((4,))],
         compiler_params=pltpu.CompilerParams(vmem_limit_bytes=16 * 2**20),
@@ -95,8 +70,8 @@
     me = lax.axis_index("ctx")
     pair, core, col = me // 2, me % 2, (me // 2) % 2
     if stage == "first":
-        weight_ref, queries_ref, q_recv_ref = refs[:3]
-        refs = refs[3:]
+        queries_ref, q_recv_ref = refs[:2]
+        refs = refs[2:]
     else:
         q_ref, top_in, acc_in = refs[:3]
         refs = refs[3:]
@@ -104,7 +79,7 @@
     pieces = refs[:n_pieces]
     refs = refs[n_pieces:]
     if stage == "first":
-        q_ref, top_ref, acc_ref, common_ref, single_ref, held_ref = refs
+        q_ref, top_ref, acc_ref, held_ref = refs
     elif stage == "next":
         top_ref, acc_ref, held_ref = refs
     else:
@@ -216,7 +191,6 @@
             out_ref[:, pl.ds(pl.multiple_of((1 - core) * rows, rows), rows)] = swapped_ref[...]
 
     if stage == "first":
-        slice_weight(weight_ref, common_ref, single_ref)
         attend_own()
     elif stage == "next":
         attend_next()
@@ -226,7 +200,7 @@
 
 def attention_call(stage, distances, starts, recv_starts, operands):
     tok, half = starts.shape[0] * BLOCK, starts.shape[0]
-    rows = operands[2].shape[1] if stage == "first" else operands[1].shape[1]
+    rows = operands[1].shape[1]
     blocks, n_head, n_pieces = 2 * half, rows // BLOCK, len(distances)
     state = [
         jax.ShapeDtypeStruct((blocks, rows, HEAD_SIZE), jnp.float32),
@@ -236,9 +210,6 @@
     share = n_pieces
     if stage == "first":
         outs, share = [jax.ShapeDtypeStruct((blocks, rows, HEAD_SIZE), jnp.bfloat16)] + state, 0.6
-        weight = operands[0]
-        deep, wide = weight.shape[0] // 2, weight.shape[1] // 8
-        outs += [jax.ShapeDtypeStruct((deep, n * wide), weight.dtype) for n in (2, 1)]
     elif stage == "next":
         outs = state
     else:
@@ -279,23 +250,29 @@
     recv_starts = swap(block_start, 1)
     own = jnp.concatenate([mine, recv])
     starts = (block_start, recv_starts)
-    q, *state, common, single = attention_call(
-        "first", ((0, 0),), *starts, (out_weight, queries, q_recv, own)
-    )
-    single, common = cross(single, 0), cross(common, 0)
-    weights = [common, single, swap(single, 4)]
-    one_behind = join(*one_behind, q)
+    tile = cols // 4
+    part_id = me // 4 % 2
+    q_recv, weight = lax.optimization_barrier((q_recv, out_weight))
+    first_col = ((1 - head) * 4 + part_id) * tile
+    sent = lax.dynamic_slice(weight, (core * group, first_col), (group, 3 * tile))
+    q_recv, sent = lax.optimization_barrier((q_recv, sent))
+    fetched = cross(sent, 0)
+    q, *state = attention_call("first", ((0, 0),), *starts, (queries, q_recv, own))
+    q, one_behind = lax.optimization_barrier((q, one_behind))
+    one_behind = jnp.concatenate(one_behind)
     two_behind = rotate(one_behind, 4)
     across = swap(one_behind, 2)
     third = swap(jnp.where(col == 1, two_behind, own), 2)
     state = attention_call("next", ((2, 2),), *starts, (q, *state, one_behind))
     state = attention_call("next", ((1, 3), (4, 4)), *starts, (q, *state, across, two_behind))
+    state, fetched = lax.optimization_barrier((state, fetched))
+    weights = [fetched, swap(lax.dynamic_slice_in_dim(fetched, 2 * tile * part_id, tile, 1), 4)]
     (o_other,) = attention_call("other", ((3, 1),), *starts, (q, *state, third))
     (heads,) = attention_call("own", ((3, 1),), *starts, (q, *state, third, swap(o_other, 1)))
     heads_across = cross(heads, 0)
+    other_weights = [swap(x, 1) for x in weights]
     here = jnp.dot(heads, part(out_weight, head, cols), preferred_element_type=jnp.float32)
-    weights += [swap(x, 1) for x in weights]
-    return project(here.astype(jnp.bfloat16), heads_across, weights)
+    return project(here.astype(jnp.bfloat16), heads_across, (*weights, *other_weights))
 
 
 def solution(mesh):

time: 84.8 us -> 82.8 us (0.976)
  waiting for transfers between devices: 37.8 us -> 33.4 us
  Pallas kernels: 16.6 us -> 18.5 us
    ppermute x3 -> x2, waiting for transfers between devices: 25 us -> 20.1 us  [cross(): return lax.ppermute(x, ('ctx', 'head'), route)]
    ppermute x3, waiting for transfers between devices: 4.31 us -> 8.31 us  [rotate(): return lax.ppermute(x, 'ctx', [(i, (i + distance) % n) for i in range(n)])]
    dynamic_slice x0 -> x2, local copies, waits for them, and re-layouts: none -> 3.86 us  [the longest x1 2.71 us: per_device(): lax.dynamic_slice(weight, (core * group, first_col), (group, 3 * tile))]
    ppermute x10 -> x9, waiting for transfers between devices: 8.47 us -> 5 us  [swap(): lax.ppermute(x, 'ctx', [(i, i ^ mask) for i in range(lax.axis_size('ctx'))])]
    unnamed x18 -> x23, local copies, waits for them, and re-layouts: 11.2 us -> 8.02 us
    pallas_call x5, Pallas kernels: 12.6 us -> 13.8 us  [attention_call(): pl.pallas_call(functools.partial(attention_kernel, stage, distances, n_he...]
    ppermute x10 -> x9, starting transfers between devices: 3.38 us -> 4.12 us  [swap(): lax.ppermute(x, 'ctx', [(i, i ^ mask) for i in range(lax.axis_size('ctx'))])]
    ppermute x3 -> x2, starting transfers between devices: 3.55 us -> 3.04 us  [cross(): return lax.ppermute(x, ('ctx', 'head'), route)]
  transfers between devices with their start and end apart: 16 -> 14, of which waited for: 4 -> 5; matrix products, arithmetic and copies ran while one was open for 7% -> 13% of each run, Pallas kernels for 15% -> 17%
where the time goes in v6:
time: 82.8 us; the launch traced here: 82.3 us
  waiting for transfers between devices  33.4 us (40%)
  Pallas kernels  18.5 us (22%)
  local copies, waits for them, and re-layouts  14 us (17%)
  starting transfers between devices  11.7 us (14%)
  matrix products  4.22 us (5%)
    ppermute x2, waiting for transfers between devices, cross(): return lax.ppermute(x, ('ctx', 'head'), route)  20.1 us
    pallas_call x5, Pallas kernels, attention_call(): pl.pallas_call(functools.partial(attention_kernel, stage, distances, n_he...  13.8 us
    ppermute x3, waiting for transfers between devices, rotate(): return lax.ppermute(x, 'ctx', [(i, (i + distance) % n) for i in range(n)])  8.31 us
    unnamed x23, local copies, waits for them, and re-layouts  8.02 us
    ppermute x9, waiting for transfers between devices, swap(): lax.ppermute(x, 'ctx', [(i, i ^ mask) for i in range(lax.axis_size('ctx'))])  5 us
    pallas_call x1, Pallas kernels, project(): pl.pallas_call(project_kernel, out_shape=jax.ShapeDtypeStruct(given.shape...  4.65 us
    ppermute x3, starting transfers between devices, rotate(): return lax.ppermute(x, 'ctx', [(i, (i + distance) % n) for i in range(n)])  4.57 us
    dot_general x1, matrix products, per_device(): jnp.dot(heads, part(out_weight, head, cols), preferred_element_type=jnp.f...  4.22 us
  transfers between devices with their start and end apart: 14, of which 5 were waited for; matrix products, arithmetic and copies ran while one was open for 13% of the time, Pallas kernels for 17%

profile of v6, /device:TPU:2, one launch (start us, length us, event | category | flops | bytes accessed | tf_op | source)
XLA Modules:
  0.0 82.3 jit_solution(10494376640948963386)
XLA Ops:
  0.0 0.0 copy-start.8
  0.0 1.0 %constant_dynamic-slice_fusion.5 = bf16[384,512]{1,0:T(8,128)(2,1)S(1)} fusion(bf16[384,1024]{1,0:T(8,128)(2,1)} %refs_0_.1, s32[]{:T(128)S(6)} %select_n.54), kind=kLoop, calls=%fused_computation.15 | loop fusion | bytes 786436 | tf_op jit(solution)/shard_map/dynamic_slice | solution.py:242
  1.0 0.1 collective-permute-start.1
  1.1 1.1 %constant_dynamic-slice_fusion.3 = (bf16[384,128]{1,0:T(8,128)(2,1)S(1)}, bf16[384,128]{1,0:T(8,128)(2,1)S(1)}, bf16[384,128]{1,0:T(8,128)(2,1)S(1)}, bf16[384,128]{1,0:T(8,128)(2,1)S(1)}) fusion(bf16[384,256]{1,0:T(8,128)(2,1)} %param.7, s32[]{:T(128)S(6)} %select_n.59, s32[]{:T(128)S(6)} %select_n.60, bf16[384,256]{1,0:T(8,128)(2,1)} %param.6), kind=kLoop, calls=%fused_computation.13 | loop fusion | bytes 786440 | tf_op jit(solution)/shard_map/dynamic_slice | solution.py:242
  2.2 0.5 collective-permute-start.2
  2.8 0.0 copy-done.8
  2.8 0.1 collective-permute-start
  2.9 1.6 %collective-permute-start.3 = (bf16[384,256]{1,0:T(8,128)(2,1)S(1)}, bf16[384,256]{1,0:T(8,128)(2,1)}, u32[]{:S(2)}, u32[]{:S(2)}) collective-permute-start(bf16[384,256]{1,0:T(8,128)(2,1)S(1)} %pad_maximum_fusion.1), channel_id=1, source_target_pairs={{0,8},{2,10},{4,12},{6,14},{8,16},{10,18},{12,20},{14,22},{16,24},... | collective-permute-start | bytes 589832 | tf_op jit(solution)/shard_map/ppermute | solution.py:19
  4.5 0.0 copy-start.7
  4.5 0.0 collective-permute-done.2
  4.5 1.6 %collective-permute-start.4 = (bf16[384,256]{1,0:T(8,128)(2,1)S(1)}, bf16[384,256]{1,0:T(8,128)(2,1)S(1)}, u32[]{:S(2)}, u32[]{:S(2)}) collective-permute-start(bf16[384,256]{1,0:T(8,128)(2,1)S(1)} %collective-permute-done.2), channel_id=1, source_target_pairs={{0,8},{2,10},{4,12},{6,14},{8,16},{10,18},{12,20},{14,22},{16,24},... | collective-permute-start | bytes 589832 | tf_op jit(solution)/shard_map/ppermute | solution.py:19
  6.1 0.0 collective-permute-done.1.refs_1_
  6.1 2.7 %dynamic_slice.25 = bf16[512,1536]{1,0:T(8,128)(2,1)} dynamic-slice(bf16[1024,4096]{1,0:T(8,128)(2,1)} %param.9, s32[]{:T(128)S(6)} %select_n.55, s32[]{:T(128)S(6)} %select_n.58), dynamic_slice_sizes={512,1536} | dynamic-slice | bytes 3145732 | tf_op jit(solution)/shard_map/dynamic_slice | solution.py:257
  8.8 1.5 %collective-permute-start.7 = (bf16[512,1536]{1,0:T(8,128)(2,1)}, bf16[512,1536]{1,0:T(8,128)(2,1)}, u32[]{:S(2)}, u32[]{:S(2)}) collective-permute-start(bf16[512,1536]{1,0:T(8,128)(2,1)} %dynamic_slice.25), channel_id=1, source_target_pairs={{0,1},{1,0},{2,3},{3,2},{4,5},{5,4},{6,7},{7,6},{8,9},{9,8},{10,11... | collective-permute-start | bytes 4718600 | tf_op jit(solution)/shard_map/ppermute | solution.py:29
  10.4 0.0 collective-permute-done.recv_starts_ref
  10.4 0.0 copy-done.7
  10.4 3.7 %shard_map.55 = (bf16[6,512,128]{2,1,0:T(8,128)(2,1)S(1)}, f32[6,512,128]{2,1,0:T(8,128)S(1)}, f32[6,512,256]{2,1,0:T(8,128)S(1)}) custom-call(s32[3]{0:T(128)S(1)} %copy-done.8, s32[3]{0:T(128)S(1)} %collective-permute-done.recv_starts_ref, bf16[384,1024]{1,0:T(8,128)(2,1)S(1)} %copy-done.7, bf16[384,512]{1,0:T(8,128)(2,1)S(1)} %collective-permute-done.1.refs_1_, ...), custom_call_target="tpu_custom_call" | custom-call | flops 1449551488 | bytes 8388608 | tf_op jit(solution)/shard_map/pallas_call | solution.py:220
  14.1 0.0 copy-start.9
  14.1 1.6 %copy-done.9 = f32[6,512,256]{2,1,0:T(8,128)} copy-done((f32[6,512,256]{2,1,0:T(8,128)}, f32[6,512,256]{2,1,0:T(8,128)S(1)}, u32[]{:S(2)}) %copy-start.9) | copy-done | bytes 3145752
  15.8 0.0 copy-start.2
  15.8 0.0 collective-permute-done.3
  15.8 0.5 collective-permute-done.4
  16.3 0.9 %constant_dynamic-update-slice_fusion.1 = bf16[768,256]{1,0:T(8,128)(2,1)S(1)} fusion(bf16[384,256]{1,0:T(8,128)(2,1)} %collective-permute-done.3), kind=kLoop, calls=%fused_computation.8 | loop fusion | bytes 393216
  17.2 1.4 %collective-permute-start.6 = (bf16[768,256]{1,0:T(8,128)(2,1)S(1)}, bf16[768,256]{1,0:T(8,128)(2,1)S(1)}, u32[]{:S(2)}, u32[]{:S(2)}) collective-permute-start(bf16[768,256]{1,0:T(8,128)(2,1)S(1)} %constant_dynamic-update-slice_fusion.refs_3_), channel_id=1, source_target_pairs={{0,8},{2,10},{4,12},{6,14},{8,16},{10,18},{12,20},{14,22},{16,24},... | collective-permute-start | bytes 1179656 | tf_op jit(solution)/shard_map/ppermute | solution.py:19
  18.6 0.5 collective-permute-start.5
  19.1 0.0 copy-start.10
  19.1 1.9 %copy-done.10 = f32[6,512,256]{2,1,0:T(8,128)S(1)} copy-done((f32[6,512,256]{2,1,0:T(8,128)S(1)}, f32[6,512,256]{2,1,0:T(8,128)}, u32[]{:S(2)}) %copy-start.10) | copy-done | bytes 3145752
  21.0 1.0 %shard_map.56 = (f32[6,512,128]{2,1,0:T(8,128)S(1)}, f32[6,512,256]{2,1,0:T(8,128)S(1)}) custom-call(s32[3]{0:T(128)S(1)} %copy-done.8, s32[3]{0:T(128)S(1)} %collective-permute-done.recv_starts_ref, bf16[6,512,128]{2,1,0:T(8,128)(2,1)S(1)} %get-tuple-element.26.refs_0_, f32[6,512,128]{2,1,0:T(8,128)S(1)} %get-tuple-element.27.refs_1_, ...), custom_call_target="tpu_custom_call" | custom-call | flops 2415919104 | bytes 8388608 | tf_op jit(solution)/shard_map/pallas_call | solution.py:220
  22.0 0.0 copy-done.2
  22.0 7.8 %collective-permute-done.6.refs_4_ = bf16[768,256]{1,0:T(8,128)(2,1)S(1)} collective-permute-done((bf16[768,256]{1,0:T(8,128)(2,1)S(1)}, bf16[768,256]{1,0:T(8,128)(2,1)S(1)}, u32[]{:S(2)}, u32[]{:S(2)}) %collective-permute-start.6) | collective-permute-done | bytes 393248 | tf_op jit(solution)/shard_map/ppermute | solution.py:19
  29.8 0.0 copy-start.5
  29.8 0.1 broadcast_select_fusion
  29.9 0.7 collective-permute-start.8
  30.6 0.0 collective-permute-done.5.refs_3_
  30.6 0.0 copy-done.5
  30.7 0.0 copy-start.3
  30.7 1.1 %copy-done.3 = bf16[6,512,128]{2,1,0:T(8,128)(2,1)S(1)} copy-done((bf16[6,512,128]{2,1,0:T(8,128)(2,1)S(1)}, bf16[6,512,128]{2,1,0:T(8,128)(2,1)}, u32[]{:S(2)}) %copy-start.3) | copy-done | bytes 786456
  31.8 0.0 copy-start.6
  31.8 1.0 %copy-done.6 = bf16[768,256]{1,0:T(8,128)(2,1)S(1)} copy-done((bf16[768,256]{1,0:T(8,128)(2,1)S(1)}, bf16[768,256]{1,0:T(8,128)(2,1)}, u32[]{:S(2)}) %copy-start.6) | copy-done | bytes 393240
  32.8 1.0 %shard_map.57 = (f32[6,512,128]{2,1,0:T(8,128)S(1)}, f32[6,512,256]{2,1,0:T(8,128)S(1)}) custom-call(s32[3]{0:T(128)S(1)} %copy-done.8, s32[3]{0:T(128)S(1)} %collective-permute-done.recv_starts_ref, bf16[6,512,128]{2,1,0:T(8,128)(2,1)S(1)} %copy-done.3, f32[6,512,128]{2,1,0:T(8,128)S(1)} %get-tuple-element.31.refs_1_, ...), custom_call_target="tpu_custom_call" | custom-call | flops 4831838208 | bytes 8388608 | tf_op jit(solution)/shard_map/pallas_call | solution.py:220
  33.8 0.0 copy-start
  33.8 11.5 %collective-permute-done.7.refs_0_ = bf16[512,1536]{1,0:T(8,128)(2,1)} collective-permute-done((bf16[512,1536]{1,0:T(8,128)(2,1)}, bf16[512,1536]{1,0:T(8,128)(2,1)}, u32[]{:S(2)}, u32[]{:S(2)}) %collective-permute-start.7) | collective-permute-done | bytes 1572896 | tf_op jit(solution)/shard_map/ppermute | solution.py:29
  45.3 0.0 collective-permute-start.12
  45.3 0.0 collective-permute-done.8.refs_3_
  45.3 3.7 %shard_map.58 = bf16[384,512]{1,0:T(8,128)(2,1)} custom-call(s32[3]{0:T(128)S(1)} %copy-done.8, s32[3]{0:T(128)S(1)} %collective-permute-done.recv_starts_ref, bf16[6,512,128]{2,1,0:T(8,128)(2,1)S(1)} %copy-done.3, f32[6,512,128]{2,1,0:T(8,128)S(1)} %get-tuple-element.36.refs_1_, f32[6,512,256]{2,1,0:T(8,128)S(1)} %get-tuple-element.37.refs_2_, ...), custom_call_target="tpu_custom_call" | custom-call | flops 1207959552 | bytes 8388608 | tf_op jit(solution)/shard_map/pallas_call | solution.py:220
  49.0 0.0 copy-done
  49.0 0.5 collective-permute-start.9
  49.5 0.0 copy-start.4
  49.5 1.1 %constant_dynamic-slice_fusion = bf16[512,512]{1,0:T(8,128)(2,1)S(1)} fusion(bf16[512,1536]{1,0:T(8,128)(2,1)} %collective-permute-done.7.refs_0_, s32[]{:T(128)S(6)} %select_n.66), kind=kLoop, calls=%fused_computation.9 | loop fusion | bytes 1048580 | tf_op jit(solution)/shard_map/dynamic_slice | solution.py:269
  50.6 1.6 %collective-permute-start.11 = (bf16[512,512]{1,0:T(8,128)(2,1)S(1)}, bf16[512,512]{1,0:T(8,128)(2,1)}, u32[]{:S(2)}, u32[]{:S(2)}) collective-permute-start(bf16[512,512]{1,0:T(8,128)(2,1)S(1)} %constant_dynamic-slice_fusion), channel_id=1, source_target_pairs={{0,8},{2,10},{4,12},{6,14},{8,0},{10,2},{12,4},{14,6},{16,24},{18,... | collective-permute-start | bytes 1572872 | tf_op jit(solution)/shard_map/ppermute | solution.py:23
  52.3 0.0 collective-permute-done.9.refs_4_
  52.3 0.0 copy-done.4
  52.3 0.0 copy-start.1
  52.3 1.4 %copy-done.1 = f32[6,512,128]{2,1,0:T(8,128)S(1)} copy-done((f32[6,512,128]{2,1,0:T(8,128)S(1)}, f32[6,512,128]{2,1,0:T(8,128)}, u32[]{:S(2)}) %copy-start.1) | copy-done | bytes 1572888
  53.7 4.5 %shard_map.59 = bf16[384,1024]{1,0:T(8,128)(2,1)} custom-call(s32[3]{0:T(128)S(1)} %copy-done.8, s32[3]{0:T(128)S(1)} %collective-permute-done.recv_starts_ref, bf16[6,512,128]{2,1,0:T(8,128)(2,1)S(1)} %copy-done.4, f32[6,512,128]{2,1,0:T(8,128)S(1)} %copy-done.1, f32[6,512,256]{2,1,0:T(8,128)S(1)} %get-tuple-element.37.refs_2_, ...), custom_call_target="tpu_custom_call" | custom-call | flops 1207959552 | bytes 8388608 | tf_op jit(solution)/shard_map/pallas_call | solution.py:220
  58.1 1.5 %collective-permute-start.10 = (bf16[384,1024]{1,0:T(8,128)(2,1)}, bf16[384,1024]{1,0:T(8,128)(2,1)S(1)}, u32[]{:S(2)}, u32[]{:S(2)}) collective-permute-start(bf16[384,1024]{1,0:T(8,128)(2,1)} %shard_map.59), channel_id=1, source_target_pairs={{0,1},{1,0},{2,3},{3,2},{4,5},{5,4},{6,7},{7,6},{8,9},{9,8},{10,11... | collective-permute-start | bytes 2359304 | tf_op jit(solution)/shard_map/ppermute | solution.py:29
  59.7 5.0 %collective-permute-done.11.refs_1_ = bf16[512,512]{1,0:T(8,128)(2,1)} collective-permute-done((bf16[512,512]{1,0:T(8,128)(2,1)S(1)}, bf16[512,512]{1,0:T(8,128)(2,1)}, u32[]{:S(2)}, u32[]{:S(2)}) %collective-permute-start.11) | collective-permute-done | bytes 524320 | tf_op jit(solution)/shard_map/ppermute | solution.py:23
  64.6 0.0 collective-permute-start.13
  64.7 4.2 %fusion.2.given_ref = bf16[384,2048]{1,0:T(8,128)(2,1)S(1)} fusion(bf16[384,1024]{1,0:T(8,128)(2,1)} %shard_map.59, bf16[1024,4096]{1,0:T(8,128)(2,1)} %param.9, s32[]{:T(128)S(6)} %select_n.65), kind=kOutput, calls=%fused_computation.2 | convolution fusion | flops 1611399168 | bytes 6553604 | tf_op jit(solution)/shard_map/dot_general | solution.py:274
  68.9 0.0 collective-permute-done.13.refs_3_
  68.9 8.6 %collective-permute-done.10.heads_ref = bf16[384,1024]{1,0:T(8,128)(2,1)S(1)} collective-permute-done((bf16[384,1024]{1,0:T(8,128)(2,1)}, bf16[384,1024]{1,0:T(8,128)(2,1)S(1)}, u32[]{:S(2)}, u32[]{:S(2)}) %collective-permute-start.10) | collective-permute-done | bytes 786464 | tf_op jit(solution)/shard_map/ppermute | solution.py:29
  77.5 0.0 collective-permute-done.12.refs_2_
  77.5 4.6 %shard_map.60 = bf16[384,2048]{1,0:T(8,128)(2,1)} custom-call(bf16[384,2048]{1,0:T(8,128)(2,1)S(1)} %fusion.2.given_ref, bf16[384,1024]{1,0:T(8,128)(2,1)S(1)} %collective-permute-done.10.heads_ref, bf16[512,1536]{1,0:T(8,128)(2,1)} %collective-permute-done.7.refs_0_, bf16[512,512]{1,0:T(8,128)(2,1)} %collective-permute-done.11.refs_1_, ...), custom_call_target="tpu_custom_call" | custom-call | flops 1610612736 | bytes 4194304 | tf_op jit(solution)/shard_map/pallas_call | solution.py:55
  (4 shorter events, 0.1 us)
Async XLA Ops:
  0.0 2.8 %copy-start.8 = (s32[3]{0:T(128)S(1)}, s32[3]{0:T(128)}, u32[]{:S(2)}) copy-start(s32[3]{0:T(128)} %starts_ref.9) | copy-start | bytes 40
  1.0 5.1 %collective-permute-start.1 = (bf16[384,512]{1,0:T(8,128)(2,1)S(1)}, bf16[384,512]{1,0:T(8,128)(2,1)S(1)}, u32[]{:S(2)}, u32[]{:S(2)}) collective-permute-start(bf16[384,512]{1,0:T(8,128)(2,1)S(1)} %constant_dynamic-slice_fusion.5), channel_id=1, source_target_pairs={{0,2},{2,0},{4,6},{6,4},{8,10},{10,8},{12,14},{14,12},{16,18},{18,... | collective-permute-start | bytes 1179656 | tf_op jit(solution)/shard_map/ppermute | solution.py:23
  2.2 2.3 %collective-permute-start.2 = (bf16[384,256]{1,0:T(8,128)(2,1)S(1)}, bf16[384,256]{1,0:T(8,128)(2,1)S(1)}, u32[]{:S(2)}, u32[]{:S(2)}) collective-permute-start(bf16[384,256]{1,0:T(8,128)(2,1)S(1)} %pad_maximum_fusion.2), channel_id=1, source_target_pairs={{0,2},{2,0},{4,6},{6,4},{8,10},{10,8},{12,14},{14,12},{16,18},{18,... | collective-permute-start | bytes 589832 | tf_op jit(solution)/shard_map/ppermute | solution.py:23
  2.8 7.6 %collective-permute-start = (s32[3]{0:T(128)S(1)}, s32[3]{0:T(128)S(1)}, u32[]{:S(2)}, u32[]{:S(2)}) collective-permute-start(s32[3]{0:T(128)S(1)} %copy-done.8), channel_id=1, source_target_pairs={{0,2},{2,0},{4,6},{6,4},{8,10},{10,8},{12,14},{14,12},{16,18},{18,... | collective-permute-start | bytes 44 | tf_op jit(solution)/shard_map/ppermute | solution.py:23
  2.9 12.9 %collective-permute-start.3 = (bf16[384,256]{1,0:T(8,128)(2,1)S(1)}, bf16[384,256]{1,0:T(8,128)(2,1)}, u32[]{:S(2)}, u32[]{:S(2)}) collective-permute-start(bf16[384,256]{1,0:T(8,128)(2,1)S(1)} %pad_maximum_fusion.1), channel_id=1, source_target_pairs={{0,8},{2,10},{4,12},{6,14},{8,16},{10,18},{12,20},{14,22},{16,24},... | collective-permute-start | bytes 589832 | tf_op jit(solution)/shard_map/ppermute | solution.py:19
  4.5 5.9 %copy-start.7 = (bf16[384,1024]{1,0:T(8,128)(2,1)S(1)}, bf16[384,1024]{1,0:T(8,128)(2,1)}, u32[]{:S(2)}) copy-start(bf16[384,1024]{1,0:T(8,128)(2,1)} %refs_0_.1) | copy-start | bytes 2359300
  4.5 11.7 %collective-permute-start.4 = (bf16[384,256]{1,0:T(8,128)(2,1)S(1)}, bf16[384,256]{1,0:T(8,128)(2,1)S(1)}, u32[]{:S(2)}, u32[]{:S(2)}) collective-permute-start(bf16[384,256]{1,0:T(8,128)(2,1)S(1)} %collective-permute-done.2), channel_id=1, source_target_pairs={{0,8},{2,10},{4,12},{6,14},{8,16},{10,18},{12,20},{14,22},{16,24},... | collective-permute-start | bytes 589832 | tf_op jit(solution)/shard_map/ppermute | solution.py:19
  8.8 36.5 %collective-permute-start.7 = (bf16[512,1536]{1,0:T(8,128)(2,1)}, bf16[512,1536]{1,0:T(8,128)(2,1)}, u32[]{:S(2)}, u32[]{:S(2)}) collective-permute-start(bf16[512,1536]{1,0:T(8,128)(2,1)} %dynamic_slice.25), channel_id=1, source_target_pairs={{0,1},{1,0},{2,3},{3,2},{4,5},{5,4},{6,7},{7,6},{8,9},{9,8},{10,11... | collective-permute-start | bytes 4718600 | tf_op jit(solution)/shard_map/ppermute | solution.py:29
  14.1 1.6 %copy-start.9 = (f32[6,512,256]{2,1,0:T(8,128)}, f32[6,512,256]{2,1,0:T(8,128)S(1)}, u32[]{:S(2)}) copy-start(f32[6,512,256]{2,1,0:T(8,128)S(1)} %get-tuple-element.28.refs_2_) | copy-start | bytes 9437188
  15.8 6.2 %copy-start.2 = (bf16[6,512,128]{2,1,0:T(8,128)(2,1)}, bf16[6,512,128]{2,1,0:T(8,128)(2,1)S(1)}, u32[]{:S(2)}) copy-start(bf16[6,512,128]{2,1,0:T(8,128)(2,1)S(1)} %get-tuple-element.26.refs_0_) | copy-start | bytes 2359300
  17.2 12.6 %collective-permute-start.6 = (bf16[768,256]{1,0:T(8,128)(2,1)S(1)}, bf16[768,256]{1,0:T(8,128)(2,1)S(1)}, u32[]{:S(2)}, u32[]{:S(2)}) collective-permute-start(bf16[768,256]{1,0:T(8,128)(2,1)S(1)} %constant_dynamic-update-slice_fusion.refs_3_), channel_id=1, source_target_pairs={{0,8},{2,10},{4,12},{6,14},{8,16},{10,18},{12,20},{14,22},{16,24},... | collective-permute-start | bytes 1179656 | tf_op jit(solution)/shard_map/ppermute | solution.py:19
  18.6 12.1 %collective-permute-start.5 = (bf16[768,256]{1,0:T(8,128)(2,1)S(1)}, bf16[768,256]{1,0:T(8,128)(2,1)S(1)}, u32[]{:S(2)}, u32[]{:S(2)}) collective-permute-start(bf16[768,256]{1,0:T(8,128)(2,1)S(1)} %constant_dynamic-update-slice_fusion.refs_3_), channel_id=1, source_target_pairs={{0,4},{2,6},{4,0},{6,2},{8,12},{10,14},{12,8},{14,10},{16,20},{18,... | collective-permute-start | bytes 1179656 | tf_op jit(solution)/shard_map/ppermute | solution.py:23
  19.1 1.9 %copy-start.10 = (f32[6,512,256]{2,1,0:T(8,128)S(1)}, f32[6,512,256]{2,1,0:T(8,128)}, u32[]{:S(2)}) copy-start(f32[6,512,256]{2,1,0:T(8,128)} %copy-done.9) | copy-start | bytes 9437188
  29.8 0.8 %copy-start.5 = (bf16[768,256]{1,0:T(8,128)(2,1)}, bf16[768,256]{1,0:T(8,128)(2,1)S(1)}, u32[]{:S(2)}) copy-start(bf16[768,256]{1,0:T(8,128)(2,1)S(1)} %collective-permute-done.6.refs_4_) | copy-start | bytes 1179652
  29.9 15.4 %collective-permute-start.8 = (bf16[768,256]{1,0:T(8,128)(2,1)S(1)}, bf16[768,256]{1,0:T(8,128)(2,1)S(1)}, u32[]{:S(2)}, u32[]{:S(2)}) collective-permute-start(bf16[768,256]{1,0:T(8,128)(2,1)S(1)} %broadcast_select_fusion), channel_id=1, source_target_pairs={{0,4},{2,6},{4,0},{6,2},{8,12},{10,14},{12,8},{14,10},{16,20},{18,... | collective-permute-start | bytes 1179656 | tf_op jit(solution)/shard_map/ppermute | solution.py:23
  30.7 1.1 %copy-start.3 = (bf16[6,512,128]{2,1,0:T(8,128)(2,1)S(1)}, bf16[6,512,128]{2,1,0:T(8,128)(2,1)}, u32[]{:S(2)}) copy-start(bf16[6,512,128]{2,1,0:T(8,128)(2,1)} %copy-done.2) | copy-start | bytes 2359300
  31.8 1.0 %copy-start.6 = (bf16[768,256]{1,0:T(8,128)(2,1)S(1)}, bf16[768,256]{1,0:T(8,128)(2,1)}, u32[]{:S(2)}) copy-start(bf16[768,256]{1,0:T(8,128)(2,1)} %copy-done.5) | copy-start | bytes 1179652
  33.8 15.1 %copy-start = (f32[6,512,128]{2,1,0:T(8,128)}, f32[6,512,128]{2,1,0:T(8,128)S(1)}, u32[]{:S(2)}) copy-start(f32[6,512,128]{2,1,0:T(8,128)S(1)} %get-tuple-element.36.refs_1_) | copy-start | bytes 4718596
  45.3 32.2 %collective-permute-start.12 = (bf16[512,1536]{1,0:T(8,128)(2,1)}, bf16[512,1536]{1,0:T(8,128)(2,1)}, u32[]{:S(2)}, u32[]{:S(2)}) collective-permute-start(bf16[512,1536]{1,0:T(8,128)(2,1)} %collective-permute-done.7.refs_0_), channel_id=1, source_target_pairs={{0,2},{2,0},{4,6},{6,4},{8,10},{10,8},{12,14},{14,12},{16,18},{18,... | collective-permute-start | bytes 4718600 | tf_op jit(solution)/shard_map/ppermute | solution.py:23
  49.0 3.3 %collective-permute-start.9 = (bf16[384,512]{1,0:T(8,128)(2,1)}, bf16[384,512]{1,0:T(8,128)(2,1)}, u32[]{:S(2)}, u32[]{:S(2)}) collective-permute-start(bf16[384,512]{1,0:T(8,128)(2,1)} %shard_map.58), channel_id=1, source_target_pairs={{0,2},{2,0},{4,6},{6,4},{8,10},{10,8},{12,14},{14,12},{16,18},{18,... | collective-permute-start | bytes 1179656 | tf_op jit(solution)/shard_map/ppermute | solution.py:23
  49.5 2.8 %copy-start.4 = (bf16[6,512,128]{2,1,0:T(8,128)(2,1)S(1)}, bf16[6,512,128]{2,1,0:T(8,128)(2,1)}, u32[]{:S(2)}) copy-start(bf16[6,512,128]{2,1,0:T(8,128)(2,1)} %copy-done.2) | copy-start | bytes 2359300
  50.6 14.0 %collective-permute-start.11 = (bf16[512,512]{1,0:T(8,128)(2,1)S(1)}, bf16[512,512]{1,0:T(8,128)(2,1)}, u32[]{:S(2)}, u32[]{:S(2)}) collective-permute-start(bf16[512,512]{1,0:T(8,128)(2,1)S(1)} %constant_dynamic-slice_fusion), channel_id=1, source_target_pairs={{0,8},{2,10},{4,12},{6,14},{8,0},{10,2},{12,4},{14,6},{16,24},{18,... | collective-permute-start | bytes 1572872 | tf_op jit(solution)/shard_map/ppermute | solution.py:23
  52.3 1.4 %copy-start.1 = (f32[6,512,128]{2,1,0:T(8,128)S(1)}, f32[6,512,128]{2,1,0:T(8,128)}, u32[]{:S(2)}) copy-start(f32[6,512,128]{2,1,0:T(8,128)} %copy-done) | copy-start | bytes 4718596
  58.1 19.4 %collective-permute-start.10 = (bf16[384,1024]{1,0:T(8,128)(2,1)}, bf16[384,1024]{1,0:T(8,128)(2,1)S(1)}, u32[]{:S(2)}, u32[]{:S(2)}) collective-permute-start(bf16[384,1024]{1,0:T(8,128)(2,1)} %shard_map.59), channel_id=1, source_target_pairs={{0,1},{1,0},{2,3},{3,2},{4,5},{5,4},{6,7},{7,6},{8,9},{9,8},{10,11... | collective-permute-start | bytes 2359304 | tf_op jit(solution)/shard_map/ppermute | solution.py:29
  64.6 4.2 %collective-permute-start.13 = (bf16[512,512]{1,0:T(8,128)(2,1)}, bf16[512,512]{1,0:T(8,128)(2,1)S(1)}, u32[]{:S(2)}, u32[]{:S(2)}) collective-permute-start(bf16[512,512]{1,0:T(8,128)(2,1)} %collective-permute-done.11.refs_1_), channel_id=1, source_target_pairs={{0,2},{2,0},{4,6},{6,4},{8,10},{10,8},{12,14},{14,12},{16,18},{18,... | collective-permute-start | bytes 1572872 | tf_op jit(solution)/shard_map/ppermute | solution.py:23

commit v7 on v6

--- a/solution.py
+++ b/solution.py
@@ -27,6 +27,23 @@
     n = lax.axis_size("ctx")
     route = [(2 * i + h, 2 * (i ^ mask) + 1 - h) for i in range(n) for h in range(2)]
     return lax.ppermute(x, ("ctx", "head"), route)
+
+
+def join_kernel(first_ref, second_ref, out_ref):
+    tok = first_ref.shape[0]
+    out_ref[:tok] = first_ref[...]
+    out_ref[tok:] = second_ref[...]
+
+
+def join(first, second):
+    vmem = pl.BlockSpec(memory_space=pltpu.VMEM)
+    return pl.pallas_call(
+        join_kernel,
+        out_shape=jax.ShapeDtypeStruct((2 * first.shape[0], first.shape[1]), first.dtype),
+        in_specs=[vmem, vmem],
+        out_specs=vmem,
+        compiler_params=pltpu.CompilerParams(vmem_limit_bytes=4 * 2**20),
+    )(first, second)
 
 
 def project_kernel(given_ref, heads_ref, *refs):
@@ -73,19 +90,19 @@
         queries_ref, q_recv_ref = refs[:2]
         refs = refs[2:]
     else:
-        q_ref, top_in, acc_in = refs[:3]
+        q_ref, stats_in, acc_in = refs[:3]
         refs = refs[3:]
     n_pieces = len(distances)
     pieces = refs[:n_pieces]
     refs = refs[n_pieces:]
     if stage == "first":
-        q_ref, top_ref, acc_ref, held_ref = refs
+        q_ref, stats_ref, acc_ref, held_ref = refs
     elif stage == "next":
-        top_ref, acc_ref, held_ref = refs
+        stats_ref, acc_ref, held_ref = refs
     else:
         if stage == "own":
             swapped_ref, *refs = refs
-        out_ref, acc_ref, held_ref = refs
+        out_ref, stats_ref, acc_ref, held_ref = refs
     tok = starts_ref.shape[0] * BLOCK
     half = tok // BLOCK
     blocks = 2 * half
@@ -122,14 +139,20 @@
         k_id = lax.broadcasted_iota(jnp.int32, (1, s.shape[1]), 1)
         return jnp.where(k_id >= since, s, MASKED)
 
-    def update(i, base, b, r, top_from, acc_from, to):
+    def both(top, total):
+        lane = lax.broadcasted_iota(jnp.int32, total.shape, 1)
+        return jnp.where(lane < HEAD_SIZE // 2, top, total)
+
+    def update(i, base, b, r, stats_from, acc_from, to):
         s = keep(scores(b, r, i, 2 * tok), start_of(b) - base)
-        old = top_from[b, r][:, :1]
+        stats = stats_from[b, r]
+        old = stats[:, :1]
         top = jnp.maximum(old, jnp.max(s, axis=1, keepdims=True))
         p = jnp.exp2(s * factor - top * factor)
-        if stage == "next":
-            top_ref[to, r] = jnp.broadcast_to(top, (TILE, HEAD_SIZE))
-        acc_ref[to, r] = acc_from[b, r] * jnp.exp2((old - top) * factor) + weigh(p, i, 2 * tok)
+        decay = jnp.exp2((old - top) * factor)
+        added = weigh(p, i, 2 * tok)
+        stats_ref[to, r] = both(top, stats * decay + added[:, HEAD_SIZE:])
+        acc_ref[to, r] = acc_from[b, r] * decay + added[:, :HEAD_SIZE]
 
     def attend_own():
         for j in range(half):
@@ -146,11 +169,12 @@
             s = jnp.concatenate([keep(s[:, : b * BLOCK], since), diag], 1) if b else diag
             top = jnp.max(s, axis=1, keepdims=True)
             p = jnp.exp2(s * factor - top * factor)
-            top_ref[b, r] = jnp.broadcast_to(top, (TILE, HEAD_SIZE))
-            acc_ref[b, r] = weigh(p, 0, width)
+            added = weigh(p, 0, width)
+            stats_ref[b, r] = both(top, added[:, HEAD_SIZE:])
+            acc_ref[b, r] = added[:, :HEAD_SIZE]
 
     def attend_next():
-        top_ref[...] = top_in[...]
+        stats_ref[...] = stats_in[...]
         acc_ref[...] = acc_in[...]
 
         @pl.loop(0, 2 * n_pieces)
@@ -165,7 +189,7 @@
             def _():
                 for b, r in tiles[: len(tiles) // 2]:
                     b = first_block + b
-                    update(i, base, b, r, top_ref, acc_ref, b)
+                    update(i, base, b, r, stats_ref, acc_ref, b)
 
     def attend_last(shard):
         first_block = shard * half
@@ -175,14 +199,16 @@
         @pl.when(needed)
         def _():
             for b, r in tiles[: len(tiles) // 2]:
-                update(0, base, first_block + b, r, top_in, acc_in, b)
+                update(0, base, first_block + b, r, stats_in, acc_in, b)
 
         @pl.when(jnp.logical_not(needed))
         def _():
+            stats_ref[...] = stats_in[pl.ds(first_block, half)]
             acc_ref[...] = acc_in[pl.ds(first_block, half)]
 
         for j in range(half):
-            o = (acc_ref[j, :, :HEAD_SIZE] / acc_ref[j, :, HEAD_SIZE:]).astype(jnp.bfloat16)
+            total = stats_ref[j, :, HEAD_SIZE // 2 : HEAD_SIZE // 2 + 1]
+            o = (acc_ref[j] / total).astype(jnp.bfloat16)
             for h in range(n_head):
                 first = core * rows + h * HEAD_SIZE if stage == "own" else h * HEAD_SIZE
                 lanes = pl.ds(pl.multiple_of(first, HEAD_SIZE), HEAD_SIZE)
@@ -202,10 +228,7 @@
     tok, half = starts.shape[0] * BLOCK, starts.shape[0]
     rows = operands[1].shape[1]
     blocks, n_head, n_pieces = 2 * half, rows // BLOCK, len(distances)
-    state = [
-        jax.ShapeDtypeStruct((blocks, rows, HEAD_SIZE), jnp.float32),
-        jax.ShapeDtypeStruct((blocks, rows, 2 * HEAD_SIZE), jnp.float32),
-    ]
+    state = [jax.ShapeDtypeStruct((blocks, rows, HEAD_SIZE), jnp.float32)] * 2
     scratch = [pltpu.VMEM((n_pieces, 2 * tok, 2 * HEAD_SIZE), jnp.bfloat16)]
     share = n_pieces
     if stage == "first":
@@ -215,7 +238,7 @@
     else:
         width = rows * (2 if stage == "own" else 1)
         outs, share = [jax.ShapeDtypeStruct((tok, width), jnp.bfloat16)], 0.5
-        scratch = [pltpu.VMEM((half, rows, 2 * HEAD_SIZE), jnp.float32)] + scratch
+        scratch = [pltpu.VMEM((half, rows, HEAD_SIZE), jnp.float32)] * 2 + scratch
     vmem, smem = pl.BlockSpec(memory_space=pltpu.VMEM), pl.BlockSpec(memory_space=pltpu.SMEM)
     return pl.pallas_call(
         functools.partial(attention_kernel, stage, distances, n_head),
@@ -250,29 +273,28 @@
     recv_starts = swap(block_start, 1)
     own = jnp.concatenate([mine, recv])
     starts = (block_start, recv_starts)
-    tile = cols // 4
-    part_id = me // 4 % 2
+    tile, quarter = cols // 4, me // 4 % 2
     q_recv, weight = lax.optimization_barrier((q_recv, out_weight))
-    first_col = ((1 - head) * 4 + part_id) * tile
+    first_col = ((1 - head) * 4 + quarter) * tile
     sent = lax.dynamic_slice(weight, (core * group, first_col), (group, 3 * tile))
     q_recv, sent = lax.optimization_barrier((q_recv, sent))
     fetched = cross(sent, 0)
     q, *state = attention_call("first", ((0, 0),), *starts, (queries, q_recv, own))
     q, one_behind = lax.optimization_barrier((q, one_behind))
-    one_behind = jnp.concatenate(one_behind)
+    one_behind = join(*one_behind)
     two_behind = rotate(one_behind, 4)
     across = swap(one_behind, 2)
     third = swap(jnp.where(col == 1, two_behind, own), 2)
     state = attention_call("next", ((2, 2),), *starts, (q, *state, one_behind))
     state = attention_call("next", ((1, 3), (4, 4)), *starts, (q, *state, across, two_behind))
-    state, fetched = lax.optimization_barrier((state, fetched))
-    weights = [fetched, swap(lax.dynamic_slice_in_dim(fetched, 2 * tile * part_id, tile, 1), 4)]
     (o_other,) = attention_call("other", ((3, 1),), *starts, (q, *state, third))
+    _, fetched = lax.optimization_barrier((o_other, fetched))
+    weights = [fetched, swap(lax.dynamic_slice_in_dim(fetched, 2 * tile * quarter, tile, 1), 4)]
     (heads,) = attention_call("own", ((3, 1),), *starts, (q, *state, third, swap(o_other, 1)))
     heads_across = cross(heads, 0)
-    other_weights = [swap(x, 1) for x in weights]
     here = jnp.dot(heads, part(out_weight, head, cols), preferred_element_type=jnp.float32)
-    return project(here.astype(jnp.bfloat16), heads_across, (*weights, *other_weights))
+    weights += [swap(x, 1) for x in weights]
+    return project(here.astype(jnp.bfloat16), heads_across, weights)
 
 
 def solution(mesh):

time: 82.8 us -> 80 us (0.966)
  waiting for transfers between devices: 33.4 us -> 37.7 us
  starting transfers between devices: 11.7 us -> 7.77 us
  local copies, waits for them, and re-layouts: 14 us -> 10.7 us
    ppermute x2, waiting for transfers between devices: 20.1 us -> 8.84 us  [cross(): return lax.ppermute(x, ('ctx', 'head'), route)]
    ppermute x9, waiting for transfers between devices: 5 us -> 14.6 us  [swap(): lax.ppermute(x, 'ctx', [(i, i ^ mask) for i in range(lax.axis_size('ctx'))])]
    ppermute x3, waiting for transfers between devices: 8.31 us -> 14.2 us  [rotate(): return lax.ppermute(x, 'ctx', [(i, (i + distance) % n) for i in range(n)])]
    unnamed x23 -> x18, local copies, waits for them, and re-layouts: 8.02 us -> 4.71 us
    ppermute x9, starting transfers between devices: 4.12 us -> 2.48 us  [swap(): lax.ppermute(x, 'ctx', [(i, i ^ mask) for i in range(lax.axis_size('ctx'))])]
    ppermute x3, starting transfers between devices: 4.57 us -> 3.26 us  [rotate(): return lax.ppermute(x, 'ctx', [(i, (i + distance) % n) for i in range(n)])]
    ppermute x2, starting transfers between devices: 3.04 us -> 2.03 us  [cross(): return lax.ppermute(x, ('ctx', 'head'), route)]
  transfers between devices with their start and end apart: 14 -> 14, of which waited for: 5 -> 7; matrix products, arithmetic and copies ran while one was open for 13% -> 12% of each run, Pallas kernels for 17% -> 18%
where the time goes in v7:
time: 80 us; the launch traced here: 79.6 us
  waiting for transfers between devices  37.7 us (47%)
  Pallas kernels  18.7 us (23%)
  local copies, waits for them, and re-layouts  10.7 us (13%)
  starting transfers between devices  7.77 us (10%)
  matrix products  4.22 us (5%)
    ppermute x9, waiting for transfers between devices, swap(): lax.ppermute(x, 'ctx', [(i, i ^ mask) for i in range(lax.axis_size('ctx'))])  14.6 us
    ppermute x3, waiting for transfers between devices, rotate(): return lax.ppermute(x, 'ctx', [(i, (i + distance) % n) for i in range(n)])  14.2 us
    pallas_call x5, Pallas kernels, attention_call(): pl.pallas_call(functools.partial(attention_kernel, stage, distances, n_he...  14 us
    ppermute x2, waiting for transfers between devices, cross(): return lax.ppermute(x, ('ctx', 'head'), route)  8.84 us
    unnamed x18, local copies, waits for them, and re-layouts  4.71 us
    pallas_call x1, Pallas kernels, project(): pl.pallas_call(project_kernel, out_shape=jax.ShapeDtypeStruct(given.shape...  4.65 us
    dot_general x1, matrix products, per_device(): jnp.dot(heads, part(out_weight, head, cols), preferred_element_type=jnp.f...  4.22 us
    ppermute x3, starting transfers between devices, rotate(): return lax.ppermute(x, 'ctx', [(i, (i + distance) % n) for i in range(n)])  3.26 us
  transfers between devices with their start and end apart: 14, of which 7 were waited for; matrix products, arithmetic and copies ran while one was open for 12% of the time, Pallas kernels for 18%

profile of v7, /device:TPU:2, one launch (start us, length us, event | category | flops | bytes accessed | tf_op | source)
XLA Modules:
  0.0 79.6 jit_solution(284515342680448512)
XLA Ops:
  0.0 0.0 copy-start.6
  0.0 1.0 %constant_dynamic-slice_fusion.5 = bf16[384,512]{1,0:T(8,128)(2,1)S(1)} fusion(bf16[384,1024]{1,0:T(8,128)(2,1)} %refs_0_.1, s32[]{:T(128)S(6)} %select_n.54), kind=kLoop, calls=%fused_computation.13 | loop fusion | bytes 786436 | tf_op jit(solution)/shard_map/dynamic_slice | solution.py:265
  1.0 0.1 collective-permute-start.1
  1.1 1.1 %constant_dynamic-slice_fusion.3 = (bf16[384,128]{1,0:T(8,128)(2,1)S(1)}, bf16[384,128]{1,0:T(8,128)(2,1)S(1)}, bf16[384,128]{1,0:T(8,128)(2,1)S(1)}, bf16[384,128]{1,0:T(8,128)(2,1)S(1)}) fusion(bf16[384,256]{1,0:T(8,128)(2,1)} %param.7, s32[]{:T(128)S(6)} %select_n.59, s32[]{:T(128)S(6)} %select_n.60, bf16[384,256]{1,0:T(8,128)(2,1)} %param.6), kind=kLoop, calls=%fused_computation.11 | loop fusion | bytes 786440 | tf_op jit(solution)/shard_map/dynamic_slice | solution.py:265
  2.2 0.5 collective-permute-start.2
  2.8 0.0 copy-done.6
  2.8 0.1 collective-permute-start
  2.9 0.0 copy-start.5
  2.9 0.0 collective-permute-done.1.refs_1_
  2.9 2.7 %dynamic_slice.25 = bf16[512,1536]{1,0:T(8,128)(2,1)} dynamic-slice(bf16[1024,4096]{1,0:T(8,128)(2,1)} %param.9, s32[]{:T(128)S(6)} %select_n.55, s32[]{:T(128)S(6)} %select_n.58), dynamic_slice_sizes={512,1536} | dynamic-slice | bytes 3145732 | tf_op jit(solution)/shard_map/dynamic_slice | solution.py:279
  5.6 1.5 %collective-permute-start.10 = (bf16[512,1536]{1,0:T(8,128)(2,1)}, bf16[512,1536]{1,0:T(8,128)(2,1)}, u32[]{:S(2)}, u32[]{:S(2)}) collective-permute-start(bf16[512,1536]{1,0:T(8,128)(2,1)} %dynamic_slice.25), channel_id=1, source_target_pairs={{0,1},{1,0},{2,3},{3,2},{4,5},{5,4},{6,7},{7,6},{8,9},{9,8},{10,11... | collective-permute-start | bytes 4718600 | tf_op jit(solution)/shard_map/ppermute | solution.py:29
  7.1 1.6 %collective-permute-start.3 = (bf16[384,256]{1,0:T(8,128)(2,1)S(1)}, bf16[384,256]{1,0:T(8,128)(2,1)S(1)}, u32[]{:S(2)}, u32[]{:S(2)}) collective-permute-start(bf16[384,256]{1,0:T(8,128)(2,1)S(1)} %pad_maximum_fusion.1), channel_id=1, source_target_pairs={{0,8},{2,10},{4,12},{6,14},{8,16},{10,18},{12,20},{14,22},{16,24},... | collective-permute-start | bytes 589832 | tf_op jit(solution)/shard_map/ppermute | solution.py:19
  8.8 0.0 collective-permute-done.2
  8.8 1.6 %collective-permute-start.4 = (bf16[384,256]{1,0:T(8,128)(2,1)S(1)}, bf16[384,256]{1,0:T(8,128)(2,1)S(1)}, u32[]{:S(2)}, u32[]{:S(2)}) collective-permute-start(bf16[384,256]{1,0:T(8,128)(2,1)S(1)} %collective-permute-done.2), channel_id=1, source_target_pairs={{0,8},{2,10},{4,12},{6,14},{8,16},{10,18},{12,20},{14,22},{16,24},... | collective-permute-start | bytes 589832 | tf_op jit(solution)/shard_map/ppermute | solution.py:19
  10.4 0.0 collective-permute-done.recv_starts_ref
  10.4 0.0 copy-done.5
  10.4 3.7 %shard_map.55 = (bf16[6,512,128]{2,1,0:T(8,128)(2,1)S(1)}, f32[6,512,128]{2,1,0:T(8,128)S(1)}, f32[6,512,128]{2,1,0:T(8,128)S(1)}) custom-call(s32[3]{0:T(128)S(1)} %copy-done.6, s32[3]{0:T(128)S(1)} %collective-permute-done.recv_starts_ref, bf16[384,1024]{1,0:T(8,128)(2,1)S(1)} %copy-done.5, bf16[384,512]{1,0:T(8,128)(2,1)S(1)} %collective-permute-done.1.refs_1_, ...), custom_call_target="tpu_custom_call" | custom-call | flops 1449551488 | bytes 8388608 | tf_op jit(solution)/shard_map/pallas_call | solution.py:243
  14.2 0.0 copy-start.7
  14.2 1.1 %copy-done.7 = f32[6,512,128]{2,1,0:T(8,128)} copy-done((f32[6,512,128]{2,1,0:T(8,128)}, f32[6,512,128]{2,1,0:T(8,128)S(1)}, u32[]{:S(2)}) %copy-start.7) | copy-done | bytes 1572888
  15.3 0.0 copy-start
  15.3 1.4 %collective-permute-done.3.first_ref = bf16[384,256]{1,0:T(8,128)(2,1)S(1)} collective-permute-done((bf16[384,256]{1,0:T(8,128)(2,1)S(1)}, bf16[384,256]{1,0:T(8,128)(2,1)S(1)}, u32[]{:S(2)}, u32[]{:S(2)}) %collective-permute-start.3) | collective-permute-done | bytes 196640 | tf_op jit(solution)/shard_map/ppermute | solution.py:19
  16.7 3.5 %collective-permute-done.4.second_ref = bf16[384,256]{1,0:T(8,128)(2,1)S(1)} collective-permute-done((bf16[384,256]{1,0:T(8,128)(2,1)S(1)}, bf16[384,256]{1,0:T(8,128)(2,1)S(1)}, u32[]{:S(2)}, u32[]{:S(2)}) %collective-permute-start.4) | collective-permute-done | bytes 196640 | tf_op jit(solution)/shard_map/ppermute | solution.py:19
  20.3 0.1 collective-permute-start.6
  20.4 0.6 collective-permute-start.5
  21.0 0.0 copy-start.8
  21.0 1.4 %copy-done.8 = f32[6,512,128]{2,1,0:T(8,128)S(1)} copy-done((f32[6,512,128]{2,1,0:T(8,128)S(1)}, f32[6,512,128]{2,1,0:T(8,128)}, u32[]{:S(2)}) %copy-start.8) | copy-done | bytes 1572888
  22.4 0.8 %shard_map.57 = (f32[6,512,128]{2,1,0:T(8,128)S(1)}, f32[6,512,128]{2,1,0:T(8,128)S(1)}) custom-call(s32[3]{0:T(128)S(1)} %copy-done.6, s32[3]{0:T(128)S(1)} %collective-permute-done.recv_starts_ref, bf16[6,512,128]{2,1,0:T(8,128)(2,1)S(1)} %get-tuple-element.24.refs_0_, f32[6,512,128]{2,1,0:T(8,128)S(1)} %get-tuple-element.25.refs_1_, ...), custom_call_target="tpu_custom_call" | custom-call | flops 2415919104 | bytes 8388608 | tf_op jit(solution)/shard_map/pallas_call | solution.py:243
  23.2 0.0 copy-done
  23.2 9.3 %collective-permute-done.6.refs_4_ = bf16[768,256]{1,0:T(8,128)(2,1)S(1)} collective-permute-done((bf16[768,256]{1,0:T(8,128)(2,1)S(1)}, bf16[768,256]{1,0:T(8,128)(2,1)S(1)}, u32[]{:S(2)}, u32[]{:S(2)}) %collective-permute-start.6) | collective-permute-done | bytes 393248 | tf_op jit(solution)/shard_map/ppermute | solution.py:19
  32.5 0.0 copy-start.3
  32.5 0.1 broadcast_select_fusion
  32.7 0.6 collective-permute-start.7
  33.3 0.0 collective-permute-done.5.refs_3_
  33.3 0.0 copy-done.3
  33.3 0.0 copy-start.1
  33.3 1.1 %copy-done.1 = bf16[6,512,128]{2,1,0:T(8,128)(2,1)S(1)} copy-done((bf16[6,512,128]{2,1,0:T(8,128)(2,1)S(1)}, bf16[6,512,128]{2,1,0:T(8,128)(2,1)}, u32[]{:S(2)}) %copy-start.1) | copy-done | bytes 786456
  34.4 0.0 copy-start.4
  34.4 1.0 %copy-done.4 = bf16[768,256]{1,0:T(8,128)(2,1)S(1)} copy-done((bf16[768,256]{1,0:T(8,128)(2,1)S(1)}, bf16[768,256]{1,0:T(8,128)(2,1)}, u32[]{:S(2)}) %copy-start.4) | copy-done | bytes 393240
  35.4 0.9 %shard_map.58 = (f32[6,512,128]{2,1,0:T(8,128)S(1)}, f32[6,512,128]{2,1,0:T(8,128)S(1)}) custom-call(s32[3]{0:T(128)S(1)} %copy-done.6, s32[3]{0:T(128)S(1)} %collective-permute-done.recv_starts_ref, bf16[6,512,128]{2,1,0:T(8,128)(2,1)S(1)} %copy-done.1, f32[6,512,128]{2,1,0:T(8,128)S(1)} %get-tuple-element.29.refs_1_, ...), custom_call_target="tpu_custom_call" | custom-call | flops 4831838208 | bytes 8388608 | tf_op jit(solution)/shard_map/pallas_call | solution.py:243
  36.4 5.9 %collective-permute-done.7.refs_3_ = bf16[768,256]{1,0:T(8,128)(2,1)S(1)} collective-permute-done((bf16[768,256]{1,0:T(8,128)(2,1)S(1)}, bf16[768,256]{1,0:T(8,128)(2,1)S(1)}, u32[]{:S(2)}, u32[]{:S(2)}) %collective-permute-start.7) | collective-permute-done | bytes 393248 | tf_op jit(solution)/shard_map/ppermute | solution.py:23
  42.2 3.8 %shard_map.59 = bf16[384,512]{1,0:T(8,128)(2,1)} custom-call(s32[3]{0:T(128)S(1)} %copy-done.6, s32[3]{0:T(128)S(1)} %collective-permute-done.recv_starts_ref, bf16[6,512,128]{2,1,0:T(8,128)(2,1)S(1)} %copy-done.1, f32[6,512,128]{2,1,0:T(8,128)S(1)} %get-tuple-element.31.refs_1_, f32[6,512,128]{2,1,0:T(8,128)S(1)} %get-tuple-element.32.refs_2_, ...), custom_call_target="tpu_custom_call" | custom-call | flops 1207959552 | bytes 8388608 | tf_op jit(solution)/shard_map/pallas_call | solution.py:243
  46.1 0.0 collective-permute-done.10.refs_0_
  46.1 0.0 collective-permute-start.12
  46.1 0.5 collective-permute-start.8
  46.6 0.0 copy-start.2
  46.6 1.1 %constant_dynamic-slice_fusion = bf16[512,512]{1,0:T(8,128)(2,1)S(1)} fusion(bf16[512,1536]{1,0:T(8,128)(2,1)} %collective-permute-done.10.refs_0_, s32[]{:T(128)S(6)} %select_n.66), kind=kLoop, calls=%fused_computation.7 | loop fusion | bytes 1048580 | tf_op jit(solution)/shard_map/dynamic_slice | solution.py:292
  47.7 0.1 collective-permute-start.11
  47.8 2.6 %collective-permute-done.8.refs_4_ = bf16[384,512]{1,0:T(8,128)(2,1)} collective-permute-done((bf16[384,512]{1,0:T(8,128)(2,1)}, bf16[384,512]{1,0:T(8,128)(2,1)}, u32[]{:S(2)}, u32[]{:S(2)}) %collective-permute-start.8) | collective-permute-done | bytes 393248 | tf_op jit(solution)/shard_map/ppermute | solution.py:23
  50.4 0.0 copy-done.2
  50.4 4.6 %shard_map.60 = bf16[384,1024]{1,0:T(8,128)(2,1)} custom-call(s32[3]{0:T(128)S(1)} %copy-done.6, s32[3]{0:T(128)S(1)} %collective-permute-done.recv_starts_ref, bf16[6,512,128]{2,1,0:T(8,128)(2,1)S(1)} %copy-done.2, f32[6,512,128]{2,1,0:T(8,128)S(1)} %get-tuple-element.31.refs_1_, f32[6,512,128]{2,1,0:T(8,128)S(1)} %get-tuple-element.32.refs_2_, ...), custom_call_target="tpu_custom_call" | custom-call | flops 1207959552 | bytes 8388608 | tf_op jit(solution)/shard_map/pallas_call | solution.py:243
  55.0 0.5 collective-permute-start.9
  55.5 6.2 %collective-permute-done.11.refs_1_ = bf16[512,512]{1,0:T(8,128)(2,1)} collective-permute-done((bf16[512,512]{1,0:T(8,128)(2,1)S(1)}, bf16[512,512]{1,0:T(8,128)(2,1)}, u32[]{:S(2)}, u32[]{:S(2)}) %collective-permute-start.11) | collective-permute-done | bytes 524320 | tf_op jit(solution)/shard_map/ppermute | solution.py:23
  61.7 0.0 collective-permute-start.13
  61.7 4.2 %fusion.2.given_ref = bf16[384,2048]{1,0:T(8,128)(2,1)S(1)} fusion(bf16[384,1024]{1,0:T(8,128)(2,1)} %shard_map.60, bf16[1024,4096]{1,0:T(8,128)(2,1)} %param.9, s32[]{:T(128)S(6)} %select_n.65), kind=kOutput, calls=%fused_computation.2 | convolution fusion | flops 1611399168 | bytes 6553604 | tf_op jit(solution)/shard_map/dot_general | solution.py:295
  66.0 8.8 %collective-permute-done.9.heads_ref = bf16[384,1024]{1,0:T(8,128)(2,1)S(1)} collective-permute-done((bf16[384,1024]{1,0:T(8,128)(2,1)}, bf16[384,1024]{1,0:T(8,128)(2,1)S(1)}, u32[]{:S(2)}, u32[]{:S(2)}) %collective-permute-start.9) | collective-permute-done | bytes 786464 | tf_op jit(solution)/shard_map/ppermute | solution.py:29
  74.8 0.0 collective-permute-done.13.refs_3_
  74.8 0.0 collective-permute-done.12.refs_2_
  74.8 4.6 %shard_map.61 = bf16[384,2048]{1,0:T(8,128)(2,1)} custom-call(bf16[384,2048]{1,0:T(8,128)(2,1)S(1)} %fusion.2.given_ref, bf16[384,1024]{1,0:T(8,128)(2,1)S(1)} %collective-permute-done.9.heads_ref, bf16[512,1536]{1,0:T(8,128)(2,1)} %collective-permute-done.10.refs_0_, bf16[512,512]{1,0:T(8,128)(2,1)} %collective-permute-done.11.refs_1_, ...), custom_call_target="tpu_custom_call" | custom-call | flops 1610612736 | bytes 4194304 | tf_op jit(solution)/shard_map/pallas_call | solution.py:72
  (4 shorter events, 0.1 us)
Async XLA Ops:
  0.0 2.8 %copy-start.6 = (s32[3]{0:T(128)S(1)}, s32[3]{0:T(128)}, u32[]{:S(2)}) copy-start(s32[3]{0:T(128)} %starts_ref.9) | copy-start | bytes 40
  1.0 1.8 %collective-permute-start.1 = (bf16[384,512]{1,0:T(8,128)(2,1)S(1)}, bf16[384,512]{1,0:T(8,128)(2,1)S(1)}, u32[]{:S(2)}, u32[]{:S(2)}) collective-permute-start(bf16[384,512]{1,0:T(8,128)(2,1)S(1)} %constant_dynamic-slice_fusion.5), channel_id=1, source_target_pairs={{0,2},{2,0},{4,6},{6,4},{8,10},{10,8},{12,14},{14,12},{16,18},{18,... | collective-permute-start | bytes 1179656 | tf_op jit(solution)/shard_map/ppermute | solution.py:23
  2.2 6.5 %collective-permute-start.2 = (bf16[384,256]{1,0:T(8,128)(2,1)S(1)}, bf16[384,256]{1,0:T(8,128)(2,1)S(1)}, u32[]{:S(2)}, u32[]{:S(2)}) collective-permute-start(bf16[384,256]{1,0:T(8,128)(2,1)S(1)} %pad_maximum_fusion.2), channel_id=1, source_target_pairs={{0,2},{2,0},{4,6},{6,4},{8,10},{10,8},{12,14},{14,12},{16,18},{18,... | collective-permute-start | bytes 589832 | tf_op jit(solution)/shard_map/ppermute | solution.py:23
  2.8 7.6 %collective-permute-start = (s32[3]{0:T(128)S(1)}, s32[3]{0:T(128)S(1)}, u32[]{:S(2)}, u32[]{:S(2)}) collective-permute-start(s32[3]{0:T(128)S(1)} %copy-done.6), channel_id=1, source_target_pairs={{0,2},{2,0},{4,6},{6,4},{8,10},{10,8},{12,14},{14,12},{16,18},{18,... | collective-permute-start | bytes 44 | tf_op jit(solution)/shard_map/ppermute | solution.py:23
  2.9 7.5 %copy-start.5 = (bf16[384,1024]{1,0:T(8,128)(2,1)S(1)}, bf16[384,1024]{1,0:T(8,128)(2,1)}, u32[]{:S(2)}) copy-start(bf16[384,1024]{1,0:T(8,128)(2,1)} %refs_0_.1) | copy-start | bytes 2359300
  5.6 40.5 %collective-permute-start.10 = (bf16[512,1536]{1,0:T(8,128)(2,1)}, bf16[512,1536]{1,0:T(8,128)(2,1)}, u32[]{:S(2)}, u32[]{:S(2)}) collective-permute-start(bf16[512,1536]{1,0:T(8,128)(2,1)} %dynamic_slice.25), channel_id=1, source_target_pairs={{0,1},{1,0},{2,3},{3,2},{4,5},{5,4},{6,7},{7,6},{8,9},{9,8},{10,11... | collective-permute-start | bytes 4718600 | tf_op jit(solution)/shard_map/ppermute | solution.py:29
  7.1 9.6 %collective-permute-start.3 = (bf16[384,256]{1,0:T(8,128)(2,1)S(1)}, bf16[384,256]{1,0:T(8,128)(2,1)S(1)}, u32[]{:S(2)}, u32[]{:S(2)}) collective-permute-start(bf16[384,256]{1,0:T(8,128)(2,1)S(1)} %pad_maximum_fusion.1), channel_id=1, source_target_pairs={{0,8},{2,10},{4,12},{6,14},{8,16},{10,18},{12,20},{14,22},{16,24},... | collective-permute-start | bytes 589832 | tf_op jit(solution)/shard_map/ppermute | solution.py:19
  8.8 11.5 %collective-permute-start.4 = (bf16[384,256]{1,0:T(8,128)(2,1)S(1)}, bf16[384,256]{1,0:T(8,128)(2,1)S(1)}, u32[]{:S(2)}, u32[]{:S(2)}) collective-permute-start(bf16[384,256]{1,0:T(8,128)(2,1)S(1)} %collective-permute-done.2), channel_id=1, source_target_pairs={{0,8},{2,10},{4,12},{6,14},{8,16},{10,18},{12,20},{14,22},{16,24},... | collective-permute-start | bytes 589832 | tf_op jit(solution)/shard_map/ppermute | solution.py:19
  14.2 1.1 %copy-start.7 = (f32[6,512,128]{2,1,0:T(8,128)}, f32[6,512,128]{2,1,0:T(8,128)S(1)}, u32[]{:S(2)}) copy-start(f32[6,512,128]{2,1,0:T(8,128)S(1)} %get-tuple-element.26.refs_2_) | copy-start | bytes 4718596
  15.3 7.9 %copy-start = (bf16[6,512,128]{2,1,0:T(8,128)(2,1)}, bf16[6,512,128]{2,1,0:T(8,128)(2,1)S(1)}, u32[]{:S(2)}) copy-start(bf16[6,512,128]{2,1,0:T(8,128)(2,1)S(1)} %get-tuple-element.24.refs_0_) | copy-start | bytes 2359300
  20.3 12.3 %collective-permute-start.6 = (bf16[768,256]{1,0:T(8,128)(2,1)S(1)}, bf16[768,256]{1,0:T(8,128)(2,1)S(1)}, u32[]{:S(2)}, u32[]{:S(2)}) collective-permute-start(bf16[768,256]{1,0:T(8,128)(2,1)S(1)} %shard_map.56.refs_3_), channel_id=1, source_target_pairs={{0,8},{2,10},{4,12},{6,14},{8,16},{10,18},{12,20},{14,22},{16,24},... | collective-permute-start | bytes 1179656 | tf_op jit(solution)/shard_map/ppermute | solution.py:19
  20.4 12.9 %collective-permute-start.5 = (bf16[768,256]{1,0:T(8,128)(2,1)S(1)}, bf16[768,256]{1,0:T(8,128)(2,1)S(1)}, u32[]{:S(2)}, u32[]{:S(2)}) collective-permute-start(bf16[768,256]{1,0:T(8,128)(2,1)S(1)} %shard_map.56.refs_3_), channel_id=1, source_target_pairs={{0,4},{2,6},{4,0},{6,2},{8,12},{10,14},{12,8},{14,10},{16,20},{18,... | collective-permute-start | bytes 1179656 | tf_op jit(solution)/shard_map/ppermute | solution.py:23
  21.0 1.4 %copy-start.8 = (f32[6,512,128]{2,1,0:T(8,128)S(1)}, f32[6,512,128]{2,1,0:T(8,128)}, u32[]{:S(2)}) copy-start(f32[6,512,128]{2,1,0:T(8,128)} %copy-done.7) | copy-start | bytes 4718596
  32.5 0.7 copy-start.3
  32.7 9.6 %collective-permute-start.7 = (bf16[768,256]{1,0:T(8,128)(2,1)S(1)}, bf16[768,256]{1,0:T(8,128)(2,1)S(1)}, u32[]{:S(2)}, u32[]{:S(2)}) collective-permute-start(bf16[768,256]{1,0:T(8,128)(2,1)S(1)} %broadcast_select_fusion), channel_id=1, source_target_pairs={{0,4},{2,6},{4,0},{6,2},{8,12},{10,14},{12,8},{14,10},{16,20},{18,... | collective-permute-start | bytes 1179656 | tf_op jit(solution)/shard_map/ppermute | solution.py:23
  33.3 1.1 %copy-start.1 = (bf16[6,512,128]{2,1,0:T(8,128)(2,1)S(1)}, bf16[6,512,128]{2,1,0:T(8,128)(2,1)}, u32[]{:S(2)}) copy-start(bf16[6,512,128]{2,1,0:T(8,128)(2,1)} %copy-done) | copy-start | bytes 2359300
  34.4 1.0 %copy-start.4 = (bf16[768,256]{1,0:T(8,128)(2,1)S(1)}, bf16[768,256]{1,0:T(8,128)(2,1)}, u32[]{:S(2)}) copy-start(bf16[768,256]{1,0:T(8,128)(2,1)} %copy-done.3) | copy-start | bytes 1179652
  46.1 28.7 %collective-permute-start.12 = (bf16[512,1536]{1,0:T(8,128)(2,1)}, bf16[512,1536]{1,0:T(8,128)(2,1)}, u32[]{:S(2)}, u32[]{:S(2)}) collective-permute-start(bf16[512,1536]{1,0:T(8,128)(2,1)} %collective-permute-done.10.refs_0_), channel_id=1, source_target_pairs={{0,2},{2,0},{4,6},{6,4},{8,10},{10,8},{12,14},{14,12},{16,18},{18,... | collective-permute-start | bytes 4718600 | tf_op jit(solution)/shard_map/ppermute | solution.py:23
  46.1 4.3 %collective-permute-start.8 = (bf16[384,512]{1,0:T(8,128)(2,1)}, bf16[384,512]{1,0:T(8,128)(2,1)}, u32[]{:S(2)}, u32[]{:S(2)}) collective-permute-start(bf16[384,512]{1,0:T(8,128)(2,1)} %shard_map.59), channel_id=1, source_target_pairs={{0,2},{2,0},{4,6},{6,4},{8,10},{10,8},{12,14},{14,12},{16,18},{18,... | collective-permute-start | bytes 1179656 | tf_op jit(solution)/shard_map/ppermute | solution.py:23
  46.6 3.8 %copy-start.2 = (bf16[6,512,128]{2,1,0:T(8,128)(2,1)S(1)}, bf16[6,512,128]{2,1,0:T(8,128)(2,1)}, u32[]{:S(2)}) copy-start(bf16[6,512,128]{2,1,0:T(8,128)(2,1)} %copy-done) | copy-start | bytes 2359300
  47.7 14.0 %collective-permute-start.11 = (bf16[512,512]{1,0:T(8,128)(2,1)S(1)}, bf16[512,512]{1,0:T(8,128)(2,1)}, u32[]{:S(2)}, u32[]{:S(2)}) collective-permute-start(bf16[512,512]{1,0:T(8,128)(2,1)S(1)} %constant_dynamic-slice_fusion), channel_id=1, source_target_pairs={{0,8},{2,10},{4,12},{6,14},{8,0},{10,2},{12,4},{14,6},{16,24},{18,... | collective-permute-start | bytes 1572872 | tf_op jit(solution)/shard_map/ppermute | solution.py:23
  55.0 19.8 %collective-permute-start.9 = (bf16[384,1024]{1,0:T(8,128)(2,1)}, bf16[384,1024]{1,0:T(8,128)(2,1)S(1)}, u32[]{:S(2)}, u32[]{:S(2)}) collective-permute-start(bf16[384,1024]{1,0:T(8,128)(2,1)} %shard_map.60), channel_id=1, source_target_pairs={{0,1},{1,0},{2,3},{3,2},{4,5},{5,4},{6,7},{7,6},{8,9},{9,8},{10,11... | collective-permute-start | bytes 2359304 | tf_op jit(solution)/shard_map/ppermute | solution.py:29
  61.7 13.1 %collective-permute-start.13 = (bf16[512,512]{1,0:T(8,128)(2,1)}, bf16[512,512]{1,0:T(8,128)(2,1)S(1)}, u32[]{:S(2)}, u32[]{:S(2)}) collective-permute-start(bf16[512,512]{1,0:T(8,128)(2,1)} %collective-permute-done.11.refs_1_), channel_id=1, source_target_pairs={{0,2},{2,0},{4,6},{6,4},{8,10},{10,8},{12,14},{14,12},{16,18},{18,... | collective-permute-start | bytes 1572872 | tf_op jit(solution)/shard_map/ppermute | solution.py:23

commit v8 on v7

--- a/solution.py
+++ b/solution.py
@@ -29,21 +29,44 @@
     return lax.ppermute(x, ("ctx", "head"), route)
 
 
+def small_call(kernel, shapes, operands):
+    vmem = pl.BlockSpec(memory_space=pltpu.VMEM)
+    return pl.pallas_call(
+        kernel,
+        out_shape=[jax.ShapeDtypeStruct(shape, operands[0].dtype) for shape in shapes],
+        in_specs=[vmem] * len(operands),
+        out_specs=[vmem] * len(shapes),
+        compiler_params=pltpu.CompilerParams(vmem_limit_bytes=6 * 2**20),
+        cost_estimate=pl.CostEstimate(flops=2**20, bytes_accessed=2**20, transcendentals=0),
+    )(*operands)
+
+
+def prepare_kernel(keys_ref, values_ref, queries_ref, mine_ref, theirs_ref, queries_out):
+    core = lax.axis_index("ctx") % 2
+    for out, index in ((mine_ref, core), (theirs_ref, 1 - core)):
+        lanes = pl.ds(pl.multiple_of(index * HEAD_SIZE, HEAD_SIZE), HEAD_SIZE)
+        out[:, :HEAD_SIZE] = keys_ref[:, lanes]
+        out[:, HEAD_SIZE:] = values_ref[:, lanes]
+    group = queries_out.shape[1]
+    queries_out[...] = queries_ref[:, pl.ds(pl.multiple_of((1 - core) * group, group), group)]
+
+
 def join_kernel(first_ref, second_ref, out_ref):
     tok = first_ref.shape[0]
     out_ref[:tok] = first_ref[...]
     out_ref[tok:] = second_ref[...]
 
 
-def join(first, second):
-    vmem = pl.BlockSpec(memory_space=pltpu.VMEM)
-    return pl.pallas_call(
-        join_kernel,
-        out_shape=jax.ShapeDtypeStruct((2 * first.shape[0], first.shape[1]), first.dtype),
-        in_specs=[vmem, vmem],
-        out_specs=vmem,
-        compiler_params=pltpu.CompilerParams(vmem_limit_bytes=4 * 2**20),
-    )(first, second)
+def pick_kernel(even_ref, odd_ref, out_ref):
+    odd = lax.axis_index("ctx") // 2 % 2 == 1
+
+    @pl.when(odd)
+    def _():
+        out_ref[...] = odd_ref[...]
+
+    @pl.when(jnp.logical_not(odd))
+    def _():
+        out_ref[...] = even_ref[...]
 
 
 def project_kernel(given_ref, heads_ref, *refs):
@@ -248,7 +271,7 @@
         scratch_shapes=scratch,
         compiler_params=pltpu.CompilerParams(vmem_limit_bytes=24 * 2**20),
         cost_estimate=pl.CostEstimate(
-            flops=int(share * blocks * rows * 2 * tok * HEAD_SIZE * 8),
+            flops=int(share * blocks * rows * 2 * tok * HEAD_SIZE * 14),
             bytes_accessed=8 * 2**20,
             transcendentals=int(share * blocks * rows * 2 * tok),
         ),
@@ -256,43 +279,44 @@
 
 
 def per_device(queries, keys, values, block_start, out_weight):
-    group = queries.shape[1] // 2
-    me = lax.axis_index("ctx")
-    core, col = me % 2, (me // 2) % 2
-    head = lax.axis_index("head")
-
-    def part(x, index, size):
-        return lax.dynamic_slice_in_dim(x, index * size, size, 1)
-
+    tok, group = queries.shape[0], queries.shape[1] // 2
+    me, head = lax.axis_index("ctx"), lax.axis_index("head")
     cols = out_weight.shape[1] // 2
-    mine = jnp.concatenate([part(keys, core, HEAD_SIZE), part(values, core, HEAD_SIZE)], 1)
-    theirs = jnp.concatenate([part(keys, 1 - core, HEAD_SIZE), part(values, 1 - core, HEAD_SIZE)], 1)
+    tile, quarter = cols // 4, me // 4 % 2
+    places = (me % 2 * group, ((1 - head) * 4 + quarter) * tile, 2 * quarter * tile, head * cols)
+    keys, places = lax.optimization_barrier((keys, places))
+    first_row, first_col, spare_col, here_col = places
+
+    mine, theirs, q_send = small_call(
+        prepare_kernel,
+        [(tok, 2 * HEAD_SIZE)] * 2 + [(tok, group)],
+        (keys, values, queries),
+    )
     recv = swap(theirs, 1)
     one_behind = [rotate(mine, 4), rotate(recv, 4)]
-    q_recv = swap(part(queries, 1 - core, group), 1)
+    q_recv = swap(q_send, 1)
     recv_starts = swap(block_start, 1)
-    own = jnp.concatenate([mine, recv])
+    (own,) = small_call(join_kernel, [(2 * tok, 2 * HEAD_SIZE)], (mine, recv))
     starts = (block_start, recv_starts)
-    tile, quarter = cols // 4, me // 4 % 2
     q_recv, weight = lax.optimization_barrier((q_recv, out_weight))
-    first_col = ((1 - head) * 4 + quarter) * tile
-    sent = lax.dynamic_slice(weight, (core * group, first_col), (group, 3 * tile))
+    sent = lax.dynamic_slice(weight, (first_row, first_col), (group, 3 * tile))
     q_recv, sent = lax.optimization_barrier((q_recv, sent))
     fetched = cross(sent, 0)
     q, *state = attention_call("first", ((0, 0),), *starts, (queries, q_recv, own))
     q, one_behind = lax.optimization_barrier((q, one_behind))
-    one_behind = join(*one_behind)
+    (one_behind,) = small_call(join_kernel, [own.shape], one_behind)
     two_behind = rotate(one_behind, 4)
     across = swap(one_behind, 2)
-    third = swap(jnp.where(col == 1, two_behind, own), 2)
+    third = swap(small_call(pick_kernel, [own.shape], (own, two_behind))[0], 2)
     state = attention_call("next", ((2, 2),), *starts, (q, *state, one_behind))
     state = attention_call("next", ((1, 3), (4, 4)), *starts, (q, *state, across, two_behind))
     (o_other,) = attention_call("other", ((3, 1),), *starts, (q, *state, third))
     _, fetched = lax.optimization_barrier((o_other, fetched))
-    weights = [fetched, swap(lax.dynamic_slice_in_dim(fetched, 2 * tile * quarter, tile, 1), 4)]
+    weights = [fetched, swap(lax.dynamic_slice_in_dim(fetched, spare_col, tile, 1), 4)]
     (heads,) = attention_call("own", ((3, 1),), *starts, (q, *state, third, swap(o_other, 1)))
     heads_across = cross(heads, 0)
-    here = jnp.dot(heads, part(out_weight, head, cols), preferred_element_type=jnp.float32)
+    rows_here = lax.dynamic_slice_in_dim(out_weight, here_col, cols, 1)
+    here = jnp.dot(heads, rows_here, preferred_element_type=jnp.float32)
     weights += [swap(x, 1) for x in weights]
     return project(here.astype(jnp.bfloat16), heads_across, weights)
 

time: 80 us -> 82.7 us (1.034)
  starting transfers between devices: 7.77 us -> 10.4 us
  waiting for transfers between devices: 37.7 us -> 39.3 us
  local copies, waits for them, and re-layouts: 10.7 us -> 9.68 us
    ppermute x2, waiting for transfers between devices: 8.84 us -> 15.1 us  [cross(): return lax.ppermute(x, ('ctx', 'head'), route)]
    ppermute x9, waiting for transfers between devices: 14.6 us -> 10.8 us  [swap(): lax.ppermute(x, 'ctx', [(i, i ^ mask) for i in range(lax.axis_size('ctx'))])]
    dynamic_slice x4 -> x2, local copies, waits for them, and re-layouts: 5.97 us -> 2.72 us  [the longest x1 2.45 us: per_device(): sent = lax.dynamic_slice(weight, (first_row, first_col), (group, 3 * tile))]
    unnamed x18 -> x22, local copies, waits for them, and re-layouts: 4.71 us -> 6.96 us
    ppermute x9, starting transfers between devices: 2.48 us -> 4.09 us  [swap(): lax.ppermute(x, 'ctx', [(i, i ^ mask) for i in range(lax.axis_size('ctx'))])]
    ppermute x2, starting transfers between devices: 2.03 us -> 3.12 us  [cross(): return lax.ppermute(x, ('ctx', 'head'), route)]
    ppermute x3, waiting for transfers between devices: 14.2 us -> 13.3 us  [rotate(): return lax.ppermute(x, 'ctx', [(i, (i + distance) % n) for i in range(n)])]
  transfers between devices with their start and end apart: 14 -> 14, of which waited for: 7 -> 7; matrix products, arithmetic and copies ran while one was open for 12% -> 9% of each run, Pallas kernels for 18% -> 17%
where the time goes in v8:
time: 82.7 us; the launch traced here: 82.2 us
  waiting for transfers between devices  39.3 us (48%)
  Pallas kernels  18 us (22%)
  starting transfers between devices  10.4 us (13%)
  local copies, waits for them, and re-layouts  9.68 us (12%)
  matrix products  4.55 us (6%)
    ppermute x2, waiting for transfers between devices, cross(): return lax.ppermute(x, ('ctx', 'head'), route)  15.1 us
    pallas_call x5, Pallas kernels, attention_call(): pl.pallas_call(functools.partial(attention_kernel, stage, distances, n_he...  13.8 us
    ppermute x3, waiting for transfers between devices, rotate(): return lax.ppermute(x, 'ctx', [(i, (i + distance) % n) for i in range(n)])  13.3 us
    ppermute x9, waiting for transfers between devices, swap(): lax.ppermute(x, 'ctx', [(i, i ^ mask) for i in range(lax.axis_size('ctx'))])  10.8 us
    unnamed x22, local copies, waits for them, and re-layouts  6.96 us
    dot_general x1, matrix products, per_device(): here = jnp.dot(heads, rows_here, preferred_element_type=jnp.float32)  4.55 us
    ppermute x9, starting transfers between devices, swap(): lax.ppermute(x, 'ctx', [(i, i ^ mask) for i in range(lax.axis_size('ctx'))])  4.09 us
    pallas_call x1, Pallas kernels, project(): pl.pallas_call(project_kernel, out_shape=jax.ShapeDtypeStruct(given.shape...  4.05 us
  transfers between devices with their start and end apart: 14, of which 7 were waited for; matrix products, arithmetic and copies ran while one was open for 9% of the time, Pallas kernels for 17%

profile of v8, /device:TPU:2, one launch (start us, length us, event | category | flops | bytes accessed | tf_op | source)
XLA Modules:
  0.0 82.2 jit_solution(10650350709524654259)
XLA Ops:
  0.0 0.0 copy-start
  0.0 1.1 %copy-done = bf16[384,1024]{1,0:T(8,128)(2,1)S(1)} copy-done((bf16[384,1024]{1,0:T(8,128)(2,1)S(1)}, bf16[384,1024]{1,0:T(8,128)(2,1)}, u32[]{:S(2)}) %copy-start) | copy-done | bytes 786456
  1.1 0.0 copy-start.2
  1.1 0.9 %copy-done.2 = bf16[384,256]{1,0:T(8,128)(2,1)S(1)} copy-done((bf16[384,256]{1,0:T(8,128)(2,1)S(1)}, bf16[384,256]{1,0:T(8,128)(2,1)}, u32[]{:S(2)}) %copy-start.2) | copy-done | bytes 196632
  2.1 0.0 copy-start.3
  2.1 0.9 %copy-done.3 = bf16[384,256]{1,0:T(8,128)(2,1)S(1)} copy-done((bf16[384,256]{1,0:T(8,128)(2,1)S(1)}, bf16[384,256]{1,0:T(8,128)(2,1)}, u32[]{:S(2)}) %copy-start.3) | copy-done | bytes 196632
  3.0 0.1 shard_map.55
  3.1 0.1 collective-permute-start.1
  3.2 0.5 collective-permute-start.2
  3.7 0.1 collective-permute-start
  3.7 1.6 %collective-permute-start.3 = (bf16[384,256]{1,0:T(8,128)(2,1)S(1)}, bf16[384,256]{1,0:T(8,128)(2,1)S(1)}, u32[]{:S(2)}, u32[]{:S(2)}) collective-permute-start(bf16[384,256]{1,0:T(8,128)(2,1)S(1)} %get-tuple-element.35.first_ref), channel_id=1, source_target_pairs={{0,8},{2,10},{4,12},{6,14},{8,16},{10,18},{12,20},{14,22},{16,24},... | collective-permute-start | bytes 589832 | tf_op jit(solution)/shard_map/ppermute | solution.py:19
  5.3 0.0 collective-permute-done.2.second_ref
  5.3 1.6 %collective-permute-start.4 = (bf16[384,256]{1,0:T(8,128)(2,1)S(1)}, bf16[384,256]{1,0:T(8,128)(2,1)S(1)}, u32[]{:S(2)}, u32[]{:S(2)}) collective-permute-start(bf16[384,256]{1,0:T(8,128)(2,1)S(1)} %collective-permute-done.2.second_ref), channel_id=1, source_target_pairs={{0,8},{2,10},{4,12},{6,14},{8,16},{10,18},{12,20},{14,22},{16,24},... | collective-permute-start | bytes 589832 | tf_op jit(solution)/shard_map/ppermute | solution.py:19
  6.9 0.0 copy-start.1
  6.9 0.0 copy-start.4
  7.0 0.0 collective-permute-done.1.refs_1_
  7.0 2.4 %dynamic_slice.9 = bf16[512,1536]{1,0:T(8,128)(2,1)S(1)} dynamic-slice(bf16[1024,4096]{1,0:T(8,128)(2,1)} %param.9, s32[]{:T(128)S(6)} %select_n.30, s32[]{:T(128)S(6)} %select_n.31), dynamic_slice_sizes={512,1536} | dynamic-slice | bytes 3145732 | tf_op jit(solution)/shard_map/dynamic_slice | solution.py:302
  9.4 1.6 %collective-permute-start.10 = (bf16[512,1536]{1,0:T(8,128)(2,1)S(1)}, bf16[512,1536]{1,0:T(8,128)(2,1)S(1)}, u32[]{:S(2)}, u32[]{:S(2)}) collective-permute-start(bf16[512,1536]{1,0:T(8,128)(2,1)S(1)} %dynamic_slice.9), channel_id=1, source_target_pairs={{0,1},{1,0},{2,3},{3,2},{4,5},{5,4},{6,7},{7,6},{8,9},{9,8},{10,11... | collective-permute-start | bytes 4718600 | tf_op jit(solution)/shard_map/ppermute | solution.py:29
  11.0 0.0 collective-permute-done.recv_starts_ref
  11.0 0.0 copy-done.1
  11.0 0.0 copy-done.4
  11.0 3.7 %shard_map.57 = (bf16[6,512,128]{2,1,0:T(8,128)(2,1)S(1)}, f32[6,512,128]{2,1,0:T(8,128)S(1)}, f32[6,512,128]{2,1,0:T(8,128)S(1)}) custom-call(s32[3]{0:T(128)S(1)} %copy-done.4, s32[3]{0:T(128)S(1)} %collective-permute-done.recv_starts_ref, bf16[384,1024]{1,0:T(8,128)(2,1)S(1)} %copy-done.1, bf16[384,512]{1,0:T(8,128)(2,1)S(1)} %collective-permute-done.1.refs_1_, ...), custom_call_target="tpu_custom_call" | custom-call | flops 2536715008 | bytes 8388608 | tf_op jit(solution)/shard_map/pallas_call | solution.py:266
  14.7 0.0 copy-start.9
  14.8 0.0 collective-permute-done.3.first_ref
  14.8 2.3 %collective-permute-done.4.second_ref = bf16[384,256]{1,0:T(8,128)(2,1)S(1)} collective-permute-done((bf16[384,256]{1,0:T(8,128)(2,1)S(1)}, bf16[384,256]{1,0:T(8,128)(2,1)S(1)}, u32[]{:S(2)}, u32[]{:S(2)}) %collective-permute-start.4) | collective-permute-done | bytes 196640 | tf_op jit(solution)/shard_map/ppermute | solution.py:19
  17.1 0.1 collective-permute-start.6
  17.1 0.6 collective-permute-start.5
  17.7 0.8 %shard_map.59 = (f32[6,512,128]{2,1,0:T(8,128)S(1)}, f32[6,512,128]{2,1,0:T(8,128)S(1)}) custom-call(s32[3]{0:T(128)S(1)} %copy-done.4, s32[3]{0:T(128)S(1)} %collective-permute-done.recv_starts_ref, bf16[6,512,128]{2,1,0:T(8,128)(2,1)S(1)} %get-tuple-element.38.refs_0_, f32[6,512,128]{2,1,0:T(8,128)S(1)} %get-tuple-element.39.refs_1_, ...), custom_call_target="tpu_custom_call" | custom-call | flops 4227858432 | bytes 8388608 | tf_op jit(solution)/shard_map/pallas_call | solution.py:266
  18.6 11.1 %collective-permute-done.6.refs_4_.odd_ref = bf16[768,256]{1,0:T(8,128)(2,1)S(1)} collective-permute-done((bf16[768,256]{1,0:T(8,128)(2,1)S(1)}, bf16[768,256]{1,0:T(8,128)(2,1)S(1)}, u32[]{:S(2)}, u32[]{:S(2)}) %collective-permute-start.6) | collective-permute-done | bytes 393248 | tf_op jit(solution)/shard_map/ppermute | solution.py:19
  29.7 0.7 collective-permute-start.7
  30.4 0.0 collective-permute-done.5.refs_3_
  30.4 0.9 %shard_map.60 = (f32[6,512,128]{2,1,0:T(8,128)S(1)}, f32[6,512,128]{2,1,0:T(8,128)S(1)}) custom-call(s32[3]{0:T(128)S(1)} %copy-done.4, s32[3]{0:T(128)S(1)} %collective-permute-done.recv_starts_ref, bf16[6,512,128]{2,1,0:T(8,128)(2,1)S(1)} %get-tuple-element.38.refs_0_, f32[6,512,128]{2,1,0:T(8,128)S(1)} %get-tuple-element.43.refs_1_, ...), custom_call_target="tpu_custom_call" | custom-call | flops 8455716864 | bytes 8388608 | tf_op jit(solution)/shard_map/pallas_call | solution.py:266
  31.4 0.0 copy-start.5
  31.4 0.0 copy-start.7
  31.4 8.2 %collective-permute-done.7.refs_3_ = bf16[768,256]{1,0:T(8,128)(2,1)S(1)} collective-permute-done((bf16[768,256]{1,0:T(8,128)(2,1)S(1)}, bf16[768,256]{1,0:T(8,128)(2,1)S(1)}, u32[]{:S(2)}, u32[]{:S(2)}) %collective-permute-start.7) | collective-permute-done | bytes 393248 | tf_op jit(solution)/shard_map/ppermute | solution.py:23
  39.6 0.0 copy-done.9
  39.6 3.9 %shard_map.62 = bf16[384,512]{1,0:T(8,128)(2,1)} custom-call(s32[3]{0:T(128)S(1)} %copy-done.4, s32[3]{0:T(128)S(1)} %collective-permute-done.recv_starts_ref, bf16[6,512,128]{2,1,0:T(8,128)(2,1)S(1)} %get-tuple-element.38.refs_0_, f32[6,512,128]{2,1,0:T(8,128)S(1)} %get-tuple-element.45.refs_1_, f32[6,512,128]{2,1,0:T(8,128)S(1)} %get-tuple-element.46.refs_2_, ...), custom_call_target="tpu_custom_call" | custom-call | flops 2113929216 | bytes 8388608 | tf_op jit(solution)/shard_map/pallas_call | solution.py:266
  43.5 0.0 copy-done.5
  43.5 0.0 copy-done.7
  43.5 2.1 %collective-permute-done.10.refs_0_ = bf16[512,1536]{1,0:T(8,128)(2,1)S(1)} collective-permute-done((bf16[512,1536]{1,0:T(8,128)(2,1)S(1)}, bf16[512,1536]{1,0:T(8,128)(2,1)S(1)}, u32[]{:S(2)}, u32[]{:S(2)}) %collective-permute-start.10) | collective-permute-done | bytes 1572896 | tf_op jit(solution)/shard_map/ppermute | solution.py:29
  45.7 0.0 collective-permute-start.12
  45.7 0.5 collective-permute-start.8
  46.2 0.3 constant_dynamic-slice_fusion
  46.4 1.6 %collective-permute-start.11 = (bf16[512,512]{1,0:T(8,128)(2,1)S(1)}, bf16[512,512]{1,0:T(8,128)(2,1)}, u32[]{:S(2)}, u32[]{:S(2)}) collective-permute-start(bf16[512,512]{1,0:T(8,128)(2,1)S(1)} %constant_dynamic-slice_fusion), channel_id=1, source_target_pairs={{0,8},{2,10},{4,12},{6,14},{8,0},{10,2},{12,4},{14,6},{16,24},{18,... | collective-permute-start | bytes 1572872 | tf_op jit(solution)/shard_map/ppermute | solution.py:23
  48.0 1.6 %collective-permute-done.8.refs_4_ = bf16[384,512]{1,0:T(8,128)(2,1)} collective-permute-done((bf16[384,512]{1,0:T(8,128)(2,1)}, bf16[384,512]{1,0:T(8,128)(2,1)}, u32[]{:S(2)}, u32[]{:S(2)}) %collective-permute-start.8) | collective-permute-done | bytes 393248 | tf_op jit(solution)/shard_map/ppermute | solution.py:23
  49.6 0.0 copy-start.6
  49.6 1.4 %copy-done.6 = f32[6,512,128]{2,1,0:T(8,128)S(1)} copy-done((f32[6,512,128]{2,1,0:T(8,128)S(1)}, f32[6,512,128]{2,1,0:T(8,128)}, u32[]{:S(2)}) %copy-start.6) | copy-done | bytes 1572888
  51.0 0.0 copy-start.8
  51.0 1.4 %copy-done.8 = f32[6,512,128]{2,1,0:T(8,128)S(1)} copy-done((f32[6,512,128]{2,1,0:T(8,128)S(1)}, f32[6,512,128]{2,1,0:T(8,128)}, u32[]{:S(2)}) %copy-start.8) | copy-done | bytes 1572888
  52.4 0.0 copy-start.10
  52.4 1.1 %copy-done.10 = bf16[6,512,128]{2,1,0:T(8,128)(2,1)S(1)} copy-done((bf16[6,512,128]{2,1,0:T(8,128)(2,1)S(1)}, bf16[6,512,128]{2,1,0:T(8,128)(2,1)}, u32[]{:S(2)}) %copy-start.10) | copy-done | bytes 786456
  53.6 4.3 %shard_map.63 = bf16[384,1024]{1,0:T(8,128)(2,1)} custom-call(s32[3]{0:T(128)S(1)} %copy-done.4, s32[3]{0:T(128)S(1)} %collective-permute-done.recv_starts_ref, bf16[6,512,128]{2,1,0:T(8,128)(2,1)S(1)} %copy-done.10, f32[6,512,128]{2,1,0:T(8,128)S(1)} %copy-done.6, f32[6,512,128]{2,1,0:T(8,128)S(1)} %copy-done.8, ...), custom_call_target="tpu_custom_call" | custom-call | flops 2113929216 | bytes 8388608 | tf_op jit(solution)/shard_map/pallas_call | solution.py:266
  57.9 1.5 %collective-permute-start.9 = (bf16[384,1024]{1,0:T(8,128)(2,1)}, bf16[384,1024]{1,0:T(8,128)(2,1)}, u32[]{:S(2)}, u32[]{:S(2)}) collective-permute-start(bf16[384,1024]{1,0:T(8,128)(2,1)} %shard_map.63), channel_id=1, source_target_pairs={{0,1},{1,0},{2,3},{3,2},{4,5},{5,4},{6,7},{7,6},{8,9},{9,8},{10,11... | collective-permute-start | bytes 2359304 | tf_op jit(solution)/shard_map/ppermute | solution.py:29
  59.4 1.0 %collective-permute-done.11.refs_1_ = bf16[512,512]{1,0:T(8,128)(2,1)} collective-permute-done((bf16[512,512]{1,0:T(8,128)(2,1)S(1)}, bf16[512,512]{1,0:T(8,128)(2,1)}, u32[]{:S(2)}, u32[]{:S(2)}) %collective-permute-start.11) | collective-permute-done | bytes 524320 | tf_op jit(solution)/shard_map/ppermute | solution.py:23
  60.5 0.0 collective-permute-start.13
  60.5 4.5 %fusion.2.given_ref = bf16[384,2048]{1,0:T(8,128)(2,1)S(1)} fusion(bf16[384,1024]{1,0:T(8,128)(2,1)} %shard_map.63, bf16[1024,4096]{1,0:T(8,128)(2,1)} %param.9, s32[]{:T(128)S(6)} %select_n.32), kind=kOutput, calls=%fused_computation.2 | convolution fusion | flops 1611399168 | bytes 6553604 | tf_op jit(solution)/shard_map/dot_general | solution.py:319
  65.0 13.0 %collective-permute-done.9.heads_ref = bf16[384,1024]{1,0:T(8,128)(2,1)} collective-permute-done((bf16[384,1024]{1,0:T(8,128)(2,1)}, bf16[384,1024]{1,0:T(8,128)(2,1)}, u32[]{:S(2)}, u32[]{:S(2)}) %collective-permute-start.9) | collective-permute-done | bytes 786464 | tf_op jit(solution)/shard_map/ppermute | solution.py:29
  78.0 0.0 collective-permute-done.13.refs_3_
  78.0 0.0 collective-permute-done.12.refs_2_
  78.0 4.0 %shard_map.64 = bf16[384,2048]{1,0:T(8,128)(2,1)} custom-call(bf16[384,2048]{1,0:T(8,128)(2,1)S(1)} %fusion.2.given_ref, bf16[384,1024]{1,0:T(8,128)(2,1)} %collective-permute-done.9.heads_ref, bf16[512,1536]{1,0:T(8,128)(2,1)S(1)} %collective-permute-done.10.refs_0_, bf16[512,512]{1,0:T(8,128)(2,1)} %collective-permute-done.11.refs_1_, ...), custom_call_target="tpu_custom_call" | custom-call | flops 1610612736 | bytes 4194304 | tf_op jit(solution)/shard_map/pallas_call | solution.py:95
  (3 shorter events, 0.1 us)
Async XLA Ops:
  0.0 1.1 %copy-start = (bf16[384,1024]{1,0:T(8,128)(2,1)S(1)}, bf16[384,1024]{1,0:T(8,128)(2,1)}, u32[]{:S(2)}) copy-start(bf16[384,1024]{1,0:T(8,128)(2,1)} %refs_0_.1) | copy-start | bytes 2359300
  1.1 0.9 %copy-start.2 = (bf16[384,256]{1,0:T(8,128)(2,1)S(1)}, bf16[384,256]{1,0:T(8,128)(2,1)}, u32[]{:S(2)}) copy-start(bf16[384,256]{1,0:T(8,128)(2,1)} %keys_ref) | copy-start | bytes 589828
  2.1 0.9 %copy-start.3 = (bf16[384,256]{1,0:T(8,128)(2,1)S(1)}, bf16[384,256]{1,0:T(8,128)(2,1)}, u32[]{:S(2)}) copy-start(bf16[384,256]{1,0:T(8,128)(2,1)} %values_ref.1) | copy-start | bytes 589828
  3.1 3.9 %collective-permute-start.1 = (bf16[384,512]{1,0:T(8,128)(2,1)S(1)}, bf16[384,512]{1,0:T(8,128)(2,1)S(1)}, u32[]{:S(2)}, u32[]{:S(2)}) collective-permute-start(bf16[384,512]{1,0:T(8,128)(2,1)S(1)} %get-tuple-element.29), channel_id=1, source_target_pairs={{0,2},{2,0},{4,6},{6,4},{8,10},{10,8},{12,14},{14,12},{16,18},{18,... | collective-permute-start | bytes 1179656 | tf_op jit(solution)/shard_map/ppermute | solution.py:23
  3.2 2.2 %collective-permute-start.2 = (bf16[384,256]{1,0:T(8,128)(2,1)S(1)}, bf16[384,256]{1,0:T(8,128)(2,1)S(1)}, u32[]{:S(2)}, u32[]{:S(2)}) collective-permute-start(bf16[384,256]{1,0:T(8,128)(2,1)S(1)} %get-tuple-element.36), channel_id=1, source_target_pairs={{0,2},{2,0},{4,6},{6,4},{8,10},{10,8},{12,14},{14,12},{16,18},{18,... | collective-permute-start | bytes 589832 | tf_op jit(solution)/shard_map/ppermute | solution.py:23
  3.7 7.3 %collective-permute-start = (s32[3]{0:T(128)}, s32[3]{0:T(128)S(1)}, u32[]{:S(2)}, u32[]{:S(2)}) collective-permute-start(s32[3]{0:T(128)} %starts_ref.9), channel_id=1, source_target_pairs={{0,2},{2,0},{4,6},{6,4},{8,10},{10,8},{12,14},{14,12},{16,18},{18,... | collective-permute-start | bytes 44 | tf_op jit(solution)/shard_map/ppermute | solution.py:23
  3.7 11.0 %collective-permute-start.3 = (bf16[384,256]{1,0:T(8,128)(2,1)S(1)}, bf16[384,256]{1,0:T(8,128)(2,1)S(1)}, u32[]{:S(2)}, u32[]{:S(2)}) collective-permute-start(bf16[384,256]{1,0:T(8,128)(2,1)S(1)} %get-tuple-element.35.first_ref), channel_id=1, source_target_pairs={{0,8},{2,10},{4,12},{6,14},{8,16},{10,18},{12,20},{14,22},{16,24},... | collective-permute-start | bytes 589832 | tf_op jit(solution)/shard_map/ppermute | solution.py:19
  5.3 11.7 %collective-permute-start.4 = (bf16[384,256]{1,0:T(8,128)(2,1)S(1)}, bf16[384,256]{1,0:T(8,128)(2,1)S(1)}, u32[]{:S(2)}, u32[]{:S(2)}) collective-permute-start(bf16[384,256]{1,0:T(8,128)(2,1)S(1)} %collective-permute-done.2.second_ref), channel_id=1, source_target_pairs={{0,8},{2,10},{4,12},{6,14},{8,16},{10,18},{12,20},{14,22},{16,24},... | collective-permute-start | bytes 589832 | tf_op jit(solution)/shard_map/ppermute | solution.py:19
  6.9 4.1 %copy-start.1 = (bf16[384,1024]{1,0:T(8,128)(2,1)S(1)}, bf16[384,1024]{1,0:T(8,128)(2,1)}, u32[]{:S(2)}) copy-start(bf16[384,1024]{1,0:T(8,128)(2,1)} %refs_0_.1) | copy-start | bytes 2359300
  6.9 4.1 %copy-start.4 = (s32[3]{0:T(128)S(1)}, s32[3]{0:T(128)}, u32[]{:S(2)}) copy-start(s32[3]{0:T(128)} %starts_ref.9) | copy-start | bytes 40
  9.4 36.2 %collective-permute-start.10 = (bf16[512,1536]{1,0:T(8,128)(2,1)S(1)}, bf16[512,1536]{1,0:T(8,128)(2,1)S(1)}, u32[]{:S(2)}, u32[]{:S(2)}) collective-permute-start(bf16[512,1536]{1,0:T(8,128)(2,1)S(1)} %dynamic_slice.9), channel_id=1, source_target_pairs={{0,1},{1,0},{2,3},{3,2},{4,5},{5,4},{6,7},{7,6},{8,9},{9,8},{10,11... | collective-permute-start | bytes 4718600 | tf_op jit(solution)/shard_map/ppermute | solution.py:29
  14.7 24.9 %copy-start.9 = (bf16[6,512,128]{2,1,0:T(8,128)(2,1)}, bf16[6,512,128]{2,1,0:T(8,128)(2,1)S(1)}, u32[]{:S(2)}) copy-start(bf16[6,512,128]{2,1,0:T(8,128)(2,1)S(1)} %get-tuple-element.38.refs_0_) | copy-start | bytes 2359300
  17.1 12.6 %collective-permute-start.6 = (bf16[768,256]{1,0:T(8,128)(2,1)S(1)}, bf16[768,256]{1,0:T(8,128)(2,1)S(1)}, u32[]{:S(2)}, u32[]{:S(2)}) collective-permute-start(bf16[768,256]{1,0:T(8,128)(2,1)S(1)} %shard_map.58.refs_3_), channel_id=1, source_target_pairs={{0,8},{2,10},{4,12},{6,14},{8,16},{10,18},{12,20},{14,22},{16,24},... | collective-permute-start | bytes 1179656 | tf_op jit(solution)/shard_map/ppermute | solution.py:19
  17.1 13.3 %collective-permute-start.5 = (bf16[768,256]{1,0:T(8,128)(2,1)S(1)}, bf16[768,256]{1,0:T(8,128)(2,1)S(1)}, u32[]{:S(2)}, u32[]{:S(2)}) collective-permute-start(bf16[768,256]{1,0:T(8,128)(2,1)S(1)} %shard_map.58.refs_3_), channel_id=1, source_target_pairs={{0,4},{2,6},{4,0},{6,2},{8,12},{10,14},{12,8},{14,10},{16,20},{18,... | collective-permute-start | bytes 1179656 | tf_op jit(solution)/shard_map/ppermute | solution.py:23
  29.7 9.9 %collective-permute-start.7 = (bf16[768,256]{1,0:T(8,128)(2,1)S(1)}, bf16[768,256]{1,0:T(8,128)(2,1)S(1)}, u32[]{:S(2)}, u32[]{:S(2)}) collective-permute-start(bf16[768,256]{1,0:T(8,128)(2,1)S(1)} %shard_map.61), channel_id=1, source_target_pairs={{0,4},{2,6},{4,0},{6,2},{8,12},{10,14},{12,8},{14,10},{16,20},{18,... | collective-permute-start | bytes 1179656 | tf_op jit(solution)/shard_map/ppermute | solution.py:23
  31.4 12.2 %copy-start.5 = (f32[6,512,128]{2,1,0:T(8,128)}, f32[6,512,128]{2,1,0:T(8,128)S(1)}, u32[]{:S(2)}) copy-start(f32[6,512,128]{2,1,0:T(8,128)S(1)} %get-tuple-element.45.refs_1_) | copy-start | bytes 4718596
  31.4 12.1 %copy-start.7 = (f32[6,512,128]{2,1,0:T(8,128)}, f32[6,512,128]{2,1,0:T(8,128)S(1)}, u32[]{:S(2)}) copy-start(f32[6,512,128]{2,1,0:T(8,128)S(1)} %get-tuple-element.46.refs_2_) | copy-start | bytes 4718596
  45.7 32.4 %collective-permute-start.12 = (bf16[512,1536]{1,0:T(8,128)(2,1)S(1)}, bf16[512,1536]{1,0:T(8,128)(2,1)S(1)}, u32[]{:S(2)}, u32[]{:S(2)}) collective-permute-start(bf16[512,1536]{1,0:T(8,128)(2,1)S(1)} %collective-permute-done.10.refs_0_), channel_id=1, source_target_pairs={{0,2},{2,0},{4,6},{6,4},{8,10},{10,8},{12,14},{14,12},{16,18},{18,... | collective-permute-start | bytes 4718600 | tf_op jit(solution)/shard_map/ppermute | solution.py:23
  45.7 3.9 %collective-permute-start.8 = (bf16[384,512]{1,0:T(8,128)(2,1)}, bf16[384,512]{1,0:T(8,128)(2,1)}, u32[]{:S(2)}, u32[]{:S(2)}) collective-permute-start(bf16[384,512]{1,0:T(8,128)(2,1)} %shard_map.62), channel_id=1, source_target_pairs={{0,2},{2,0},{4,6},{6,4},{8,10},{10,8},{12,14},{14,12},{16,18},{18,... | collective-permute-start | bytes 1179656 | tf_op jit(solution)/shard_map/ppermute | solution.py:23
  46.4 14.0 %collective-permute-start.11 = (bf16[512,512]{1,0:T(8,128)(2,1)S(1)}, bf16[512,512]{1,0:T(8,128)(2,1)}, u32[]{:S(2)}, u32[]{:S(2)}) collective-permute-start(bf16[512,512]{1,0:T(8,128)(2,1)S(1)} %constant_dynamic-slice_fusion), channel_id=1, source_target_pairs={{0,8},{2,10},{4,12},{6,14},{8,0},{10,2},{12,4},{14,6},{16,24},{18,... | collective-permute-start | bytes 1572872 | tf_op jit(solution)/shard_map/ppermute | solution.py:23
  49.6 1.4 %copy-start.6 = (f32[6,512,128]{2,1,0:T(8,128)S(1)}, f32[6,512,128]{2,1,0:T(8,128)}, u32[]{:S(2)}) copy-start(f32[6,512,128]{2,1,0:T(8,128)} %copy-done.5) | copy-start | bytes 4718596
  51.0 1.4 %copy-start.8 = (f32[6,512,128]{2,1,0:T(8,128)S(1)}, f32[6,512,128]{2,1,0:T(8,128)}, u32[]{:S(2)}) copy-start(f32[6,512,128]{2,1,0:T(8,128)} %copy-done.7) | copy-start | bytes 4718596
  52.4 1.1 %copy-start.10 = (bf16[6,512,128]{2,1,0:T(8,128)(2,1)S(1)}, bf16[6,512,128]{2,1,0:T(8,128)(2,1)}, u32[]{:S(2)}) copy-start(bf16[6,512,128]{2,1,0:T(8,128)(2,1)} %copy-done.9) | copy-start | bytes 2359300
  57.9 20.1 %collective-permute-start.9 = (bf16[384,1024]{1,0:T(8,128)(2,1)}, bf16[384,1024]{1,0:T(8,128)(2,1)}, u32[]{:S(2)}, u32[]{:S(2)}) collective-permute-start(bf16[384,1024]{1,0:T(8,128)(2,1)} %shard_map.63), channel_id=1, source_target_pairs={{0,1},{1,0},{2,3},{3,2},{4,5},{5,4},{6,7},{7,6},{8,9},{9,8},{10,11... | collective-permute-start | bytes 2359304 | tf_op jit(solution)/shard_map/ppermute | solution.py:29
  60.5 17.6 %collective-permute-start.13 = (bf16[512,512]{1,0:T(8,128)(2,1)}, bf16[512,512]{1,0:T(8,128)(2,1)}, u32[]{:S(2)}, u32[]{:S(2)}) collective-permute-start(bf16[512,512]{1,0:T(8,128)(2,1)} %collective-permute-done.11.refs_1_), channel_id=1, source_target_pairs={{0,2},{2,0},{4,6},{6,4},{8,10},{10,8},{12,14},{14,12},{16,18},{18,... | collective-permute-start | bytes 1572872 | tf_op jit(solution)/shard_map/ppermute | solution.py:23

commit v9 on v8

--- a/solution.py
+++ b/solution.py
@@ -39,16 +39,6 @@
         compiler_params=pltpu.CompilerParams(vmem_limit_bytes=6 * 2**20),
         cost_estimate=pl.CostEstimate(flops=2**20, bytes_accessed=2**20, transcendentals=0),
     )(*operands)
-
-
-def prepare_kernel(keys_ref, values_ref, queries_ref, mine_ref, theirs_ref, queries_out):
-    core = lax.axis_index("ctx") % 2
-    for out, index in ((mine_ref, core), (theirs_ref, 1 - core)):
-        lanes = pl.ds(pl.multiple_of(index * HEAD_SIZE, HEAD_SIZE), HEAD_SIZE)
-        out[:, :HEAD_SIZE] = keys_ref[:, lanes]
-        out[:, HEAD_SIZE:] = values_ref[:, lanes]
-    group = queries_out.shape[1]
-    queries_out[...] = queries_ref[:, pl.ds(pl.multiple_of((1 - core) * group, group), group)]
 
 
 def join_kernel(first_ref, second_ref, out_ref):
@@ -179,9 +169,9 @@
 
     def attend_own():
         for j in range(half):
-            mine = rows_of(queries_ref, j, pl.multiple_of(core * rows, rows))
-            q_ref[core * half + j] = mine
-            q_ref[(1 - core) * half + j] = rows_of(q_recv_ref, j, 0)
+            lanes = pl.multiple_of(core * rows, rows)
+            q_ref[core * half + j] = rows_of(queries_ref, j, lanes)
+            q_ref[(1 - core) * half + j] = rows_of(q_recv_ref, j, lanes)
         t_id = lax.broadcasted_iota(jnp.int32, (TILE, BLOCK), 0) % BLOCK
         causal = lax.broadcasted_iota(jnp.int32, (TILE, BLOCK), 1) <= t_id
         for b, r in tiles:
@@ -249,7 +239,7 @@
 
 def attention_call(stage, distances, starts, recv_starts, operands):
     tok, half = starts.shape[0] * BLOCK, starts.shape[0]
-    rows = operands[1].shape[1]
+    rows = operands[1].shape[1] // (2 if stage == "first" else 1)
     blocks, n_head, n_pieces = 2 * half, rows // BLOCK, len(distances)
     state = [jax.ShapeDtypeStruct((blocks, rows, HEAD_SIZE), jnp.float32)] * 2
     scratch = [pltpu.VMEM((n_pieces, 2 * tok, 2 * HEAD_SIZE), jnp.bfloat16)]
@@ -271,7 +261,7 @@
         scratch_shapes=scratch,
         compiler_params=pltpu.CompilerParams(vmem_limit_bytes=24 * 2**20),
         cost_estimate=pl.CostEstimate(
-            flops=int(share * blocks * rows * 2 * tok * HEAD_SIZE * 14),
+            flops=int(share * blocks * rows * 2 * tok * HEAD_SIZE * 7),
             bytes_accessed=8 * 2**20,
             transcendentals=int(share * blocks * rows * 2 * tok),
         ),
@@ -283,18 +273,18 @@
     me, head = lax.axis_index("ctx"), lax.axis_index("head")
     cols = out_weight.shape[1] // 2
     tile, quarter = cols // 4, me // 4 % 2
-    places = (me % 2 * group, ((1 - head) * 4 + quarter) * tile, 2 * quarter * tile, head * cols)
-    keys, places = lax.optimization_barrier((keys, places))
-    first_row, first_col, spare_col, here_col = places
-
-    mine, theirs, q_send = small_call(
-        prepare_kernel,
-        [(tok, 2 * HEAD_SIZE)] * 2 + [(tok, group)],
-        (keys, values, queries),
-    )
+    core = me % 2
+    places = (core, 1 - core, core * group, ((1 - head) * 4 + quarter) * tile, 2 * quarter * tile)
+    keys, (core, other, first_row, first_col, spare_col) = lax.optimization_barrier((keys, places))
+
+    def part(x, index, size):
+        return lax.dynamic_slice_in_dim(x, index * size, size, 1)
+
+    mine = jnp.concatenate([part(keys, core, HEAD_SIZE), part(values, core, HEAD_SIZE)], 1)
+    theirs = jnp.concatenate([part(keys, other, HEAD_SIZE), part(values, other, HEAD_SIZE)], 1)
     recv = swap(theirs, 1)
     one_behind = [rotate(mine, 4), rotate(recv, 4)]
-    q_recv = swap(q_send, 1)
+    q_recv = swap(queries, 1)
     recv_starts = swap(block_start, 1)
     (own,) = small_call(join_kernel, [(2 * tok, 2 * HEAD_SIZE)], (mine, recv))
     starts = (block_start, recv_starts)
@@ -311,12 +301,11 @@
     state = attention_call("next", ((2, 2),), *starts, (q, *state, one_behind))
     state = attention_call("next", ((1, 3), (4, 4)), *starts, (q, *state, across, two_behind))
     (o_other,) = attention_call("other", ((3, 1),), *starts, (q, *state, third))
-    _, fetched = lax.optimization_barrier((o_other, fetched))
+    (heads,) = attention_call("own", ((3, 1),), *starts, (q, *state, third, swap(o_other, 1)))
+    _, fetched = lax.optimization_barrier((heads, fetched))
     weights = [fetched, swap(lax.dynamic_slice_in_dim(fetched, spare_col, tile, 1), 4)]
-    (heads,) = attention_call("own", ((3, 1),), *starts, (q, *state, third, swap(o_other, 1)))
     heads_across = cross(heads, 0)
-    rows_here = lax.dynamic_slice_in_dim(out_weight, here_col, cols, 1)
-    here = jnp.dot(heads, rows_here, preferred_element_type=jnp.float32)
+    here = jnp.dot(heads, part(out_weight, head, cols), preferred_element_type=jnp.float32)
     weights += [swap(x, 1) for x in weights]
     return project(here.astype(jnp.bfloat16), heads_across, weights)
 

time: 82.7 us -> 71 us (0.86)
  local copies, waits for them, and re-layouts: 9.68 us -> 4.65 us
  waiting for transfers between devices: 39.3 us -> 36.7 us
  Pallas kernels: 18 us -> 15.8 us
  starting transfers between devices: 10.4 us -> 8.98 us
    ppermute x2, waiting for transfers between devices: 15.1 us -> 2.02 us  [cross(): return lax.ppermute(x, ('ctx', 'head'), route)]
    ppermute x9, waiting for transfers between devices: 10.8 us -> 23.7 us  [swap(): lax.ppermute(x, 'ctx', [(i, i ^ mask) for i in range(lax.axis_size('ctx'))])]
    unnamed x22 -> x6, local copies, waits for them, and re-layouts: 6.96 us -> 0.88 us
    ppermute x3, waiting for transfers between devices: 13.3 us -> 10.9 us  [rotate(): return lax.ppermute(x, 'ctx', [(i, (i + distance) % n) for i in range(n)])]
    pallas_call x5, Pallas kernels: 13.8 us -> 11.7 us  [attention_call(): pl.pallas_call(functools.partial(attention_kernel, stage, distances, n_he...]
    ppermute x9, starting transfers between devices: 4.09 us -> 2.8 us  [swap(): lax.ppermute(x, 'ctx', [(i, i ^ mask) for i in range(lax.axis_size('ctx'))])]
    dynamic_slice x0 -> x1, local copies, waits for them, and re-layouts: none -> 1.06 us  [part(): return lax.dynamic_slice_in_dim(x, index * size, size, 1)]
    ppermute x2, starting transfers between devices: 3.12 us -> 2.17 us  [cross(): return lax.ppermute(x, ('ctx', 'head'), route)]
  transfers between devices with their start and end apart: 14 -> 14, of which waited for: 7 -> 7; matrix products, arithmetic and copies ran while one was open for 9% -> 11% of each run, Pallas kernels for 17% -> 17%
where the time goes in v9:
time: 71 us; the launch traced here: 70.6 us
  waiting for transfers between devices  36.7 us (52%)
  Pallas kernels  15.8 us (22%)
  starting transfers between devices  8.98 us (13%)
  local copies, waits for them, and re-layouts  4.65 us (7%)
  matrix products  4.22 us (6%)
    ppermute x9, waiting for transfers between devices, swap(): lax.ppermute(x, 'ctx', [(i, i ^ mask) for i in range(lax.axis_size('ctx'))])  23.7 us
    pallas_call x5, Pallas kernels, attention_call(): pl.pallas_call(functools.partial(attention_kernel, stage, distances, n_he...  11.7 us
    ppermute x3, waiting for transfers between devices, rotate(): return lax.ppermute(x, 'ctx', [(i, (i + distance) % n) for i in range(n)])  10.9 us
    dot_general x1, matrix products, per_device(): jnp.dot(heads, part(out_weight, head, cols), preferred_element_type=jnp.f...  4.22 us
    pallas_call x1, Pallas kernels, project(): pl.pallas_call(project_kernel, out_shape=jax.ShapeDtypeStruct(given.shape...  4.03 us
    ppermute x3, starting transfers between devices, rotate(): return lax.ppermute(x, 'ctx', [(i, (i + distance) % n) for i in range(n)])  4.01 us
    ppermute x9, starting transfers between devices, swap(): lax.ppermute(x, 'ctx', [(i, i ^ mask) for i in range(lax.axis_size('ctx'))])  2.8 us
    dynamic_slice x1, local copies, waits for them, and re-layouts, per_device(): sent = lax.dynamic_slice(weight, (first_row, first_col), (group, 3 * tile))  2.44 us
  transfers between devices with their start and end apart: 14, of which 7 were waited for; matrix products, arithmetic and copies ran while one was open for 11% of the time, Pallas kernels for 17%

profile of v9, /device:TPU:2, one launch (start us, length us, event | category | flops | bytes accessed | tf_op | source)
XLA Modules:
  0.0 70.6 jit_solution(16788237520512872791)
XLA Ops:
  0.0 0.0 collective-permute-start.1
  0.0 1.1 %constant_dynamic-slice_fusion.1 = (bf16[384,128]{1,0:T(8,128)(2,1)S(1)}, bf16[384,128]{1,0:T(8,128)(2,1)S(1)}, bf16[384,128]{1,0:T(8,128)(2,1)S(1)}, bf16[384,128]{1,0:T(8,128)(2,1)S(1)}) fusion(bf16[384,256]{1,0:T(8,128)(2,1)} %param.7, s32[]{:T(128)S(6)} %select_n.41, s32[]{:T(128)S(6)} %select_n.40, bf16[384,256]{1,0:T(8,128)(2,1)} %param.6), kind=kLoop, calls=%fused_computation.7 | loop fusion | bytes 786440 | tf_op jit(solution)/shard_map/dynamic_slice | solution.py:281
  1.1 0.6 collective-permute-start.2
  1.7 1.6 %collective-permute-start.3 = (bf16[384,256]{1,0:T(8,128)(2,1)S(1)}, bf16[384,256]{1,0:T(8,128)(2,1)S(1)}, u32[]{:S(2)}, u32[]{:S(2)}) collective-permute-start(bf16[384,256]{1,0:T(8,128)(2,1)S(1)} %pad_maximum_fusion.first_ref), channel_id=1, source_target_pairs={{0,8},{2,10},{4,12},{6,14},{8,16},{10,18},{12,20},{14,22},{16,24},... | collective-permute-start | bytes 589832 | tf_op jit(solution)/shard_map/ppermute | solution.py:19
  3.3 0.0 collective-permute-done.2.second_ref
  3.3 1.6 %collective-permute-start.4 = (bf16[384,256]{1,0:T(8,128)(2,1)S(1)}, bf16[384,256]{1,0:T(8,128)(2,1)S(1)}, u32[]{:S(2)}, u32[]{:S(2)}) collective-permute-start(bf16[384,256]{1,0:T(8,128)(2,1)S(1)} %collective-permute-done.2.second_ref), channel_id=1, source_target_pairs={{0,8},{2,10},{4,12},{6,14},{8,16},{10,18},{12,20},{14,22},{16,24},... | collective-permute-start | bytes 589832 | tf_op jit(solution)/shard_map/ppermute | solution.py:19
  4.9 0.0 copy-start.1
  4.9 0.0 copy-start.2
  4.9 0.0 collective-permute-done.1.refs_1_
  4.9 2.4 %dynamic_slice.21 = bf16[512,1536]{1,0:T(8,128)(2,1)S(1)} dynamic-slice(bf16[1024,4096]{1,0:T(8,128)(2,1)} %param.9, s32[]{:T(128)S(6)} %select_n.38, s32[]{:T(128)S(6)} %select_n.39), dynamic_slice_sizes={512,1536} | dynamic-slice | bytes 3145732 | tf_op jit(solution)/shard_map/dynamic_slice | solution.py:292
  7.4 1.6 %collective-permute-start.10 = (bf16[512,1536]{1,0:T(8,128)(2,1)S(1)}, bf16[512,1536]{1,0:T(8,128)(2,1)S(1)}, u32[]{:S(2)}, u32[]{:S(2)}) collective-permute-start(bf16[512,1536]{1,0:T(8,128)(2,1)S(1)} %dynamic_slice.21), channel_id=1, source_target_pairs={{0,1},{1,0},{2,3},{3,2},{4,5},{5,4},{6,7},{7,6},{8,9},{9,8},{10,11... | collective-permute-start | bytes 4718600 | tf_op jit(solution)/shard_map/ppermute | solution.py:29
  9.0 0.0 copy-done.1
  9.0 0.0 collective-permute-start
  9.0 1.1 %collective-permute-done.recv_starts_ref = s32[3]{0:T(128)S(1)} collective-permute-done((s32[3]{0:T(128)S(1)}, s32[3]{0:T(128)S(1)}, u32[]{:S(2)}, u32[]{:S(2)}) %collective-permute-start) | collective-permute-done | bytes 44 | tf_op jit(solution)/shard_map/ppermute | solution.py:23
  10.1 0.0 copy-done.2
  10.1 3.7 %shard_map.56 = (bf16[6,512,128]{2,1,0:T(8,128)(2,1)S(1)}, f32[6,512,128]{2,1,0:T(8,128)S(1)}, f32[6,512,128]{2,1,0:T(8,128)S(1)}) custom-call(s32[3]{0:T(128)S(1)} %copy-done.1, s32[3]{0:T(128)S(1)} %collective-permute-done.recv_starts_ref, bf16[384,1024]{1,0:T(8,128)(2,1)S(1)} %copy-done.2, bf16[384,1024]{1,0:T(8,128)(2,1)S(1)} %collective-permute-done.1.refs_1_, ...), custom_call_target="tpu_custom_call" | custom-call | flops 1268357504 | bytes 8388608 | tf_op jit(solution)/shard_map/pallas_call | solution.py:256
  13.8 0.0 collective-permute-done.3.first_ref
  13.8 0.8 %collective-permute-done.4.second_ref = bf16[384,256]{1,0:T(8,128)(2,1)S(1)} collective-permute-done((bf16[384,256]{1,0:T(8,128)(2,1)S(1)}, bf16[384,256]{1,0:T(8,128)(2,1)S(1)}, u32[]{:S(2)}, u32[]{:S(2)}) %collective-permute-start.4) | collective-permute-done | bytes 196640 | tf_op jit(solution)/shard_map/ppermute | solution.py:19
  14.7 0.8 %collective-permute-start.6 = (bf16[768,256]{1,0:T(8,128)(2,1)S(1)}, bf16[768,256]{1,0:T(8,128)(2,1)S(1)}, u32[]{:S(2)}, u32[]{:S(2)}) collective-permute-start(bf16[768,256]{1,0:T(8,128)(2,1)S(1)} %shard_map.57.refs_3_), channel_id=1, source_target_pairs={{0,8},{2,10},{4,12},{6,14},{8,16},{10,18},{12,20},{14,22},{16,24},... | collective-permute-start | bytes 1179656 | tf_op jit(solution)/shard_map/ppermute | solution.py:19
  15.5 0.5 collective-permute-start.5
  16.0 0.8 %shard_map.58 = (f32[6,512,128]{2,1,0:T(8,128)S(1)}, f32[6,512,128]{2,1,0:T(8,128)S(1)}) custom-call(s32[3]{0:T(128)S(1)} %copy-done.1, s32[3]{0:T(128)S(1)} %collective-permute-done.recv_starts_ref, bf16[6,512,128]{2,1,0:T(8,128)(2,1)S(1)} %get-tuple-element.35.refs_0_, f32[6,512,128]{2,1,0:T(8,128)S(1)} %get-tuple-element.36.refs_1_, ...), custom_call_target="tpu_custom_call" | custom-call | flops 2113929216 | bytes 8388608 | tf_op jit(solution)/shard_map/pallas_call | solution.py:256
  16.9 10.1 %collective-permute-done.6.refs_4_.odd_ref = bf16[768,256]{1,0:T(8,128)(2,1)S(1)} collective-permute-done((bf16[768,256]{1,0:T(8,128)(2,1)S(1)}, bf16[768,256]{1,0:T(8,128)(2,1)S(1)}, u32[]{:S(2)}, u32[]{:S(2)}) %collective-permute-start.6) | collective-permute-done | bytes 393248 | tf_op jit(solution)/shard_map/ppermute | solution.py:19
  27.0 0.7 collective-permute-start.7
  27.7 0.0 collective-permute-done.5.refs_3_
  27.7 0.9 %shard_map.59 = (f32[6,512,128]{2,1,0:T(8,128)S(1)}, f32[6,512,128]{2,1,0:T(8,128)S(1)}) custom-call(s32[3]{0:T(128)S(1)} %copy-done.1, s32[3]{0:T(128)S(1)} %collective-permute-done.recv_starts_ref, bf16[6,512,128]{2,1,0:T(8,128)(2,1)S(1)} %get-tuple-element.35.refs_0_, f32[6,512,128]{2,1,0:T(8,128)S(1)} %get-tuple-element.40.refs_1_, ...), custom_call_target="tpu_custom_call" | custom-call | flops 4227858432 | bytes 8388608 | tf_op jit(solution)/shard_map/pallas_call | solution.py:256
  28.6 7.9 %collective-permute-done.7.refs_3_ = bf16[768,256]{1,0:T(8,128)(2,1)S(1)} collective-permute-done((bf16[768,256]{1,0:T(8,128)(2,1)S(1)}, bf16[768,256]{1,0:T(8,128)(2,1)S(1)}, u32[]{:S(2)}, u32[]{:S(2)}) %collective-permute-start.7) | collective-permute-done | bytes 393248 | tf_op jit(solution)/shard_map/ppermute | solution.py:23
  36.6 3.2 %shard_map.61 = bf16[384,512]{1,0:T(8,128)(2,1)S(1)} custom-call(s32[3]{0:T(128)S(1)} %copy-done.1, s32[3]{0:T(128)S(1)} %collective-permute-done.recv_starts_ref, bf16[6,512,128]{2,1,0:T(8,128)(2,1)S(1)} %get-tuple-element.35.refs_0_, f32[6,512,128]{2,1,0:T(8,128)S(1)} %get-tuple-element.42.refs_1_, f32[6,512,128]{2,1,0:T(8,128)S(1)} %get-tuple-element.43.refs_2_, ...), custom_call_target="tpu_custom_call" | custom-call | flops 1056964608 | bytes 8388608 | tf_op jit(solution)/shard_map/pallas_call | solution.py:256
  39.7 0.1 collective-permute-start.8
  39.8 1.7 %collective-permute-done.8.refs_4_ = bf16[384,512]{1,0:T(8,128)(2,1)S(1)} collective-permute-done((bf16[384,512]{1,0:T(8,128)(2,1)S(1)}, bf16[384,512]{1,0:T(8,128)(2,1)S(1)}, u32[]{:S(2)}, u32[]{:S(2)}) %collective-permute-start.8) | collective-permute-done | bytes 393248 | tf_op jit(solution)/shard_map/ppermute | solution.py:23
  41.5 3.0 %shard_map.62 = bf16[384,1024]{1,0:T(8,128)(2,1)S(1)} custom-call(s32[3]{0:T(128)S(1)} %copy-done.1, s32[3]{0:T(128)S(1)} %collective-permute-done.recv_starts_ref, bf16[6,512,128]{2,1,0:T(8,128)(2,1)S(1)} %get-tuple-element.35.refs_0_, f32[6,512,128]{2,1,0:T(8,128)S(1)} %get-tuple-element.42.refs_1_, f32[6,512,128]{2,1,0:T(8,128)S(1)} %get-tuple-element.43.refs_2_, ...), custom_call_target="tpu_custom_call" | custom-call | flops 1056964608 | bytes 8388608 | tf_op jit(solution)/shard_map/pallas_call | solution.py:256
  44.5 0.0 copy-start
  44.5 0.9 %copy-done = bf16[384,1024]{1,0:T(8,128)(2,1)} copy-done((bf16[384,1024]{1,0:T(8,128)(2,1)}, bf16[384,1024]{1,0:T(8,128)(2,1)S(1)}, u32[]{:S(2)}) %copy-start) | copy-done | bytes 786456
  45.4 0.0 collective-permute-done.10.refs_0_
  45.4 0.1 collective-permute-start.12
  45.5 0.3 constant_dynamic-slice_fusion
  45.8 0.8 %collective-permute-start.11 = (bf16[512,512]{1,0:T(8,128)(2,1)S(1)}, bf16[512,512]{1,0:T(8,128)(2,1)}, u32[]{:S(2)}, u32[]{:S(2)}) collective-permute-start(bf16[512,512]{1,0:T(8,128)(2,1)S(1)} %constant_dynamic-slice_fusion), channel_id=1, source_target_pairs={{0,8},{2,10},{4,12},{6,14},{8,0},{10,2},{12,4},{14,6},{16,24},{18,... | collective-permute-start | bytes 1572872 | tf_op jit(solution)/shard_map/ppermute | solution.py:23
  46.6 0.6 collective-permute-start.9
  47.2 13.0 %collective-permute-done.11.refs_1_ = bf16[512,512]{1,0:T(8,128)(2,1)} collective-permute-done((bf16[512,512]{1,0:T(8,128)(2,1)S(1)}, bf16[512,512]{1,0:T(8,128)(2,1)}, u32[]{:S(2)}, u32[]{:S(2)}) %collective-permute-start.11) | collective-permute-done | bytes 524320 | tf_op jit(solution)/shard_map/ppermute | solution.py:23
  60.2 0.0 collective-permute-start.13
  60.2 4.2 %fusion.2.given_ref = bf16[384,2048]{1,0:T(8,128)(2,1)S(1)} fusion(bf16[384,1024]{1,0:T(8,128)(2,1)} %copy-done, bf16[1024,4096]{1,0:T(8,128)(2,1)} %param.9, s32[]{:T(128)S(6)} %select_n.42), kind=kOutput, calls=%fused_computation.2 | convolution fusion | flops 1611399168 | bytes 6553604 | tf_op jit(solution)/shard_map/dot_general | solution.py:308
  64.4 2.0 %collective-permute-done.9.heads_ref = bf16[384,1024]{1,0:T(8,128)(2,1)} collective-permute-done((bf16[384,1024]{1,0:T(8,128)(2,1)}, bf16[384,1024]{1,0:T(8,128)(2,1)}, u32[]{:S(2)}, u32[]{:S(2)}) %collective-permute-start.9) | collective-permute-done | bytes 786464 | tf_op jit(solution)/shard_map/ppermute | solution.py:29
  66.4 0.0 collective-permute-done.13.refs_3_
  66.4 0.0 collective-permute-done.12.refs_2_
  66.5 4.0 %shard_map.63 = bf16[384,2048]{1,0:T(8,128)(2,1)} custom-call(bf16[384,2048]{1,0:T(8,128)(2,1)S(1)} %fusion.2.given_ref, bf16[384,1024]{1,0:T(8,128)(2,1)} %collective-permute-done.9.heads_ref, bf16[512,1536]{1,0:T(8,128)(2,1)S(1)} %collective-permute-done.10.refs_0_, bf16[512,512]{1,0:T(8,128)(2,1)} %collective-permute-done.11.refs_1_, ...), custom_call_target="tpu_custom_call" | custom-call | flops 1610612736 | bytes 4194304 | tf_op jit(solution)/shard_map/pallas_call | solution.py:85
  (5 shorter events, 0.1 us)
Async XLA Ops:
  0.0 4.9 %collective-permute-start.1 = (bf16[384,1024]{1,0:T(8,128)(2,1)}, bf16[384,1024]{1,0:T(8,128)(2,1)S(1)}, u32[]{:S(2)}, u32[]{:S(2)}) collective-permute-start(bf16[384,1024]{1,0:T(8,128)(2,1)} %refs_0_.1), channel_id=1, source_target_pairs={{0,2},{2,0},{4,6},{6,4},{8,10},{10,8},{12,14},{14,12},{16,18},{18,... | collective-permute-start | bytes 2359304 | tf_op jit(solution)/shard_map/ppermute | solution.py:23
  1.1 2.2 %collective-permute-start.2 = (bf16[384,256]{1,0:T(8,128)(2,1)S(1)}, bf16[384,256]{1,0:T(8,128)(2,1)S(1)}, u32[]{:S(2)}, u32[]{:S(2)}) collective-permute-start(bf16[384,256]{1,0:T(8,128)(2,1)S(1)} %pad_maximum_fusion.1), channel_id=1, source_target_pairs={{0,2},{2,0},{4,6},{6,4},{8,10},{10,8},{12,14},{14,12},{16,18},{18,... | collective-permute-start | bytes 589832 | tf_op jit(solution)/shard_map/ppermute | solution.py:23
  1.7 12.1 %collective-permute-start.3 = (bf16[384,256]{1,0:T(8,128)(2,1)S(1)}, bf16[384,256]{1,0:T(8,128)(2,1)S(1)}, u32[]{:S(2)}, u32[]{:S(2)}) collective-permute-start(bf16[384,256]{1,0:T(8,128)(2,1)S(1)} %pad_maximum_fusion.first_ref), channel_id=1, source_target_pairs={{0,8},{2,10},{4,12},{6,14},{8,16},{10,18},{12,20},{14,22},{16,24},... | collective-permute-start | bytes 589832 | tf_op jit(solution)/shard_map/ppermute | solution.py:19
  3.3 11.3 %collective-permute-start.4 = (bf16[384,256]{1,0:T(8,128)(2,1)S(1)}, bf16[384,256]{1,0:T(8,128)(2,1)S(1)}, u32[]{:S(2)}, u32[]{:S(2)}) collective-permute-start(bf16[384,256]{1,0:T(8,128)(2,1)S(1)} %collective-permute-done.2.second_ref), channel_id=1, source_target_pairs={{0,8},{2,10},{4,12},{6,14},{8,16},{10,18},{12,20},{14,22},{16,24},... | collective-permute-start | bytes 589832 | tf_op jit(solution)/shard_map/ppermute | solution.py:19
  4.9 4.0 %copy-start.1 = (s32[3]{0:T(128)S(1)}, s32[3]{0:T(128)}, u32[]{:S(2)}) copy-start(s32[3]{0:T(128)} %starts_ref.9) | copy-start | bytes 40
  4.9 5.2 %copy-start.2 = (bf16[384,1024]{1,0:T(8,128)(2,1)S(1)}, bf16[384,1024]{1,0:T(8,128)(2,1)}, u32[]{:S(2)}) copy-start(bf16[384,1024]{1,0:T(8,128)(2,1)} %refs_0_.1) | copy-start | bytes 2359300
  7.4 38.0 %collective-permute-start.10 = (bf16[512,1536]{1,0:T(8,128)(2,1)S(1)}, bf16[512,1536]{1,0:T(8,128)(2,1)S(1)}, u32[]{:S(2)}, u32[]{:S(2)}) collective-permute-start(bf16[512,1536]{1,0:T(8,128)(2,1)S(1)} %dynamic_slice.21), channel_id=1, source_target_pairs={{0,1},{1,0},{2,3},{3,2},{4,5},{5,4},{6,7},{7,6},{8,9},{9,8},{10,11... | collective-permute-start | bytes 4718600 | tf_op jit(solution)/shard_map/ppermute | solution.py:29
  9.0 1.1 %collective-permute-start = (s32[3]{0:T(128)S(1)}, s32[3]{0:T(128)S(1)}, u32[]{:S(2)}, u32[]{:S(2)}) collective-permute-start(s32[3]{0:T(128)S(1)} %copy-done.1), channel_id=1, source_target_pairs={{0,2},{2,0},{4,6},{6,4},{8,10},{10,8},{12,14},{14,12},{16,18},{18,... | collective-permute-start | bytes 44 | tf_op jit(solution)/shard_map/ppermute | solution.py:23
  14.7 12.3 %collective-permute-start.6 = (bf16[768,256]{1,0:T(8,128)(2,1)S(1)}, bf16[768,256]{1,0:T(8,128)(2,1)S(1)}, u32[]{:S(2)}, u32[]{:S(2)}) collective-permute-start(bf16[768,256]{1,0:T(8,128)(2,1)S(1)} %shard_map.57.refs_3_), channel_id=1, source_target_pairs={{0,8},{2,10},{4,12},{6,14},{8,16},{10,18},{12,20},{14,22},{16,24},... | collective-permute-start | bytes 1179656 | tf_op jit(solution)/shard_map/ppermute | solution.py:19
  15.5 12.2 %collective-permute-start.5 = (bf16[768,256]{1,0:T(8,128)(2,1)S(1)}, bf16[768,256]{1,0:T(8,128)(2,1)S(1)}, u32[]{:S(2)}, u32[]{:S(2)}) collective-permute-start(bf16[768,256]{1,0:T(8,128)(2,1)S(1)} %shard_map.57.refs_3_), channel_id=1, source_target_pairs={{0,4},{2,6},{4,0},{6,2},{8,12},{10,14},{12,8},{14,10},{16,20},{18,... | collective-permute-start | bytes 1179656 | tf_op jit(solution)/shard_map/ppermute | solution.py:23
  27.0 9.6 %collective-permute-start.7 = (bf16[768,256]{1,0:T(8,128)(2,1)S(1)}, bf16[768,256]{1,0:T(8,128)(2,1)S(1)}, u32[]{:S(2)}, u32[]{:S(2)}) collective-permute-start(bf16[768,256]{1,0:T(8,128)(2,1)S(1)} %shard_map.60), channel_id=1, source_target_pairs={{0,4},{2,6},{4,0},{6,2},{8,12},{10,14},{12,8},{14,10},{16,20},{18,... | collective-permute-start | bytes 1179656 | tf_op jit(solution)/shard_map/ppermute | solution.py:23
  39.7 1.8 %collective-permute-start.8 = (bf16[384,512]{1,0:T(8,128)(2,1)S(1)}, bf16[384,512]{1,0:T(8,128)(2,1)S(1)}, u32[]{:S(2)}, u32[]{:S(2)}) collective-permute-start(bf16[384,512]{1,0:T(8,128)(2,1)S(1)} %shard_map.61), channel_id=1, source_target_pairs={{0,2},{2,0},{4,6},{6,4},{8,10},{10,8},{12,14},{14,12},{16,18},{18,... | collective-permute-start | bytes 1179656 | tf_op jit(solution)/shard_map/ppermute | solution.py:23
  44.5 0.9 %copy-start = (bf16[384,1024]{1,0:T(8,128)(2,1)}, bf16[384,1024]{1,0:T(8,128)(2,1)S(1)}, u32[]{:S(2)}) copy-start(bf16[384,1024]{1,0:T(8,128)(2,1)S(1)} %shard_map.62) | copy-start | bytes 2359300
  45.4 21.0 %collective-permute-start.12 = (bf16[512,1536]{1,0:T(8,128)(2,1)S(1)}, bf16[512,1536]{1,0:T(8,128)(2,1)S(1)}, u32[]{:S(2)}, u32[]{:S(2)}) collective-permute-start(bf16[512,1536]{1,0:T(8,128)(2,1)S(1)} %collective-permute-done.10.refs_0_), channel_id=1, source_target_pairs={{0,2},{2,0},{4,6},{6,4},{8,10},{10,8},{12,14},{14,12},{16,18},{18,... | collective-permute-start | bytes 4718600 | tf_op jit(solution)/shard_map/ppermute | solution.py:23
  45.8 14.4 %collective-permute-start.11 = (bf16[512,512]{1,0:T(8,128)(2,1)S(1)}, bf16[512,512]{1,0:T(8,128)(2,1)}, u32[]{:S(2)}, u32[]{:S(2)}) collective-permute-start(bf16[512,512]{1,0:T(8,128)(2,1)S(1)} %constant_dynamic-slice_fusion), channel_id=1, source_target_pairs={{0,8},{2,10},{4,12},{6,14},{8,0},{10,2},{12,4},{14,6},{16,24},{18,... | collective-permute-start | bytes 1572872 | tf_op jit(solution)/shard_map/ppermute | solution.py:23
  46.6 19.8 %collective-permute-start.9 = (bf16[384,1024]{1,0:T(8,128)(2,1)}, bf16[384,1024]{1,0:T(8,128)(2,1)}, u32[]{:S(2)}, u32[]{:S(2)}) collective-permute-start(bf16[384,1024]{1,0:T(8,128)(2,1)} %copy-done), channel_id=1, source_target_pairs={{0,1},{1,0},{2,3},{3,2},{4,5},{5,4},{6,7},{7,6},{8,9},{9,8},{10,11... | collective-permute-start | bytes 2359304 | tf_op jit(solution)/shard_map/ppermute | solution.py:29
  60.2 6.3 %collective-permute-start.13 = (bf16[512,512]{1,0:T(8,128)(2,1)}, bf16[512,512]{1,0:T(8,128)(2,1)}, u32[]{:S(2)}, u32[]{:S(2)}) collective-permute-start(bf16[512,512]{1,0:T(8,128)(2,1)} %collective-permute-done.11.refs_1_), channel_id=1, source_target_pairs={{0,2},{2,0},{4,6},{6,4},{8,10},{10,8},{12,14},{14,12},{16,18},{18,... | collective-permute-start | bytes 1572872 | tf_op jit(solution)/shard_map/ppermute | solution.py:23

commit v10 on v9

--- a/solution.py
+++ b/solution.py
@@ -60,18 +60,20 @@
 
 
 def project_kernel(given_ref, heads_ref, *refs):
-    parts, out_ref, built, sems = refs[:4], refs[4], refs[5], refs[6]
+    parts, out_ref, built, sems = refs[:5], refs[5], refs[6], refs[7]
     me = lax.axis_index("ctx")
-    core, part = me % 2, me // 4 % 2
-    group, width = parts[1].shape
+    core, fetched = me % 2, me // 4 % 2
+    group, width = parts[3].shape
+    tiles = [x.at[:, n * width : (n + 1) * width] for x in parts[:3] for n in range(2)]
+    tiles += parts[3:]
     copies = []
-    for n, first in enumerate((part, part + 1, part + 2, 3 - 3 * part)):
+    for n in range(4):
+        first = (fetched if n < 2 else 1 - fetched) * 2 + n % 2
         cols = pl.ds(pl.multiple_of(first * width, width), width)
         total = given_ref[:, cols].astype(jnp.float32)
-        for index, (fetched, single) in ((core, parts[:2]), (1 - core, parts[2:])):
+        for index, tile in ((core, tiles[n]), (1 - core, tiles[4 + n])):
             heads = heads_ref[:, pl.ds(pl.multiple_of(index * group, group), group)]
-            tile = fetched[:, n * width : (n + 1) * width] if n < 3 else single[...]
-            total += jnp.dot(heads, tile, preferred_element_type=jnp.float32)
+            total += jnp.dot(heads, tile[...], preferred_element_type=jnp.float32)
         built[n] = total.astype(out_ref.dtype)
         copies.append(pltpu.make_async_copy(built.at[n], out_ref.at[:, cols], sems.at[n]))
         copies[-1].start()
@@ -85,7 +87,7 @@
     return pl.pallas_call(
         project_kernel,
         out_shape=jax.ShapeDtypeStruct(given.shape, jnp.bfloat16),
-        in_specs=[vmem] * 6,
+        in_specs=[vmem] * 7,
         out_specs=pl.BlockSpec(memory_space=pltpu.HBM),
         scratch_shapes=[pltpu.VMEM((4, tok, cols // 4), jnp.bfloat16), pltpu.SemaphoreType.DMA((4,))],
         compiler_params=pltpu.CompilerParams(vmem_limit_bytes=16 * 2**20),
@@ -253,6 +255,7 @@
         outs, share = [jax.ShapeDtypeStruct((tok, width), jnp.bfloat16)], 0.5
         scratch = [pltpu.VMEM((half, rows, HEAD_SIZE), jnp.float32)] * 2 + scratch
     vmem, smem = pl.BlockSpec(memory_space=pltpu.VMEM), pl.BlockSpec(memory_space=pltpu.SMEM)
+    late = stage in ("own", "other")
     return pl.pallas_call(
         functools.partial(attention_kernel, stage, distances, n_head),
         out_shape=outs,
@@ -261,7 +264,7 @@
         scratch_shapes=scratch,
         compiler_params=pltpu.CompilerParams(vmem_limit_bytes=24 * 2**20),
         cost_estimate=pl.CostEstimate(
-            flops=int(share * blocks * rows * 2 * tok * HEAD_SIZE * 7),
+            flops=int(share * blocks * rows * 2 * tok * HEAD_SIZE * (25 if late else 10)),
             bytes_accessed=8 * 2**20,
             transcendentals=int(share * blocks * rows * 2 * tok),
         ),
@@ -272,24 +275,22 @@
     tok, group = queries.shape[0], queries.shape[1] // 2
     me, head = lax.axis_index("ctx"), lax.axis_index("head")
     cols = out_weight.shape[1] // 2
-    tile, quarter = cols // 4, me // 4 % 2
     core = me % 2
-    places = (core, 1 - core, core * group, ((1 - head) * 4 + quarter) * tile, 2 * quarter * tile)
-    keys, (core, other, first_row, first_col, spare_col) = lax.optimization_barrier((keys, places))
+    places = (core, 1 - core, core * group, ((1 - head) * 2 + me // 4 % 2) * (cols // 2))
+    keys, (core, other, first_row, first_col) = lax.optimization_barrier((keys, places))
 
     def part(x, index, size):
         return lax.dynamic_slice_in_dim(x, index * size, size, 1)
 
     mine = jnp.concatenate([part(keys, core, HEAD_SIZE), part(values, core, HEAD_SIZE)], 1)
     theirs = jnp.concatenate([part(keys, other, HEAD_SIZE), part(values, other, HEAD_SIZE)], 1)
-    recv = swap(theirs, 1)
+    recv, recv_starts = lax.optimization_barrier((swap(theirs, 1), swap(block_start, 1)))
     one_behind = [rotate(mine, 4), rotate(recv, 4)]
     q_recv = swap(queries, 1)
-    recv_starts = swap(block_start, 1)
     (own,) = small_call(join_kernel, [(2 * tok, 2 * HEAD_SIZE)], (mine, recv))
     starts = (block_start, recv_starts)
     q_recv, weight = lax.optimization_barrier((q_recv, out_weight))
-    sent = lax.dynamic_slice(weight, (first_row, first_col), (group, 3 * tile))
+    sent = lax.dynamic_slice(weight, (first_row, first_col), (group, cols // 2))
     q_recv, sent = lax.optimization_barrier((q_recv, sent))
     fetched = cross(sent, 0)
     q, *state = attention_call("first", ((0, 0),), *starts, (queries, q_recv, own))
@@ -300,14 +301,17 @@
     third = swap(small_call(pick_kernel, [own.shape], (own, two_behind))[0], 2)
     state = attention_call("next", ((2, 2),), *starts, (q, *state, one_behind))
     state = attention_call("next", ((1, 3), (4, 4)), *starts, (q, *state, across, two_behind))
+    _, fetched = lax.optimization_barrier((third, fetched))
+    passed = swap(fetched, 4)
     (o_other,) = attention_call("other", ((3, 1),), *starts, (q, *state, third))
     (heads,) = attention_call("own", ((3, 1),), *starts, (q, *state, third, swap(o_other, 1)))
-    _, fetched = lax.optimization_barrier((heads, fetched))
-    weights = [fetched, swap(lax.dynamic_slice_in_dim(fetched, spare_col, tile, 1), 4)]
     heads_across = cross(heads, 0)
     here = jnp.dot(heads, part(out_weight, head, cols), preferred_element_type=jnp.float32)
-    weights += [swap(x, 1) for x in weights]
-    return project(here.astype(jnp.bfloat16), heads_across, weights)
+    here = here.astype(jnp.bfloat16)
+    _, late = lax.optimization_barrier((here, passed))
+    weights = [fetched, passed, swap(fetched, 1)]
+    weights += [swap(part(late, n, cols // 4), 1) for n in range(2)]
+    return project(here, heads_across, weights)
 
 
 def solution(mesh):

time: 71 us -> 72.8 us (1.025)
  local copies, waits for them, and re-layouts: 4.65 us -> 7 us
  Pallas kernels: 15.8 us -> 14.4 us
    ppermute x3, waiting for transfers between devices: 10.9 us -> 14 us  [rotate(): return lax.ppermute(x, 'ctx', [(i, (i + distance) % n) for i in range(n)])]
    unnamed x6 -> x16, local copies, waits for them, and re-layouts: 0.88 us -> 3.97 us
    ppermute x9 -> x10, waiting for transfers between devices: 23.7 us -> 20.8 us  [swap(): lax.ppermute(x, 'ctx', [(i, i ^ mask) for i in range(lax.axis_size('ctx'))])]
    pallas_call x1, Pallas kernels: 4.03 us -> 2.59 us  [project(): pl.pallas_call(project_kernel, out_shape=jax.ShapeDtypeStruct(given.shape...]
    ppermute x2, starting transfers between devices: 2.17 us -> 3.1 us  [cross(): return lax.ppermute(x, ('ctx', 'head'), route)]
    dynamic_slice x2 -> x1, local copies, waits for them, and re-layouts: 2.71 us -> 1.89 us  [per_device(): sent = lax.dynamic_slice(weight, (first_row, first_col), (group, cols // 2))]
    ppermute x3, starting transfers between devices: 4.01 us -> 3.27 us  [rotate(): return lax.ppermute(x, 'ctx', [(i, (i + distance) % n) for i in range(n)])]
    ppermute x9 -> x10, starting transfers between devices: 2.8 us -> 3.12 us  [swap(): lax.ppermute(x, 'ctx', [(i, i ^ mask) for i in range(lax.axis_size('ctx'))])]
  transfers between devices with their start and end apart: 14 -> 15, of which waited for: 7 -> 8; matrix products, arithmetic and copies ran while one was open for 11% -> 10% of each run, Pallas kernels for 17% -> 16%
where the time goes in v10:
time: 72.8 us; the launch traced here: 72.1 us
  waiting for transfers between devices  36.9 us (51%)
  Pallas kernels  14.4 us (20%)
  starting transfers between devices  9.49 us (13%)
  local copies, waits for them, and re-layouts  7 us (10%)
  matrix products  3.98 us (5%)
    ppermute x10, waiting for transfers between devices, swap(): lax.ppermute(x, 'ctx', [(i, i ^ mask) for i in range(lax.axis_size('ctx'))])  20.8 us
    ppermute x3, waiting for transfers between devices, rotate(): return lax.ppermute(x, 'ctx', [(i, (i + distance) % n) for i in range(n)])  14 us
    pallas_call x5, Pallas kernels, attention_call(): pl.pallas_call(functools.partial(attention_kernel, stage, distances, n_he...  11.7 us
    dot_general x1, matrix products, per_device(): jnp.dot(heads, part(out_weight, head, cols), preferred_element_type=jnp.f...  3.98 us
    unnamed x16, local copies, waits for them, and re-layouts  3.97 us
    ppermute x3, starting transfers between devices, rotate(): return lax.ppermute(x, 'ctx', [(i, (i + distance) % n) for i in range(n)])  3.27 us
    ppermute x10, starting transfers between devices, swap(): lax.ppermute(x, 'ctx', [(i, i ^ mask) for i in range(lax.axis_size('ctx'))])  3.12 us
    ppermute x2, starting transfers between devices, cross(): return lax.ppermute(x, ('ctx', 'head'), route)  3.1 us
  transfers between devices with their start and end apart: 15, of which 8 were waited for; matrix products, arithmetic and copies ran while one was open for 10% of the time, Pallas kernels for 16%

profile of v10, /device:TPU:2, one launch (start us, length us, event | category | flops | bytes accessed | tf_op | source)
XLA Modules:
  0.0 72.1 jit_solution(12324025141409362481)
XLA Ops:
  0.0 0.0 collective-permute-start.2
  0.0 1.1 %constant_dynamic-slice_fusion = (bf16[384,128]{1,0:T(8,128)(2,1)S(1)}, bf16[384,128]{1,0:T(8,128)(2,1)S(1)}, bf16[384,128]{1,0:T(8,128)(2,1)S(1)}, bf16[384,128]{1,0:T(8,128)(2,1)S(1)}) fusion(bf16[384,256]{1,0:T(8,128)(2,1)} %param.7, s32[]{:T(128)S(6)} %select_n.38, s32[]{:T(128)S(6)} %select_n.35, bf16[384,256]{1,0:T(8,128)(2,1)} %param.6), kind=kLoop, calls=%fused_computation.6 | loop fusion | bytes 786440 | tf_op jit(solution)/shard_map/dynamic_slice | solution.py:283
  1.1 0.6 collective-permute-start
  1.7 0.1 collective-permute-start.1
  1.8 0.0 copy-start
  1.8 0.0 copy-start.1
  1.8 1.6 %collective-permute-start.3 = (bf16[384,256]{1,0:T(8,128)(2,1)S(1)}, bf16[384,256]{1,0:T(8,128)(2,1)S(1)}, u32[]{:S(2)}, u32[]{:S(2)}) collective-permute-start(bf16[384,256]{1,0:T(8,128)(2,1)S(1)} %pad_maximum_fusion.1.first_ref), channel_id=1, source_target_pairs={{0,8},{2,10},{4,12},{6,14},{8,16},{10,18},{12,20},{14,22},{16,24},... | collective-permute-start | bytes 589832 | tf_op jit(solution)/shard_map/ppermute | solution.py:19
  3.4 0.0 collective-permute-done.1.recv_starts_ref
  3.4 0.0 collective-permute-done.second_ref
  3.4 1.6 %collective-permute-start.4 = (bf16[384,256]{1,0:T(8,128)(2,1)S(1)}, bf16[384,256]{1,0:T(8,128)(2,1)S(1)}, u32[]{:S(2)}, u32[]{:S(2)}) collective-permute-start(bf16[384,256]{1,0:T(8,128)(2,1)S(1)} %collective-permute-done.second_ref), channel_id=1, source_target_pairs={{0,8},{2,10},{4,12},{6,14},{8,16},{10,18},{12,20},{14,22},{16,24},... | collective-permute-start | bytes 589832 | tf_op jit(solution)/shard_map/ppermute | solution.py:19
  5.0 0.0 collective-permute-done.2.refs_1_
  5.0 1.9 %dynamic_slice.26 = bf16[512,1024]{1,0:T(8,128)(2,1)S(1)} dynamic-slice(bf16[1024,4096]{1,0:T(8,128)(2,1)} %param.9, s32[]{:T(128)S(6)} %select_n.36, s32[]{:T(128)S(6)} %select_n.37), dynamic_slice_sizes={512,1024} | dynamic-slice | bytes 2097156 | tf_op jit(solution)/shard_map/dynamic_slice | solution.py:293
  6.9 0.0 copy-done
  6.9 0.0 copy-done.1
  7.0 3.7 %shard_map.56 = (bf16[6,512,128]{2,1,0:T(8,128)(2,1)S(1)}, f32[6,512,128]{2,1,0:T(8,128)S(1)}, f32[6,512,128]{2,1,0:T(8,128)S(1)}) custom-call(s32[3]{0:T(128)S(1)} %copy-done.1, s32[3]{0:T(128)S(1)} %collective-permute-done.1.recv_starts_ref, bf16[384,1024]{1,0:T(8,128)(2,1)S(1)} %copy-done, bf16[384,1024]{1,0:T(8,128)(2,1)S(1)} %collective-permute-done.2.refs_1_, ...), custom_call_target="tpu_custom_call" | custom-call | flops 1811939328 | bytes 8388608 | tf_op jit(solution)/shard_map/pallas_call | solution.py:259
  10.7 0.0 copy-start.2
  10.7 0.6 collective-permute-done.3.first_ref
  11.3 3.8 %collective-permute-done.4.second_ref = bf16[384,256]{1,0:T(8,128)(2,1)S(1)} collective-permute-done((bf16[384,256]{1,0:T(8,128)(2,1)S(1)}, bf16[384,256]{1,0:T(8,128)(2,1)S(1)}, u32[]{:S(2)}, u32[]{:S(2)}) %collective-permute-start.4) | collective-permute-done | bytes 196640 | tf_op jit(solution)/shard_map/ppermute | solution.py:19
  15.2 0.1 collective-permute-start.6
  15.2 0.6 collective-permute-start.5
  15.8 1.5 %collective-permute-start.10 = (bf16[512,1024]{1,0:T(8,128)(2,1)S(1)}, bf16[512,1024]{1,0:T(8,128)(2,1)S(1)}, u32[]{:S(2)}, u32[]{:S(2)}) collective-permute-start(bf16[512,1024]{1,0:T(8,128)(2,1)S(1)} %dynamic_slice.26), channel_id=1, source_target_pairs={{0,1},{1,0},{2,3},{3,2},{4,5},{5,4},{6,7},{7,6},{8,9},{9,8},{10,11... | collective-permute-start | bytes 3145736 | tf_op jit(solution)/shard_map/ppermute | solution.py:29
  17.4 0.8 %shard_map.58 = (f32[6,512,128]{2,1,0:T(8,128)S(1)}, f32[6,512,128]{2,1,0:T(8,128)S(1)}) custom-call(s32[3]{0:T(128)S(1)} %copy-done.1, s32[3]{0:T(128)S(1)} %collective-permute-done.1.recv_starts_ref, bf16[6,512,128]{2,1,0:T(8,128)(2,1)S(1)} %get-tuple-element.39.refs_0_, f32[6,512,128]{2,1,0:T(8,128)S(1)} %get-tuple-element.40.refs_1_, ...), custom_call_target="tpu_custom_call" | custom-call | flops 3019898880 | bytes 8388608 | tf_op jit(solution)/shard_map/pallas_call | solution.py:259
  18.2 9.5 %collective-permute-done.6.refs_4_.odd_ref = bf16[768,256]{1,0:T(8,128)(2,1)S(1)} collective-permute-done((bf16[768,256]{1,0:T(8,128)(2,1)S(1)}, bf16[768,256]{1,0:T(8,128)(2,1)S(1)}, u32[]{:S(2)}, u32[]{:S(2)}) %collective-permute-start.6) | collective-permute-done | bytes 393248 | tf_op jit(solution)/shard_map/ppermute | solution.py:19
  27.8 0.7 %collective-permute-start.7 = (bf16[768,256]{1,0:T(8,128)(2,1)S(1)}, bf16[768,256]{1,0:T(8,128)(2,1)S(1)}, u32[]{:S(2)}, u32[]{:S(2)}) collective-permute-start(bf16[768,256]{1,0:T(8,128)(2,1)S(1)} %shard_map.60), channel_id=1, source_target_pairs={{0,4},{2,6},{4,0},{6,2},{8,12},{10,14},{12,8},{14,10},{16,20},{18,... | collective-permute-start | bytes 1179656 | tf_op jit(solution)/shard_map/ppermute | solution.py:23
  28.5 0.0 collective-permute-done.5.refs_3_
  28.5 0.9 %shard_map.59 = (f32[6,512,128]{2,1,0:T(8,128)S(1)}, f32[6,512,128]{2,1,0:T(8,128)S(1)}) custom-call(s32[3]{0:T(128)S(1)} %copy-done.1, s32[3]{0:T(128)S(1)} %collective-permute-done.1.recv_starts_ref, bf16[6,512,128]{2,1,0:T(8,128)(2,1)S(1)} %get-tuple-element.39.refs_0_, f32[6,512,128]{2,1,0:T(8,128)S(1)} %get-tuple-element.44.refs_1_, ...), custom_call_target="tpu_custom_call" | custom-call | flops 6039797760 | bytes 8388608 | tf_op jit(solution)/shard_map/pallas_call | solution.py:259
  29.5 0.0 copy-start.4
  29.5 0.0 copy-start.6
  29.5 8.2 %collective-permute-done.7.refs_3_ = bf16[768,256]{1,0:T(8,128)(2,1)S(1)} collective-permute-done((bf16[768,256]{1,0:T(8,128)(2,1)S(1)}, bf16[768,256]{1,0:T(8,128)(2,1)S(1)}, u32[]{:S(2)}, u32[]{:S(2)}) %collective-permute-start.7) | collective-permute-done | bytes 393248 | tf_op jit(solution)/shard_map/ppermute | solution.py:23
  37.7 0.0 copy-done.2
  37.7 3.2 %shard_map.61 = bf16[384,512]{1,0:T(8,128)(2,1)S(1)} custom-call(s32[3]{0:T(128)S(1)} %copy-done.1, s32[3]{0:T(128)S(1)} %collective-permute-done.1.recv_starts_ref, bf16[6,512,128]{2,1,0:T(8,128)(2,1)S(1)} %get-tuple-element.39.refs_0_, f32[6,512,128]{2,1,0:T(8,128)S(1)} %get-tuple-element.46.refs_1_, f32[6,512,128]{2,1,0:T(8,128)S(1)} %get-tuple-element.47.refs_2_, ...), custom_call_target="tpu_custom_call" | custom-call | flops 3774873600 | bytes 8388608 | tf_op jit(solution)/shard_map/pallas_call | solution.py:259
  40.9 0.0 copy-done.4
  40.9 0.0 copy-done.6
  40.9 0.1 collective-permute-start.8
  41.0 0.0 collective-permute-done.10.refs_0_
  41.0 0.2 collective-permute-start.11
  41.2 0.3 collective-permute-start.12
  41.5 1.2 %collective-permute-done.8.refs_4_ = bf16[384,512]{1,0:T(8,128)(2,1)S(1)} collective-permute-done((bf16[384,512]{1,0:T(8,128)(2,1)S(1)}, bf16[384,512]{1,0:T(8,128)(2,1)S(1)}, u32[]{:S(2)}, u32[]{:S(2)}) %collective-permute-start.8) | collective-permute-done | bytes 393248 | tf_op jit(solution)/shard_map/ppermute | solution.py:23
  42.7 0.0 copy-start.3
  42.7 1.1 %copy-done.3 = bf16[6,512,128]{2,1,0:T(8,128)(2,1)S(1)} copy-done((bf16[6,512,128]{2,1,0:T(8,128)(2,1)S(1)}, bf16[6,512,128]{2,1,0:T(8,128)(2,1)}, u32[]{:S(2)}) %copy-start.3) | copy-done | bytes 786456
  43.8 0.0 copy-start.5
  43.8 1.4 %copy-done.5 = f32[6,512,128]{2,1,0:T(8,128)S(1)} copy-done((f32[6,512,128]{2,1,0:T(8,128)S(1)}, f32[6,512,128]{2,1,0:T(8,128)}, u32[]{:S(2)}) %copy-start.5) | copy-done | bytes 1572888
  45.2 0.0 copy-start.7
  45.2 1.4 %copy-done.7 = f32[6,512,128]{2,1,0:T(8,128)S(1)} copy-done((f32[6,512,128]{2,1,0:T(8,128)S(1)}, f32[6,512,128]{2,1,0:T(8,128)}, u32[]{:S(2)}) %copy-start.7) | copy-done | bytes 1572888
  46.7 3.0 %shard_map.62 = bf16[384,1024]{1,0:T(8,128)(2,1)S(1)} custom-call(s32[3]{0:T(128)S(1)} %copy-done.1, s32[3]{0:T(128)S(1)} %collective-permute-done.1.recv_starts_ref, bf16[6,512,128]{2,1,0:T(8,128)(2,1)S(1)} %copy-done.3, f32[6,512,128]{2,1,0:T(8,128)S(1)} %copy-done.5, f32[6,512,128]{2,1,0:T(8,128)S(1)} %copy-done.7, ...), custom_call_target="tpu_custom_call" | custom-call | flops 3774873600 | bytes 8388608 | tf_op jit(solution)/shard_map/pallas_call | solution.py:259
  49.6 1.6 %collective-permute-start.9 = (bf16[384,1024]{1,0:T(8,128)(2,1)S(1)}, bf16[384,1024]{1,0:T(8,128)(2,1)S(1)}, u32[]{:S(2)}, u32[]{:S(2)}) collective-permute-start(bf16[384,1024]{1,0:T(8,128)(2,1)S(1)} %shard_map.62), channel_id=1, source_target_pairs={{0,1},{1,0},{2,3},{3,2},{4,5},{5,4},{6,7},{7,6},{8,9},{9,8},{10,11... | collective-permute-start | bytes 2359304 | tf_op jit(solution)/shard_map/ppermute | solution.py:29
  51.2 4.0 %fusion.2.given_ref = bf16[384,2048]{1,0:T(8,128)(2,1)S(1)} fusion(bf16[384,1024]{1,0:T(8,128)(2,1)S(1)} %shard_map.62, bf16[1024,4096]{1,0:T(8,128)(2,1)} %param.9, s32[]{:T(128)S(6)} %select_n.39), kind=kOutput, calls=%fused_computation.2 | convolution fusion | flops 1611399168 | bytes 6553604 | tf_op jit(solution)/shard_map/dot_general | solution.py:309
  55.2 11.4 %collective-permute-done.11.refs_1_ = bf16[512,1024]{1,0:T(8,128)(2,1)S(1)} collective-permute-done((bf16[512,1024]{1,0:T(8,128)(2,1)S(1)}, bf16[512,1024]{1,0:T(8,128)(2,1)S(1)}, u32[]{:S(2)}, u32[]{:S(2)}) %collective-permute-start.11) | collective-permute-done | bytes 1048608 | tf_op jit(solution)/shard_map/ppermute | solution.py:23
  66.6 0.1 fusion.6
  66.7 0.1 collective-permute-start.14
  66.7 0.5 collective-permute-start.13
  67.2 2.1 %collective-permute-done.9.heads_ref = bf16[384,1024]{1,0:T(8,128)(2,1)S(1)} collective-permute-done((bf16[384,1024]{1,0:T(8,128)(2,1)S(1)}, bf16[384,1024]{1,0:T(8,128)(2,1)S(1)}, u32[]{:S(2)}, u32[]{:S(2)}) %collective-permute-start.9) | collective-permute-done | bytes 786464 | tf_op jit(solution)/shard_map/ppermute | solution.py:29
  69.3 0.0 collective-permute-done.12.refs_2_
  69.3 0.0 collective-permute-done.14.refs_4_
  69.3 0.1 collective-permute-done.13.refs_3_
  69.4 2.6 %shard_map.63 = bf16[384,2048]{1,0:T(8,128)(2,1)} custom-call(bf16[384,2048]{1,0:T(8,128)(2,1)S(1)} %fusion.2.given_ref, bf16[384,1024]{1,0:T(8,128)(2,1)S(1)} %collective-permute-done.9.heads_ref, bf16[512,1024]{1,0:T(8,128)(2,1)S(1)} %collective-permute-done.10.refs_0_, bf16[512,1024]{1,0:T(8,128)(2,1)S(1)} %collective-permute-done.11.refs_1_, ...), custom_call_target="tpu_custom_call" | custom-call | flops 1610612736 | bytes 4194304 | tf_op jit(solution)/shard_map/pallas_call | solution.py:87
  (5 shorter events, 0.1 us)
Async XLA Ops:
  0.0 5.0 %collective-permute-start.2 = (bf16[384,1024]{1,0:T(8,128)(2,1)}, bf16[384,1024]{1,0:T(8,128)(2,1)S(1)}, u32[]{:S(2)}, u32[]{:S(2)}) collective-permute-start(bf16[384,1024]{1,0:T(8,128)(2,1)} %refs_0_.1), channel_id=1, source_target_pairs={{0,2},{2,0},{4,6},{6,4},{8,10},{10,8},{12,14},{14,12},{16,18},{18,... | collective-permute-start | bytes 2359304 | tf_op jit(solution)/shard_map/ppermute | solution.py:23
  1.1 2.3 %collective-permute-start = (bf16[384,256]{1,0:T(8,128)(2,1)S(1)}, bf16[384,256]{1,0:T(8,128)(2,1)S(1)}, u32[]{:S(2)}, u32[]{:S(2)}) collective-permute-start(bf16[384,256]{1,0:T(8,128)(2,1)S(1)} %pad_maximum_fusion), channel_id=1, source_target_pairs={{0,2},{2,0},{4,6},{6,4},{8,10},{10,8},{12,14},{14,12},{16,18},{18,... | collective-permute-start | bytes 589832 | tf_op jit(solution)/shard_map/ppermute | solution.py:23
  1.7 1.7 %collective-permute-start.1 = (s32[3]{0:T(128)}, s32[3]{0:T(128)S(1)}, u32[]{:S(2)}, u32[]{:S(2)}) collective-permute-start(s32[3]{0:T(128)} %starts_ref.9), channel_id=1, source_target_pairs={{0,2},{2,0},{4,6},{6,4},{8,10},{10,8},{12,14},{14,12},{16,18},{18,... | collective-permute-start | bytes 44 | tf_op jit(solution)/shard_map/ppermute | solution.py:23
  1.8 5.2 %copy-start = (bf16[384,1024]{1,0:T(8,128)(2,1)S(1)}, bf16[384,1024]{1,0:T(8,128)(2,1)}, u32[]{:S(2)}) copy-start(bf16[384,1024]{1,0:T(8,128)(2,1)} %refs_0_.1) | copy-start | bytes 2359300
  1.8 5.2 %copy-start.1 = (s32[3]{0:T(128)S(1)}, s32[3]{0:T(128)}, u32[]{:S(2)}) copy-start(s32[3]{0:T(128)} %starts_ref.9) | copy-start | bytes 40
  1.8 9.5 %collective-permute-start.3 = (bf16[384,256]{1,0:T(8,128)(2,1)S(1)}, bf16[384,256]{1,0:T(8,128)(2,1)S(1)}, u32[]{:S(2)}, u32[]{:S(2)}) collective-permute-start(bf16[384,256]{1,0:T(8,128)(2,1)S(1)} %pad_maximum_fusion.1.first_ref), channel_id=1, source_target_pairs={{0,8},{2,10},{4,12},{6,14},{8,16},{10,18},{12,20},{14,22},{16,24},... | collective-permute-start | bytes 589832 | tf_op jit(solution)/shard_map/ppermute | solution.py:19
  3.4 11.7 %collective-permute-start.4 = (bf16[384,256]{1,0:T(8,128)(2,1)S(1)}, bf16[384,256]{1,0:T(8,128)(2,1)S(1)}, u32[]{:S(2)}, u32[]{:S(2)}) collective-permute-start(bf16[384,256]{1,0:T(8,128)(2,1)S(1)} %collective-permute-done.second_ref), channel_id=1, source_target_pairs={{0,8},{2,10},{4,12},{6,14},{8,16},{10,18},{12,20},{14,22},{16,24},... | collective-permute-start | bytes 589832 | tf_op jit(solution)/shard_map/ppermute | solution.py:19
  10.7 27.0 %copy-start.2 = (bf16[6,512,128]{2,1,0:T(8,128)(2,1)}, bf16[6,512,128]{2,1,0:T(8,128)(2,1)S(1)}, u32[]{:S(2)}) copy-start(bf16[6,512,128]{2,1,0:T(8,128)(2,1)S(1)} %get-tuple-element.39.refs_0_) | copy-start | bytes 2359300
  15.2 12.6 %collective-permute-start.6 = (bf16[768,256]{1,0:T(8,128)(2,1)S(1)}, bf16[768,256]{1,0:T(8,128)(2,1)S(1)}, u32[]{:S(2)}, u32[]{:S(2)}) collective-permute-start(bf16[768,256]{1,0:T(8,128)(2,1)S(1)} %shard_map.57.refs_3_), channel_id=1, source_target_pairs={{0,8},{2,10},{4,12},{6,14},{8,16},{10,18},{12,20},{14,22},{16,24},... | collective-permute-start | bytes 1179656 | tf_op jit(solution)/shard_map/ppermute | solution.py:19
  15.2 13.3 %collective-permute-start.5 = (bf16[768,256]{1,0:T(8,128)(2,1)S(1)}, bf16[768,256]{1,0:T(8,128)(2,1)S(1)}, u32[]{:S(2)}, u32[]{:S(2)}) collective-permute-start(bf16[768,256]{1,0:T(8,128)(2,1)S(1)} %shard_map.57.refs_3_), channel_id=1, source_target_pairs={{0,4},{2,6},{4,0},{6,2},{8,12},{10,14},{12,8},{14,10},{16,20},{18,... | collective-permute-start | bytes 1179656 | tf_op jit(solution)/shard_map/ppermute | solution.py:23
  15.8 25.1 %collective-permute-start.10 = (bf16[512,1024]{1,0:T(8,128)(2,1)S(1)}, bf16[512,1024]{1,0:T(8,128)(2,1)S(1)}, u32[]{:S(2)}, u32[]{:S(2)}) collective-permute-start(bf16[512,1024]{1,0:T(8,128)(2,1)S(1)} %dynamic_slice.26), channel_id=1, source_target_pairs={{0,1},{1,0},{2,3},{3,2},{4,5},{5,4},{6,7},{7,6},{8,9},{9,8},{10,11... | collective-permute-start | bytes 3145736 | tf_op jit(solution)/shard_map/ppermute | solution.py:29
  27.8 9.9 %collective-permute-start.7 = (bf16[768,256]{1,0:T(8,128)(2,1)S(1)}, bf16[768,256]{1,0:T(8,128)(2,1)S(1)}, u32[]{:S(2)}, u32[]{:S(2)}) collective-permute-start(bf16[768,256]{1,0:T(8,128)(2,1)S(1)} %shard_map.60), channel_id=1, source_target_pairs={{0,4},{2,6},{4,0},{6,2},{8,12},{10,14},{12,8},{14,10},{16,20},{18,... | collective-permute-start | bytes 1179656 | tf_op jit(solution)/shard_map/ppermute | solution.py:23
  29.5 11.4 %copy-start.4 = (f32[6,512,128]{2,1,0:T(8,128)}, f32[6,512,128]{2,1,0:T(8,128)S(1)}, u32[]{:S(2)}) copy-start(f32[6,512,128]{2,1,0:T(8,128)S(1)} %get-tuple-element.46.refs_1_) | copy-start | bytes 4718596
  29.5 11.4 %copy-start.6 = (f32[6,512,128]{2,1,0:T(8,128)}, f32[6,512,128]{2,1,0:T(8,128)S(1)}, u32[]{:S(2)}) copy-start(f32[6,512,128]{2,1,0:T(8,128)S(1)} %get-tuple-element.47.refs_2_) | copy-start | bytes 4718596
  40.9 1.8 %collective-permute-start.8 = (bf16[384,512]{1,0:T(8,128)(2,1)S(1)}, bf16[384,512]{1,0:T(8,128)(2,1)S(1)}, u32[]{:S(2)}, u32[]{:S(2)}) collective-permute-start(bf16[384,512]{1,0:T(8,128)(2,1)S(1)} %shard_map.61), channel_id=1, source_target_pairs={{0,2},{2,0},{4,6},{6,4},{8,10},{10,8},{12,14},{14,12},{16,18},{18,... | collective-permute-start | bytes 1179656 | tf_op jit(solution)/shard_map/ppermute | solution.py:23
  41.0 25.6 %collective-permute-start.11 = (bf16[512,1024]{1,0:T(8,128)(2,1)S(1)}, bf16[512,1024]{1,0:T(8,128)(2,1)S(1)}, u32[]{:S(2)}, u32[]{:S(2)}) collective-permute-start(bf16[512,1024]{1,0:T(8,128)(2,1)S(1)} %collective-permute-done.10.refs_0_), channel_id=1, source_target_pairs={{0,8},{2,10},{4,12},{6,14},{8,0},{10,2},{12,4},{14,6},{16,24},{18,... | collective-permute-start | bytes 3145736 | tf_op jit(solution)/shard_map/ppermute | solution.py:23
  41.2 28.1 %collective-permute-start.12 = (bf16[512,1024]{1,0:T(8,128)(2,1)S(1)}, bf16[512,1024]{1,0:T(8,128)(2,1)S(1)}, u32[]{:S(2)}, u32[]{:S(2)}) collective-permute-start(bf16[512,1024]{1,0:T(8,128)(2,1)S(1)} %collective-permute-done.10.refs_0_), channel_id=1, source_target_pairs={{0,2},{2,0},{4,6},{6,4},{8,10},{10,8},{12,14},{14,12},{16,18},{18,... | collective-permute-start | bytes 3145736 | tf_op jit(solution)/shard_map/ppermute | solution.py:23
  42.7 1.1 %copy-start.3 = (bf16[6,512,128]{2,1,0:T(8,128)(2,1)S(1)}, bf16[6,512,128]{2,1,0:T(8,128)(2,1)}, u32[]{:S(2)}) copy-start(bf16[6,512,128]{2,1,0:T(8,128)(2,1)} %copy-done.2) | copy-start | bytes 2359300
  43.8 1.4 %copy-start.5 = (f32[6,512,128]{2,1,0:T(8,128)S(1)}, f32[6,512,128]{2,1,0:T(8,128)}, u32[]{:S(2)}) copy-start(f32[6,512,128]{2,1,0:T(8,128)} %copy-done.4) | copy-start | bytes 4718596
  45.2 1.4 %copy-start.7 = (f32[6,512,128]{2,1,0:T(8,128)S(1)}, f32[6,512,128]{2,1,0:T(8,128)}, u32[]{:S(2)}) copy-start(f32[6,512,128]{2,1,0:T(8,128)} %copy-done.6) | copy-start | bytes 4718596
  49.6 19.6 %collective-permute-start.9 = (bf16[384,1024]{1,0:T(8,128)(2,1)S(1)}, bf16[384,1024]{1,0:T(8,128)(2,1)S(1)}, u32[]{:S(2)}, u32[]{:S(2)}) collective-permute-start(bf16[384,1024]{1,0:T(8,128)(2,1)S(1)} %shard_map.62), channel_id=1, source_target_pairs={{0,1},{1,0},{2,3},{3,2},{4,5},{5,4},{6,7},{7,6},{8,9},{9,8},{10,11... | collective-permute-start | bytes 2359304 | tf_op jit(solution)/shard_map/ppermute | solution.py:29
  66.7 2.7 %collective-permute-start.14 = (bf16[512,512]{1,0:T(8,128)(2,1)S(1)}, bf16[512,512]{1,0:T(8,128)(2,1)S(1)}, u32[]{:S(2)}, u32[]{:S(2)}) collective-permute-start(bf16[512,512]{1,0:T(8,128)(2,1)S(1)} %get-tuple-element.51), channel_id=1, source_target_pairs={{0,2},{2,0},{4,6},{6,4},{8,10},{10,8},{12,14},{14,12},{16,18},{18,... | collective-permute-start | bytes 1572872 | tf_op jit(solution)/shard_map/ppermute | solution.py:23
  66.7 2.6 %collective-permute-start.13 = (bf16[512,512]{1,0:T(8,128)(2,1)S(1)}, bf16[512,512]{1,0:T(8,128)(2,1)S(1)}, u32[]{:S(2)}, u32[]{:S(2)}) collective-permute-start(bf16[512,512]{1,0:T(8,128)(2,1)S(1)} %get-tuple-element.52), channel_id=1, source_target_pairs={{0,2},{2,0},{4,6},{6,4},{8,10},{10,8},{12,14},{14,12},{16,18},{18,... | collective-permute-start | bytes 1572872 | tf_op jit(solution)/shard_map/ppermute | solution.py:23

commit v11 on v10

--- a/solution.py
+++ b/solution.py
@@ -239,7 +239,7 @@
         attend_last(core if stage == "own" else 1 - core)
 
 
-def attention_call(stage, distances, starts, recv_starts, operands):
+def attention_call(stage, distances, cost, starts, recv_starts, operands):
     tok, half = starts.shape[0] * BLOCK, starts.shape[0]
     rows = operands[1].shape[1] // (2 if stage == "first" else 1)
     blocks, n_head, n_pieces = 2 * half, rows // BLOCK, len(distances)
@@ -255,7 +255,6 @@
         outs, share = [jax.ShapeDtypeStruct((tok, width), jnp.bfloat16)], 0.5
         scratch = [pltpu.VMEM((half, rows, HEAD_SIZE), jnp.float32)] * 2 + scratch
     vmem, smem = pl.BlockSpec(memory_space=pltpu.VMEM), pl.BlockSpec(memory_space=pltpu.SMEM)
-    late = stage in ("own", "other")
     return pl.pallas_call(
         functools.partial(attention_kernel, stage, distances, n_head),
         out_shape=outs,
@@ -264,7 +263,7 @@
         scratch_shapes=scratch,
         compiler_params=pltpu.CompilerParams(vmem_limit_bytes=24 * 2**20),
         cost_estimate=pl.CostEstimate(
-            flops=int(share * blocks * rows * 2 * tok * HEAD_SIZE * (25 if late else 10)),
+            flops=int(cost * 1e9),
             bytes_accessed=8 * 2**20,
             transcendentals=int(share * blocks * rows * 2 * tok),
         ),
@@ -276,41 +275,46 @@
     me, head = lax.axis_index("ctx"), lax.axis_index("head")
     cols = out_weight.shape[1] // 2
     core = me % 2
-    places = (core, 1 - core, core * group, ((1 - head) * 2 + me // 4 % 2) * (cols // 2))
-    keys, (core, other, first_row, first_col) = lax.optimization_barrier((keys, places))
-
-    def part(x, index, size):
-        return lax.dynamic_slice_in_dim(x, index * size, size, 1)
-
-    mine = jnp.concatenate([part(keys, core, HEAD_SIZE), part(values, core, HEAD_SIZE)], 1)
-    theirs = jnp.concatenate([part(keys, other, HEAD_SIZE), part(values, other, HEAD_SIZE)], 1)
+    lanes = (core * HEAD_SIZE, (1 - core) * HEAD_SIZE)
+    corner = (core * group, ((1 - head) * 2 + me // 4 % 2) * (cols // 2))
+    keys, lanes, corner, here_col = lax.optimization_barrier((keys, lanes, corner, head * cols))
+
+    def cut(x, start, size):
+        return lax.dynamic_slice(x, start, size, allow_negative_indices=False)
+
+    def group_of(n):
+        size = (tok, HEAD_SIZE)
+        return jnp.concatenate([cut(keys, (0, lanes[n]), size), cut(values, (0, lanes[n]), size)], 1)
+
+    mine, theirs = group_of(0), group_of(1)
     recv, recv_starts = lax.optimization_barrier((swap(theirs, 1), swap(block_start, 1)))
     one_behind = [rotate(mine, 4), rotate(recv, 4)]
     q_recv = swap(queries, 1)
     (own,) = small_call(join_kernel, [(2 * tok, 2 * HEAD_SIZE)], (mine, recv))
     starts = (block_start, recv_starts)
     q_recv, weight = lax.optimization_barrier((q_recv, out_weight))
-    sent = lax.dynamic_slice(weight, (first_row, first_col), (group, cols // 2))
+    sent = cut(weight, corner, (group, cols // 2))
     q_recv, sent = lax.optimization_barrier((q_recv, sent))
     fetched = cross(sent, 0)
-    q, *state = attention_call("first", ((0, 0),), *starts, (queries, q_recv, own))
+    q, *state = attention_call("first", ((0, 0),), 5, *starts, (queries, q_recv, own))
     q, one_behind = lax.optimization_barrier((q, one_behind))
     (one_behind,) = small_call(join_kernel, [own.shape], one_behind)
     two_behind = rotate(one_behind, 4)
     across = swap(one_behind, 2)
     third = swap(small_call(pick_kernel, [own.shape], (own, two_behind))[0], 2)
-    state = attention_call("next", ((2, 2),), *starts, (q, *state, one_behind))
-    state = attention_call("next", ((1, 3), (4, 4)), *starts, (q, *state, across, two_behind))
-    _, fetched = lax.optimization_barrier((third, fetched))
+    state = attention_call("next", ((2, 2),), 2.1, *starts, (q, *state, one_behind))
+    across, fetched = lax.optimization_barrier((across, fetched))
+    state = attention_call("next", ((1, 3), (4, 4)), 4, *starts, (q, *state, across, two_behind))
     passed = swap(fetched, 4)
-    (o_other,) = attention_call("other", ((3, 1),), *starts, (q, *state, third))
-    (heads,) = attention_call("own", ((3, 1),), *starts, (q, *state, third, swap(o_other, 1)))
+    (o_other,) = attention_call("other", ((3, 1),), 2, *starts, (q, *state, third))
+    (heads,) = attention_call("own", ((3, 1),), 2, *starts, (q, *state, third, swap(o_other, 1)))
     heads_across = cross(heads, 0)
-    here = jnp.dot(heads, part(out_weight, head, cols), preferred_element_type=jnp.float32)
+    rows_here = cut(out_weight, (0, here_col), (2 * group, cols))
+    here = jnp.dot(heads, rows_here, preferred_element_type=jnp.float32)
     here = here.astype(jnp.bfloat16)
     _, late = lax.optimization_barrier((here, passed))
     weights = [fetched, passed, swap(fetched, 1)]
-    weights += [swap(part(late, n, cols // 4), 1) for n in range(2)]
+    weights += [swap(x, 1) for x in jnp.split(late, 2, 1)]
     return project(here, heads_across, weights)
 
 

time: 72.8 us -> 68.5 us (0.941)
  local copies, waits for them, and re-layouts: 7 us -> 3.27 us
  matrix products: 3.98 us -> 2.07 us
  starting transfers between devices: 9.49 us -> 11.1 us
    ppermute x10, waiting for transfers between devices: 20.8 us -> 11.2 us  [swap(): lax.ppermute(x, 'ctx', [(i, i ^ mask) for i in range(lax.axis_size('ctx'))])]
    ppermute x2, waiting for transfers between devices: 2.07 us -> 11.2 us  [cross(): return lax.ppermute(x, ('ctx', 'head'), route)]
    unnamed x16 -> x8, local copies, waits for them, and re-layouts: 3.97 us -> 0.01 us
    dot_general x1, matrix products: 3.98 us -> 2.07 us  [per_device(): here = jnp.dot(heads, rows_here, preferred_element_type=jnp.float32)]
    ppermute x10, starting transfers between devices: 3.12 us -> 4.66 us  [swap(): lax.ppermute(x, 'ctx', [(i, i ^ mask) for i in range(lax.axis_size('ctx'))])]
    ppermute x3, waiting for transfers between devices: 14 us -> 14.8 us  [rotate(): return lax.ppermute(x, 'ctx', [(i, (i + distance) % n) for i in range(n)])]
    dynamic_slice x3 -> x2, local copies, waits for them, and re-layouts: 3.03 us -> 3.18 us  [cut(): return lax.dynamic_slice(x, start, size, allow_negative_indices=False)]
  transfers between devices with their start and end apart: 15 -> 15, of which waited for: 8 -> 7; matrix products, arithmetic and copies ran while one was open for 10% -> 8% of each run, Pallas kernels for 16% -> 17%
where the time goes in v11:
time: 68.5 us; the launch traced here: 68.4 us
  waiting for transfers between devices  37.2 us (54%)
  Pallas kernels  14.4 us (21%)
  starting transfers between devices  11.1 us (16%)
  local copies, waits for them, and re-layouts  3.27 us (5%)
  matrix products  2.07 us (3%)
    ppermute x3, waiting for transfers between devices, rotate(): return lax.ppermute(x, 'ctx', [(i, (i + distance) % n) for i in range(n)])  14.8 us
    pallas_call x5, Pallas kernels, attention_call(): pl.pallas_call(functools.partial(attention_kernel, stage, distances, n_he...  11.7 us
    ppermute x2, waiting for transfers between devices, cross(): return lax.ppermute(x, ('ctx', 'head'), route)  11.2 us
    ppermute x10, waiting for transfers between devices, swap(): lax.ppermute(x, 'ctx', [(i, i ^ mask) for i in range(lax.axis_size('ctx'))])  11.2 us
    ppermute x10, starting transfers between devices, swap(): lax.ppermute(x, 'ctx', [(i, i ^ mask) for i in range(lax.axis_size('ctx'))])  4.66 us
    ppermute x3, starting transfers between devices, rotate(): return lax.ppermute(x, 'ctx', [(i, (i + distance) % n) for i in range(n)])  3.27 us
    dynamic_slice x2, local copies, waits for them, and re-layouts, cut(): return lax.dynamic_slice(x, start, size, allow_negative_indices=False)  3.18 us
    ppermute x2, starting transfers between devices, cross(): return lax.ppermute(x, ('ctx', 'head'), route)  3.17 us
  transfers between devices with their start and end apart: 15, of which 7 were waited for; matrix products, arithmetic and copies ran while one was open for 8% of the time, Pallas kernels for 17%

profile of v11, /device:TPU:2, one launch (start us, length us, event | category | flops | bytes accessed | tf_op | source)
XLA Modules:
  0.0 68.4 jit_solution(874435854165571449)
XLA Ops:
  0.0 0.0 collective-permute-start.2
  0.0 1.3 %constant_dynamic-slice_fusion = (bf16[384,128]{1,0:T(8,128)(2,1)S(1)}, bf16[384,128]{1,0:T(8,128)(2,1)S(1)}, bf16[384,128]{1,0:T(8,128)(2,1)S(1)}, bf16[384,128]{1,0:T(8,128)(2,1)S(1)}) fusion(bf16[384,256]{1,0:T(8,128)(2,1)} %param.7, s32[]{:T(128)S(6)} %mul.18, s32[]{:T(128)S(6)} %mul.19, bf16[384,256]{1,0:T(8,128)(2,1)} %param.6), kind=kLoop, calls=%fused_computation.6 | loop fusion | bytes 786440 | tf_op jit(solution)/shard_map/dynamic_slice | solution.py:283
  1.3 0.6 collective-permute-start
  1.9 0.1 collective-permute-start.1
  2.0 0.0 copy-start
  2.0 0.0 copy-start.1
  2.0 1.6 %collective-permute-start.3 = (bf16[384,256]{1,0:T(8,128)(2,1)S(1)}, bf16[384,256]{1,0:T(8,128)(2,1)S(1)}, u32[]{:S(2)}, u32[]{:S(2)}) collective-permute-start(bf16[384,256]{1,0:T(8,128)(2,1)S(1)} %pad_maximum_fusion.1.first_ref), channel_id=1, source_target_pairs={{0,8},{2,10},{4,12},{6,14},{8,16},{10,18},{12,20},{14,22},{16,24},... | collective-permute-start | bytes 589832 | tf_op jit(solution)/shard_map/ppermute | solution.py:19
  3.7 0.0 collective-permute-done.1.recv_starts_ref
  3.7 0.0 collective-permute-done.second_ref
  3.7 1.6 %collective-permute-start.4 = (bf16[384,256]{1,0:T(8,128)(2,1)S(1)}, bf16[384,256]{1,0:T(8,128)(2,1)S(1)}, u32[]{:S(2)}, u32[]{:S(2)}) collective-permute-start(bf16[384,256]{1,0:T(8,128)(2,1)S(1)} %collective-permute-done.second_ref), channel_id=1, source_target_pairs={{0,8},{2,10},{4,12},{6,14},{8,16},{10,18},{12,20},{14,22},{16,24},... | collective-permute-start | bytes 589832 | tf_op jit(solution)/shard_map/ppermute | solution.py:19
  5.3 0.0 collective-permute-done.2.refs_1_
  5.3 1.9 %dynamic_slice.20 = bf16[512,1024]{1,0:T(8,128)(2,1)S(1)} dynamic-slice(bf16[1024,4096]{1,0:T(8,128)(2,1)} %param.9, s32[]{:T(128)S(6)} %mul.20, s32[]{:T(128)S(6)} %mul.22), dynamic_slice_sizes={512,1024} | dynamic-slice | bytes 2097156 | tf_op jit(solution)/shard_map/dynamic_slice | solution.py:283
  7.2 1.6 %collective-permute-start.6 = (bf16[512,1024]{1,0:T(8,128)(2,1)S(1)}, bf16[512,1024]{1,0:T(8,128)(2,1)S(1)}, u32[]{:S(2)}, u32[]{:S(2)}) collective-permute-start(bf16[512,1024]{1,0:T(8,128)(2,1)S(1)} %dynamic_slice.20), channel_id=1, source_target_pairs={{0,1},{1,0},{2,3},{3,2},{4,5},{5,4},{6,7},{7,6},{8,9},{9,8},{10,11... | collective-permute-start | bytes 3145736 | tf_op jit(solution)/shard_map/ppermute | solution.py:29
  8.8 0.0 copy-done
  8.8 0.0 copy-done.1
  8.8 3.7 %shard_map.56 = (bf16[6,512,128]{2,1,0:T(8,128)(2,1)S(1)}, f32[6,512,128]{2,1,0:T(8,128)S(1)}, f32[6,512,128]{2,1,0:T(8,128)S(1)}) custom-call(s32[3]{0:T(128)S(1)} %copy-done.1, s32[3]{0:T(128)S(1)} %collective-permute-done.1.recv_starts_ref, bf16[384,1024]{1,0:T(8,128)(2,1)S(1)} %copy-done, bf16[384,1024]{1,0:T(8,128)(2,1)S(1)} %collective-permute-done.2.refs_1_, ...), custom_call_target="tpu_custom_call" | custom-call | flops 5000000000 | bytes 8388608 | tf_op jit(solution)/shard_map/pallas_call | solution.py:258
  12.5 0.0 collective-permute-done.3.first_ref
  12.5 2.9 %collective-permute-done.4.second_ref = bf16[384,256]{1,0:T(8,128)(2,1)S(1)} collective-permute-done((bf16[384,256]{1,0:T(8,128)(2,1)S(1)}, bf16[384,256]{1,0:T(8,128)(2,1)S(1)}, u32[]{:S(2)}, u32[]{:S(2)}) %collective-permute-start.4) | collective-permute-done | bytes 196640 | tf_op jit(solution)/shard_map/ppermute | solution.py:19
  15.4 0.1 collective-permute-start.7
  15.5 0.6 collective-permute-start.5
  16.1 11.9 %collective-permute-done.7.refs_4_.odd_ref = bf16[768,256]{1,0:T(8,128)(2,1)S(1)} collective-permute-done((bf16[768,256]{1,0:T(8,128)(2,1)S(1)}, bf16[768,256]{1,0:T(8,128)(2,1)S(1)}, u32[]{:S(2)}, u32[]{:S(2)}) %collective-permute-start.7) | collective-permute-done | bytes 393248 | tf_op jit(solution)/shard_map/ppermute | solution.py:19
  28.0 0.7 %collective-permute-start.8 = (bf16[768,256]{1,0:T(8,128)(2,1)S(1)}, bf16[768,256]{1,0:T(8,128)(2,1)S(1)}, u32[]{:S(2)}, u32[]{:S(2)}) collective-permute-start(bf16[768,256]{1,0:T(8,128)(2,1)S(1)} %shard_map.60), channel_id=1, source_target_pairs={{0,4},{2,6},{4,0},{6,2},{8,12},{10,14},{12,8},{14,10},{16,20},{18,... | collective-permute-start | bytes 1179656 | tf_op jit(solution)/shard_map/ppermute | solution.py:23
  28.8 0.8 %shard_map.58 = (f32[6,512,128]{2,1,0:T(8,128)S(1)}, f32[6,512,128]{2,1,0:T(8,128)S(1)}) custom-call(s32[3]{0:T(128)S(1)} %copy-done.1, s32[3]{0:T(128)S(1)} %collective-permute-done.1.recv_starts_ref, bf16[6,512,128]{2,1,0:T(8,128)(2,1)S(1)} %get-tuple-element.41.refs_0_, f32[6,512,128]{2,1,0:T(8,128)S(1)} %get-tuple-element.42.refs_1_, ...), custom_call_target="tpu_custom_call" | custom-call | flops 2100000000 | bytes 8388608 | tf_op jit(solution)/shard_map/pallas_call | solution.py:258
  29.6 0.0 collective-permute-done.5.refs_3_
  29.6 2.5 %collective-permute-done.6.refs_0_ = bf16[512,1024]{1,0:T(8,128)(2,1)S(1)} collective-permute-done((bf16[512,1024]{1,0:T(8,128)(2,1)S(1)}, bf16[512,1024]{1,0:T(8,128)(2,1)S(1)}, u32[]{:S(2)}, u32[]{:S(2)}) %collective-permute-start.6) | collective-permute-done | bytes 1048608 | tf_op jit(solution)/shard_map/ppermute | solution.py:29
  32.2 1.5 %collective-permute-start.11 = (bf16[512,1024]{1,0:T(8,128)(2,1)S(1)}, bf16[512,1024]{1,0:T(8,128)(2,1)S(1)}, u32[]{:S(2)}, u32[]{:S(2)}) collective-permute-start(bf16[512,1024]{1,0:T(8,128)(2,1)S(1)} %collective-permute-done.6.refs_0_), channel_id=1, source_target_pairs={{0,8},{2,10},{4,12},{6,14},{8,0},{10,2},{12,4},{14,6},{16,24},{18,... | collective-permute-start | bytes 3145736 | tf_op jit(solution)/shard_map/ppermute | solution.py:23
  33.7 0.0 slice-start
  33.7 0.9 %shard_map.59 = (f32[6,512,128]{2,1,0:T(8,128)S(1)}, f32[6,512,128]{2,1,0:T(8,128)S(1)}) custom-call(s32[3]{0:T(128)S(1)} %copy-done.1, s32[3]{0:T(128)S(1)} %collective-permute-done.1.recv_starts_ref, bf16[6,512,128]{2,1,0:T(8,128)(2,1)S(1)} %get-tuple-element.41.refs_0_, f32[6,512,128]{2,1,0:T(8,128)S(1)} %get-tuple-element.46.refs_1_, ...), custom_call_target="tpu_custom_call" | custom-call | flops 4000000000 | bytes 8388608 | tf_op jit(solution)/shard_map/pallas_call | solution.py:258
  34.7 3.3 %collective-permute-done.8.refs_3_ = bf16[768,256]{1,0:T(8,128)(2,1)S(1)} collective-permute-done((bf16[768,256]{1,0:T(8,128)(2,1)S(1)}, bf16[768,256]{1,0:T(8,128)(2,1)S(1)}, u32[]{:S(2)}, u32[]{:S(2)}) %collective-permute-start.8) | collective-permute-done | bytes 393248 | tf_op jit(solution)/shard_map/ppermute | solution.py:23
  38.0 0.0 slice-start.1
  38.0 3.2 %shard_map.61 = bf16[384,512]{1,0:T(8,128)(2,1)S(1)} custom-call(s32[3]{0:T(128)S(1)} %copy-done.1, s32[3]{0:T(128)S(1)} %collective-permute-done.1.recv_starts_ref, bf16[6,512,128]{2,1,0:T(8,128)(2,1)S(1)} %get-tuple-element.41.refs_0_, f32[6,512,128]{2,1,0:T(8,128)S(1)} %get-tuple-element.50.refs_1_, f32[6,512,128]{2,1,0:T(8,128)S(1)} %get-tuple-element.51.refs_2_, ...), custom_call_target="tpu_custom_call" | custom-call | flops 2000000000 | bytes 8388608 | tf_op jit(solution)/shard_map/pallas_call | solution.py:258
  41.1 0.1 collective-permute-start.9
  41.2 0.5 collective-permute-start.12
  41.7 1.2 %collective-permute-done.9.refs_4_ = bf16[384,512]{1,0:T(8,128)(2,1)S(1)} collective-permute-done((bf16[384,512]{1,0:T(8,128)(2,1)S(1)}, bf16[384,512]{1,0:T(8,128)(2,1)S(1)}, u32[]{:S(2)}, u32[]{:S(2)}) %collective-permute-start.9) | collective-permute-done | bytes 393248 | tf_op jit(solution)/shard_map/ppermute | solution.py:23
  42.9 3.0 %shard_map.62 = bf16[384,1024]{1,0:T(8,128)(2,1)S(1)} custom-call(s32[3]{0:T(128)S(1)} %copy-done.1, s32[3]{0:T(128)S(1)} %collective-permute-done.1.recv_starts_ref, bf16[6,512,128]{2,1,0:T(8,128)(2,1)S(1)} %get-tuple-element.41.refs_0_, f32[6,512,128]{2,1,0:T(8,128)S(1)} %get-tuple-element.50.refs_1_, f32[6,512,128]{2,1,0:T(8,128)S(1)} %get-tuple-element.51.refs_2_, ...), custom_call_target="tpu_custom_call" | custom-call | flops 2000000000 | bytes 8388608 | tf_op jit(solution)/shard_map/pallas_call | solution.py:258
  45.9 1.6 %collective-permute-start.10 = (bf16[384,1024]{1,0:T(8,128)(2,1)S(1)}, bf16[384,1024]{1,0:T(8,128)(2,1)S(1)}, u32[]{:S(2)}, u32[]{:S(2)}) collective-permute-start(bf16[384,1024]{1,0:T(8,128)(2,1)S(1)} %shard_map.62), channel_id=1, source_target_pairs={{0,1},{1,0},{2,3},{3,2},{4,5},{5,4},{6,7},{7,6},{8,9},{9,8},{10,11... | collective-permute-start | bytes 2359304 | tf_op jit(solution)/shard_map/ppermute | solution.py:29
  47.5 0.0 slice-done
  47.5 0.0 slice-done.1
  47.5 2.1 %fusion.2.given_ref = bf16[384,2048]{1,0:T(8,128)(2,1)S(1)} fusion(bf16[384,1024]{1,0:T(8,128)(2,1)S(1)} %shard_map.62, bf16[1024,4096]{1,0:T(8,128)(2,1)S(1)} %bitcast.2, s32[]{:T(128)S(6)} %mul.23), kind=kOutput, calls=%fused_computation.2 | convolution fusion | flops 1611399168 | bytes 6553604 | tf_op jit(solution)/shard_map/dot_general | solution.py:313
  49.6 6.7 %collective-permute-done.11.refs_1_ = bf16[512,1024]{1,0:T(8,128)(2,1)S(1)} collective-permute-done((bf16[512,1024]{1,0:T(8,128)(2,1)S(1)}, bf16[512,1024]{1,0:T(8,128)(2,1)S(1)}, u32[]{:S(2)}, u32[]{:S(2)}) %collective-permute-start.11) | collective-permute-done | bytes 1048608 | tf_op jit(solution)/shard_map/ppermute | solution.py:23
  56.3 0.1 fusion.6
  56.3 0.1 collective-permute-start.14
  56.4 0.5 collective-permute-start.13
  56.9 0.0 collective-permute-done.12.refs_2_
  56.9 8.6 %collective-permute-done.10.heads_ref = bf16[384,1024]{1,0:T(8,128)(2,1)S(1)} collective-permute-done((bf16[384,1024]{1,0:T(8,128)(2,1)S(1)}, bf16[384,1024]{1,0:T(8,128)(2,1)S(1)}, u32[]{:S(2)}, u32[]{:S(2)}) %collective-permute-start.10) | collective-permute-done | bytes 786464 | tf_op jit(solution)/shard_map/ppermute | solution.py:29
  65.6 0.0 collective-permute-done.14.refs_4_
  65.6 0.0 collective-permute-done.13.refs_3_
  65.6 2.6 %shard_map.63 = bf16[384,2048]{1,0:T(8,128)(2,1)} custom-call(bf16[384,2048]{1,0:T(8,128)(2,1)S(1)} %fusion.2.given_ref, bf16[384,1024]{1,0:T(8,128)(2,1)S(1)} %collective-permute-done.10.heads_ref, bf16[512,1024]{1,0:T(8,128)(2,1)S(1)} %collective-permute-done.6.refs_0_, bf16[512,1024]{1,0:T(8,128)(2,1)S(1)} %collective-permute-done.11.refs_1_, ...), custom_call_target="tpu_custom_call" | custom-call | flops 1610612736 | bytes 4194304 | tf_op jit(solution)/shard_map/pallas_call | solution.py:87
  (6 shorter events, 0.1 us)
Async XLA Ops:
  0.0 5.3 %collective-permute-start.2 = (bf16[384,1024]{1,0:T(8,128)(2,1)}, bf16[384,1024]{1,0:T(8,128)(2,1)S(1)}, u32[]{:S(2)}, u32[]{:S(2)}) collective-permute-start(bf16[384,1024]{1,0:T(8,128)(2,1)} %refs_0_.1), channel_id=1, source_target_pairs={{0,2},{2,0},{4,6},{6,4},{8,10},{10,8},{12,14},{14,12},{16,18},{18,... | collective-permute-start | bytes 2359304 | tf_op jit(solution)/shard_map/ppermute | solution.py:23
  1.3 2.3 %collective-permute-start = (bf16[384,256]{1,0:T(8,128)(2,1)S(1)}, bf16[384,256]{1,0:T(8,128)(2,1)S(1)}, u32[]{:S(2)}, u32[]{:S(2)}) collective-permute-start(bf16[384,256]{1,0:T(8,128)(2,1)S(1)} %pad_maximum_fusion), channel_id=1, source_target_pairs={{0,2},{2,0},{4,6},{6,4},{8,10},{10,8},{12,14},{14,12},{16,18},{18,... | collective-permute-start | bytes 589832 | tf_op jit(solution)/shard_map/ppermute | solution.py:23
  1.9 1.7 %collective-permute-start.1 = (s32[3]{0:T(128)}, s32[3]{0:T(128)S(1)}, u32[]{:S(2)}, u32[]{:S(2)}) collective-permute-start(s32[3]{0:T(128)} %starts_ref.9), channel_id=1, source_target_pairs={{0,2},{2,0},{4,6},{6,4},{8,10},{10,8},{12,14},{14,12},{16,18},{18,... | collective-permute-start | bytes 44 | tf_op jit(solution)/shard_map/ppermute | solution.py:23
  2.0 6.8 %copy-start = (bf16[384,1024]{1,0:T(8,128)(2,1)S(1)}, bf16[384,1024]{1,0:T(8,128)(2,1)}, u32[]{:S(2)}) copy-start(bf16[384,1024]{1,0:T(8,128)(2,1)} %refs_0_.1) | copy-start | bytes 2359300
  2.0 6.8 %copy-start.1 = (s32[3]{0:T(128)S(1)}, s32[3]{0:T(128)}, u32[]{:S(2)}) copy-start(s32[3]{0:T(128)} %starts_ref.9) | copy-start | bytes 40
  2.0 10.5 %collective-permute-start.3 = (bf16[384,256]{1,0:T(8,128)(2,1)S(1)}, bf16[384,256]{1,0:T(8,128)(2,1)S(1)}, u32[]{:S(2)}, u32[]{:S(2)}) collective-permute-start(bf16[384,256]{1,0:T(8,128)(2,1)S(1)} %pad_maximum_fusion.1.first_ref), channel_id=1, source_target_pairs={{0,8},{2,10},{4,12},{6,14},{8,16},{10,18},{12,20},{14,22},{16,24},... | collective-permute-start | bytes 589832 | tf_op jit(solution)/shard_map/ppermute | solution.py:19
  3.7 11.7 %collective-permute-start.4 = (bf16[384,256]{1,0:T(8,128)(2,1)S(1)}, bf16[384,256]{1,0:T(8,128)(2,1)S(1)}, u32[]{:S(2)}, u32[]{:S(2)}) collective-permute-start(bf16[384,256]{1,0:T(8,128)(2,1)S(1)} %collective-permute-done.second_ref), channel_id=1, source_target_pairs={{0,8},{2,10},{4,12},{6,14},{8,16},{10,18},{12,20},{14,22},{16,24},... | collective-permute-start | bytes 589832 | tf_op jit(solution)/shard_map/ppermute | solution.py:19
  7.2 25.0 %collective-permute-start.6 = (bf16[512,1024]{1,0:T(8,128)(2,1)S(1)}, bf16[512,1024]{1,0:T(8,128)(2,1)S(1)}, u32[]{:S(2)}, u32[]{:S(2)}) collective-permute-start(bf16[512,1024]{1,0:T(8,128)(2,1)S(1)} %dynamic_slice.20), channel_id=1, source_target_pairs={{0,1},{1,0},{2,3},{3,2},{4,5},{5,4},{6,7},{7,6},{8,9},{9,8},{10,11... | collective-permute-start | bytes 3145736 | tf_op jit(solution)/shard_map/ppermute | solution.py:29
  15.4 12.6 %collective-permute-start.7 = (bf16[768,256]{1,0:T(8,128)(2,1)S(1)}, bf16[768,256]{1,0:T(8,128)(2,1)S(1)}, u32[]{:S(2)}, u32[]{:S(2)}) collective-permute-start(bf16[768,256]{1,0:T(8,128)(2,1)S(1)} %shard_map.57.refs_3_), channel_id=1, source_target_pairs={{0,8},{2,10},{4,12},{6,14},{8,16},{10,18},{12,20},{14,22},{16,24},... | collective-permute-start | bytes 1179656 | tf_op jit(solution)/shard_map/ppermute | solution.py:19
  15.5 14.1 %collective-permute-start.5 = (bf16[768,256]{1,0:T(8,128)(2,1)S(1)}, bf16[768,256]{1,0:T(8,128)(2,1)S(1)}, u32[]{:S(2)}, u32[]{:S(2)}) collective-permute-start(bf16[768,256]{1,0:T(8,128)(2,1)S(1)} %shard_map.57.refs_3_), channel_id=1, source_target_pairs={{0,4},{2,6},{4,0},{6,2},{8,12},{10,14},{12,8},{14,10},{16,20},{18,... | collective-permute-start | bytes 1179656 | tf_op jit(solution)/shard_map/ppermute | solution.py:23
  28.0 9.9 %collective-permute-start.8 = (bf16[768,256]{1,0:T(8,128)(2,1)S(1)}, bf16[768,256]{1,0:T(8,128)(2,1)S(1)}, u32[]{:S(2)}, u32[]{:S(2)}) collective-permute-start(bf16[768,256]{1,0:T(8,128)(2,1)S(1)} %shard_map.60), channel_id=1, source_target_pairs={{0,4},{2,6},{4,0},{6,2},{8,12},{10,14},{12,8},{14,10},{16,20},{18,... | collective-permute-start | bytes 1179656 | tf_op jit(solution)/shard_map/ppermute | solution.py:23
  32.2 24.1 %collective-permute-start.11 = (bf16[512,1024]{1,0:T(8,128)(2,1)S(1)}, bf16[512,1024]{1,0:T(8,128)(2,1)S(1)}, u32[]{:S(2)}, u32[]{:S(2)}) collective-permute-start(bf16[512,1024]{1,0:T(8,128)(2,1)S(1)} %collective-permute-done.6.refs_0_), channel_id=1, source_target_pairs={{0,8},{2,10},{4,12},{6,14},{8,0},{10,2},{12,4},{14,6},{16,24},{18,... | collective-permute-start | bytes 3145736 | tf_op jit(solution)/shard_map/ppermute | solution.py:23
  33.7 13.8 %slice-start = ((s8[8388608]{0:T(1024)(128)(4,1)}), s8[4194304]{0:T(1024)(128)(4,1)S(1)}, s32[]{:S(2)}) async-start(s8[8388608]{0:T(1024)(128)(4,1)} %bitcast.1), calls=%async_computation | async-start | bytes 8388608
  38.0 9.6 %slice-start.1 = ((s8[8388608]{0:T(1024)(128)(4,1)}), s8[4194304]{0:T(1024)(128)(4,1)S(1)}, s32[]{:S(2)}) async-start(s8[8388608]{0:T(1024)(128)(4,1)} %bitcast.1), calls=%async_computation.1 | async-start | bytes 8388608
  41.1 1.8 %collective-permute-start.9 = (bf16[384,512]{1,0:T(8,128)(2,1)S(1)}, bf16[384,512]{1,0:T(8,128)(2,1)S(1)}, u32[]{:S(2)}, u32[]{:S(2)}) collective-permute-start(bf16[384,512]{1,0:T(8,128)(2,1)S(1)} %shard_map.61), channel_id=1, source_target_pairs={{0,2},{2,0},{4,6},{6,4},{8,10},{10,8},{12,14},{14,12},{16,18},{18,... | collective-permute-start | bytes 1179656 | tf_op jit(solution)/shard_map/ppermute | solution.py:23
  41.2 15.7 %collective-permute-start.12 = (bf16[512,1024]{1,0:T(8,128)(2,1)S(1)}, bf16[512,1024]{1,0:T(8,128)(2,1)S(1)}, u32[]{:S(2)}, u32[]{:S(2)}) collective-permute-start(bf16[512,1024]{1,0:T(8,128)(2,1)S(1)} %collective-permute-done.6.refs_0_), channel_id=1, source_target_pairs={{0,2},{2,0},{4,6},{6,4},{8,10},{10,8},{12,14},{14,12},{16,18},{18,... | collective-permute-start | bytes 3145736 | tf_op jit(solution)/shard_map/ppermute | solution.py:23
  45.9 19.6 %collective-permute-start.10 = (bf16[384,1024]{1,0:T(8,128)(2,1)S(1)}, bf16[384,1024]{1,0:T(8,128)(2,1)S(1)}, u32[]{:S(2)}, u32[]{:S(2)}) collective-permute-start(bf16[384,1024]{1,0:T(8,128)(2,1)S(1)} %shard_map.62), channel_id=1, source_target_pairs={{0,1},{1,0},{2,3},{3,2},{4,5},{5,4},{6,7},{7,6},{8,9},{9,8},{10,11... | collective-permute-start | bytes 2359304 | tf_op jit(solution)/shard_map/ppermute | solution.py:29
  56.3 9.2 %collective-permute-start.14 = (bf16[512,512]{1,0:T(8,128)(2,1)S(1)}, bf16[512,512]{1,0:T(8,128)(2,1)S(1)}, u32[]{:S(2)}, u32[]{:S(2)}) collective-permute-start(bf16[512,512]{1,0:T(8,128)(2,1)S(1)} %get-tuple-element.55), channel_id=1, source_target_pairs={{0,2},{2,0},{4,6},{6,4},{8,10},{10,8},{12,14},{14,12},{16,18},{18,... | collective-permute-start | bytes 1572872 | tf_op jit(solution)/shard_map/ppermute | solution.py:23
  56.4 9.2 %collective-permute-start.13 = (bf16[512,512]{1,0:T(8,128)(2,1)S(1)}, bf16[512,512]{1,0:T(8,128)(2,1)S(1)}, u32[]{:S(2)}, u32[]{:S(2)}) collective-permute-start(bf16[512,512]{1,0:T(8,128)(2,1)S(1)} %get-tuple-element.56), channel_id=1, source_target_pairs={{0,2},{2,0},{4,6},{6,4},{8,10},{10,8},{12,14},{14,12},{16,18},{18,... | collective-permute-start | bytes 1572872 | tf_op jit(solution)/shard_map/ppermute | solution.py:23

commit v12 on v11

--- a/solution.py
+++ b/solution.py
@@ -301,10 +301,11 @@
     (one_behind,) = small_call(join_kernel, [own.shape], one_behind)
     two_behind = rotate(one_behind, 4)
     across = swap(one_behind, 2)
-    third = swap(small_call(pick_kernel, [own.shape], (own, two_behind))[0], 2)
     state = attention_call("next", ((2, 2),), 2.1, *starts, (q, *state, one_behind))
-    across, fetched = lax.optimization_barrier((across, fetched))
+    _, ready = lax.optimization_barrier((state[0], two_behind))
+    third = swap(small_call(pick_kernel, [own.shape], (own, ready))[0], 2)
     state = attention_call("next", ((1, 3), (4, 4)), 4, *starts, (q, *state, across, two_behind))
+    _, fetched = lax.optimization_barrier((state[0], fetched))
     passed = swap(fetched, 4)
     (o_other,) = attention_call("other", ((3, 1),), 2, *starts, (q, *state, third))
     (heads,) = attention_call("own", ((3, 1),), 2, *starts, (q, *state, third, swap(o_other, 1)))

time: 68.5 us -> 68.5 us (level)
    ppermute x10, waiting for transfers between devices: 11.2 us -> 12.1 us  [swap(): lax.ppermute(x, 'ctx', [(i, i ^ mask) for i in range(lax.axis_size('ctx'))])]
    ppermute x3, waiting for transfers between devices: 14.8 us -> 13.9 us  [rotate(): return lax.ppermute(x, 'ctx', [(i, (i + distance) % n) for i in range(n)])]
where the time goes in v12:
time: 68.5 us; the launch traced here: 68.4 us
  waiting for transfers between devices  37.2 us (54%)
  Pallas kernels  14.4 us (21%)
  starting transfers between devices  11.1 us (16%)
  local copies, waits for them, and re-layouts  3.27 us (5%)
  matrix products  2.07 us (3%)
    ppermute x3, waiting for transfers between devices, rotate(): return lax.ppermute(x, 'ctx', [(i, (i + distance) % n) for i in range(n)])  13.9 us
    ppermute x10, waiting for transfers between devices, swap(): lax.ppermute(x, 'ctx', [(i, i ^ mask) for i in range(lax.axis_size('ctx'))])  12.1 us
    pallas_call x5, Pallas kernels, attention_call(): pl.pallas_call(functools.partial(attention_kernel, stage, distances, n_he...  11.7 us
    ppermute x2, waiting for transfers between devices, cross(): return lax.ppermute(x, ('ctx', 'head'), route)  11.1 us
    ppermute x10, starting transfers between devices, swap(): lax.ppermute(x, 'ctx', [(i, i ^ mask) for i in range(lax.axis_size('ctx'))])  4.66 us
    ppermute x3, starting transfers between devices, rotate(): return lax.ppermute(x, 'ctx', [(i, (i + distance) % n) for i in range(n)])  3.27 us
    dynamic_slice x2, local copies, waits for them, and re-layouts, cut(): return lax.dynamic_slice(x, start, size, allow_negative_indices=False)  3.18 us
    ppermute x2, starting transfers between devices, cross(): return lax.ppermute(x, ('ctx', 'head'), route)  3.17 us
  transfers between devices with their start and end apart: 15, of which 7 were waited for; matrix products, arithmetic and copies ran while one was open for 8% of the time, Pallas kernels for 17%

profile of v12, /device:TPU:2, one launch (start us, length us, event | category | flops | bytes accessed | tf_op | source)
XLA Modules:
  0.0 68.4 jit_solution(7236500383787227356)
XLA Ops:
  0.0 0.0 collective-permute-start.2
  0.0 1.3 %constant_dynamic-slice_fusion = (bf16[384,128]{1,0:T(8,128)(2,1)S(1)}, bf16[384,128]{1,0:T(8,128)(2,1)S(1)}, bf16[384,128]{1,0:T(8,128)(2,1)S(1)}, bf16[384,128]{1,0:T(8,128)(2,1)S(1)}) fusion(bf16[384,256]{1,0:T(8,128)(2,1)} %param.7, s32[]{:T(128)S(6)} %mul.18, s32[]{:T(128)S(6)} %mul.19, bf16[384,256]{1,0:T(8,128)(2,1)} %param.6), kind=kLoop, calls=%fused_computation.6 | loop fusion | bytes 786440 | tf_op jit(solution)/shard_map/dynamic_slice | solution.py:283
  1.3 0.6 collective-permute-start
  1.9 0.1 collective-permute-start.1
  2.0 0.0 copy-start
  2.0 0.0 copy-start.1
  2.0 1.6 %collective-permute-start.3 = (bf16[384,256]{1,0:T(8,128)(2,1)S(1)}, bf16[384,256]{1,0:T(8,128)(2,1)S(1)}, u32[]{:S(2)}, u32[]{:S(2)}) collective-permute-start(bf16[384,256]{1,0:T(8,128)(2,1)S(1)} %pad_maximum_fusion.1.first_ref), channel_id=1, source_target_pairs={{0,8},{2,10},{4,12},{6,14},{8,16},{10,18},{12,20},{14,22},{16,24},... | collective-permute-start | bytes 589832 | tf_op jit(solution)/shard_map/ppermute | solution.py:19
  3.7 0.0 collective-permute-done.1.recv_starts_ref
  3.7 0.0 collective-permute-done.second_ref
  3.7 1.6 %collective-permute-start.4 = (bf16[384,256]{1,0:T(8,128)(2,1)S(1)}, bf16[384,256]{1,0:T(8,128)(2,1)S(1)}, u32[]{:S(2)}, u32[]{:S(2)}) collective-permute-start(bf16[384,256]{1,0:T(8,128)(2,1)S(1)} %collective-permute-done.second_ref), channel_id=1, source_target_pairs={{0,8},{2,10},{4,12},{6,14},{8,16},{10,18},{12,20},{14,22},{16,24},... | collective-permute-start | bytes 589832 | tf_op jit(solution)/shard_map/ppermute | solution.py:19
  5.3 0.0 collective-permute-done.2.refs_1_
  5.3 1.9 %dynamic_slice.20 = bf16[512,1024]{1,0:T(8,128)(2,1)S(1)} dynamic-slice(bf16[1024,4096]{1,0:T(8,128)(2,1)} %param.9, s32[]{:T(128)S(6)} %mul.20, s32[]{:T(128)S(6)} %mul.22), dynamic_slice_sizes={512,1024} | dynamic-slice | bytes 2097156 | tf_op jit(solution)/shard_map/dynamic_slice | solution.py:283
  7.2 1.6 %collective-permute-start.10 = (bf16[512,1024]{1,0:T(8,128)(2,1)S(1)}, bf16[512,1024]{1,0:T(8,128)(2,1)S(1)}, u32[]{:S(2)}, u32[]{:S(2)}) collective-permute-start(bf16[512,1024]{1,0:T(8,128)(2,1)S(1)} %dynamic_slice.20), channel_id=1, source_target_pairs={{0,1},{1,0},{2,3},{3,2},{4,5},{5,4},{6,7},{7,6},{8,9},{9,8},{10,11... | collective-permute-start | bytes 3145736 | tf_op jit(solution)/shard_map/ppermute | solution.py:29
  8.8 0.0 copy-done
  8.8 0.0 copy-done.1
  8.8 3.7 %shard_map.56 = (bf16[6,512,128]{2,1,0:T(8,128)(2,1)S(1)}, f32[6,512,128]{2,1,0:T(8,128)S(1)}, f32[6,512,128]{2,1,0:T(8,128)S(1)}) custom-call(s32[3]{0:T(128)S(1)} %copy-done.1, s32[3]{0:T(128)S(1)} %collective-permute-done.1.recv_starts_ref, bf16[384,1024]{1,0:T(8,128)(2,1)S(1)} %copy-done, bf16[384,1024]{1,0:T(8,128)(2,1)S(1)} %collective-permute-done.2.refs_1_, ...), custom_call_target="tpu_custom_call" | custom-call | flops 5000000000 | bytes 8388608 | tf_op jit(solution)/shard_map/pallas_call | solution.py:258
  12.5 0.0 collective-permute-done.3.first_ref
  12.5 2.9 %collective-permute-done.4.second_ref = bf16[384,256]{1,0:T(8,128)(2,1)S(1)} collective-permute-done((bf16[384,256]{1,0:T(8,128)(2,1)S(1)}, bf16[384,256]{1,0:T(8,128)(2,1)S(1)}, u32[]{:S(2)}, u32[]{:S(2)}) %collective-permute-start.4) | collective-permute-done | bytes 196640 | tf_op jit(solution)/shard_map/ppermute | solution.py:19
  15.4 0.1 collective-permute-start.6
  15.5 0.6 collective-permute-start.5
  16.1 0.8 %shard_map.58 = (f32[6,512,128]{2,1,0:T(8,128)S(1)}, f32[6,512,128]{2,1,0:T(8,128)S(1)}) custom-call(s32[3]{0:T(128)S(1)} %copy-done.1, s32[3]{0:T(128)S(1)} %collective-permute-done.1.recv_starts_ref, bf16[6,512,128]{2,1,0:T(8,128)(2,1)S(1)} %get-tuple-element.41.refs_0_, f32[6,512,128]{2,1,0:T(8,128)S(1)} %get-tuple-element.42.refs_1_, ...), custom_call_target="tpu_custom_call" | custom-call | flops 2100000000 | bytes 8388608 | tf_op jit(solution)/shard_map/pallas_call | solution.py:258
  16.9 11.1 %collective-permute-done.6.refs_4_.odd_ref = bf16[768,256]{1,0:T(8,128)(2,1)S(1)} collective-permute-done((bf16[768,256]{1,0:T(8,128)(2,1)S(1)}, bf16[768,256]{1,0:T(8,128)(2,1)S(1)}, u32[]{:S(2)}, u32[]{:S(2)}) %collective-permute-start.6) | collective-permute-done | bytes 393248 | tf_op jit(solution)/shard_map/ppermute | solution.py:19
  28.0 0.7 %collective-permute-start.7 = (bf16[768,256]{1,0:T(8,128)(2,1)S(1)}, bf16[768,256]{1,0:T(8,128)(2,1)S(1)}, u32[]{:S(2)}, u32[]{:S(2)}) collective-permute-start(bf16[768,256]{1,0:T(8,128)(2,1)S(1)} %shard_map.60), channel_id=1, source_target_pairs={{0,4},{2,6},{4,0},{6,2},{8,12},{10,14},{12,8},{14,10},{16,20},{18,... | collective-permute-start | bytes 1179656 | tf_op jit(solution)/shard_map/ppermute | solution.py:23
  28.8 0.0 collective-permute-done.5.refs_3_
  28.8 0.0 slice-start
  28.8 0.9 %shard_map.59 = (f32[6,512,128]{2,1,0:T(8,128)S(1)}, f32[6,512,128]{2,1,0:T(8,128)S(1)}) custom-call(s32[3]{0:T(128)S(1)} %copy-done.1, s32[3]{0:T(128)S(1)} %collective-permute-done.1.recv_starts_ref, bf16[6,512,128]{2,1,0:T(8,128)(2,1)S(1)} %get-tuple-element.41.refs_0_, f32[6,512,128]{2,1,0:T(8,128)S(1)} %get-tuple-element.46.refs_1_, ...), custom_call_target="tpu_custom_call" | custom-call | flops 4000000000 | bytes 8388608 | tf_op jit(solution)/shard_map/pallas_call | solution.py:258
  29.7 2.5 %collective-permute-done.10.refs_0_ = bf16[512,1024]{1,0:T(8,128)(2,1)S(1)} collective-permute-done((bf16[512,1024]{1,0:T(8,128)(2,1)S(1)}, bf16[512,1024]{1,0:T(8,128)(2,1)S(1)}, u32[]{:S(2)}, u32[]{:S(2)}) %collective-permute-start.10) | collective-permute-done | bytes 1048608 | tf_op jit(solution)/shard_map/ppermute | solution.py:29
  32.2 0.0 slice-start.1
  32.2 1.5 %collective-permute-start.11 = (bf16[512,1024]{1,0:T(8,128)(2,1)S(1)}, bf16[512,1024]{1,0:T(8,128)(2,1)S(1)}, u32[]{:S(2)}, u32[]{:S(2)}) collective-permute-start(bf16[512,1024]{1,0:T(8,128)(2,1)S(1)} %collective-permute-done.10.refs_0_), channel_id=1, source_target_pairs={{0,8},{2,10},{4,12},{6,14},{8,0},{10,2},{12,4},{14,6},{16,24},{18,... | collective-permute-start | bytes 3145736 | tf_op jit(solution)/shard_map/ppermute | solution.py:23
  33.7 4.2 %collective-permute-done.7.refs_3_ = bf16[768,256]{1,0:T(8,128)(2,1)S(1)} collective-permute-done((bf16[768,256]{1,0:T(8,128)(2,1)S(1)}, bf16[768,256]{1,0:T(8,128)(2,1)S(1)}, u32[]{:S(2)}, u32[]{:S(2)}) %collective-permute-start.7) | collective-permute-done | bytes 393248 | tf_op jit(solution)/shard_map/ppermute | solution.py:23
  38.0 3.2 %shard_map.61 = bf16[384,512]{1,0:T(8,128)(2,1)S(1)} custom-call(s32[3]{0:T(128)S(1)} %copy-done.1, s32[3]{0:T(128)S(1)} %collective-permute-done.1.recv_starts_ref, bf16[6,512,128]{2,1,0:T(8,128)(2,1)S(1)} %get-tuple-element.41.refs_0_, f32[6,512,128]{2,1,0:T(8,128)S(1)} %get-tuple-element.48.refs_1_, f32[6,512,128]{2,1,0:T(8,128)S(1)} %get-tuple-element.49.refs_2_, ...), custom_call_target="tpu_custom_call" | custom-call | flops 2000000000 | bytes 8388608 | tf_op jit(solution)/shard_map/pallas_call | solution.py:258
  41.1 0.1 collective-permute-start.8
  41.2 0.5 collective-permute-start.12
  41.7 1.2 %collective-permute-done.8.refs_4_ = bf16[384,512]{1,0:T(8,128)(2,1)S(1)} collective-permute-done((bf16[384,512]{1,0:T(8,128)(2,1)S(1)}, bf16[384,512]{1,0:T(8,128)(2,1)S(1)}, u32[]{:S(2)}, u32[]{:S(2)}) %collective-permute-start.8) | collective-permute-done | bytes 393248 | tf_op jit(solution)/shard_map/ppermute | solution.py:23
  42.9 3.0 %shard_map.62 = bf16[384,1024]{1,0:T(8,128)(2,1)S(1)} custom-call(s32[3]{0:T(128)S(1)} %copy-done.1, s32[3]{0:T(128)S(1)} %collective-permute-done.1.recv_starts_ref, bf16[6,512,128]{2,1,0:T(8,128)(2,1)S(1)} %get-tuple-element.41.refs_0_, f32[6,512,128]{2,1,0:T(8,128)S(1)} %get-tuple-element.48.refs_1_, f32[6,512,128]{2,1,0:T(8,128)S(1)} %get-tuple-element.49.refs_2_, ...), custom_call_target="tpu_custom_call" | custom-call | flops 2000000000 | bytes 8388608 | tf_op jit(solution)/shard_map/pallas_call | solution.py:258
  45.9 1.6 %collective-permute-start.9 = (bf16[384,1024]{1,0:T(8,128)(2,1)S(1)}, bf16[384,1024]{1,0:T(8,128)(2,1)S(1)}, u32[]{:S(2)}, u32[]{:S(2)}) collective-permute-start(bf16[384,1024]{1,0:T(8,128)(2,1)S(1)} %shard_map.62), channel_id=1, source_target_pairs={{0,1},{1,0},{2,3},{3,2},{4,5},{5,4},{6,7},{7,6},{8,9},{9,8},{10,11... | collective-permute-start | bytes 2359304 | tf_op jit(solution)/shard_map/ppermute | solution.py:29
  47.5 0.0 slice-done
  47.5 0.0 slice-done.1
  47.5 2.1 %fusion.2.given_ref = bf16[384,2048]{1,0:T(8,128)(2,1)S(1)} fusion(bf16[384,1024]{1,0:T(8,128)(2,1)S(1)} %shard_map.62, bf16[1024,4096]{1,0:T(8,128)(2,1)S(1)} %bitcast.2, s32[]{:T(128)S(6)} %mul.23), kind=kOutput, calls=%fused_computation.2 | convolution fusion | flops 1611399168 | bytes 6553604 | tf_op jit(solution)/shard_map/dot_general | solution.py:314
  49.6 6.7 %collective-permute-done.11.refs_1_ = bf16[512,1024]{1,0:T(8,128)(2,1)S(1)} collective-permute-done((bf16[512,1024]{1,0:T(8,128)(2,1)S(1)}, bf16[512,1024]{1,0:T(8,128)(2,1)S(1)}, u32[]{:S(2)}, u32[]{:S(2)}) %collective-permute-start.11) | collective-permute-done | bytes 1048608 | tf_op jit(solution)/shard_map/ppermute | solution.py:23
  56.3 0.1 fusion.6
  56.3 0.1 collective-permute-start.14
  56.4 0.5 collective-permute-start.13
  56.9 8.6 %collective-permute-done.9.heads_ref = bf16[384,1024]{1,0:T(8,128)(2,1)S(1)} collective-permute-done((bf16[384,1024]{1,0:T(8,128)(2,1)S(1)}, bf16[384,1024]{1,0:T(8,128)(2,1)S(1)}, u32[]{:S(2)}, u32[]{:S(2)}) %collective-permute-start.9) | collective-permute-done | bytes 786464 | tf_op jit(solution)/shard_map/ppermute | solution.py:29
  65.6 0.0 collective-permute-done.12.refs_2_
  65.6 0.0 collective-permute-done.14.refs_4_
  65.6 0.0 collective-permute-done.13.refs_3_
  65.6 2.6 %shard_map.63 = bf16[384,2048]{1,0:T(8,128)(2,1)} custom-call(bf16[384,2048]{1,0:T(8,128)(2,1)S(1)} %fusion.2.given_ref, bf16[384,1024]{1,0:T(8,128)(2,1)S(1)} %collective-permute-done.9.heads_ref, bf16[512,1024]{1,0:T(8,128)(2,1)S(1)} %collective-permute-done.10.refs_0_, bf16[512,1024]{1,0:T(8,128)(2,1)S(1)} %collective-permute-done.11.refs_1_, ...), custom_call_target="tpu_custom_call" | custom-call | flops 1610612736 | bytes 4194304 | tf_op jit(solution)/shard_map/pallas_call | solution.py:87
  (6 shorter events, 0.1 us)
Async XLA Ops:
  0.0 5.3 %collective-permute-start.2 = (bf16[384,1024]{1,0:T(8,128)(2,1)}, bf16[384,1024]{1,0:T(8,128)(2,1)S(1)}, u32[]{:S(2)}, u32[]{:S(2)}) collective-permute-start(bf16[384,1024]{1,0:T(8,128)(2,1)} %refs_0_.1), channel_id=1, source_target_pairs={{0,2},{2,0},{4,6},{6,4},{8,10},{10,8},{12,14},{14,12},{16,18},{18,... | collective-permute-start | bytes 2359304 | tf_op jit(solution)/shard_map/ppermute | solution.py:23
  1.3 2.3 %collective-permute-start = (bf16[384,256]{1,0:T(8,128)(2,1)S(1)}, bf16[384,256]{1,0:T(8,128)(2,1)S(1)}, u32[]{:S(2)}, u32[]{:S(2)}) collective-permute-start(bf16[384,256]{1,0:T(8,128)(2,1)S(1)} %pad_maximum_fusion), channel_id=1, source_target_pairs={{0,2},{2,0},{4,6},{6,4},{8,10},{10,8},{12,14},{14,12},{16,18},{18,... | collective-permute-start | bytes 589832 | tf_op jit(solution)/shard_map/ppermute | solution.py:23
  1.9 1.7 %collective-permute-start.1 = (s32[3]{0:T(128)}, s32[3]{0:T(128)S(1)}, u32[]{:S(2)}, u32[]{:S(2)}) collective-permute-start(s32[3]{0:T(128)} %starts_ref.9), channel_id=1, source_target_pairs={{0,2},{2,0},{4,6},{6,4},{8,10},{10,8},{12,14},{14,12},{16,18},{18,... | collective-permute-start | bytes 44 | tf_op jit(solution)/shard_map/ppermute | solution.py:23
  2.0 6.8 %copy-start = (bf16[384,1024]{1,0:T(8,128)(2,1)S(1)}, bf16[384,1024]{1,0:T(8,128)(2,1)}, u32[]{:S(2)}) copy-start(bf16[384,1024]{1,0:T(8,128)(2,1)} %refs_0_.1) | copy-start | bytes 2359300
  2.0 6.8 %copy-start.1 = (s32[3]{0:T(128)S(1)}, s32[3]{0:T(128)}, u32[]{:S(2)}) copy-start(s32[3]{0:T(128)} %starts_ref.9) | copy-start | bytes 40
  2.0 10.5 %collective-permute-start.3 = (bf16[384,256]{1,0:T(8,128)(2,1)S(1)}, bf16[384,256]{1,0:T(8,128)(2,1)S(1)}, u32[]{:S(2)}, u32[]{:S(2)}) collective-permute-start(bf16[384,256]{1,0:T(8,128)(2,1)S(1)} %pad_maximum_fusion.1.first_ref), channel_id=1, source_target_pairs={{0,8},{2,10},{4,12},{6,14},{8,16},{10,18},{12,20},{14,22},{16,24},... | collective-permute-start | bytes 589832 | tf_op jit(solution)/shard_map/ppermute | solution.py:19
  3.7 11.7 %collective-permute-start.4 = (bf16[384,256]{1,0:T(8,128)(2,1)S(1)}, bf16[384,256]{1,0:T(8,128)(2,1)S(1)}, u32[]{:S(2)}, u32[]{:S(2)}) collective-permute-start(bf16[384,256]{1,0:T(8,128)(2,1)S(1)} %collective-permute-done.second_ref), channel_id=1, source_target_pairs={{0,8},{2,10},{4,12},{6,14},{8,16},{10,18},{12,20},{14,22},{16,24},... | collective-permute-start | bytes 589832 | tf_op jit(solution)/shard_map/ppermute | solution.py:19
  7.2 25.0 %collective-permute-start.10 = (bf16[512,1024]{1,0:T(8,128)(2,1)S(1)}, bf16[512,1024]{1,0:T(8,128)(2,1)S(1)}, u32[]{:S(2)}, u32[]{:S(2)}) collective-permute-start(bf16[512,1024]{1,0:T(8,128)(2,1)S(1)} %dynamic_slice.20), channel_id=1, source_target_pairs={{0,1},{1,0},{2,3},{3,2},{4,5},{5,4},{6,7},{7,6},{8,9},{9,8},{10,11... | collective-permute-start | bytes 3145736 | tf_op jit(solution)/shard_map/ppermute | solution.py:29
  15.4 12.6 %collective-permute-start.6 = (bf16[768,256]{1,0:T(8,128)(2,1)S(1)}, bf16[768,256]{1,0:T(8,128)(2,1)S(1)}, u32[]{:S(2)}, u32[]{:S(2)}) collective-permute-start(bf16[768,256]{1,0:T(8,128)(2,1)S(1)} %shard_map.57.refs_3_), channel_id=1, source_target_pairs={{0,8},{2,10},{4,12},{6,14},{8,16},{10,18},{12,20},{14,22},{16,24},... | collective-permute-start | bytes 1179656 | tf_op jit(solution)/shard_map/ppermute | solution.py:19
  15.5 13.3 %collective-permute-start.5 = (bf16[768,256]{1,0:T(8,128)(2,1)S(1)}, bf16[768,256]{1,0:T(8,128)(2,1)S(1)}, u32[]{:S(2)}, u32[]{:S(2)}) collective-permute-start(bf16[768,256]{1,0:T(8,128)(2,1)S(1)} %shard_map.57.refs_3_), channel_id=1, source_target_pairs={{0,4},{2,6},{4,0},{6,2},{8,12},{10,14},{12,8},{14,10},{16,20},{18,... | collective-permute-start | bytes 1179656 | tf_op jit(solution)/shard_map/ppermute | solution.py:23
  28.0 9.9 %collective-permute-start.7 = (bf16[768,256]{1,0:T(8,128)(2,1)S(1)}, bf16[768,256]{1,0:T(8,128)(2,1)S(1)}, u32[]{:S(2)}, u32[]{:S(2)}) collective-permute-start(bf16[768,256]{1,0:T(8,128)(2,1)S(1)} %shard_map.60), channel_id=1, source_target_pairs={{0,4},{2,6},{4,0},{6,2},{8,12},{10,14},{12,8},{14,10},{16,20},{18,... | collective-permute-start | bytes 1179656 | tf_op jit(solution)/shard_map/ppermute | solution.py:23
  28.8 18.7 %slice-start = ((s8[8388608]{0:T(1024)(128)(4,1)}), s8[4194304]{0:T(1024)(128)(4,1)S(1)}, s32[]{:S(2)}) async-start(s8[8388608]{0:T(1024)(128)(4,1)} %bitcast.1), calls=%async_computation | async-start | bytes 8388608
  32.2 15.3 %slice-start.1 = ((s8[8388608]{0:T(1024)(128)(4,1)}), s8[4194304]{0:T(1024)(128)(4,1)S(1)}, s32[]{:S(2)}) async-start(s8[8388608]{0:T(1024)(128)(4,1)} %bitcast.1), calls=%async_computation.1 | async-start | bytes 8388608
  32.2 24.1 %collective-permute-start.11 = (bf16[512,1024]{1,0:T(8,128)(2,1)S(1)}, bf16[512,1024]{1,0:T(8,128)(2,1)S(1)}, u32[]{:S(2)}, u32[]{:S(2)}) collective-permute-start(bf16[512,1024]{1,0:T(8,128)(2,1)S(1)} %collective-permute-done.10.refs_0_), channel_id=1, source_target_pairs={{0,8},{2,10},{4,12},{6,14},{8,0},{10,2},{12,4},{14,6},{16,24},{18,... | collective-permute-start | bytes 3145736 | tf_op jit(solution)/shard_map/ppermute | solution.py:23
  41.1 1.8 %collective-permute-start.8 = (bf16[384,512]{1,0:T(8,128)(2,1)S(1)}, bf16[384,512]{1,0:T(8,128)(2,1)S(1)}, u32[]{:S(2)}, u32[]{:S(2)}) collective-permute-start(bf16[384,512]{1,0:T(8,128)(2,1)S(1)} %shard_map.61), channel_id=1, source_target_pairs={{0,2},{2,0},{4,6},{6,4},{8,10},{10,8},{12,14},{14,12},{16,18},{18,... | collective-permute-start | bytes 1179656 | tf_op jit(solution)/shard_map/ppermute | solution.py:23
  41.2 24.4 %collective-permute-start.12 = (bf16[512,1024]{1,0:T(8,128)(2,1)S(1)}, bf16[512,1024]{1,0:T(8,128)(2,1)S(1)}, u32[]{:S(2)}, u32[]{:S(2)}) collective-permute-start(bf16[512,1024]{1,0:T(8,128)(2,1)S(1)} %collective-permute-done.10.refs_0_), channel_id=1, source_target_pairs={{0,2},{2,0},{4,6},{6,4},{8,10},{10,8},{12,14},{14,12},{16,18},{18,... | collective-permute-start | bytes 3145736 | tf_op jit(solution)/shard_map/ppermute | solution.py:23
  45.9 19.6 %collective-permute-start.9 = (bf16[384,1024]{1,0:T(8,128)(2,1)S(1)}, bf16[384,1024]{1,0:T(8,128)(2,1)S(1)}, u32[]{:S(2)}, u32[]{:S(2)}) collective-permute-start(bf16[384,1024]{1,0:T(8,128)(2,1)S(1)} %shard_map.62), channel_id=1, source_target_pairs={{0,1},{1,0},{2,3},{3,2},{4,5},{5,4},{6,7},{7,6},{8,9},{9,8},{10,11... | collective-permute-start | bytes 2359304 | tf_op jit(solution)/shard_map/ppermute | solution.py:29
  56.3 9.2 %collective-permute-start.14 = (bf16[512,512]{1,0:T(8,128)(2,1)S(1)}, bf16[512,512]{1,0:T(8,128)(2,1)S(1)}, u32[]{:S(2)}, u32[]{:S(2)}) collective-permute-start(bf16[512,512]{1,0:T(8,128)(2,1)S(1)} %get-tuple-element.55), channel_id=1, source_target_pairs={{0,2},{2,0},{4,6},{6,4},{8,10},{10,8},{12,14},{14,12},{16,18},{18,... | collective-permute-start | bytes 1572872 | tf_op jit(solution)/shard_map/ppermute | solution.py:23
  56.4 9.2 %collective-permute-start.13 = (bf16[512,512]{1,0:T(8,128)(2,1)S(1)}, bf16[512,512]{1,0:T(8,128)(2,1)S(1)}, u32[]{:S(2)}, u32[]{:S(2)}) collective-permute-start(bf16[512,512]{1,0:T(8,128)(2,1)S(1)} %get-tuple-element.56), channel_id=1, source_target_pairs={{0,2},{2,0},{4,6},{6,4},{8,10},{10,8},{12,14},{14,12},{16,18},{18,... | collective-permute-start | bytes 1572872 | tf_op jit(solution)/shard_map/ppermute | solution.py:23

commit v13 on v12

--- a/solution.py
+++ b/solution.py
@@ -59,42 +59,54 @@
         out_ref[...] = even_ref[...]
 
 
-def project_kernel(given_ref, heads_ref, *refs):
-    parts, out_ref, built, sems = refs[:5], refs[5], refs[6], refs[7]
-    me = lax.axis_index("ctx")
-    core, fetched = me % 2, me // 4 % 2
-    group, width = parts[3].shape
-    tiles = [x.at[:, n * width : (n + 1) * width] for x in parts[:3] for n in range(2)]
-    tiles += parts[3:]
+def spare_kernel(window_ref, out_ref):
+    fetched = lax.axis_index("ctx") // 4 % 2
+    first = fetched * (window_ref.shape[1] - out_ref.shape[1])
+    out_ref[...] = window_ref[:, pl.ds(pl.multiple_of(first, HEAD_SIZE), out_ref.shape[1])]
+
+
+def project_kernel(final, given_ref, heads_ref, window_ref, rest_ref, *refs):
+    fetched = lax.axis_index("ctx") // 4 % 2
+    wide, narrow = window_ref.shape[1], rest_ref.shape[1]
+    half = wide // 2
+    tiles = (
+        (window_ref.at[:, :half], fetched * narrow),
+        (window_ref.at[:, half:], fetched * narrow + half),
+        (rest_ref, (1 - fetched) * wide),
+    )
     copies = []
-    for n in range(4):
-        first = (fetched if n < 2 else 1 - fetched) * 2 + n % 2
-        cols = pl.ds(pl.multiple_of(first * width, width), width)
+    for n, (tile, col) in enumerate(tiles):
+        cols = pl.ds(pl.multiple_of(col, HEAD_SIZE), tile.shape[1])
         total = given_ref[:, cols].astype(jnp.float32)
-        for index, tile in ((core, tiles[n]), (1 - core, tiles[4 + n])):
-            heads = heads_ref[:, pl.ds(pl.multiple_of(index * group, group), group)]
-            total += jnp.dot(heads, tile[...], preferred_element_type=jnp.float32)
-        built[n] = total.astype(out_ref.dtype)
-        copies.append(pltpu.make_async_copy(built.at[n], out_ref.at[:, cols], sems.at[n]))
-        copies[-1].start()
+        total += jnp.dot(heads_ref[...], tile[...], preferred_element_type=jnp.float32)
+        if final:
+            out_ref, built, sems = refs[0], refs[1 + n], refs[4]
+            built[...] = total.astype(out_ref.dtype)
+            copies.append(pltpu.make_async_copy(built, out_ref.at[:, cols], sems.at[n]))
+            copies[-1].start()
+        else:
+            refs[0][:, cols] = total
     for copy in copies:
         copy.wait()
 
 
-def project(given, heads, tiles):
+def project(final, given, heads, parts):
     tok, cols = given.shape
     vmem = pl.BlockSpec(memory_space=pltpu.VMEM)
+    half = parts[0].shape[1] // 2
+    scratch = [pltpu.VMEM((tok, n), jnp.bfloat16) for n in (half, half, parts[1].shape[1])]
+    scratch += [pltpu.SemaphoreType.DMA((3,))]
     return pl.pallas_call(
-        project_kernel,
-        out_shape=jax.ShapeDtypeStruct(given.shape, jnp.bfloat16),
-        in_specs=[vmem] * 7,
-        out_specs=pl.BlockSpec(memory_space=pltpu.HBM),
-        scratch_shapes=[pltpu.VMEM((4, tok, cols // 4), jnp.bfloat16), pltpu.SemaphoreType.DMA((4,))],
+        functools.partial(project_kernel, final),
+        out_shape=jax.ShapeDtypeStruct(given.shape, jnp.bfloat16 if final else jnp.float32),
+        in_specs=[vmem] * 4,
+        out_specs=pl.BlockSpec(memory_space=pltpu.HBM) if final else vmem,
+        scratch_shapes=scratch if final else [],
         compiler_params=pltpu.CompilerParams(vmem_limit_bytes=16 * 2**20),
         cost_estimate=pl.CostEstimate(
             flops=2 * tok * heads.shape[1] * cols, bytes_accessed=4 * 2**20, transcendentals=0
         ),
-    )(given, heads, *tiles)
+    )(given, heads, *parts)
 
 
 def attention_kernel(stage, distances, n_head, starts_ref, recv_starts_ref, *refs):
@@ -115,8 +127,6 @@
     elif stage == "next":
         stats_ref, acc_ref, held_ref = refs
     else:
-        if stage == "own":
-            swapped_ref, *refs = refs
         out_ref, stats_ref, acc_ref, held_ref = refs
     tok = starts_ref.shape[0] * BLOCK
     half = tok // BLOCK
@@ -225,11 +235,9 @@
             total = stats_ref[j, :, HEAD_SIZE // 2 : HEAD_SIZE // 2 + 1]
             o = (acc_ref[j] / total).astype(jnp.bfloat16)
             for h in range(n_head):
-                first = core * rows + h * HEAD_SIZE if stage == "own" else h * HEAD_SIZE
-                lanes = pl.ds(pl.multiple_of(first, HEAD_SIZE), HEAD_SIZE)
-                out_ref[j * BLOCK : (j + 1) * BLOCK, lanes] = o[h * BLOCK : (h + 1) * BLOCK]
-        if stage == "own":
-            out_ref[:, pl.ds(pl.multiple_of((1 - core) * rows, rows), rows)] = swapped_ref[...]
+                out_ref[j * BLOCK : (j + 1) * BLOCK, h * HEAD_SIZE : (h + 1) * HEAD_SIZE] = o[
+                    h * BLOCK : (h + 1) * BLOCK
+                ]
 
     if stage == "first":
         attend_own()
@@ -251,8 +259,7 @@
     elif stage == "next":
         outs = state
     else:
-        width = rows * (2 if stage == "own" else 1)
-        outs, share = [jax.ShapeDtypeStruct((tok, width), jnp.bfloat16)], 0.5
+        outs, share = [jax.ShapeDtypeStruct((tok, rows), jnp.bfloat16)], 0.5
         scratch = [pltpu.VMEM((half, rows, HEAD_SIZE), jnp.float32)] * 2 + scratch
     vmem, smem = pl.BlockSpec(memory_space=pltpu.VMEM), pl.BlockSpec(memory_space=pltpu.SMEM)
     return pl.pallas_call(
@@ -276,8 +283,10 @@
     cols = out_weight.shape[1] // 2
     core = me % 2
     lanes = (core * HEAD_SIZE, (1 - core) * HEAD_SIZE)
-    corner = (core * group, ((1 - head) * 2 + me // 4 % 2) * (cols // 2))
-    keys, lanes, corner, here_col = lax.optimization_barrier((keys, lanes, corner, head * cols))
+    narrow = cols * 3 // 8
+    corner = (core * group, (1 - head) * cols + me // 4 % 2 * narrow)
+    corners = ((core * group, head * cols), ((1 - core) * group, head * cols))
+    keys, lanes, corner, corners = lax.optimization_barrier((keys, lanes, corner, corners))
 
     def cut(x, start, size):
         return lax.dynamic_slice(x, start, size, allow_negative_indices=False)
@@ -293,7 +302,7 @@
     (own,) = small_call(join_kernel, [(2 * tok, 2 * HEAD_SIZE)], (mine, recv))
     starts = (block_start, recv_starts)
     q_recv, weight = lax.optimization_barrier((q_recv, out_weight))
-    sent = cut(weight, corner, (group, cols // 2))
+    sent = cut(weight, corner, (group, cols - narrow))
     q_recv, sent = lax.optimization_barrier((q_recv, sent))
     fetched = cross(sent, 0)
     q, *state = attention_call("first", ((0, 0),), 5, *starts, (queries, q_recv, own))
@@ -305,18 +314,22 @@
     _, ready = lax.optimization_barrier((state[0], two_behind))
     third = swap(small_call(pick_kernel, [own.shape], (own, ready))[0], 2)
     state = attention_call("next", ((1, 3), (4, 4)), 4, *starts, (q, *state, across, two_behind))
-    _, fetched = lax.optimization_barrier((state[0], fetched))
-    passed = swap(fetched, 4)
     (o_other,) = attention_call("other", ((3, 1),), 2, *starts, (q, *state, third))
-    (heads,) = attention_call("own", ((3, 1),), 2, *starts, (q, *state, third, swap(o_other, 1)))
-    heads_across = cross(heads, 0)
-    rows_here = cut(out_weight, (0, here_col), (2 * group, cols))
-    here = jnp.dot(heads, rows_here, preferred_element_type=jnp.float32)
+    _, fetched = lax.optimization_barrier((o_other, fetched))
+    passed = swap(small_call(spare_kernel, [(group, narrow)], (fetched,))[0], 4)
+    across_other = cross(o_other, 1)
+    swapped_other = swap(o_other, 1)
+    (o_own,) = attention_call("own", ((3, 1),), 2, *starts, (q, *state, third))
+    across_own = cross(o_own, 0)
+    here = sum(
+        jnp.dot(o, cut(out_weight, at, (group, cols)), preferred_element_type=jnp.float32)
+        for o, at in zip((o_own, swapped_other), corners, strict=True)
+    )
     here = here.astype(jnp.bfloat16)
-    _, late = lax.optimization_barrier((here, passed))
-    weights = [fetched, passed, swap(fetched, 1)]
-    weights += [swap(x, 1) for x in jnp.split(late, 2, 1)]
-    return project(here, heads_across, weights)
+    _, _, _, late = lax.optimization_barrier((here, across_own, across_other, passed))
+    other_rows = (swap(fetched, 1), swap(late, 1))
+    here = project(False, here, across_own, (fetched, passed))
+    return project(True, here, across_other, other_rows)
 
 
 def solution(mesh):

time: 68.5 us -> 67.5 us (0.985)
  starting transfers between devices: 11.1 us -> 9.2 us
  waiting for transfers between devices: 37.2 us -> 36.4 us
    ppermute x10 -> x9, starting transfers between devices: 4.66 us -> 2.15 us  [swap(): lax.ppermute(x, 'ctx', [(i, i ^ mask) for i in range(lax.axis_size('ctx'))])]
    ppermute x10 -> x9, waiting for transfers between devices: 12.1 us -> 10.7 us  [swap(): lax.ppermute(x, 'ctx', [(i, i ^ mask) for i in range(lax.axis_size('ctx'))])]
    ppermute x2 -> x3, waiting for transfers between devices: 11.1 us -> 12 us  [cross(): return lax.ppermute(x, ('ctx', 'head'), route)]
    ppermute x2 -> x3, starting transfers between devices: 3.17 us -> 3.79 us  [cross(): return lax.ppermute(x, ('ctx', 'head'), route)]
    pallas_call x1 -> x2, Pallas kernels: 2.63 us -> 3.19 us  [project(): pl.pallas_call(functools.partial(project_kernel, final), out_shape=jax.Sh...]
    dot_general x1 -> x2, matrix products: 2.07 us -> 2.52 us  [per_device(): jnp.dot(o, cut(out_weight, at, (group, cols)), preferred_element_type=jnp...]
  transfers between devices with their start and end apart: 15 -> 15, of which waited for: 7 -> 6; matrix products, arithmetic and copies ran while one was open for 8% -> 9% of each run, Pallas kernels for 17% -> 19%
where the time goes in v13:
time: 67.5 us; the launch traced here: 67 us
  waiting for transfers between devices  36.4 us (54%)
  Pallas kernels  15 us (22%)
  starting transfers between devices  9.2 us (14%)
  local copies, waits for them, and re-layouts  3.46 us (5%)
  matrix products  2.52 us (4%)
    ppermute x3, waiting for transfers between devices, rotate(): return lax.ppermute(x, 'ctx', [(i, (i + distance) % n) for i in range(n)])  13.7 us
    ppermute x3, waiting for transfers between devices, cross(): return lax.ppermute(x, ('ctx', 'head'), route)  12 us
    pallas_call x5, Pallas kernels, attention_call(): pl.pallas_call(functools.partial(attention_kernel, stage, distances, n_he...  11.7 us
    ppermute x9, waiting for transfers between devices, swap(): lax.ppermute(x, 'ctx', [(i, i ^ mask) for i in range(lax.axis_size('ctx'))])  10.7 us
    ppermute x3, starting transfers between devices, cross(): return lax.ppermute(x, ('ctx', 'head'), route)  3.79 us
    dynamic_slice x2, local copies, waits for them, and re-layouts, cut(): return lax.dynamic_slice(x, start, size, allow_negative_indices=False)  3.44 us
    ppermute x3, starting transfers between devices, rotate(): return lax.ppermute(x, 'ctx', [(i, (i + distance) % n) for i in range(n)])  3.27 us
    pallas_call x2, Pallas kernels, project(): pl.pallas_call(functools.partial(project_kernel, final), out_shape=jax.Sh...  3.19 us
  transfers between devices with their start and end apart: 15, of which 6 were waited for; matrix products, arithmetic and copies ran while one was open for 9% of the time, Pallas kernels for 19%

profile of v13, /device:TPU:2, one launch (start us, length us, event | category | flops | bytes accessed | tf_op | source)
XLA Modules:
  0.0 67.0 jit_solution(7167207523864239472)
XLA Ops:
  0.0 0.0 collective-permute-start.2
  0.0 1.3 %constant_dynamic-slice_fusion = (bf16[384,128]{1,0:T(8,128)(2,1)S(1)}, bf16[384,128]{1,0:T(8,128)(2,1)S(1)}, bf16[384,128]{1,0:T(8,128)(2,1)S(1)}, bf16[384,128]{1,0:T(8,128)(2,1)S(1)}) fusion(bf16[384,256]{1,0:T(8,128)(2,1)} %param.7, s32[]{:T(128)S(6)} %mul.23, s32[]{:T(128)S(6)} %mul.24, bf16[384,256]{1,0:T(8,128)(2,1)} %param.6), kind=kLoop, calls=%fused_computation.6 | loop fusion | bytes 786440 | tf_op jit(solution)/shard_map/dynamic_slice | solution.py:292
  1.3 0.0 copy-start
  1.3 0.0 copy-start.1
  1.4 0.6 collective-permute-start
  1.9 0.1 collective-permute-start.1
  2.0 1.6 %collective-permute-start.3 = (bf16[384,256]{1,0:T(8,128)(2,1)S(1)}, bf16[384,256]{1,0:T(8,128)(2,1)S(1)}, u32[]{:S(2)}, u32[]{:S(2)}) collective-permute-start(bf16[384,256]{1,0:T(8,128)(2,1)S(1)} %pad_maximum_fusion.1.first_ref), channel_id=1, source_target_pairs={{0,8},{2,10},{4,12},{6,14},{8,16},{10,18},{12,20},{14,22},{16,24},... | collective-permute-start | bytes 589832 | tf_op jit(solution)/shard_map/ppermute | solution.py:19
  3.7 0.0 collective-permute-done.1.recv_starts_ref
  3.7 0.0 collective-permute-done.second_ref
  3.7 1.6 %collective-permute-start.4 = (bf16[384,256]{1,0:T(8,128)(2,1)S(1)}, bf16[384,256]{1,0:T(8,128)(2,1)S(1)}, u32[]{:S(2)}, u32[]{:S(2)}) collective-permute-start(bf16[384,256]{1,0:T(8,128)(2,1)S(1)} %collective-permute-done.second_ref), channel_id=1, source_target_pairs={{0,8},{2,10},{4,12},{6,14},{8,16},{10,18},{12,20},{14,22},{16,24},... | collective-permute-start | bytes 589832 | tf_op jit(solution)/shard_map/ppermute | solution.py:19
  5.3 0.0 collective-permute-done.2.refs_1_
  5.3 2.1 %dynamic_slice.23 = bf16[512,1280]{1,0:T(8,128)(2,1)S(1)} dynamic-slice(bf16[1024,4096]{1,0:T(8,128)(2,1)} %param.9, s32[]{:T(128)S(6)} %mul.25, s32[]{:T(128)S(6)} %add.16), dynamic_slice_sizes={512,1280} | dynamic-slice | bytes 2621444 | tf_op jit(solution)/shard_map/dynamic_slice | solution.py:292
  7.5 1.6 %collective-permute-start.10 = (bf16[512,1280]{1,0:T(8,128)(2,1)S(1)}, bf16[512,1280]{1,0:T(8,128)(2,1)S(1)}, u32[]{:S(2)}, u32[]{:S(2)}) collective-permute-start(bf16[512,1280]{1,0:T(8,128)(2,1)S(1)} %dynamic_slice.23), channel_id=1, source_target_pairs={{0,1},{1,0},{2,3},{3,2},{4,5},{5,4},{6,7},{7,6},{8,9},{9,8},{10,11... | collective-permute-start | bytes 3932168 | tf_op jit(solution)/shard_map/ppermute | solution.py:29
  9.0 0.0 copy-done
  9.0 0.0 copy-done.1
  9.0 3.7 %shard_map.56 = (bf16[6,512,128]{2,1,0:T(8,128)(2,1)S(1)}, f32[6,512,128]{2,1,0:T(8,128)S(1)}, f32[6,512,128]{2,1,0:T(8,128)S(1)}) custom-call(s32[3]{0:T(128)S(1)} %copy-done.1, s32[3]{0:T(128)S(1)} %collective-permute-done.1.recv_starts_ref, bf16[384,1024]{1,0:T(8,128)(2,1)S(1)} %copy-done, bf16[384,1024]{1,0:T(8,128)(2,1)S(1)} %collective-permute-done.2.refs_1_, ...), custom_call_target="tpu_custom_call" | custom-call | flops 5000000000 | bytes 8388608 | tf_op jit(solution)/shard_map/pallas_call | solution.py:265
  12.8 0.0 collective-permute-done.3.first_ref
  12.8 2.6 %collective-permute-done.4.second_ref = bf16[384,256]{1,0:T(8,128)(2,1)S(1)} collective-permute-done((bf16[384,256]{1,0:T(8,128)(2,1)S(1)}, bf16[384,256]{1,0:T(8,128)(2,1)S(1)}, u32[]{:S(2)}, u32[]{:S(2)}) %collective-permute-start.4) | collective-permute-done | bytes 196640 | tf_op jit(solution)/shard_map/ppermute | solution.py:19
  15.4 0.1 collective-permute-start.6
  15.5 0.6 collective-permute-start.5
  16.1 0.8 %shard_map.58 = (f32[6,512,128]{2,1,0:T(8,128)S(1)}, f32[6,512,128]{2,1,0:T(8,128)S(1)}) custom-call(s32[3]{0:T(128)S(1)} %copy-done.1, s32[3]{0:T(128)S(1)} %collective-permute-done.1.recv_starts_ref, bf16[6,512,128]{2,1,0:T(8,128)(2,1)S(1)} %get-tuple-element.44.refs_0_, f32[6,512,128]{2,1,0:T(8,128)S(1)} %get-tuple-element.45.refs_1_, ...), custom_call_target="tpu_custom_call" | custom-call | flops 2100000000 | bytes 8388608 | tf_op jit(solution)/shard_map/pallas_call | solution.py:265
  17.0 11.1 %collective-permute-done.6.refs_4_.odd_ref = bf16[768,256]{1,0:T(8,128)(2,1)S(1)} collective-permute-done((bf16[768,256]{1,0:T(8,128)(2,1)S(1)}, bf16[768,256]{1,0:T(8,128)(2,1)S(1)}, u32[]{:S(2)}, u32[]{:S(2)}) %collective-permute-start.6) | collective-permute-done | bytes 393248 | tf_op jit(solution)/shard_map/ppermute | solution.py:19
  28.1 0.7 %collective-permute-start.7 = (bf16[768,256]{1,0:T(8,128)(2,1)S(1)}, bf16[768,256]{1,0:T(8,128)(2,1)S(1)}, u32[]{:S(2)}, u32[]{:S(2)}) collective-permute-start(bf16[768,256]{1,0:T(8,128)(2,1)S(1)} %shard_map.60), channel_id=1, source_target_pairs={{0,4},{2,6},{4,0},{6,2},{8,12},{10,14},{12,8},{14,10},{16,20},{18,... | collective-permute-start | bytes 1179656 | tf_op jit(solution)/shard_map/ppermute | solution.py:23
  28.8 0.0 collective-permute-done.5.refs_3_
  28.8 0.9 %shard_map.59 = (f32[6,512,128]{2,1,0:T(8,128)S(1)}, f32[6,512,128]{2,1,0:T(8,128)S(1)}) custom-call(s32[3]{0:T(128)S(1)} %copy-done.1, s32[3]{0:T(128)S(1)} %collective-permute-done.1.recv_starts_ref, bf16[6,512,128]{2,1,0:T(8,128)(2,1)S(1)} %get-tuple-element.44.refs_0_, f32[6,512,128]{2,1,0:T(8,128)S(1)} %get-tuple-element.49.refs_1_, ...), custom_call_target="tpu_custom_call" | custom-call | flops 4000000000 | bytes 8388608 | tf_op jit(solution)/shard_map/pallas_call | solution.py:265
  29.8 8.2 %collective-permute-done.7.refs_3_ = bf16[768,256]{1,0:T(8,128)(2,1)S(1)} collective-permute-done((bf16[768,256]{1,0:T(8,128)(2,1)S(1)}, bf16[768,256]{1,0:T(8,128)(2,1)S(1)}, u32[]{:S(2)}, u32[]{:S(2)}) %collective-permute-start.7) | collective-permute-done | bytes 393248 | tf_op jit(solution)/shard_map/ppermute | solution.py:23
  38.0 0.0 slice-start
  38.0 3.2 %shard_map.62 = bf16[384,512]{1,0:T(8,128)(2,1)S(1)} custom-call(s32[3]{0:T(128)S(1)} %copy-done.1, s32[3]{0:T(128)S(1)} %collective-permute-done.1.recv_starts_ref, bf16[6,512,128]{2,1,0:T(8,128)(2,1)S(1)} %get-tuple-element.44.refs_0_, f32[6,512,128]{2,1,0:T(8,128)S(1)} %get-tuple-element.51.refs_1_, f32[6,512,128]{2,1,0:T(8,128)S(1)} %get-tuple-element.52.refs_2_, ...), custom_call_target="tpu_custom_call" | custom-call | flops 2000000000 | bytes 8388608 | tf_op jit(solution)/shard_map/pallas_call | solution.py:265
  41.2 0.0 slice-start.1
  41.2 0.1 collective-permute-start.8
  41.2 1.6 %collective-permute-start.12 = (bf16[384,512]{1,0:T(8,128)(2,1)S(1)}, bf16[384,512]{1,0:T(8,128)(2,1)S(1)}, u32[]{:S(2)}, u32[]{:S(2)}) collective-permute-start(bf16[384,512]{1,0:T(8,128)(2,1)S(1)} %shard_map.62), channel_id=1, source_target_pairs={{0,3},{1,2},{2,1},{3,0},{4,7},{5,6},{6,5},{7,4},{8,11},{9,10},{10,... | collective-permute-start | bytes 1179656 | tf_op jit(solution)/shard_map/ppermute | solution.py:29
  42.9 0.0 collective-permute-done.10.window_ref
  42.9 0.1 shard_map.63
  42.9 0.1 collective-permute-start.11
  43.0 3.0 %shard_map.61 = bf16[384,512]{1,0:T(8,128)(2,1)S(1)} custom-call(s32[3]{0:T(128)S(1)} %copy-done.1, s32[3]{0:T(128)S(1)} %collective-permute-done.1.recv_starts_ref, bf16[6,512,128]{2,1,0:T(8,128)(2,1)S(1)} %get-tuple-element.44.refs_0_, f32[6,512,128]{2,1,0:T(8,128)S(1)} %get-tuple-element.51.refs_1_, f32[6,512,128]{2,1,0:T(8,128)S(1)} %get-tuple-element.52.refs_2_, ...), custom_call_target="tpu_custom_call" | custom-call | flops 2000000000 | bytes 8388608 | tf_op jit(solution)/shard_map/pallas_call | solution.py:265
  46.0 0.6 collective-permute-start.9
  46.6 0.0 collective-permute-start.13
  46.6 0.0 collective-permute-done.8
  46.6 0.0 slice-done
  46.6 0.0 slice-done.1
  46.6 1.2 %fusion = f32[384,2048]{1,0:T(8,128)S(1)} fusion(bf16[384,512]{1,0:T(8,128)(2,1)S(1)} %collective-permute-done.8, bf16[1024,4096]{1,0:T(8,128)(2,1)S(1)} %bitcast.3, s32[]{:T(128)S(6)} %mul.29, s32[]{:T(128)S(6)} %mul.28), kind=kOutput, calls=%fused_computation.1 | convolution fusion | flops 805306368 | bytes 5636104 | tf_op jit(solution)/shard_map/dot_general | solution.py:325
  47.8 1.3 %add_convert_fusion.given_ref = bf16[384,2048]{1,0:T(8,128)(2,1)S(1)} fusion(f32[384,2048]{1,0:T(8,128)S(1)} %fusion, bf16[384,512]{1,0:T(8,128)(2,1)S(1)} %shard_map.61, bf16[1024,4096]{1,0:T(8,128)(2,1)S(1)} %bitcast.3, s32[]{:T(128)S(6)} %mul.25, s32[]{:T(128)S(6)} %mul.28), kind=kOutput, calls=%fused_computation | convolution fusion | flops 806879232 | bytes 7208968 | tf_op jit(solution)/shard_map/dot_general | solution.py:325
  49.1 12.0 %collective-permute-done.9.heads_ref = bf16[384,512]{1,0:T(8,128)(2,1)S(1)} collective-permute-done((bf16[384,512]{1,0:T(8,128)(2,1)S(1)}, bf16[384,512]{1,0:T(8,128)(2,1)S(1)}, u32[]{:S(2)}, u32[]{:S(2)}) %collective-permute-start.9) | collective-permute-done | bytes 393248 | tf_op jit(solution)/shard_map/ppermute | solution.py:29
  61.2 0.0 collective-permute-done.12.heads_ref
  61.2 1.4 %collective-permute-done.11.rest_ref = bf16[512,768]{1,0:T(8,128)(2,1)S(1)} collective-permute-done((bf16[512,768]{1,0:T(8,128)(2,1)S(1)}, bf16[512,768]{1,0:T(8,128)(2,1)S(1)}, u32[]{:S(2)}, u32[]{:S(2)}) %collective-permute-start.11) | collective-permute-done | bytes 786464 | tf_op jit(solution)/shard_map/ppermute | solution.py:23
  62.5 0.0 collective-permute-start.14
  62.5 1.1 %shard_map.64.given_ref = f32[384,2048]{1,0:T(8,128)S(1)} custom-call(bf16[384,2048]{1,0:T(8,128)(2,1)S(1)} %add_convert_fusion.given_ref, bf16[384,512]{1,0:T(8,128)(2,1)S(1)} %collective-permute-done.9.heads_ref, bf16[512,1280]{1,0:T(8,128)(2,1)S(1)} %collective-permute-done.10.window_ref, bf16[512,768]{1,0:T(8,128)(2,1)S(1)} %collective-permute-done.11.rest_ref), custom_call_target="tpu_custom_call" | custom-call | flops 805306368 | bytes 4194304 | tf_op jit(solution)/shard_map/pallas_call | solution.py:99
  63.6 0.0 collective-permute-done.13.window_ref
  63.7 1.1 %collective-permute-done.14.rest_ref = bf16[512,768]{1,0:T(8,128)(2,1)S(1)} collective-permute-done((bf16[512,768]{1,0:T(8,128)(2,1)S(1)}, bf16[512,768]{1,0:T(8,128)(2,1)S(1)}, u32[]{:S(2)}, u32[]{:S(2)}) %collective-permute-start.14) | collective-permute-done | bytes 786464 | tf_op jit(solution)/shard_map/ppermute | solution.py:23
  64.8 2.1 %shard_map.65 = bf16[384,2048]{1,0:T(8,128)(2,1)} custom-call(f32[384,2048]{1,0:T(8,128)S(1)} %shard_map.64.given_ref, bf16[384,512]{1,0:T(8,128)(2,1)S(1)} %collective-permute-done.12.heads_ref, bf16[512,1280]{1,0:T(8,128)(2,1)S(1)} %collective-permute-done.13.window_ref, bf16[512,768]{1,0:T(8,128)(2,1)S(1)} %collective-permute-done.14.rest_ref), custom_call_target="tpu_custom_call" | custom-call | flops 805306368 | bytes 4194304 | tf_op jit(solution)/shard_map/pallas_call | solution.py:99
  (6 shorter events, 0.1 us)
Async XLA Ops:
  0.0 5.3 %collective-permute-start.2 = (bf16[384,1024]{1,0:T(8,128)(2,1)}, bf16[384,1024]{1,0:T(8,128)(2,1)S(1)}, u32[]{:S(2)}, u32[]{:S(2)}) collective-permute-start(bf16[384,1024]{1,0:T(8,128)(2,1)} %refs_0_.1), channel_id=1, source_target_pairs={{0,2},{2,0},{4,6},{6,4},{8,10},{10,8},{12,14},{14,12},{16,18},{18,... | collective-permute-start | bytes 2359304 | tf_op jit(solution)/shard_map/ppermute | solution.py:23
  1.3 7.7 %copy-start = (bf16[384,1024]{1,0:T(8,128)(2,1)S(1)}, bf16[384,1024]{1,0:T(8,128)(2,1)}, u32[]{:S(2)}) copy-start(bf16[384,1024]{1,0:T(8,128)(2,1)} %refs_0_.1) | copy-start | bytes 2359300
  1.3 7.7 %copy-start.1 = (s32[3]{0:T(128)S(1)}, s32[3]{0:T(128)}, u32[]{:S(2)}) copy-start(s32[3]{0:T(128)} %starts_ref.9) | copy-start | bytes 40
  1.4 2.3 %collective-permute-start = (bf16[384,256]{1,0:T(8,128)(2,1)S(1)}, bf16[384,256]{1,0:T(8,128)(2,1)S(1)}, u32[]{:S(2)}, u32[]{:S(2)}) collective-permute-start(bf16[384,256]{1,0:T(8,128)(2,1)S(1)} %pad_maximum_fusion), channel_id=1, source_target_pairs={{0,2},{2,0},{4,6},{6,4},{8,10},{10,8},{12,14},{14,12},{16,18},{18,... | collective-permute-start | bytes 589832 | tf_op jit(solution)/shard_map/ppermute | solution.py:23
  1.9 1.7 %collective-permute-start.1 = (s32[3]{0:T(128)}, s32[3]{0:T(128)S(1)}, u32[]{:S(2)}, u32[]{:S(2)}) collective-permute-start(s32[3]{0:T(128)} %starts_ref.9), channel_id=1, source_target_pairs={{0,2},{2,0},{4,6},{6,4},{8,10},{10,8},{12,14},{14,12},{16,18},{18,... | collective-permute-start | bytes 44 | tf_op jit(solution)/shard_map/ppermute | solution.py:23
  2.0 10.7 %collective-permute-start.3 = (bf16[384,256]{1,0:T(8,128)(2,1)S(1)}, bf16[384,256]{1,0:T(8,128)(2,1)S(1)}, u32[]{:S(2)}, u32[]{:S(2)}) collective-permute-start(bf16[384,256]{1,0:T(8,128)(2,1)S(1)} %pad_maximum_fusion.1.first_ref), channel_id=1, source_target_pairs={{0,8},{2,10},{4,12},{6,14},{8,16},{10,18},{12,20},{14,22},{16,24},... | collective-permute-start | bytes 589832 | tf_op jit(solution)/shard_map/ppermute | solution.py:19
  3.7 11.7 %collective-permute-start.4 = (bf16[384,256]{1,0:T(8,128)(2,1)S(1)}, bf16[384,256]{1,0:T(8,128)(2,1)S(1)}, u32[]{:S(2)}, u32[]{:S(2)}) collective-permute-start(bf16[384,256]{1,0:T(8,128)(2,1)S(1)} %collective-permute-done.second_ref), channel_id=1, source_target_pairs={{0,8},{2,10},{4,12},{6,14},{8,16},{10,18},{12,20},{14,22},{16,24},... | collective-permute-start | bytes 589832 | tf_op jit(solution)/shard_map/ppermute | solution.py:19
  7.5 35.4 %collective-permute-start.10 = (bf16[512,1280]{1,0:T(8,128)(2,1)S(1)}, bf16[512,1280]{1,0:T(8,128)(2,1)S(1)}, u32[]{:S(2)}, u32[]{:S(2)}) collective-permute-start(bf16[512,1280]{1,0:T(8,128)(2,1)S(1)} %dynamic_slice.23), channel_id=1, source_target_pairs={{0,1},{1,0},{2,3},{3,2},{4,5},{5,4},{6,7},{7,6},{8,9},{9,8},{10,11... | collective-permute-start | bytes 3932168 | tf_op jit(solution)/shard_map/ppermute | solution.py:29
  15.4 12.6 %collective-permute-start.6 = (bf16[768,256]{1,0:T(8,128)(2,1)S(1)}, bf16[768,256]{1,0:T(8,128)(2,1)S(1)}, u32[]{:S(2)}, u32[]{:S(2)}) collective-permute-start(bf16[768,256]{1,0:T(8,128)(2,1)S(1)} %shard_map.57.refs_3_), channel_id=1, source_target_pairs={{0,8},{2,10},{4,12},{6,14},{8,16},{10,18},{12,20},{14,22},{16,24},... | collective-permute-start | bytes 1179656 | tf_op jit(solution)/shard_map/ppermute | solution.py:19
  15.5 13.3 %collective-permute-start.5 = (bf16[768,256]{1,0:T(8,128)(2,1)S(1)}, bf16[768,256]{1,0:T(8,128)(2,1)S(1)}, u32[]{:S(2)}, u32[]{:S(2)}) collective-permute-start(bf16[768,256]{1,0:T(8,128)(2,1)S(1)} %shard_map.57.refs_3_), channel_id=1, source_target_pairs={{0,4},{2,6},{4,0},{6,2},{8,12},{10,14},{12,8},{14,10},{16,20},{18,... | collective-permute-start | bytes 1179656 | tf_op jit(solution)/shard_map/ppermute | solution.py:23
  28.1 9.9 %collective-permute-start.7 = (bf16[768,256]{1,0:T(8,128)(2,1)S(1)}, bf16[768,256]{1,0:T(8,128)(2,1)S(1)}, u32[]{:S(2)}, u32[]{:S(2)}) collective-permute-start(bf16[768,256]{1,0:T(8,128)(2,1)S(1)} %shard_map.60), channel_id=1, source_target_pairs={{0,4},{2,6},{4,0},{6,2},{8,12},{10,14},{12,8},{14,10},{16,20},{18,... | collective-permute-start | bytes 1179656 | tf_op jit(solution)/shard_map/ppermute | solution.py:23
  38.0 8.6 %slice-start = ((s8[8388608]{0:T(1024)(128)(4,1)}), s8[4194304]{0:T(1024)(128)(4,1)S(1)}, s32[]{:S(2)}) async-start(s8[8388608]{0:T(1024)(128)(4,1)} %bitcast.2), calls=%async_computation | async-start | bytes 8388608
  41.2 5.5 %slice-start.1 = ((s8[8388608]{0:T(1024)(128)(4,1)}), s8[4194304]{0:T(1024)(128)(4,1)S(1)}, s32[]{:S(2)}) async-start(s8[8388608]{0:T(1024)(128)(4,1)} %bitcast.2), calls=%async_computation.1 | async-start | bytes 8388608
  41.2 5.4 %collective-permute-start.8 = (bf16[384,512]{1,0:T(8,128)(2,1)S(1)}, bf16[384,512]{1,0:T(8,128)(2,1)S(1)}, u32[]{:S(2)}, u32[]{:S(2)}) collective-permute-start(bf16[384,512]{1,0:T(8,128)(2,1)S(1)} %shard_map.62), channel_id=1, source_target_pairs={{0,2},{2,0},{4,6},{6,4},{8,10},{10,8},{12,14},{14,12},{16,18},{18,... | collective-permute-start | bytes 1179656 | tf_op jit(solution)/shard_map/ppermute | solution.py:23
  41.2 19.9 %collective-permute-start.12 = (bf16[384,512]{1,0:T(8,128)(2,1)S(1)}, bf16[384,512]{1,0:T(8,128)(2,1)S(1)}, u32[]{:S(2)}, u32[]{:S(2)}) collective-permute-start(bf16[384,512]{1,0:T(8,128)(2,1)S(1)} %shard_map.62), channel_id=1, source_target_pairs={{0,3},{1,2},{2,1},{3,0},{4,7},{5,6},{6,5},{7,4},{8,11},{9,10},{10,... | collective-permute-start | bytes 1179656 | tf_op jit(solution)/shard_map/ppermute | solution.py:29
  42.9 19.6 %collective-permute-start.11 = (bf16[512,768]{1,0:T(8,128)(2,1)S(1)}, bf16[512,768]{1,0:T(8,128)(2,1)S(1)}, u32[]{:S(2)}, u32[]{:S(2)}) collective-permute-start(bf16[512,768]{1,0:T(8,128)(2,1)S(1)} %shard_map.63), channel_id=1, source_target_pairs={{0,8},{2,10},{4,12},{6,14},{8,0},{10,2},{12,4},{14,6},{16,24},{18,... | collective-permute-start | bytes 2359304 | tf_op jit(solution)/shard_map/ppermute | solution.py:23
  46.0 15.1 %collective-permute-start.9 = (bf16[384,512]{1,0:T(8,128)(2,1)S(1)}, bf16[384,512]{1,0:T(8,128)(2,1)S(1)}, u32[]{:S(2)}, u32[]{:S(2)}) collective-permute-start(bf16[384,512]{1,0:T(8,128)(2,1)S(1)} %shard_map.61), channel_id=1, source_target_pairs={{0,1},{1,0},{2,3},{3,2},{4,5},{5,4},{6,7},{7,6},{8,9},{9,8},{10,11... | collective-permute-start | bytes 1179656 | tf_op jit(solution)/shard_map/ppermute | solution.py:29
  46.6 17.1 %collective-permute-start.13 = (bf16[512,1280]{1,0:T(8,128)(2,1)S(1)}, bf16[512,1280]{1,0:T(8,128)(2,1)S(1)}, u32[]{:S(2)}, u32[]{:S(2)}) collective-permute-start(bf16[512,1280]{1,0:T(8,128)(2,1)S(1)} %collective-permute-done.10.window_ref), channel_id=1, source_target_pairs={{0,2},{2,0},{4,6},{6,4},{8,10},{10,8},{12,14},{14,12},{16,18},{18,... | collective-permute-start | bytes 3932168 | tf_op jit(solution)/shard_map/ppermute | solution.py:23
  62.5 2.3 %collective-permute-start.14 = (bf16[512,768]{1,0:T(8,128)(2,1)S(1)}, bf16[512,768]{1,0:T(8,128)(2,1)S(1)}, u32[]{:S(2)}, u32[]{:S(2)}) collective-permute-start(bf16[512,768]{1,0:T(8,128)(2,1)S(1)} %collective-permute-done.11.rest_ref), channel_id=1, source_target_pairs={{0,2},{2,0},{4,6},{6,4},{8,10},{10,8},{12,14},{14,12},{16,18},{18,... | collective-permute-start | bytes 2359304 | tf_op jit(solution)/shard_map/ppermute | solution.py:23

commit v14 on v13

--- a/solution.py
+++ b/solution.py
@@ -17,6 +17,11 @@
 def rotate(x, distance):
     n = lax.axis_size("ctx")
     return lax.ppermute(x, "ctx", [(i, (i + distance) % n) for i in range(n)])
+
+
+def shift(x, distance):
+    n = lax.axis_size("ctx")
+    return lax.ppermute(x, "ctx", [(i, i + distance) for i in range(n - distance)])
 
 
 def swap(x, mask):
@@ -308,7 +313,7 @@
     q, *state = attention_call("first", ((0, 0),), 5, *starts, (queries, q_recv, own))
     q, one_behind = lax.optimization_barrier((q, one_behind))
     (one_behind,) = small_call(join_kernel, [own.shape], one_behind)
-    two_behind = rotate(one_behind, 4)
+    two_behind = shift(one_behind, 4)
     across = swap(one_behind, 2)
     state = attention_call("next", ((2, 2),), 2.1, *starts, (q, *state, one_behind))
     _, ready = lax.optimization_barrier((state[0], two_behind))

time: 67.5 us -> 65.6 us (0.972)
  waiting for transfers between devices: 36.4 us -> 31.3 us
  starting transfers between devices: 9.2 us -> 12.4 us
    ppermute x3 -> x2, waiting for transfers between devices: 13.7 us -> 2.63 us  [rotate(): return lax.ppermute(x, 'ctx', [(i, (i + distance) % n) for i in range(n)])]
    ppermute x0 -> x1, waiting for transfers between devices: none -> 6.7 us  [shift(): lax.ppermute(x, 'ctx', [(i, i + distance) for i in range(n - distance)])]
    ppermute x0 -> x1, starting transfers between devices: none -> 1.66 us  [shift(): lax.ppermute(x, 'ctx', [(i, i + distance) for i in range(n - distance)])]
    ppermute x3, waiting for transfers between devices: 12 us -> 10.4 us  [cross(): return lax.ppermute(x, ('ctx', 'head'), route)]
    ppermute x9, starting transfers between devices: 2.15 us -> 3.76 us  [swap(): lax.ppermute(x, 'ctx', [(i, i ^ mask) for i in range(lax.axis_size('ctx'))])]
    ppermute x9, waiting for transfers between devices: 10.7 us -> 11.5 us  [swap(): lax.ppermute(x, 'ctx', [(i, i ^ mask) for i in range(lax.axis_size('ctx'))])]
    ppermute x3 -> x2, starting transfers between devices: 3.27 us -> 3.21 us  [rotate(): return lax.ppermute(x, 'ctx', [(i, (i + distance) % n) for i in range(n)])]
  transfers between devices with their start and end apart: 15 -> 15, of which waited for: 6 -> 7; matrix products, arithmetic and copies ran while one was open for 9% -> 9% of each run, Pallas kernels for 19% -> 20%
where the time goes in v14:
time: 65.6 us; the launch traced here: 65.1 us
  waiting for transfers between devices  31.3 us (48%)
  Pallas kernels  15 us (23%)
  starting transfers between devices  12.4 us (19%)
  local copies, waits for them, and re-layouts  3.46 us (5%)
  matrix products  2.51 us (4%)
    pallas_call x5, Pallas kernels, attention_call(): pl.pallas_call(functools.partial(attention_kernel, stage, distances, n_he...  11.7 us
    ppermute x9, waiting for transfers between devices, swap(): lax.ppermute(x, 'ctx', [(i, i ^ mask) for i in range(lax.axis_size('ctx'))])  11.5 us
    ppermute x3, waiting for transfers between devices, cross(): return lax.ppermute(x, ('ctx', 'head'), route)  10.4 us
    ppermute x1, waiting for transfers between devices, shift(): lax.ppermute(x, 'ctx', [(i, i + distance) for i in range(n - distance)])  6.7 us
    ppermute x3, starting transfers between devices, cross(): return lax.ppermute(x, ('ctx', 'head'), route)  3.8 us
    ppermute x9, starting transfers between devices, swap(): lax.ppermute(x, 'ctx', [(i, i ^ mask) for i in range(lax.axis_size('ctx'))])  3.76 us
    dynamic_slice x2, local copies, waits for them, and re-layouts, cut(): return lax.dynamic_slice(x, start, size, allow_negative_indices=False)  3.44 us
    ppermute x2, starting transfers between devices, rotate(): return lax.ppermute(x, 'ctx', [(i, (i + distance) % n) for i in range(n)])  3.21 us
  transfers between devices with their start and end apart: 15, of which 7 were waited for; matrix products, arithmetic and copies ran while one was open for 9% of the time, Pallas kernels for 20%

profile of v14, /device:TPU:2, one launch (start us, length us, event | category | flops | bytes accessed | tf_op | source)
XLA Modules:
  0.0 65.1 jit_solution(17376455832565897669)
XLA Ops:
  0.0 0.0 collective-permute-start.2
  0.0 1.3 %constant_dynamic-slice_fusion = (bf16[384,128]{1,0:T(8,128)(2,1)S(1)}, bf16[384,128]{1,0:T(8,128)(2,1)S(1)}, bf16[384,128]{1,0:T(8,128)(2,1)S(1)}, bf16[384,128]{1,0:T(8,128)(2,1)S(1)}) fusion(bf16[384,256]{1,0:T(8,128)(2,1)} %param.7, s32[]{:T(128)S(6)} %mul.23, s32[]{:T(128)S(6)} %mul.24, bf16[384,256]{1,0:T(8,128)(2,1)} %param.6), kind=kLoop, calls=%fused_computation.6 | loop fusion | bytes 786440 | tf_op jit(solution)/shard_map/dynamic_slice | solution.py:297
  1.3 0.0 copy-start
  1.3 0.0 copy-start.1
  1.4 0.6 collective-permute-start
  1.9 0.1 collective-permute-start.1
  2.0 1.6 %collective-permute-start.3 = (bf16[384,256]{1,0:T(8,128)(2,1)S(1)}, bf16[384,256]{1,0:T(8,128)(2,1)S(1)}, u32[]{:S(2)}, u32[]{:S(2)}) collective-permute-start(bf16[384,256]{1,0:T(8,128)(2,1)S(1)} %pad_maximum_fusion.1.first_ref), channel_id=1, source_target_pairs={{0,8},{2,10},{4,12},{6,14},{8,16},{10,18},{12,20},{14,22},{16,24},... | collective-permute-start | bytes 589832 | tf_op jit(solution)/shard_map/ppermute | solution.py:19
  3.7 0.0 collective-permute-done.1.recv_starts_ref
  3.7 0.0 collective-permute-done.second_ref
  3.7 1.6 %collective-permute-start.4 = (bf16[384,256]{1,0:T(8,128)(2,1)S(1)}, bf16[384,256]{1,0:T(8,128)(2,1)S(1)}, u32[]{:S(2)}, u32[]{:S(2)}) collective-permute-start(bf16[384,256]{1,0:T(8,128)(2,1)S(1)} %collective-permute-done.second_ref), channel_id=1, source_target_pairs={{0,8},{2,10},{4,12},{6,14},{8,16},{10,18},{12,20},{14,22},{16,24},... | collective-permute-start | bytes 589832 | tf_op jit(solution)/shard_map/ppermute | solution.py:19
  5.3 0.0 collective-permute-done.2.refs_1_
  5.3 2.1 %dynamic_slice.23 = bf16[512,1280]{1,0:T(8,128)(2,1)S(1)} dynamic-slice(bf16[1024,4096]{1,0:T(8,128)(2,1)} %param.9, s32[]{:T(128)S(6)} %mul.25, s32[]{:T(128)S(6)} %add.16), dynamic_slice_sizes={512,1280} | dynamic-slice | bytes 2621444 | tf_op jit(solution)/shard_map/dynamic_slice | solution.py:297
  7.5 1.6 %collective-permute-start.10 = (bf16[512,1280]{1,0:T(8,128)(2,1)S(1)}, bf16[512,1280]{1,0:T(8,128)(2,1)S(1)}, u32[]{:S(2)}, u32[]{:S(2)}) collective-permute-start(bf16[512,1280]{1,0:T(8,128)(2,1)S(1)} %dynamic_slice.23), channel_id=1, source_target_pairs={{0,1},{1,0},{2,3},{3,2},{4,5},{5,4},{6,7},{7,6},{8,9},{9,8},{10,11... | collective-permute-start | bytes 3932168 | tf_op jit(solution)/shard_map/ppermute | solution.py:34
  9.0 0.0 copy-done
  9.0 0.0 copy-done.1
  9.0 3.7 %shard_map.56 = (bf16[6,512,128]{2,1,0:T(8,128)(2,1)S(1)}, f32[6,512,128]{2,1,0:T(8,128)S(1)}, f32[6,512,128]{2,1,0:T(8,128)S(1)}) custom-call(s32[3]{0:T(128)S(1)} %copy-done.1, s32[3]{0:T(128)S(1)} %collective-permute-done.1.recv_starts_ref, bf16[384,1024]{1,0:T(8,128)(2,1)S(1)} %copy-done, bf16[384,1024]{1,0:T(8,128)(2,1)S(1)} %collective-permute-done.2.refs_1_, ...), custom_call_target="tpu_custom_call" | custom-call | flops 5000000000 | bytes 8388608 | tf_op jit(solution)/shard_map/pallas_call | solution.py:270
  12.8 0.0 collective-permute-done.3.first_ref
  12.8 2.6 %collective-permute-done.4.second_ref = bf16[384,256]{1,0:T(8,128)(2,1)S(1)} collective-permute-done((bf16[384,256]{1,0:T(8,128)(2,1)S(1)}, bf16[384,256]{1,0:T(8,128)(2,1)S(1)}, u32[]{:S(2)}, u32[]{:S(2)}) %collective-permute-start.4) | collective-permute-done | bytes 196640 | tf_op jit(solution)/shard_map/ppermute | solution.py:19
  15.4 1.7 %collective-permute-start.6 = (bf16[768,256]{1,0:T(8,128)(2,1)S(1)}, bf16[768,256]{1,0:T(8,128)(2,1)S(1)}, u32[]{:S(2)}, u32[]{:S(2)}) collective-permute-start(bf16[768,256]{1,0:T(8,128)(2,1)S(1)} %shard_map.57.refs_3_), channel_id=1, source_target_pairs={{0,8},{2,10},{4,12},{6,14},{8,16},{10,18},{12,20},{14,22},{16,24},... | collective-permute-start | bytes 1179656 | tf_op jit(solution)/shard_map/ppermute | solution.py:24
  17.1 0.6 collective-permute-start.5
  17.7 0.8 %shard_map.58 = (f32[6,512,128]{2,1,0:T(8,128)S(1)}, f32[6,512,128]{2,1,0:T(8,128)S(1)}) custom-call(s32[3]{0:T(128)S(1)} %copy-done.1, s32[3]{0:T(128)S(1)} %collective-permute-done.1.recv_starts_ref, bf16[6,512,128]{2,1,0:T(8,128)(2,1)S(1)} %get-tuple-element.44.refs_0_, f32[6,512,128]{2,1,0:T(8,128)S(1)} %get-tuple-element.45.refs_1_, ...), custom_call_target="tpu_custom_call" | custom-call | flops 2100000000 | bytes 8388608 | tf_op jit(solution)/shard_map/pallas_call | solution.py:270
  18.6 6.7 %collective-permute-done.6.refs_4_.odd_ref = bf16[768,256]{1,0:T(8,128)(2,1)S(1)} collective-permute-done((bf16[768,256]{1,0:T(8,128)(2,1)S(1)}, bf16[768,256]{1,0:T(8,128)(2,1)S(1)}, u32[]{:S(2)}, u32[]{:S(2)}) %collective-permute-start.6) | collective-permute-done | bytes 393248 | tf_op jit(solution)/shard_map/ppermute | solution.py:24
  25.3 0.7 %collective-permute-start.7 = (bf16[768,256]{1,0:T(8,128)(2,1)S(1)}, bf16[768,256]{1,0:T(8,128)(2,1)S(1)}, u32[]{:S(2)}, u32[]{:S(2)}) collective-permute-start(bf16[768,256]{1,0:T(8,128)(2,1)S(1)} %shard_map.60), channel_id=1, source_target_pairs={{0,4},{2,6},{4,0},{6,2},{8,12},{10,14},{12,8},{14,10},{16,20},{18,... | collective-permute-start | bytes 1179656 | tf_op jit(solution)/shard_map/ppermute | solution.py:28
  26.0 2.3 %collective-permute-done.5.refs_3_ = bf16[768,256]{1,0:T(8,128)(2,1)S(1)} collective-permute-done((bf16[768,256]{1,0:T(8,128)(2,1)S(1)}, bf16[768,256]{1,0:T(8,128)(2,1)S(1)}, u32[]{:S(2)}, u32[]{:S(2)}) %collective-permute-start.5) | collective-permute-done | bytes 393248 | tf_op jit(solution)/shard_map/ppermute | solution.py:28
  28.4 0.9 %shard_map.59 = (f32[6,512,128]{2,1,0:T(8,128)S(1)}, f32[6,512,128]{2,1,0:T(8,128)S(1)}) custom-call(s32[3]{0:T(128)S(1)} %copy-done.1, s32[3]{0:T(128)S(1)} %collective-permute-done.1.recv_starts_ref, bf16[6,512,128]{2,1,0:T(8,128)(2,1)S(1)} %get-tuple-element.44.refs_0_, f32[6,512,128]{2,1,0:T(8,128)S(1)} %get-tuple-element.49.refs_1_, ...), custom_call_target="tpu_custom_call" | custom-call | flops 4000000000 | bytes 8388608 | tf_op jit(solution)/shard_map/pallas_call | solution.py:270
  29.3 6.7 %collective-permute-done.7.refs_3_ = bf16[768,256]{1,0:T(8,128)(2,1)S(1)} collective-permute-done((bf16[768,256]{1,0:T(8,128)(2,1)S(1)}, bf16[768,256]{1,0:T(8,128)(2,1)S(1)}, u32[]{:S(2)}, u32[]{:S(2)}) %collective-permute-start.7) | collective-permute-done | bytes 393248 | tf_op jit(solution)/shard_map/ppermute | solution.py:28
  36.0 0.0 slice-start
  36.0 3.2 %shard_map.62 = bf16[384,512]{1,0:T(8,128)(2,1)S(1)} custom-call(s32[3]{0:T(128)S(1)} %copy-done.1, s32[3]{0:T(128)S(1)} %collective-permute-done.1.recv_starts_ref, bf16[6,512,128]{2,1,0:T(8,128)(2,1)S(1)} %get-tuple-element.44.refs_0_, f32[6,512,128]{2,1,0:T(8,128)S(1)} %get-tuple-element.51.refs_1_, f32[6,512,128]{2,1,0:T(8,128)S(1)} %get-tuple-element.52.refs_2_, ...), custom_call_target="tpu_custom_call" | custom-call | flops 2000000000 | bytes 8388608 | tf_op jit(solution)/shard_map/pallas_call | solution.py:270
  39.2 0.0 slice-start.1
  39.2 0.1 collective-permute-start.8
  39.3 1.6 %collective-permute-start.12 = (bf16[384,512]{1,0:T(8,128)(2,1)S(1)}, bf16[384,512]{1,0:T(8,128)(2,1)S(1)}, u32[]{:S(2)}, u32[]{:S(2)}) collective-permute-start(bf16[384,512]{1,0:T(8,128)(2,1)S(1)} %shard_map.62), channel_id=1, source_target_pairs={{0,3},{1,2},{2,1},{3,0},{4,7},{5,6},{6,5},{7,4},{8,11},{9,10},{10,... | collective-permute-start | bytes 1179656 | tf_op jit(solution)/shard_map/ppermute | solution.py:34
  40.9 0.0 collective-permute-done.10.window_ref
  40.9 0.1 shard_map.63
  41.0 1.7 %collective-permute-start.11 = (bf16[512,768]{1,0:T(8,128)(2,1)S(1)}, bf16[512,768]{1,0:T(8,128)(2,1)S(1)}, u32[]{:S(2)}, u32[]{:S(2)}) collective-permute-start(bf16[512,768]{1,0:T(8,128)(2,1)S(1)} %shard_map.63), channel_id=1, source_target_pairs={{0,8},{2,10},{4,12},{6,14},{8,0},{10,2},{12,4},{14,6},{16,24},{18,... | collective-permute-start | bytes 2359304 | tf_op jit(solution)/shard_map/ppermute | solution.py:28
  42.7 3.0 %shard_map.61 = bf16[384,512]{1,0:T(8,128)(2,1)S(1)} custom-call(s32[3]{0:T(128)S(1)} %copy-done.1, s32[3]{0:T(128)S(1)} %collective-permute-done.1.recv_starts_ref, bf16[6,512,128]{2,1,0:T(8,128)(2,1)S(1)} %get-tuple-element.44.refs_0_, f32[6,512,128]{2,1,0:T(8,128)S(1)} %get-tuple-element.51.refs_1_, f32[6,512,128]{2,1,0:T(8,128)S(1)} %get-tuple-element.52.refs_2_, ...), custom_call_target="tpu_custom_call" | custom-call | flops 2000000000 | bytes 8388608 | tf_op jit(solution)/shard_map/pallas_call | solution.py:270
  45.7 0.6 collective-permute-start.9
  46.2 0.0 collective-permute-start.13
  46.2 0.0 collective-permute-done.8
  46.2 0.0 slice-done
  46.2 0.0 slice-done.1
  46.3 1.2 %fusion = f32[384,2048]{1,0:T(8,128)S(1)} fusion(bf16[384,512]{1,0:T(8,128)(2,1)S(1)} %collective-permute-done.8, bf16[1024,4096]{1,0:T(8,128)(2,1)S(1)} %bitcast.3, s32[]{:T(128)S(6)} %mul.29, s32[]{:T(128)S(6)} %mul.28), kind=kOutput, calls=%fused_computation.1 | convolution fusion | flops 805306368 | bytes 5636104 | tf_op jit(solution)/shard_map/dot_general | solution.py:330
  47.5 1.3 %add_convert_fusion.given_ref = bf16[384,2048]{1,0:T(8,128)(2,1)S(1)} fusion(f32[384,2048]{1,0:T(8,128)S(1)} %fusion, bf16[384,512]{1,0:T(8,128)(2,1)S(1)} %shard_map.61, bf16[1024,4096]{1,0:T(8,128)(2,1)S(1)} %bitcast.3, s32[]{:T(128)S(6)} %mul.25, s32[]{:T(128)S(6)} %mul.28), kind=kOutput, calls=%fused_computation | convolution fusion | flops 806879232 | bytes 7208968 | tf_op jit(solution)/shard_map/dot_general | solution.py:330
  48.8 10.4 %collective-permute-done.9.heads_ref = bf16[384,512]{1,0:T(8,128)(2,1)S(1)} collective-permute-done((bf16[384,512]{1,0:T(8,128)(2,1)S(1)}, bf16[384,512]{1,0:T(8,128)(2,1)S(1)}, u32[]{:S(2)}, u32[]{:S(2)}) %collective-permute-start.9) | collective-permute-done | bytes 393248 | tf_op jit(solution)/shard_map/ppermute | solution.py:34
  59.2 0.0 collective-permute-done.12.heads_ref
  59.2 1.4 %collective-permute-done.11.rest_ref = bf16[512,768]{1,0:T(8,128)(2,1)S(1)} collective-permute-done((bf16[512,768]{1,0:T(8,128)(2,1)S(1)}, bf16[512,768]{1,0:T(8,128)(2,1)S(1)}, u32[]{:S(2)}, u32[]{:S(2)}) %collective-permute-start.11) | collective-permute-done | bytes 786464 | tf_op jit(solution)/shard_map/ppermute | solution.py:28
  60.5 0.0 collective-permute-start.14
  60.5 1.1 %shard_map.64.given_ref = f32[384,2048]{1,0:T(8,128)S(1)} custom-call(bf16[384,2048]{1,0:T(8,128)(2,1)S(1)} %add_convert_fusion.given_ref, bf16[384,512]{1,0:T(8,128)(2,1)S(1)} %collective-permute-done.9.heads_ref, bf16[512,1280]{1,0:T(8,128)(2,1)S(1)} %collective-permute-done.10.window_ref, bf16[512,768]{1,0:T(8,128)(2,1)S(1)} %collective-permute-done.11.rest_ref), custom_call_target="tpu_custom_call" | custom-call | flops 805306368 | bytes 4194304 | tf_op jit(solution)/shard_map/pallas_call | solution.py:104
  61.7 0.0 collective-permute-done.13.window_ref
  61.7 1.1 %collective-permute-done.14.rest_ref = bf16[512,768]{1,0:T(8,128)(2,1)S(1)} collective-permute-done((bf16[512,768]{1,0:T(8,128)(2,1)S(1)}, bf16[512,768]{1,0:T(8,128)(2,1)S(1)}, u32[]{:S(2)}, u32[]{:S(2)}) %collective-permute-start.14) | collective-permute-done | bytes 786464 | tf_op jit(solution)/shard_map/ppermute | solution.py:28
  62.8 2.1 %shard_map.65 = bf16[384,2048]{1,0:T(8,128)(2,1)} custom-call(f32[384,2048]{1,0:T(8,128)S(1)} %shard_map.64.given_ref, bf16[384,512]{1,0:T(8,128)(2,1)S(1)} %collective-permute-done.12.heads_ref, bf16[512,1280]{1,0:T(8,128)(2,1)S(1)} %collective-permute-done.13.window_ref, bf16[512,768]{1,0:T(8,128)(2,1)S(1)} %collective-permute-done.14.rest_ref), custom_call_target="tpu_custom_call" | custom-call | flops 805306368 | bytes 4194304 | tf_op jit(solution)/shard_map/pallas_call | solution.py:104
  (6 shorter events, 0.1 us)
Async XLA Ops:
  0.0 5.3 %collective-permute-start.2 = (bf16[384,1024]{1,0:T(8,128)(2,1)}, bf16[384,1024]{1,0:T(8,128)(2,1)S(1)}, u32[]{:S(2)}, u32[]{:S(2)}) collective-permute-start(bf16[384,1024]{1,0:T(8,128)(2,1)} %refs_0_.1), channel_id=1, source_target_pairs={{0,2},{2,0},{4,6},{6,4},{8,10},{10,8},{12,14},{14,12},{16,18},{18,... | collective-permute-start | bytes 2359304 | tf_op jit(solution)/shard_map/ppermute | solution.py:28
  1.3 7.7 %copy-start = (bf16[384,1024]{1,0:T(8,128)(2,1)S(1)}, bf16[384,1024]{1,0:T(8,128)(2,1)}, u32[]{:S(2)}) copy-start(bf16[384,1024]{1,0:T(8,128)(2,1)} %refs_0_.1) | copy-start | bytes 2359300
  1.3 7.7 %copy-start.1 = (s32[3]{0:T(128)S(1)}, s32[3]{0:T(128)}, u32[]{:S(2)}) copy-start(s32[3]{0:T(128)} %starts_ref.9) | copy-start | bytes 40
  1.4 2.3 %collective-permute-start = (bf16[384,256]{1,0:T(8,128)(2,1)S(1)}, bf16[384,256]{1,0:T(8,128)(2,1)S(1)}, u32[]{:S(2)}, u32[]{:S(2)}) collective-permute-start(bf16[384,256]{1,0:T(8,128)(2,1)S(1)} %pad_maximum_fusion), channel_id=1, source_target_pairs={{0,2},{2,0},{4,6},{6,4},{8,10},{10,8},{12,14},{14,12},{16,18},{18,... | collective-permute-start | bytes 589832 | tf_op jit(solution)/shard_map/ppermute | solution.py:28
  1.9 1.7 %collective-permute-start.1 = (s32[3]{0:T(128)}, s32[3]{0:T(128)S(1)}, u32[]{:S(2)}, u32[]{:S(2)}) collective-permute-start(s32[3]{0:T(128)} %starts_ref.9), channel_id=1, source_target_pairs={{0,2},{2,0},{4,6},{6,4},{8,10},{10,8},{12,14},{14,12},{16,18},{18,... | collective-permute-start | bytes 44 | tf_op jit(solution)/shard_map/ppermute | solution.py:28
  2.0 10.7 %collective-permute-start.3 = (bf16[384,256]{1,0:T(8,128)(2,1)S(1)}, bf16[384,256]{1,0:T(8,128)(2,1)S(1)}, u32[]{:S(2)}, u32[]{:S(2)}) collective-permute-start(bf16[384,256]{1,0:T(8,128)(2,1)S(1)} %pad_maximum_fusion.1.first_ref), channel_id=1, source_target_pairs={{0,8},{2,10},{4,12},{6,14},{8,16},{10,18},{12,20},{14,22},{16,24},... | collective-permute-start | bytes 589832 | tf_op jit(solution)/shard_map/ppermute | solution.py:19
  3.7 11.7 %collective-permute-start.4 = (bf16[384,256]{1,0:T(8,128)(2,1)S(1)}, bf16[384,256]{1,0:T(8,128)(2,1)S(1)}, u32[]{:S(2)}, u32[]{:S(2)}) collective-permute-start(bf16[384,256]{1,0:T(8,128)(2,1)S(1)} %collective-permute-done.second_ref), channel_id=1, source_target_pairs={{0,8},{2,10},{4,12},{6,14},{8,16},{10,18},{12,20},{14,22},{16,24},... | collective-permute-start | bytes 589832 | tf_op jit(solution)/shard_map/ppermute | solution.py:19
  7.5 33.5 %collective-permute-start.10 = (bf16[512,1280]{1,0:T(8,128)(2,1)S(1)}, bf16[512,1280]{1,0:T(8,128)(2,1)S(1)}, u32[]{:S(2)}, u32[]{:S(2)}) collective-permute-start(bf16[512,1280]{1,0:T(8,128)(2,1)S(1)} %dynamic_slice.23), channel_id=1, source_target_pairs={{0,1},{1,0},{2,3},{3,2},{4,5},{5,4},{6,7},{7,6},{8,9},{9,8},{10,11... | collective-permute-start | bytes 3932168 | tf_op jit(solution)/shard_map/ppermute | solution.py:34
  15.4 9.8 %collective-permute-start.6 = (bf16[768,256]{1,0:T(8,128)(2,1)S(1)}, bf16[768,256]{1,0:T(8,128)(2,1)S(1)}, u32[]{:S(2)}, u32[]{:S(2)}) collective-permute-start(bf16[768,256]{1,0:T(8,128)(2,1)S(1)} %shard_map.57.refs_3_), channel_id=1, source_target_pairs={{0,8},{2,10},{4,12},{6,14},{8,16},{10,18},{12,20},{14,22},{16,24},... | collective-permute-start | bytes 1179656 | tf_op jit(solution)/shard_map/ppermute | solution.py:24
  17.1 11.2 %collective-permute-start.5 = (bf16[768,256]{1,0:T(8,128)(2,1)S(1)}, bf16[768,256]{1,0:T(8,128)(2,1)S(1)}, u32[]{:S(2)}, u32[]{:S(2)}) collective-permute-start(bf16[768,256]{1,0:T(8,128)(2,1)S(1)} %shard_map.57.refs_3_), channel_id=1, source_target_pairs={{0,4},{2,6},{4,0},{6,2},{8,12},{10,14},{12,8},{14,10},{16,20},{18,... | collective-permute-start | bytes 1179656 | tf_op jit(solution)/shard_map/ppermute | solution.py:28
  25.3 10.7 %collective-permute-start.7 = (bf16[768,256]{1,0:T(8,128)(2,1)S(1)}, bf16[768,256]{1,0:T(8,128)(2,1)S(1)}, u32[]{:S(2)}, u32[]{:S(2)}) collective-permute-start(bf16[768,256]{1,0:T(8,128)(2,1)S(1)} %shard_map.60), channel_id=1, source_target_pairs={{0,4},{2,6},{4,0},{6,2},{8,12},{10,14},{12,8},{14,10},{16,20},{18,... | collective-permute-start | bytes 1179656 | tf_op jit(solution)/shard_map/ppermute | solution.py:28
  36.0 10.2 %slice-start = ((s8[8388608]{0:T(1024)(128)(4,1)}), s8[4194304]{0:T(1024)(128)(4,1)S(1)}, s32[]{:S(2)}) async-start(s8[8388608]{0:T(1024)(128)(4,1)} %bitcast.2), calls=%async_computation | async-start | bytes 8388608
  39.2 7.1 %slice-start.1 = ((s8[8388608]{0:T(1024)(128)(4,1)}), s8[4194304]{0:T(1024)(128)(4,1)S(1)}, s32[]{:S(2)}) async-start(s8[8388608]{0:T(1024)(128)(4,1)} %bitcast.2), calls=%async_computation.1 | async-start | bytes 8388608
  39.2 7.1 %collective-permute-start.8 = (bf16[384,512]{1,0:T(8,128)(2,1)S(1)}, bf16[384,512]{1,0:T(8,128)(2,1)S(1)}, u32[]{:S(2)}, u32[]{:S(2)}) collective-permute-start(bf16[384,512]{1,0:T(8,128)(2,1)S(1)} %shard_map.62), channel_id=1, source_target_pairs={{0,2},{2,0},{4,6},{6,4},{8,10},{10,8},{12,14},{14,12},{16,18},{18,... | collective-permute-start | bytes 1179656 | tf_op jit(solution)/shard_map/ppermute | solution.py:28
  39.3 19.9 %collective-permute-start.12 = (bf16[384,512]{1,0:T(8,128)(2,1)S(1)}, bf16[384,512]{1,0:T(8,128)(2,1)S(1)}, u32[]{:S(2)}, u32[]{:S(2)}) collective-permute-start(bf16[384,512]{1,0:T(8,128)(2,1)S(1)} %shard_map.62), channel_id=1, source_target_pairs={{0,3},{1,2},{2,1},{3,0},{4,7},{5,6},{6,5},{7,4},{8,11},{9,10},{10,... | collective-permute-start | bytes 1179656 | tf_op jit(solution)/shard_map/ppermute | solution.py:34
  41.0 19.6 %collective-permute-start.11 = (bf16[512,768]{1,0:T(8,128)(2,1)S(1)}, bf16[512,768]{1,0:T(8,128)(2,1)S(1)}, u32[]{:S(2)}, u32[]{:S(2)}) collective-permute-start(bf16[512,768]{1,0:T(8,128)(2,1)S(1)} %shard_map.63), channel_id=1, source_target_pairs={{0,8},{2,10},{4,12},{6,14},{8,0},{10,2},{12,4},{14,6},{16,24},{18,... | collective-permute-start | bytes 2359304 | tf_op jit(solution)/shard_map/ppermute | solution.py:28
  45.7 13.5 %collective-permute-start.9 = (bf16[384,512]{1,0:T(8,128)(2,1)S(1)}, bf16[384,512]{1,0:T(8,128)(2,1)S(1)}, u32[]{:S(2)}, u32[]{:S(2)}) collective-permute-start(bf16[384,512]{1,0:T(8,128)(2,1)S(1)} %shard_map.61), channel_id=1, source_target_pairs={{0,1},{1,0},{2,3},{3,2},{4,5},{5,4},{6,7},{7,6},{8,9},{9,8},{10,11... | collective-permute-start | bytes 1179656 | tf_op jit(solution)/shard_map/ppermute | solution.py:34
  46.2 15.4 %collective-permute-start.13 = (bf16[512,1280]{1,0:T(8,128)(2,1)S(1)}, bf16[512,1280]{1,0:T(8,128)(2,1)S(1)}, u32[]{:S(2)}, u32[]{:S(2)}) collective-permute-start(bf16[512,1280]{1,0:T(8,128)(2,1)S(1)} %collective-permute-done.10.window_ref), channel_id=1, source_target_pairs={{0,2},{2,0},{4,6},{6,4},{8,10},{10,8},{12,14},{14,12},{16,18},{18,... | collective-permute-start | bytes 3932168 | tf_op jit(solution)/shard_map/ppermute | solution.py:28
  60.5 2.3 %collective-permute-start.14 = (bf16[512,768]{1,0:T(8,128)(2,1)S(1)}, bf16[512,768]{1,0:T(8,128)(2,1)S(1)}, u32[]{:S(2)}, u32[]{:S(2)}) collective-permute-start(bf16[512,768]{1,0:T(8,128)(2,1)S(1)} %collective-permute-done.11.rest_ref), channel_id=1, source_target_pairs={{0,2},{2,0},{4,6},{6,4},{8,10},{10,8},{12,14},{14,12},{16,18},{18,... | collective-permute-start | bytes 2359304 | tf_op jit(solution)/shard_map/ppermute | solution.py:28

commit v15 on v14

--- a/solution.py
+++ b/solution.py
@@ -70,20 +70,26 @@
     out_ref[...] = window_ref[:, pl.ds(pl.multiple_of(first, HEAD_SIZE), out_ref.shape[1])]
 
 
-def project_kernel(final, given_ref, heads_ref, window_ref, rest_ref, *refs):
+def project_kernel(final, wide, has_window, given_ref, heads_ref, *refs):
+    cols_all = given_ref.shape[1]
+    narrow = cols_all - wide
     fetched = lax.axis_index("ctx") // 4 % 2
-    wide, narrow = window_ref.shape[1], rest_ref.shape[1]
-    half = wide // 2
+    window_ref, refs = (refs[0], refs[1:]) if has_window else (None, refs)
+    n_out = 5 if final else 1
+    rest_ref, refs = (refs[0], refs[1:]) if len(refs) > n_out else (None, refs)
+    half = -(-wide // 256) * 128
     tiles = (
-        (window_ref.at[:, :half], fetched * narrow),
-        (window_ref.at[:, half:], fetched * narrow + half),
-        (rest_ref, (1 - fetched) * wide),
+        (window_ref, 0, half, fetched * narrow),
+        (window_ref, half, wide - half, fetched * narrow + half),
+        (rest_ref, 0, narrow, (1 - fetched) * wide),
     )
     copies = []
-    for n, (tile, col) in enumerate(tiles):
-        cols = pl.ds(pl.multiple_of(col, HEAD_SIZE), tile.shape[1])
+    for n, (ref, start, width, col) in enumerate(tiles):
+        cols = pl.ds(pl.multiple_of(col, HEAD_SIZE), width)
         total = given_ref[:, cols].astype(jnp.float32)
-        total += jnp.dot(heads_ref[...], tile[...], preferred_element_type=jnp.float32)
+        if ref is not None:
+            rows = ref[:, start : start + width]
+            total += jnp.dot(heads_ref[...], rows, preferred_element_type=jnp.float32)
         if final:
             out_ref, built, sems = refs[0], refs[1 + n], refs[4]
             built[...] = total.astype(out_ref.dtype)
@@ -95,16 +101,17 @@
         copy.wait()
 
 
-def project(final, given, heads, parts):
+def project(final, wide, given, heads, window, rest):
     tok, cols = given.shape
+    parts = [x for x in (window, rest) if x is not None]
     vmem = pl.BlockSpec(memory_space=pltpu.VMEM)
-    half = parts[0].shape[1] // 2
-    scratch = [pltpu.VMEM((tok, n), jnp.bfloat16) for n in (half, half, parts[1].shape[1])]
+    half = -(-wide // 256) * 128
+    scratch = [pltpu.VMEM((tok, n), jnp.bfloat16) for n in (half, wide - half, cols - wide)]
     scratch += [pltpu.SemaphoreType.DMA((3,))]
     return pl.pallas_call(
-        functools.partial(project_kernel, final),
+        functools.partial(project_kernel, final, wide, window is not None),
         out_shape=jax.ShapeDtypeStruct(given.shape, jnp.bfloat16 if final else jnp.float32),
-        in_specs=[vmem] * 4,
+        in_specs=[vmem] * (2 + len(parts)),
         out_specs=pl.BlockSpec(memory_space=pltpu.HBM) if final else vmem,
         scratch_shapes=scratch if final else [],
         compiler_params=pltpu.CompilerParams(vmem_limit_bytes=16 * 2**20),
@@ -238,7 +245,7 @@
 
         for j in range(half):
             total = stats_ref[j, :, HEAD_SIZE // 2 : HEAD_SIZE // 2 + 1]
-            o = (acc_ref[j] / total).astype(jnp.bfloat16)
+            o = (acc_ref[j] * (1.0 / total)).astype(jnp.bfloat16)
             for h in range(n_head):
                 out_ref[j * BLOCK : (j + 1) * BLOCK, h * HEAD_SIZE : (h + 1) * HEAD_SIZE] = o[
                     h * BLOCK : (h + 1) * BLOCK
@@ -332,9 +339,9 @@
     )
     here = here.astype(jnp.bfloat16)
     _, _, _, late = lax.optimization_barrier((here, across_own, across_other, passed))
-    other_rows = (swap(fetched, 1), swap(late, 1))
-    here = project(False, here, across_own, (fetched, passed))
-    return project(True, here, across_other, other_rows)
+    here = project(False, cols - narrow, here, across_other, swap(fetched, 1), None)
+    here = project(False, cols - narrow, here, across_own, fetched, passed)
+    return project(True, cols - narrow, here, across_other, None, swap(late, 1))
 
 
 def solution(mesh):

time: 65.6 us -> 65.7 us (level)
    pallas_call x2 -> x3, Pallas kernels: 3.19 us -> 3.64 us  [project(): pl.pallas_call(functools.partial(project_kernel, final, wide, window is n...]
  transfers between devices with their start and end apart: 15 -> 15, of which waited for: 7 -> 7; matrix products, arithmetic and copies ran while one was open for 9% -> 9% of each run, Pallas kernels for 20% -> 21%
where the time goes in v15:
time: 65.7 us; the launch traced here: 65.1 us
  waiting for transfers between devices  30.7 us (47%)
  Pallas kernels  15.4 us (23%)
  starting transfers between devices  12.5 us (19%)
  local copies, waits for them, and re-layouts  3.46 us (5%)
  matrix products  2.6 us (4%)
    pallas_call x5, Pallas kernels, attention_call(): pl.pallas_call(functools.partial(attention_kernel, stage, distances, n_he...  11.7 us
    ppermute x9, waiting for transfers between devices, swap(): lax.ppermute(x, 'ctx', [(i, i ^ mask) for i in range(lax.axis_size('ctx'))])  11.1 us
    ppermute x3, waiting for transfers between devices, cross(): return lax.ppermute(x, ('ctx', 'head'), route)  10.3 us
    ppermute x1, waiting for transfers between devices, shift(): lax.ppermute(x, 'ctx', [(i, i + distance) for i in range(n - distance)])  6.7 us
    ppermute x9, starting transfers between devices, swap(): lax.ppermute(x, 'ctx', [(i, i ^ mask) for i in range(lax.axis_size('ctx'))])  3.83 us
    ppermute x3, starting transfers between devices, cross(): return lax.ppermute(x, ('ctx', 'head'), route)  3.8 us
    pallas_call x3, Pallas kernels, project(): pl.pallas_call(functools.partial(project_kernel, final, wide, window is n...  3.64 us
    dynamic_slice x2, local copies, waits for them, and re-layouts, cut(): return lax.dynamic_slice(x, start, size, allow_negative_indices=False)  3.44 us
  transfers between devices with their start and end apart: 15, of which 7 were waited for; matrix products, arithmetic and copies ran while one was open for 9% of the time, Pallas kernels for 21%

profile of v15, /device:TPU:2, one launch (start us, length us, event | category | flops | bytes accessed | tf_op | source)
XLA Modules:
  0.0 65.1 jit_solution(10175779817541096397)
XLA Ops:
  0.0 0.0 collective-permute-start.2
  0.0 1.3 %constant_dynamic-slice_fusion = (bf16[384,128]{1,0:T(8,128)(2,1)S(1)}, bf16[384,128]{1,0:T(8,128)(2,1)S(1)}, bf16[384,128]{1,0:T(8,128)(2,1)S(1)}, bf16[384,128]{1,0:T(8,128)(2,1)S(1)}) fusion(bf16[384,256]{1,0:T(8,128)(2,1)} %param.7, s32[]{:T(128)S(6)} %mul.23, s32[]{:T(128)S(6)} %mul.24, bf16[384,256]{1,0:T(8,128)(2,1)} %param.6), kind=kLoop, calls=%fused_computation.6 | loop fusion | bytes 786440 | tf_op jit(solution)/shard_map/dynamic_slice | solution.py:304
  1.3 0.0 copy-start
  1.3 0.0 copy-start.1
  1.4 0.6 collective-permute-start
  1.9 0.1 collective-permute-start.1
  2.0 1.6 %collective-permute-start.3 = (bf16[384,256]{1,0:T(8,128)(2,1)S(1)}, bf16[384,256]{1,0:T(8,128)(2,1)S(1)}, u32[]{:S(2)}, u32[]{:S(2)}) collective-permute-start(bf16[384,256]{1,0:T(8,128)(2,1)S(1)} %pad_maximum_fusion.1.first_ref), channel_id=1, source_target_pairs={{0,8},{2,10},{4,12},{6,14},{8,16},{10,18},{12,20},{14,22},{16,24},... | collective-permute-start | bytes 589832 | tf_op jit(solution)/shard_map/ppermute | solution.py:19
  3.7 0.0 collective-permute-done.1.recv_starts_ref
  3.7 0.0 collective-permute-done.second_ref
  3.7 1.6 %collective-permute-start.4 = (bf16[384,256]{1,0:T(8,128)(2,1)S(1)}, bf16[384,256]{1,0:T(8,128)(2,1)S(1)}, u32[]{:S(2)}, u32[]{:S(2)}) collective-permute-start(bf16[384,256]{1,0:T(8,128)(2,1)S(1)} %collective-permute-done.second_ref), channel_id=1, source_target_pairs={{0,8},{2,10},{4,12},{6,14},{8,16},{10,18},{12,20},{14,22},{16,24},... | collective-permute-start | bytes 589832 | tf_op jit(solution)/shard_map/ppermute | solution.py:19
  5.3 0.0 collective-permute-done.2.refs_1_
  5.3 2.1 %dynamic_slice.23 = bf16[512,1280]{1,0:T(8,128)(2,1)S(1)} dynamic-slice(bf16[1024,4096]{1,0:T(8,128)(2,1)} %param.9, s32[]{:T(128)S(6)} %mul.25, s32[]{:T(128)S(6)} %add.16), dynamic_slice_sizes={512,1280} | dynamic-slice | bytes 2621444 | tf_op jit(solution)/shard_map/dynamic_slice | solution.py:304
  7.5 1.6 %collective-permute-start.10 = (bf16[512,1280]{1,0:T(8,128)(2,1)S(1)}, bf16[512,1280]{1,0:T(8,128)(2,1)S(1)}, u32[]{:S(2)}, u32[]{:S(2)}) collective-permute-start(bf16[512,1280]{1,0:T(8,128)(2,1)S(1)} %dynamic_slice.23), channel_id=1, source_target_pairs={{0,1},{1,0},{2,3},{3,2},{4,5},{5,4},{6,7},{7,6},{8,9},{9,8},{10,11... | collective-permute-start | bytes 3932168 | tf_op jit(solution)/shard_map/ppermute | solution.py:34
  9.0 0.0 copy-done
  9.0 0.0 copy-done.1
  9.0 3.7 %shard_map.56 = (bf16[6,512,128]{2,1,0:T(8,128)(2,1)S(1)}, f32[6,512,128]{2,1,0:T(8,128)S(1)}, f32[6,512,128]{2,1,0:T(8,128)S(1)}) custom-call(s32[3]{0:T(128)S(1)} %copy-done.1, s32[3]{0:T(128)S(1)} %collective-permute-done.1.recv_starts_ref, bf16[384,1024]{1,0:T(8,128)(2,1)S(1)} %copy-done, bf16[384,1024]{1,0:T(8,128)(2,1)S(1)} %collective-permute-done.2.refs_1_, ...), custom_call_target="tpu_custom_call" | custom-call | flops 5000000000 | bytes 8388608 | tf_op jit(solution)/shard_map/pallas_call | solution.py:277
  12.8 0.0 collective-permute-done.3.first_ref
  12.8 2.6 %collective-permute-done.4.second_ref = bf16[384,256]{1,0:T(8,128)(2,1)S(1)} collective-permute-done((bf16[384,256]{1,0:T(8,128)(2,1)S(1)}, bf16[384,256]{1,0:T(8,128)(2,1)S(1)}, u32[]{:S(2)}, u32[]{:S(2)}) %collective-permute-start.4) | collective-permute-done | bytes 196640 | tf_op jit(solution)/shard_map/ppermute | solution.py:19
  15.4 1.7 %collective-permute-start.6 = (bf16[768,256]{1,0:T(8,128)(2,1)S(1)}, bf16[768,256]{1,0:T(8,128)(2,1)S(1)}, u32[]{:S(2)}, u32[]{:S(2)}) collective-permute-start(bf16[768,256]{1,0:T(8,128)(2,1)S(1)} %shard_map.57.refs_3_), channel_id=1, source_target_pairs={{0,8},{2,10},{4,12},{6,14},{8,16},{10,18},{12,20},{14,22},{16,24},... | collective-permute-start | bytes 1179656 | tf_op jit(solution)/shard_map/ppermute | solution.py:24
  17.1 0.6 collective-permute-start.5
  17.7 0.8 %shard_map.58 = (f32[6,512,128]{2,1,0:T(8,128)S(1)}, f32[6,512,128]{2,1,0:T(8,128)S(1)}) custom-call(s32[3]{0:T(128)S(1)} %copy-done.1, s32[3]{0:T(128)S(1)} %collective-permute-done.1.recv_starts_ref, bf16[6,512,128]{2,1,0:T(8,128)(2,1)S(1)} %get-tuple-element.44.refs_0_, f32[6,512,128]{2,1,0:T(8,128)S(1)} %get-tuple-element.45.refs_1_, ...), custom_call_target="tpu_custom_call" | custom-call | flops 2100000000 | bytes 8388608 | tf_op jit(solution)/shard_map/pallas_call | solution.py:277
  18.6 6.7 %collective-permute-done.6.refs_4_.odd_ref = bf16[768,256]{1,0:T(8,128)(2,1)S(1)} collective-permute-done((bf16[768,256]{1,0:T(8,128)(2,1)S(1)}, bf16[768,256]{1,0:T(8,128)(2,1)S(1)}, u32[]{:S(2)}, u32[]{:S(2)}) %collective-permute-start.6) | collective-permute-done | bytes 393248 | tf_op jit(solution)/shard_map/ppermute | solution.py:24
  25.3 0.7 %collective-permute-start.7 = (bf16[768,256]{1,0:T(8,128)(2,1)S(1)}, bf16[768,256]{1,0:T(8,128)(2,1)S(1)}, u32[]{:S(2)}, u32[]{:S(2)}) collective-permute-start(bf16[768,256]{1,0:T(8,128)(2,1)S(1)} %shard_map.60), channel_id=1, source_target_pairs={{0,4},{2,6},{4,0},{6,2},{8,12},{10,14},{12,8},{14,10},{16,20},{18,... | collective-permute-start | bytes 1179656 | tf_op jit(solution)/shard_map/ppermute | solution.py:28
  26.0 2.3 %collective-permute-done.5.refs_3_ = bf16[768,256]{1,0:T(8,128)(2,1)S(1)} collective-permute-done((bf16[768,256]{1,0:T(8,128)(2,1)S(1)}, bf16[768,256]{1,0:T(8,128)(2,1)S(1)}, u32[]{:S(2)}, u32[]{:S(2)}) %collective-permute-start.5) | collective-permute-done | bytes 393248 | tf_op jit(solution)/shard_map/ppermute | solution.py:28
  28.4 0.9 %shard_map.59 = (f32[6,512,128]{2,1,0:T(8,128)S(1)}, f32[6,512,128]{2,1,0:T(8,128)S(1)}) custom-call(s32[3]{0:T(128)S(1)} %copy-done.1, s32[3]{0:T(128)S(1)} %collective-permute-done.1.recv_starts_ref, bf16[6,512,128]{2,1,0:T(8,128)(2,1)S(1)} %get-tuple-element.44.refs_0_, f32[6,512,128]{2,1,0:T(8,128)S(1)} %get-tuple-element.49.refs_1_, ...), custom_call_target="tpu_custom_call" | custom-call | flops 4000000000 | bytes 8388608 | tf_op jit(solution)/shard_map/pallas_call | solution.py:277
  29.3 6.7 %collective-permute-done.7.refs_3_ = bf16[768,256]{1,0:T(8,128)(2,1)S(1)} collective-permute-done((bf16[768,256]{1,0:T(8,128)(2,1)S(1)}, bf16[768,256]{1,0:T(8,128)(2,1)S(1)}, u32[]{:S(2)}, u32[]{:S(2)}) %collective-permute-start.7) | collective-permute-done | bytes 393248 | tf_op jit(solution)/shard_map/ppermute | solution.py:28
  36.0 0.0 slice-start
  36.0 3.2 %shard_map.62 = bf16[384,512]{1,0:T(8,128)(2,1)S(1)} custom-call(s32[3]{0:T(128)S(1)} %copy-done.1, s32[3]{0:T(128)S(1)} %collective-permute-done.1.recv_starts_ref, bf16[6,512,128]{2,1,0:T(8,128)(2,1)S(1)} %get-tuple-element.44.refs_0_, f32[6,512,128]{2,1,0:T(8,128)S(1)} %get-tuple-element.51.refs_1_, f32[6,512,128]{2,1,0:T(8,128)S(1)} %get-tuple-element.52.refs_2_, ...), custom_call_target="tpu_custom_call" | custom-call | flops 2000000000 | bytes 8388608 | tf_op jit(solution)/shard_map/pallas_call | solution.py:277
  39.2 0.0 slice-start.1
  39.2 0.1 collective-permute-start.8
  39.3 1.6 %collective-permute-start.9 = (bf16[384,512]{1,0:T(8,128)(2,1)S(1)}, bf16[384,512]{1,0:T(8,128)(2,1)S(1)}, u32[]{:S(2)}, u32[]{:S(2)}) collective-permute-start(bf16[384,512]{1,0:T(8,128)(2,1)S(1)} %shard_map.62), channel_id=1, source_target_pairs={{0,3},{1,2},{2,1},{3,0},{4,7},{5,6},{6,5},{7,4},{8,11},{9,10},{10,... | collective-permute-start | bytes 1179656 | tf_op jit(solution)/shard_map/ppermute | solution.py:34
  40.9 0.0 collective-permute-done.10.window_ref.refs_0_
  40.9 0.1 collective-permute-start.11
  41.0 0.1 shard_map.64
  41.0 1.7 %collective-permute-start.13 = (bf16[512,768]{1,0:T(8,128)(2,1)S(1)}, bf16[512,768]{1,0:T(8,128)(2,1)S(1)}, u32[]{:S(2)}, u32[]{:S(2)}) collective-permute-start(bf16[512,768]{1,0:T(8,128)(2,1)S(1)} %shard_map.64), channel_id=1, source_target_pairs={{0,8},{2,10},{4,12},{6,14},{8,0},{10,2},{12,4},{14,6},{16,24},{18,... | collective-permute-start | bytes 2359304 | tf_op jit(solution)/shard_map/ppermute | solution.py:28
  42.7 3.0 %shard_map.61 = bf16[384,512]{1,0:T(8,128)(2,1)S(1)} custom-call(s32[3]{0:T(128)S(1)} %copy-done.1, s32[3]{0:T(128)S(1)} %collective-permute-done.1.recv_starts_ref, bf16[6,512,128]{2,1,0:T(8,128)(2,1)S(1)} %get-tuple-element.44.refs_0_, f32[6,512,128]{2,1,0:T(8,128)S(1)} %get-tuple-element.51.refs_1_, f32[6,512,128]{2,1,0:T(8,128)S(1)} %get-tuple-element.52.refs_2_, ...), custom_call_target="tpu_custom_call" | custom-call | flops 2000000000 | bytes 8388608 | tf_op jit(solution)/shard_map/pallas_call | solution.py:277
  45.7 0.6 collective-permute-start.12
  46.3 0.0 collective-permute-done.8
  46.3 0.0 slice-done
  46.3 0.0 slice-done.1
  46.3 1.2 %fusion = f32[384,2048]{1,0:T(8,128)S(1)} fusion(bf16[384,512]{1,0:T(8,128)(2,1)S(1)} %collective-permute-done.8, bf16[1024,4096]{1,0:T(8,128)(2,1)S(1)} %bitcast.3, s32[]{:T(128)S(6)} %mul.29, s32[]{:T(128)S(6)} %mul.28), kind=kOutput, calls=%fused_computation.1 | convolution fusion | flops 805306368 | bytes 5636104 | tf_op jit(solution)/shard_map/dot_general | solution.py:337
  47.6 1.4 %add_convert_fusion.given_ref = bf16[384,2048]{1,0:T(8,128)(2,1)S(1)} fusion(f32[384,2048]{1,0:T(8,128)S(1)} %fusion, bf16[384,512]{1,0:T(8,128)(2,1)S(1)} %shard_map.61, bf16[1024,4096]{1,0:T(8,128)(2,1)S(1)} %bitcast.3, s32[]{:T(128)S(6)} %mul.25, s32[]{:T(128)S(6)} %mul.28), kind=kOutput, calls=%fused_computation | convolution fusion | flops 806879232 | bytes 7208968 | tf_op jit(solution)/shard_map/dot_general | solution.py:337
  48.9 10.2 %collective-permute-done.12.heads_ref = bf16[384,512]{1,0:T(8,128)(2,1)S(1)} collective-permute-done((bf16[384,512]{1,0:T(8,128)(2,1)S(1)}, bf16[384,512]{1,0:T(8,128)(2,1)S(1)}, u32[]{:S(2)}, u32[]{:S(2)}) %collective-permute-start.12) | collective-permute-done | bytes 393248 | tf_op jit(solution)/shard_map/ppermute | solution.py:34
  59.2 0.0 collective-permute-done.9.heads_ref
  59.2 1.8 %collective-permute-done.13.refs_1_ = bf16[512,768]{1,0:T(8,128)(2,1)S(1)} collective-permute-done((bf16[512,768]{1,0:T(8,128)(2,1)S(1)}, bf16[512,768]{1,0:T(8,128)(2,1)S(1)}, u32[]{:S(2)}, u32[]{:S(2)}) %collective-permute-start.13) | collective-permute-done | bytes 786464 | tf_op jit(solution)/shard_map/ppermute | solution.py:28
  61.0 0.0 collective-permute-start.14
  61.0 0.0 collective-permute-done.11.refs_0_
  61.0 0.8 %shard_map.63.given_ref = f32[384,2048]{1,0:T(8,128)S(1)} custom-call(bf16[384,2048]{1,0:T(8,128)(2,1)S(1)} %add_convert_fusion.given_ref, bf16[384,512]{1,0:T(8,128)(2,1)S(1)} %collective-permute-done.9.heads_ref, bf16[512,1280]{1,0:T(8,128)(2,1)S(1)} %collective-permute-done.11.refs_0_), custom_call_target="tpu_custom_call" | custom-call | flops 805306368 | bytes 4194304 | tf_op jit(solution)/shard_map/pallas_call | solution.py:111
  61.8 1.2 %shard_map.65.given_ref = f32[384,2048]{1,0:T(8,128)S(1)} custom-call(f32[384,2048]{1,0:T(8,128)S(1)} %shard_map.63.given_ref, bf16[384,512]{1,0:T(8,128)(2,1)S(1)} %collective-permute-done.12.heads_ref, bf16[512,1280]{1,0:T(8,128)(2,1)S(1)} %collective-permute-done.10.window_ref.refs_0_, bf16[512,768]{1,0:T(8,128)(2,1)S(1)} %collective-permute-done.13.refs_1_), custom_call_target="tpu_custom_call" | custom-call | flops 805306368 | bytes 4194304 | tf_op jit(solution)/shard_map/pallas_call | solution.py:111
  63.0 0.3 collective-permute-done.14.refs_0_
  63.3 1.7 %shard_map.66 = bf16[384,2048]{1,0:T(8,128)(2,1)} custom-call(f32[384,2048]{1,0:T(8,128)S(1)} %shard_map.65.given_ref, bf16[384,512]{1,0:T(8,128)(2,1)S(1)} %collective-permute-done.9.heads_ref, bf16[512,768]{1,0:T(8,128)(2,1)S(1)} %collective-permute-done.14.refs_0_), custom_call_target="tpu_custom_call" | custom-call | flops 805306368 | bytes 4194304 | tf_op jit(solution)/shard_map/pallas_call | solution.py:111
  (6 shorter events, 0.1 us)
Async XLA Ops:
  0.0 5.3 %collective-permute-start.2 = (bf16[384,1024]{1,0:T(8,128)(2,1)}, bf16[384,1024]{1,0:T(8,128)(2,1)S(1)}, u32[]{:S(2)}, u32[]{:S(2)}) collective-permute-start(bf16[384,1024]{1,0:T(8,128)(2,1)} %refs_0_.1), channel_id=1, source_target_pairs={{0,2},{2,0},{4,6},{6,4},{8,10},{10,8},{12,14},{14,12},{16,18},{18,... | collective-permute-start | bytes 2359304 | tf_op jit(solution)/shard_map/ppermute | solution.py:28
  1.3 7.7 %copy-start = (bf16[384,1024]{1,0:T(8,128)(2,1)S(1)}, bf16[384,1024]{1,0:T(8,128)(2,1)}, u32[]{:S(2)}) copy-start(bf16[384,1024]{1,0:T(8,128)(2,1)} %refs_0_.1) | copy-start | bytes 2359300
  1.3 7.7 %copy-start.1 = (s32[3]{0:T(128)S(1)}, s32[3]{0:T(128)}, u32[]{:S(2)}) copy-start(s32[3]{0:T(128)} %starts_ref.9) | copy-start | bytes 40
  1.4 2.3 %collective-permute-start = (bf16[384,256]{1,0:T(8,128)(2,1)S(1)}, bf16[384,256]{1,0:T(8,128)(2,1)S(1)}, u32[]{:S(2)}, u32[]{:S(2)}) collective-permute-start(bf16[384,256]{1,0:T(8,128)(2,1)S(1)} %pad_maximum_fusion), channel_id=1, source_target_pairs={{0,2},{2,0},{4,6},{6,4},{8,10},{10,8},{12,14},{14,12},{16,18},{18,... | collective-permute-start | bytes 589832 | tf_op jit(solution)/shard_map/ppermute | solution.py:28
  1.9 1.7 %collective-permute-start.1 = (s32[3]{0:T(128)}, s32[3]{0:T(128)S(1)}, u32[]{:S(2)}, u32[]{:S(2)}) collective-permute-start(s32[3]{0:T(128)} %starts_ref.9), channel_id=1, source_target_pairs={{0,2},{2,0},{4,6},{6,4},{8,10},{10,8},{12,14},{14,12},{16,18},{18,... | collective-permute-start | bytes 44 | tf_op jit(solution)/shard_map/ppermute | solution.py:28
  2.0 10.7 %collective-permute-start.3 = (bf16[384,256]{1,0:T(8,128)(2,1)S(1)}, bf16[384,256]{1,0:T(8,128)(2,1)S(1)}, u32[]{:S(2)}, u32[]{:S(2)}) collective-permute-start(bf16[384,256]{1,0:T(8,128)(2,1)S(1)} %pad_maximum_fusion.1.first_ref), channel_id=1, source_target_pairs={{0,8},{2,10},{4,12},{6,14},{8,16},{10,18},{12,20},{14,22},{16,24},... | collective-permute-start | bytes 589832 | tf_op jit(solution)/shard_map/ppermute | solution.py:19
  3.7 11.7 %collective-permute-start.4 = (bf16[384,256]{1,0:T(8,128)(2,1)S(1)}, bf16[384,256]{1,0:T(8,128)(2,1)S(1)}, u32[]{:S(2)}, u32[]{:S(2)}) collective-permute-start(bf16[384,256]{1,0:T(8,128)(2,1)S(1)} %collective-permute-done.second_ref), channel_id=1, source_target_pairs={{0,8},{2,10},{4,12},{6,14},{8,16},{10,18},{12,20},{14,22},{16,24},... | collective-permute-start | bytes 589832 | tf_op jit(solution)/shard_map/ppermute | solution.py:19
  7.5 33.5 %collective-permute-start.10 = (bf16[512,1280]{1,0:T(8,128)(2,1)S(1)}, bf16[512,1280]{1,0:T(8,128)(2,1)S(1)}, u32[]{:S(2)}, u32[]{:S(2)}) collective-permute-start(bf16[512,1280]{1,0:T(8,128)(2,1)S(1)} %dynamic_slice.23), channel_id=1, source_target_pairs={{0,1},{1,0},{2,3},{3,2},{4,5},{5,4},{6,7},{7,6},{8,9},{9,8},{10,11... | collective-permute-start | bytes 3932168 | tf_op jit(solution)/shard_map/ppermute | solution.py:34
  15.4 9.8 %collective-permute-start.6 = (bf16[768,256]{1,0:T(8,128)(2,1)S(1)}, bf16[768,256]{1,0:T(8,128)(2,1)S(1)}, u32[]{:S(2)}, u32[]{:S(2)}) collective-permute-start(bf16[768,256]{1,0:T(8,128)(2,1)S(1)} %shard_map.57.refs_3_), channel_id=1, source_target_pairs={{0,8},{2,10},{4,12},{6,14},{8,16},{10,18},{12,20},{14,22},{16,24},... | collective-permute-start | bytes 1179656 | tf_op jit(solution)/shard_map/ppermute | solution.py:24
  17.1 11.2 %collective-permute-start.5 = (bf16[768,256]{1,0:T(8,128)(2,1)S(1)}, bf16[768,256]{1,0:T(8,128)(2,1)S(1)}, u32[]{:S(2)}, u32[]{:S(2)}) collective-permute-start(bf16[768,256]{1,0:T(8,128)(2,1)S(1)} %shard_map.57.refs_3_), channel_id=1, source_target_pairs={{0,4},{2,6},{4,0},{6,2},{8,12},{10,14},{12,8},{14,10},{16,20},{18,... | collective-permute-start | bytes 1179656 | tf_op jit(solution)/shard_map/ppermute | solution.py:28
  25.3 10.7 %collective-permute-start.7 = (bf16[768,256]{1,0:T(8,128)(2,1)S(1)}, bf16[768,256]{1,0:T(8,128)(2,1)S(1)}, u32[]{:S(2)}, u32[]{:S(2)}) collective-permute-start(bf16[768,256]{1,0:T(8,128)(2,1)S(1)} %shard_map.60), channel_id=1, source_target_pairs={{0,4},{2,6},{4,0},{6,2},{8,12},{10,14},{12,8},{14,10},{16,20},{18,... | collective-permute-start | bytes 1179656 | tf_op jit(solution)/shard_map/ppermute | solution.py:28
  36.0 10.3 %slice-start = ((s8[8388608]{0:T(1024)(128)(4,1)}), s8[4194304]{0:T(1024)(128)(4,1)S(1)}, s32[]{:S(2)}) async-start(s8[8388608]{0:T(1024)(128)(4,1)} %bitcast.2), calls=%async_computation | async-start | bytes 8388608
  39.2 7.1 %slice-start.1 = ((s8[8388608]{0:T(1024)(128)(4,1)}), s8[4194304]{0:T(1024)(128)(4,1)S(1)}, s32[]{:S(2)}) async-start(s8[8388608]{0:T(1024)(128)(4,1)} %bitcast.2), calls=%async_computation.1 | async-start | bytes 8388608
  39.2 7.1 %collective-permute-start.8 = (bf16[384,512]{1,0:T(8,128)(2,1)S(1)}, bf16[384,512]{1,0:T(8,128)(2,1)S(1)}, u32[]{:S(2)}, u32[]{:S(2)}) collective-permute-start(bf16[384,512]{1,0:T(8,128)(2,1)S(1)} %shard_map.62), channel_id=1, source_target_pairs={{0,2},{2,0},{4,6},{6,4},{8,10},{10,8},{12,14},{14,12},{16,18},{18,... | collective-permute-start | bytes 1179656 | tf_op jit(solution)/shard_map/ppermute | solution.py:28
  39.3 19.9 %collective-permute-start.9 = (bf16[384,512]{1,0:T(8,128)(2,1)S(1)}, bf16[384,512]{1,0:T(8,128)(2,1)S(1)}, u32[]{:S(2)}, u32[]{:S(2)}) collective-permute-start(bf16[384,512]{1,0:T(8,128)(2,1)S(1)} %shard_map.62), channel_id=1, source_target_pairs={{0,3},{1,2},{2,1},{3,0},{4,7},{5,6},{6,5},{7,4},{8,11},{9,10},{10,... | collective-permute-start | bytes 1179656 | tf_op jit(solution)/shard_map/ppermute | solution.py:34
  40.9 20.1 %collective-permute-start.11 = (bf16[512,1280]{1,0:T(8,128)(2,1)S(1)}, bf16[512,1280]{1,0:T(8,128)(2,1)S(1)}, u32[]{:S(2)}, u32[]{:S(2)}) collective-permute-start(bf16[512,1280]{1,0:T(8,128)(2,1)S(1)} %collective-permute-done.10.window_ref.refs_0_), channel_id=1, source_target_pairs={{0,2},{2,0},{4,6},{6,4},{8,10},{10,8},{12,14},{14,12},{16,18},{18,... | collective-permute-start | bytes 3932168 | tf_op jit(solution)/shard_map/ppermute | solution.py:28
  41.0 20.0 %collective-permute-start.13 = (bf16[512,768]{1,0:T(8,128)(2,1)S(1)}, bf16[512,768]{1,0:T(8,128)(2,1)S(1)}, u32[]{:S(2)}, u32[]{:S(2)}) collective-permute-start(bf16[512,768]{1,0:T(8,128)(2,1)S(1)} %shard_map.64), channel_id=1, source_target_pairs={{0,8},{2,10},{4,12},{6,14},{8,0},{10,2},{12,4},{14,6},{16,24},{18,... | collective-permute-start | bytes 2359304 | tf_op jit(solution)/shard_map/ppermute | solution.py:28
  45.7 13.5 %collective-permute-start.12 = (bf16[384,512]{1,0:T(8,128)(2,1)S(1)}, bf16[384,512]{1,0:T(8,128)(2,1)S(1)}, u32[]{:S(2)}, u32[]{:S(2)}) collective-permute-start(bf16[384,512]{1,0:T(8,128)(2,1)S(1)} %shard_map.61), channel_id=1, source_target_pairs={{0,1},{1,0},{2,3},{3,2},{4,5},{5,4},{6,7},{7,6},{8,9},{9,8},{10,11... | collective-permute-start | bytes 1179656 | tf_op jit(solution)/shard_map/ppermute | solution.py:34
  61.0 2.3 %collective-permute-start.14 = (bf16[512,768]{1,0:T(8,128)(2,1)S(1)}, bf16[512,768]{1,0:T(8,128)(2,1)S(1)}, u32[]{:S(2)}, u32[]{:S(2)}) collective-permute-start(bf16[512,768]{1,0:T(8,128)(2,1)S(1)} %collective-permute-done.13.refs_1_), channel_id=1, source_target_pairs={{0,2},{2,0},{4,6},{6,4},{8,10},{10,8},{12,14},{14,12},{16,18},{18,... | collective-permute-start | bytes 2359304 | tf_op jit(solution)/shard_map/ppermute | solution.py:28

commit v16 on v15

--- a/solution.py
+++ b/solution.py
@@ -12,11 +12,6 @@
 LOG2E = 1.4426950408889634
 MASKED = -1e30
 TILE = 256
-
-
-def rotate(x, distance):
-    n = lax.axis_size("ctx")
-    return lax.ppermute(x, "ctx", [(i, (i + distance) % n) for i in range(n)])
 
 
 def shift(x, distance):
@@ -309,7 +304,7 @@
 
     mine, theirs = group_of(0), group_of(1)
     recv, recv_starts = lax.optimization_barrier((swap(theirs, 1), swap(block_start, 1)))
-    one_behind = [rotate(mine, 4), rotate(recv, 4)]
+    one_behind = [shift(mine, 4), shift(recv, 4)]
     q_recv = swap(queries, 1)
     (own,) = small_call(join_kernel, [(2 * tok, 2 * HEAD_SIZE)], (mine, recv))
     starts = (block_start, recv_starts)

time: 65.7 us -> 67.7 us (1.030)
  starting transfers between devices: 12.5 us -> 17.9 us
  waiting for transfers between devices: 30.7 us -> 27.2 us
    ppermute x1 -> x3, starting transfers between devices: 1.66 us -> 10.5 us  [shift(): lax.ppermute(x, 'ctx', [(i, i + distance) for i in range(n - distance)])]
    ppermute x2 -> x0, starting transfers between devices: 3.21 us -> none  [rotate(): return lax.ppermute(x, 'ctx', [(i, (i + distance) % n) for i in range(n)])]
    ppermute x2 -> x0, waiting for transfers between devices: 2.63 us -> none  [rotate(): return lax.ppermute(x, 'ctx', [(i, (i + distance) % n) for i in range(n)])]
    ppermute x9, waiting for transfers between devices: 11.1 us -> 10.2 us  [swap(): lax.ppermute(x, 'ctx', [(i, i ^ mask) for i in range(lax.axis_size('ctx'))])]
    ppermute x1 -> x3, waiting for transfers between devices: 6.7 us -> 6.65 us  [shift(): lax.ppermute(x, 'ctx', [(i, i + distance) for i in range(n - distance)])]
  transfers between devices with their start and end apart: 15 -> 15, of which waited for: 7 -> 6; matrix products, arithmetic and copies ran while one was open for 9% -> 9% of each run, Pallas kernels for 21% -> 21%
where the time goes in v16:
time: 67.7 us; the launch traced here: 67 us
  waiting for transfers between devices  27.2 us (40%)
  starting transfers between devices  17.9 us (26%)
  Pallas kernels  15.5 us (23%)
  local copies, waits for them, and re-layouts  3.46 us (5%)
  matrix products  2.6 us (4%)
    pallas_call x5, Pallas kernels, attention_call(): pl.pallas_call(functools.partial(attention_kernel, stage, distances, n_he...  11.7 us
    ppermute x3, starting transfers between devices, shift(): lax.ppermute(x, 'ctx', [(i, i + distance) for i in range(n - distance)])  10.5 us
    ppermute x3, waiting for transfers between devices, cross(): return lax.ppermute(x, ('ctx', 'head'), route)  10.3 us
    ppermute x9, waiting for transfers between devices, swap(): lax.ppermute(x, 'ctx', [(i, i ^ mask) for i in range(lax.axis_size('ctx'))])  10.2 us
    ppermute x3, waiting for transfers between devices, shift(): lax.ppermute(x, 'ctx', [(i, i + distance) for i in range(n - distance)])  6.65 us
    ppermute x3, starting transfers between devices, cross(): return lax.ppermute(x, ('ctx', 'head'), route)  3.78 us
    pallas_call x3, Pallas kernels, project(): pl.pallas_call(functools.partial(project_kernel, final, wide, window is n...  3.64 us
    ppermute x9, starting transfers between devices, swap(): lax.ppermute(x, 'ctx', [(i, i ^ mask) for i in range(lax.axis_size('ctx'))])  3.63 us
  transfers between devices with their start and end apart: 15, of which 6 were waited for; matrix products, arithmetic and copies ran while one was open for 9% of the time, Pallas kernels for 21%

profile of v16, /device:TPU:2, one launch (start us, length us, event | category | flops | bytes accessed | tf_op | source)
XLA Modules:
  0.0 67.0 jit_solution(14150484175943901812)
XLA Ops:
  0.0 0.0 collective-permute-start.2
  0.0 1.3 %constant_dynamic-slice_fusion = (bf16[384,128]{1,0:T(8,128)(2,1)S(1)}, bf16[384,128]{1,0:T(8,128)(2,1)S(1)}, bf16[384,128]{1,0:T(8,128)(2,1)S(1)}, bf16[384,128]{1,0:T(8,128)(2,1)S(1)}) fusion(bf16[384,256]{1,0:T(8,128)(2,1)} %param.7, s32[]{:T(128)S(6)} %mul.23, s32[]{:T(128)S(6)} %mul.24, bf16[384,256]{1,0:T(8,128)(2,1)} %param.6), kind=kLoop, calls=%fused_computation.6 | loop fusion | bytes 786440 | tf_op jit(solution)/shard_map/dynamic_slice | solution.py:299
  1.3 0.0 copy-start
  1.3 0.0 copy-start.1
  1.4 0.6 collective-permute-start
  1.9 0.1 collective-permute-start.1
  2.0 3.5 %collective-permute-start.3 = (bf16[384,256]{1,0:T(8,128)(2,1)S(1)}, bf16[384,256]{1,0:T(8,128)(2,1)S(1)}, u32[]{:S(2)}, u32[]{:S(2)}) collective-permute-start(bf16[384,256]{1,0:T(8,128)(2,1)S(1)} %pad_maximum_fusion.1.first_ref), channel_id=1, source_target_pairs={{0,8},{2,10},{4,12},{6,14},{8,16},{10,18},{12,20},{14,22},{16,24},... | collective-permute-start | bytes 589832 | tf_op jit(solution)/shard_map/ppermute | solution.py:19
  5.5 0.0 collective-permute-done.1.recv_starts_ref
  5.6 0.0 collective-permute-done.second_ref
  5.6 3.5 %collective-permute-start.4 = (bf16[384,256]{1,0:T(8,128)(2,1)S(1)}, bf16[384,256]{1,0:T(8,128)(2,1)S(1)}, u32[]{:S(2)}, u32[]{:S(2)}) collective-permute-start(bf16[384,256]{1,0:T(8,128)(2,1)S(1)} %collective-permute-done.second_ref), channel_id=1, source_target_pairs={{0,8},{2,10},{4,12},{6,14},{8,16},{10,18},{12,20},{14,22},{16,24},... | collective-permute-start | bytes 589832 | tf_op jit(solution)/shard_map/ppermute | solution.py:19
  9.1 0.0 collective-permute-done.2.refs_1_
  9.1 2.1 %dynamic_slice.23 = bf16[512,1280]{1,0:T(8,128)(2,1)S(1)} dynamic-slice(bf16[1024,4096]{1,0:T(8,128)(2,1)} %param.9, s32[]{:T(128)S(6)} %mul.25, s32[]{:T(128)S(6)} %add.16), dynamic_slice_sizes={512,1280} | dynamic-slice | bytes 2621444 | tf_op jit(solution)/shard_map/dynamic_slice | solution.py:299
  11.3 1.6 %collective-permute-start.10 = (bf16[512,1280]{1,0:T(8,128)(2,1)S(1)}, bf16[512,1280]{1,0:T(8,128)(2,1)S(1)}, u32[]{:S(2)}, u32[]{:S(2)}) collective-permute-start(bf16[512,1280]{1,0:T(8,128)(2,1)S(1)} %dynamic_slice.23), channel_id=1, source_target_pairs={{0,1},{1,0},{2,3},{3,2},{4,5},{5,4},{6,7},{7,6},{8,9},{9,8},{10,11... | collective-permute-start | bytes 3932168 | tf_op jit(solution)/shard_map/ppermute | solution.py:29
  12.8 0.0 copy-done
  12.8 0.0 copy-done.1
  12.8 3.7 %shard_map.56 = (bf16[6,512,128]{2,1,0:T(8,128)(2,1)S(1)}, f32[6,512,128]{2,1,0:T(8,128)S(1)}, f32[6,512,128]{2,1,0:T(8,128)S(1)}) custom-call(s32[3]{0:T(128)S(1)} %copy-done.1, s32[3]{0:T(128)S(1)} %collective-permute-done.1.recv_starts_ref, bf16[384,1024]{1,0:T(8,128)(2,1)S(1)} %copy-done, bf16[384,1024]{1,0:T(8,128)(2,1)S(1)} %collective-permute-done.2.refs_1_, ...), custom_call_target="tpu_custom_call" | custom-call | flops 5000000000 | bytes 8388608 | tf_op jit(solution)/shard_map/pallas_call | solution.py:272
  16.6 0.0 collective-permute-done.3.first_ref
  16.6 0.0 collective-permute-done.4.second_ref
  16.6 3.5 %collective-permute-start.6 = (bf16[768,256]{1,0:T(8,128)(2,1)S(1)}, bf16[768,256]{1,0:T(8,128)(2,1)S(1)}, u32[]{:S(2)}, u32[]{:S(2)}) collective-permute-start(bf16[768,256]{1,0:T(8,128)(2,1)S(1)} %shard_map.57.refs_3_), channel_id=1, source_target_pairs={{0,8},{2,10},{4,12},{6,14},{8,16},{10,18},{12,20},{14,22},{16,24},... | collective-permute-start | bytes 1179656 | tf_op jit(solution)/shard_map/ppermute | solution.py:19
  20.1 0.6 collective-permute-start.5
  20.7 0.8 %shard_map.58 = (f32[6,512,128]{2,1,0:T(8,128)S(1)}, f32[6,512,128]{2,1,0:T(8,128)S(1)}) custom-call(s32[3]{0:T(128)S(1)} %copy-done.1, s32[3]{0:T(128)S(1)} %collective-permute-done.1.recv_starts_ref, bf16[6,512,128]{2,1,0:T(8,128)(2,1)S(1)} %get-tuple-element.44.refs_0_, f32[6,512,128]{2,1,0:T(8,128)S(1)} %get-tuple-element.45.refs_1_, ...), custom_call_target="tpu_custom_call" | custom-call | flops 2100000000 | bytes 8388608 | tf_op jit(solution)/shard_map/pallas_call | solution.py:272
  21.6 6.6 %collective-permute-done.6.refs_4_.odd_ref = bf16[768,256]{1,0:T(8,128)(2,1)S(1)} collective-permute-done((bf16[768,256]{1,0:T(8,128)(2,1)S(1)}, bf16[768,256]{1,0:T(8,128)(2,1)S(1)}, u32[]{:S(2)}, u32[]{:S(2)}) %collective-permute-start.6) | collective-permute-done | bytes 393248 | tf_op jit(solution)/shard_map/ppermute | solution.py:19
  28.3 0.6 collective-permute-start.7
  28.9 2.5 %collective-permute-done.5.refs_3_ = bf16[768,256]{1,0:T(8,128)(2,1)S(1)} collective-permute-done((bf16[768,256]{1,0:T(8,128)(2,1)S(1)}, bf16[768,256]{1,0:T(8,128)(2,1)S(1)}, u32[]{:S(2)}, u32[]{:S(2)}) %collective-permute-start.5) | collective-permute-done | bytes 393248 | tf_op jit(solution)/shard_map/ppermute | solution.py:23
  31.4 0.9 %shard_map.59 = (f32[6,512,128]{2,1,0:T(8,128)S(1)}, f32[6,512,128]{2,1,0:T(8,128)S(1)}) custom-call(s32[3]{0:T(128)S(1)} %copy-done.1, s32[3]{0:T(128)S(1)} %collective-permute-done.1.recv_starts_ref, bf16[6,512,128]{2,1,0:T(8,128)(2,1)S(1)} %get-tuple-element.44.refs_0_, f32[6,512,128]{2,1,0:T(8,128)S(1)} %get-tuple-element.49.refs_1_, ...), custom_call_target="tpu_custom_call" | custom-call | flops 4000000000 | bytes 8388608 | tf_op jit(solution)/shard_map/pallas_call | solution.py:272
  32.4 6.6 %collective-permute-done.7.refs_3_ = bf16[768,256]{1,0:T(8,128)(2,1)S(1)} collective-permute-done((bf16[768,256]{1,0:T(8,128)(2,1)S(1)}, bf16[768,256]{1,0:T(8,128)(2,1)S(1)}, u32[]{:S(2)}, u32[]{:S(2)}) %collective-permute-start.7) | collective-permute-done | bytes 393248 | tf_op jit(solution)/shard_map/ppermute | solution.py:23
  39.0 0.0 slice-start
  39.0 3.2 %shard_map.62 = bf16[384,512]{1,0:T(8,128)(2,1)S(1)} custom-call(s32[3]{0:T(128)S(1)} %copy-done.1, s32[3]{0:T(128)S(1)} %collective-permute-done.1.recv_starts_ref, bf16[6,512,128]{2,1,0:T(8,128)(2,1)S(1)} %get-tuple-element.44.refs_0_, f32[6,512,128]{2,1,0:T(8,128)S(1)} %get-tuple-element.51.refs_1_, f32[6,512,128]{2,1,0:T(8,128)S(1)} %get-tuple-element.52.refs_2_, ...), custom_call_target="tpu_custom_call" | custom-call | flops 2000000000 | bytes 8388608 | tf_op jit(solution)/shard_map/pallas_call | solution.py:272
  42.2 0.0 slice-start.1
  42.2 0.1 collective-permute-start.8
  42.2 0.6 collective-permute-start.9
  42.8 0.0 collective-permute-done.10.window_ref.refs_0_
  42.8 0.1 collective-permute-start.11
  42.9 0.1 shard_map.64
  43.0 1.6 %collective-permute-start.13 = (bf16[512,768]{1,0:T(8,128)(2,1)S(1)}, bf16[512,768]{1,0:T(8,128)(2,1)S(1)}, u32[]{:S(2)}, u32[]{:S(2)}) collective-permute-start(bf16[512,768]{1,0:T(8,128)(2,1)S(1)} %shard_map.64), channel_id=1, source_target_pairs={{0,8},{2,10},{4,12},{6,14},{8,0},{10,2},{12,4},{14,6},{16,24},{18,... | collective-permute-start | bytes 2359304 | tf_op jit(solution)/shard_map/ppermute | solution.py:23
  44.6 3.0 %shard_map.61 = bf16[384,512]{1,0:T(8,128)(2,1)S(1)} custom-call(s32[3]{0:T(128)S(1)} %copy-done.1, s32[3]{0:T(128)S(1)} %collective-permute-done.1.recv_starts_ref, bf16[6,512,128]{2,1,0:T(8,128)(2,1)S(1)} %get-tuple-element.44.refs_0_, f32[6,512,128]{2,1,0:T(8,128)S(1)} %get-tuple-element.51.refs_1_, f32[6,512,128]{2,1,0:T(8,128)S(1)} %get-tuple-element.52.refs_2_, ...), custom_call_target="tpu_custom_call" | custom-call | flops 2000000000 | bytes 8388608 | tf_op jit(solution)/shard_map/pallas_call | solution.py:272
  47.6 1.6 %collective-permute-start.12 = (bf16[384,512]{1,0:T(8,128)(2,1)S(1)}, bf16[384,512]{1,0:T(8,128)(2,1)S(1)}, u32[]{:S(2)}, u32[]{:S(2)}) collective-permute-start(bf16[384,512]{1,0:T(8,128)(2,1)S(1)} %shard_map.61), channel_id=1, source_target_pairs={{0,1},{1,0},{2,3},{3,2},{4,5},{5,4},{6,7},{7,6},{8,9},{9,8},{10,11... | collective-permute-start | bytes 1179656 | tf_op jit(solution)/shard_map/ppermute | solution.py:29
  49.2 0.0 collective-permute-done.8
  49.2 0.0 slice-done
  49.2 0.0 slice-done.1
  49.2 1.2 %fusion = f32[384,2048]{1,0:T(8,128)S(1)} fusion(bf16[384,512]{1,0:T(8,128)(2,1)S(1)} %collective-permute-done.8, bf16[1024,4096]{1,0:T(8,128)(2,1)S(1)} %bitcast.3, s32[]{:T(128)S(6)} %mul.29, s32[]{:T(128)S(6)} %mul.28), kind=kOutput, calls=%fused_computation.1 | convolution fusion | flops 805306368 | bytes 5636104 | tf_op jit(solution)/shard_map/dot_general | solution.py:332
  50.5 1.4 %add_convert_fusion.given_ref = bf16[384,2048]{1,0:T(8,128)(2,1)S(1)} fusion(f32[384,2048]{1,0:T(8,128)S(1)} %fusion, bf16[384,512]{1,0:T(8,128)(2,1)S(1)} %shard_map.61, bf16[1024,4096]{1,0:T(8,128)(2,1)S(1)} %bitcast.3, s32[]{:T(128)S(6)} %mul.25, s32[]{:T(128)S(6)} %mul.28), kind=kOutput, calls=%fused_computation | convolution fusion | flops 806879232 | bytes 7208968 | tf_op jit(solution)/shard_map/dot_general | solution.py:332
  51.8 10.3 %collective-permute-done.12.heads_ref = bf16[384,512]{1,0:T(8,128)(2,1)S(1)} collective-permute-done((bf16[384,512]{1,0:T(8,128)(2,1)S(1)}, bf16[384,512]{1,0:T(8,128)(2,1)S(1)}, u32[]{:S(2)}, u32[]{:S(2)}) %collective-permute-start.12) | collective-permute-done | bytes 393248 | tf_op jit(solution)/shard_map/ppermute | solution.py:29
  62.2 0.0 collective-permute-done.9.heads_ref
  62.2 0.7 %collective-permute-done.13.refs_1_ = bf16[512,768]{1,0:T(8,128)(2,1)S(1)} collective-permute-done((bf16[512,768]{1,0:T(8,128)(2,1)S(1)}, bf16[512,768]{1,0:T(8,128)(2,1)S(1)}, u32[]{:S(2)}, u32[]{:S(2)}) %collective-permute-start.13) | collective-permute-done | bytes 786464 | tf_op jit(solution)/shard_map/ppermute | solution.py:23
  62.9 0.0 collective-permute-start.14
  62.9 0.0 collective-permute-done.11.refs_0_
  62.9 0.8 %shard_map.63.given_ref = f32[384,2048]{1,0:T(8,128)S(1)} custom-call(bf16[384,2048]{1,0:T(8,128)(2,1)S(1)} %add_convert_fusion.given_ref, bf16[384,512]{1,0:T(8,128)(2,1)S(1)} %collective-permute-done.9.heads_ref, bf16[512,1280]{1,0:T(8,128)(2,1)S(1)} %collective-permute-done.11.refs_0_), custom_call_target="tpu_custom_call" | custom-call | flops 805306368 | bytes 4194304 | tf_op jit(solution)/shard_map/pallas_call | solution.py:106
  63.8 1.2 %shard_map.65.given_ref = f32[384,2048]{1,0:T(8,128)S(1)} custom-call(f32[384,2048]{1,0:T(8,128)S(1)} %shard_map.63.given_ref, bf16[384,512]{1,0:T(8,128)(2,1)S(1)} %collective-permute-done.12.heads_ref, bf16[512,1280]{1,0:T(8,128)(2,1)S(1)} %collective-permute-done.10.window_ref.refs_0_, bf16[512,768]{1,0:T(8,128)(2,1)S(1)} %collective-permute-done.13.refs_1_), custom_call_target="tpu_custom_call" | custom-call | flops 805306368 | bytes 4194304 | tf_op jit(solution)/shard_map/pallas_call | solution.py:106
  64.9 0.3 collective-permute-done.14.refs_0_
  65.2 1.7 %shard_map.66 = bf16[384,2048]{1,0:T(8,128)(2,1)} custom-call(f32[384,2048]{1,0:T(8,128)S(1)} %shard_map.65.given_ref, bf16[384,512]{1,0:T(8,128)(2,1)S(1)} %collective-permute-done.9.heads_ref, bf16[512,768]{1,0:T(8,128)(2,1)S(1)} %collective-permute-done.14.refs_0_), custom_call_target="tpu_custom_call" | custom-call | flops 805306368 | bytes 4194304 | tf_op jit(solution)/shard_map/pallas_call | solution.py:106
  (6 shorter events, 0.1 us)
Async XLA Ops:
  0.0 9.1 %collective-permute-start.2 = (bf16[384,1024]{1,0:T(8,128)(2,1)}, bf16[384,1024]{1,0:T(8,128)(2,1)S(1)}, u32[]{:S(2)}, u32[]{:S(2)}) collective-permute-start(bf16[384,1024]{1,0:T(8,128)(2,1)} %refs_0_.1), channel_id=1, source_target_pairs={{0,2},{2,0},{4,6},{6,4},{8,10},{10,8},{12,14},{14,12},{16,18},{18,... | collective-permute-start | bytes 2359304 | tf_op jit(solution)/shard_map/ppermute | solution.py:23
  1.3 11.5 %copy-start = (bf16[384,1024]{1,0:T(8,128)(2,1)S(1)}, bf16[384,1024]{1,0:T(8,128)(2,1)}, u32[]{:S(2)}) copy-start(bf16[384,1024]{1,0:T(8,128)(2,1)} %refs_0_.1) | copy-start | bytes 2359300
  1.3 11.5 %copy-start.1 = (s32[3]{0:T(128)S(1)}, s32[3]{0:T(128)}, u32[]{:S(2)}) copy-start(s32[3]{0:T(128)} %starts_ref.9) | copy-start | bytes 40
  1.4 4.2 %collective-permute-start = (bf16[384,256]{1,0:T(8,128)(2,1)S(1)}, bf16[384,256]{1,0:T(8,128)(2,1)S(1)}, u32[]{:S(2)}, u32[]{:S(2)}) collective-permute-start(bf16[384,256]{1,0:T(8,128)(2,1)S(1)} %pad_maximum_fusion), channel_id=1, source_target_pairs={{0,2},{2,0},{4,6},{6,4},{8,10},{10,8},{12,14},{14,12},{16,18},{18,... | collective-permute-start | bytes 589832 | tf_op jit(solution)/shard_map/ppermute | solution.py:23
  1.9 3.6 %collective-permute-start.1 = (s32[3]{0:T(128)}, s32[3]{0:T(128)S(1)}, u32[]{:S(2)}, u32[]{:S(2)}) collective-permute-start(s32[3]{0:T(128)} %starts_ref.9), channel_id=1, source_target_pairs={{0,2},{2,0},{4,6},{6,4},{8,10},{10,8},{12,14},{14,12},{16,18},{18,... | collective-permute-start | bytes 44 | tf_op jit(solution)/shard_map/ppermute | solution.py:23
  2.0 14.5 %collective-permute-start.3 = (bf16[384,256]{1,0:T(8,128)(2,1)S(1)}, bf16[384,256]{1,0:T(8,128)(2,1)S(1)}, u32[]{:S(2)}, u32[]{:S(2)}) collective-permute-start(bf16[384,256]{1,0:T(8,128)(2,1)S(1)} %pad_maximum_fusion.1.first_ref), channel_id=1, source_target_pairs={{0,8},{2,10},{4,12},{6,14},{8,16},{10,18},{12,20},{14,22},{16,24},... | collective-permute-start | bytes 589832 | tf_op jit(solution)/shard_map/ppermute | solution.py:19
  5.6 11.0 %collective-permute-start.4 = (bf16[384,256]{1,0:T(8,128)(2,1)S(1)}, bf16[384,256]{1,0:T(8,128)(2,1)S(1)}, u32[]{:S(2)}, u32[]{:S(2)}) collective-permute-start(bf16[384,256]{1,0:T(8,128)(2,1)S(1)} %collective-permute-done.second_ref), channel_id=1, source_target_pairs={{0,8},{2,10},{4,12},{6,14},{8,16},{10,18},{12,20},{14,22},{16,24},... | collective-permute-start | bytes 589832 | tf_op jit(solution)/shard_map/ppermute | solution.py:19
  11.3 31.6 %collective-permute-start.10 = (bf16[512,1280]{1,0:T(8,128)(2,1)S(1)}, bf16[512,1280]{1,0:T(8,128)(2,1)S(1)}, u32[]{:S(2)}, u32[]{:S(2)}) collective-permute-start(bf16[512,1280]{1,0:T(8,128)(2,1)S(1)} %dynamic_slice.23), channel_id=1, source_target_pairs={{0,1},{1,0},{2,3},{3,2},{4,5},{5,4},{6,7},{7,6},{8,9},{9,8},{10,11... | collective-permute-start | bytes 3932168 | tf_op jit(solution)/shard_map/ppermute | solution.py:29
  16.6 11.6 %collective-permute-start.6 = (bf16[768,256]{1,0:T(8,128)(2,1)S(1)}, bf16[768,256]{1,0:T(8,128)(2,1)S(1)}, u32[]{:S(2)}, u32[]{:S(2)}) collective-permute-start(bf16[768,256]{1,0:T(8,128)(2,1)S(1)} %shard_map.57.refs_3_), channel_id=1, source_target_pairs={{0,8},{2,10},{4,12},{6,14},{8,16},{10,18},{12,20},{14,22},{16,24},... | collective-permute-start | bytes 1179656 | tf_op jit(solution)/shard_map/ppermute | solution.py:19
  20.1 11.3 %collective-permute-start.5 = (bf16[768,256]{1,0:T(8,128)(2,1)S(1)}, bf16[768,256]{1,0:T(8,128)(2,1)S(1)}, u32[]{:S(2)}, u32[]{:S(2)}) collective-permute-start(bf16[768,256]{1,0:T(8,128)(2,1)S(1)} %shard_map.57.refs_3_), channel_id=1, source_target_pairs={{0,4},{2,6},{4,0},{6,2},{8,12},{10,14},{12,8},{14,10},{16,20},{18,... | collective-permute-start | bytes 1179656 | tf_op jit(solution)/shard_map/ppermute | solution.py:23
  28.3 10.7 %collective-permute-start.7 = (bf16[768,256]{1,0:T(8,128)(2,1)S(1)}, bf16[768,256]{1,0:T(8,128)(2,1)S(1)}, u32[]{:S(2)}, u32[]{:S(2)}) collective-permute-start(bf16[768,256]{1,0:T(8,128)(2,1)S(1)} %shard_map.60), channel_id=1, source_target_pairs={{0,4},{2,6},{4,0},{6,2},{8,12},{10,14},{12,8},{14,10},{16,20},{18,... | collective-permute-start | bytes 1179656 | tf_op jit(solution)/shard_map/ppermute | solution.py:23
  39.0 10.2 %slice-start = ((s8[8388608]{0:T(1024)(128)(4,1)}), s8[4194304]{0:T(1024)(128)(4,1)S(1)}, s32[]{:S(2)}) async-start(s8[8388608]{0:T(1024)(128)(4,1)} %bitcast.2), calls=%async_computation | async-start | bytes 8388608
  42.2 7.1 %slice-start.1 = ((s8[8388608]{0:T(1024)(128)(4,1)}), s8[4194304]{0:T(1024)(128)(4,1)S(1)}, s32[]{:S(2)}) async-start(s8[8388608]{0:T(1024)(128)(4,1)} %bitcast.2), calls=%async_computation.1 | async-start | bytes 8388608
  42.2 7.0 %collective-permute-start.8 = (bf16[384,512]{1,0:T(8,128)(2,1)S(1)}, bf16[384,512]{1,0:T(8,128)(2,1)S(1)}, u32[]{:S(2)}, u32[]{:S(2)}) collective-permute-start(bf16[384,512]{1,0:T(8,128)(2,1)S(1)} %shard_map.62), channel_id=1, source_target_pairs={{0,2},{2,0},{4,6},{6,4},{8,10},{10,8},{12,14},{14,12},{16,18},{18,... | collective-permute-start | bytes 1179656 | tf_op jit(solution)/shard_map/ppermute | solution.py:23
  42.2 19.9 %collective-permute-start.9 = (bf16[384,512]{1,0:T(8,128)(2,1)S(1)}, bf16[384,512]{1,0:T(8,128)(2,1)S(1)}, u32[]{:S(2)}, u32[]{:S(2)}) collective-permute-start(bf16[384,512]{1,0:T(8,128)(2,1)S(1)} %shard_map.62), channel_id=1, source_target_pairs={{0,3},{1,2},{2,1},{3,0},{4,7},{5,6},{6,5},{7,4},{8,11},{9,10},{10,... | collective-permute-start | bytes 1179656 | tf_op jit(solution)/shard_map/ppermute | solution.py:29
  42.8 20.1 %collective-permute-start.11 = (bf16[512,1280]{1,0:T(8,128)(2,1)S(1)}, bf16[512,1280]{1,0:T(8,128)(2,1)S(1)}, u32[]{:S(2)}, u32[]{:S(2)}) collective-permute-start(bf16[512,1280]{1,0:T(8,128)(2,1)S(1)} %collective-permute-done.10.window_ref.refs_0_), channel_id=1, source_target_pairs={{0,2},{2,0},{4,6},{6,4},{8,10},{10,8},{12,14},{14,12},{16,18},{18,... | collective-permute-start | bytes 3932168 | tf_op jit(solution)/shard_map/ppermute | solution.py:23
  43.0 20.0 %collective-permute-start.13 = (bf16[512,768]{1,0:T(8,128)(2,1)S(1)}, bf16[512,768]{1,0:T(8,128)(2,1)S(1)}, u32[]{:S(2)}, u32[]{:S(2)}) collective-permute-start(bf16[512,768]{1,0:T(8,128)(2,1)S(1)} %shard_map.64), channel_id=1, source_target_pairs={{0,8},{2,10},{4,12},{6,14},{8,0},{10,2},{12,4},{14,6},{16,24},{18,... | collective-permute-start | bytes 2359304 | tf_op jit(solution)/shard_map/ppermute | solution.py:23
  47.6 14.6 %collective-permute-start.12 = (bf16[384,512]{1,0:T(8,128)(2,1)S(1)}, bf16[384,512]{1,0:T(8,128)(2,1)S(1)}, u32[]{:S(2)}, u32[]{:S(2)}) collective-permute-start(bf16[384,512]{1,0:T(8,128)(2,1)S(1)} %shard_map.61), channel_id=1, source_target_pairs={{0,1},{1,0},{2,3},{3,2},{4,5},{5,4},{6,7},{7,6},{8,9},{9,8},{10,11... | collective-permute-start | bytes 1179656 | tf_op jit(solution)/shard_map/ppermute | solution.py:29
  62.9 2.3 %collective-permute-start.14 = (bf16[512,768]{1,0:T(8,128)(2,1)S(1)}, bf16[512,768]{1,0:T(8,128)(2,1)S(1)}, u32[]{:S(2)}, u32[]{:S(2)}) collective-permute-start(bf16[512,768]{1,0:T(8,128)(2,1)S(1)} %collective-permute-done.13.refs_1_), channel_id=1, source_target_pairs={{0,2},{2,0},{4,6},{6,4},{8,10},{10,8},{12,14},{14,12},{16,18},{18,... | collective-permute-start | bytes 2359304 | tf_op jit(solution)/shard_map/ppermute | solution.py:23

commit v17 on v15

--- a/solution.py
+++ b/solution.py
@@ -1,4 +1,5 @@
 import functools
+import math
 
 import jax
 import jax.numpy as jnp
@@ -10,7 +11,7 @@
 HEAD_SIZE = 128
 BLOCK = 128
 LOG2E = 1.4426950408889634
-MASKED = -1e30
+MASKED = -math.inf
 TILE = 256
 
 

time: 65.7 us -> 65.7 us (level)
  no operation moved by 1% of the time
where the time goes in v17:
time: 65.7 us; the launch traced here: 65 us
  waiting for transfers between devices  30.8 us (47%)
  Pallas kernels  15.3 us (23%)
  starting transfers between devices  12.5 us (19%)
  local copies, waits for them, and re-layouts  3.46 us (5%)
  matrix products  2.6 us (4%)
    pallas_call x5, Pallas kernels, attention_call(): pl.pallas_call(functools.partial(attention_kernel, stage, distances, n_he...  11.6 us
    ppermute x9, waiting for transfers between devices, swap(): lax.ppermute(x, 'ctx', [(i, i ^ mask) for i in range(lax.axis_size('ctx'))])  11.1 us
    ppermute x3, waiting for transfers between devices, cross(): return lax.ppermute(x, ('ctx', 'head'), route)  10.3 us
    ppermute x1, waiting for transfers between devices, shift(): lax.ppermute(x, 'ctx', [(i, i + distance) for i in range(n - distance)])  6.7 us
    ppermute x9, starting transfers between devices, swap(): lax.ppermute(x, 'ctx', [(i, i ^ mask) for i in range(lax.axis_size('ctx'))])  3.83 us
    ppermute x3, starting transfers between devices, cross(): return lax.ppermute(x, ('ctx', 'head'), route)  3.79 us
    pallas_call x3, Pallas kernels, project(): pl.pallas_call(functools.partial(project_kernel, final, wide, window is n...  3.64 us
    dynamic_slice x2, local copies, waits for them, and re-layouts, cut(): return lax.dynamic_slice(x, start, size, allow_negative_indices=False)  3.44 us
  transfers between devices with their start and end apart: 15, of which 7 were waited for; matrix products, arithmetic and copies ran while one was open for 9% of the time, Pallas kernels for 21%

profile of v17, /device:TPU:2, one launch (start us, length us, event | category | flops | bytes accessed | tf_op | source)
XLA Modules:
  0.0 65.0 jit_solution(322057744318276423)
XLA Ops:
  0.0 0.0 collective-permute-start.2
  0.0 1.3 %constant_dynamic-slice_fusion = (bf16[384,128]{1,0:T(8,128)(2,1)S(1)}, bf16[384,128]{1,0:T(8,128)(2,1)S(1)}, bf16[384,128]{1,0:T(8,128)(2,1)S(1)}, bf16[384,128]{1,0:T(8,128)(2,1)S(1)}) fusion(bf16[384,256]{1,0:T(8,128)(2,1)} %param.7, s32[]{:T(128)S(6)} %mul.23, s32[]{:T(128)S(6)} %mul.24, bf16[384,256]{1,0:T(8,128)(2,1)} %param.6), kind=kLoop, calls=%fused_computation.6 | loop fusion | bytes 786440 | tf_op jit(solution)/shard_map/dynamic_slice | solution.py:305
  1.3 0.0 copy-start
  1.3 0.0 copy-start.1
  1.4 0.6 collective-permute-start
  1.9 0.1 collective-permute-start.1
  2.0 1.6 %collective-permute-start.3 = (bf16[384,256]{1,0:T(8,128)(2,1)S(1)}, bf16[384,256]{1,0:T(8,128)(2,1)S(1)}, u32[]{:S(2)}, u32[]{:S(2)}) collective-permute-start(bf16[384,256]{1,0:T(8,128)(2,1)S(1)} %pad_maximum_fusion.1.first_ref), channel_id=1, source_target_pairs={{0,8},{2,10},{4,12},{6,14},{8,16},{10,18},{12,20},{14,22},{16,24},... | collective-permute-start | bytes 589832 | tf_op jit(solution)/shard_map/ppermute | solution.py:20
  3.7 0.0 collective-permute-done.1.recv_starts_ref
  3.7 0.0 collective-permute-done.second_ref
  3.7 1.6 %collective-permute-start.4 = (bf16[384,256]{1,0:T(8,128)(2,1)S(1)}, bf16[384,256]{1,0:T(8,128)(2,1)S(1)}, u32[]{:S(2)}, u32[]{:S(2)}) collective-permute-start(bf16[384,256]{1,0:T(8,128)(2,1)S(1)} %collective-permute-done.second_ref), channel_id=1, source_target_pairs={{0,8},{2,10},{4,12},{6,14},{8,16},{10,18},{12,20},{14,22},{16,24},... | collective-permute-start | bytes 589832 | tf_op jit(solution)/shard_map/ppermute | solution.py:20
  5.3 0.0 collective-permute-done.2.refs_1_
  5.3 2.1 %dynamic_slice.23 = bf16[512,1280]{1,0:T(8,128)(2,1)S(1)} dynamic-slice(bf16[1024,4096]{1,0:T(8,128)(2,1)} %param.9, s32[]{:T(128)S(6)} %mul.25, s32[]{:T(128)S(6)} %add.16), dynamic_slice_sizes={512,1280} | dynamic-slice | bytes 2621444 | tf_op jit(solution)/shard_map/dynamic_slice | solution.py:305
  7.5 1.6 %collective-permute-start.10 = (bf16[512,1280]{1,0:T(8,128)(2,1)S(1)}, bf16[512,1280]{1,0:T(8,128)(2,1)S(1)}, u32[]{:S(2)}, u32[]{:S(2)}) collective-permute-start(bf16[512,1280]{1,0:T(8,128)(2,1)S(1)} %dynamic_slice.23), channel_id=1, source_target_pairs={{0,1},{1,0},{2,3},{3,2},{4,5},{5,4},{6,7},{7,6},{8,9},{9,8},{10,11... | collective-permute-start | bytes 3932168 | tf_op jit(solution)/shard_map/ppermute | solution.py:35
  9.0 0.0 copy-done
  9.0 0.0 copy-done.1
  9.0 3.7 %shard_map.56 = (bf16[6,512,128]{2,1,0:T(8,128)(2,1)S(1)}, f32[6,512,128]{2,1,0:T(8,128)S(1)}, f32[6,512,128]{2,1,0:T(8,128)S(1)}) custom-call(s32[3]{0:T(128)S(1)} %copy-done.1, s32[3]{0:T(128)S(1)} %collective-permute-done.1.recv_starts_ref, bf16[384,1024]{1,0:T(8,128)(2,1)S(1)} %copy-done, bf16[384,1024]{1,0:T(8,128)(2,1)S(1)} %collective-permute-done.2.refs_1_, ...), custom_call_target="tpu_custom_call" | custom-call | flops 5000000000 | bytes 8388608 | tf_op jit(solution)/shard_map/pallas_call | solution.py:278
  12.7 0.0 collective-permute-done.3.first_ref
  12.8 2.7 %collective-permute-done.4.second_ref = bf16[384,256]{1,0:T(8,128)(2,1)S(1)} collective-permute-done((bf16[384,256]{1,0:T(8,128)(2,1)S(1)}, bf16[384,256]{1,0:T(8,128)(2,1)S(1)}, u32[]{:S(2)}, u32[]{:S(2)}) %collective-permute-start.4) | collective-permute-done | bytes 196640 | tf_op jit(solution)/shard_map/ppermute | solution.py:20
  15.4 1.7 %collective-permute-start.6 = (bf16[768,256]{1,0:T(8,128)(2,1)S(1)}, bf16[768,256]{1,0:T(8,128)(2,1)S(1)}, u32[]{:S(2)}, u32[]{:S(2)}) collective-permute-start(bf16[768,256]{1,0:T(8,128)(2,1)S(1)} %shard_map.57.refs_3_), channel_id=1, source_target_pairs={{0,8},{2,10},{4,12},{6,14},{8,16},{10,18},{12,20},{14,22},{16,24},... | collective-permute-start | bytes 1179656 | tf_op jit(solution)/shard_map/ppermute | solution.py:25
  17.1 0.6 collective-permute-start.5
  17.7 0.8 %shard_map.58 = (f32[6,512,128]{2,1,0:T(8,128)S(1)}, f32[6,512,128]{2,1,0:T(8,128)S(1)}) custom-call(s32[3]{0:T(128)S(1)} %copy-done.1, s32[3]{0:T(128)S(1)} %collective-permute-done.1.recv_starts_ref, bf16[6,512,128]{2,1,0:T(8,128)(2,1)S(1)} %get-tuple-element.44.refs_0_, f32[6,512,128]{2,1,0:T(8,128)S(1)} %get-tuple-element.45.refs_1_, ...), custom_call_target="tpu_custom_call" | custom-call | flops 2100000000 | bytes 8388608 | tf_op jit(solution)/shard_map/pallas_call | solution.py:278
  18.6 6.7 %collective-permute-done.6.refs_4_.odd_ref = bf16[768,256]{1,0:T(8,128)(2,1)S(1)} collective-permute-done((bf16[768,256]{1,0:T(8,128)(2,1)S(1)}, bf16[768,256]{1,0:T(8,128)(2,1)S(1)}, u32[]{:S(2)}, u32[]{:S(2)}) %collective-permute-start.6) | collective-permute-done | bytes 393248 | tf_op jit(solution)/shard_map/ppermute | solution.py:25
  25.3 0.7 %collective-permute-start.7 = (bf16[768,256]{1,0:T(8,128)(2,1)S(1)}, bf16[768,256]{1,0:T(8,128)(2,1)S(1)}, u32[]{:S(2)}, u32[]{:S(2)}) collective-permute-start(bf16[768,256]{1,0:T(8,128)(2,1)S(1)} %shard_map.60), channel_id=1, source_target_pairs={{0,4},{2,6},{4,0},{6,2},{8,12},{10,14},{12,8},{14,10},{16,20},{18,... | collective-permute-start | bytes 1179656 | tf_op jit(solution)/shard_map/ppermute | solution.py:29
  26.0 2.3 %collective-permute-done.5.refs_3_ = bf16[768,256]{1,0:T(8,128)(2,1)S(1)} collective-permute-done((bf16[768,256]{1,0:T(8,128)(2,1)S(1)}, bf16[768,256]{1,0:T(8,128)(2,1)S(1)}, u32[]{:S(2)}, u32[]{:S(2)}) %collective-permute-start.5) | collective-permute-done | bytes 393248 | tf_op jit(solution)/shard_map/ppermute | solution.py:29
  28.4 0.9 %shard_map.59 = (f32[6,512,128]{2,1,0:T(8,128)S(1)}, f32[6,512,128]{2,1,0:T(8,128)S(1)}) custom-call(s32[3]{0:T(128)S(1)} %copy-done.1, s32[3]{0:T(128)S(1)} %collective-permute-done.1.recv_starts_ref, bf16[6,512,128]{2,1,0:T(8,128)(2,1)S(1)} %get-tuple-element.44.refs_0_, f32[6,512,128]{2,1,0:T(8,128)S(1)} %get-tuple-element.49.refs_1_, ...), custom_call_target="tpu_custom_call" | custom-call | flops 4000000000 | bytes 8388608 | tf_op jit(solution)/shard_map/pallas_call | solution.py:278
  29.3 6.7 %collective-permute-done.7.refs_3_ = bf16[768,256]{1,0:T(8,128)(2,1)S(1)} collective-permute-done((bf16[768,256]{1,0:T(8,128)(2,1)S(1)}, bf16[768,256]{1,0:T(8,128)(2,1)S(1)}, u32[]{:S(2)}, u32[]{:S(2)}) %collective-permute-start.7) | collective-permute-done | bytes 393248 | tf_op jit(solution)/shard_map/ppermute | solution.py:29
  36.0 0.0 slice-start
  36.0 3.1 %shard_map.62 = bf16[384,512]{1,0:T(8,128)(2,1)S(1)} custom-call(s32[3]{0:T(128)S(1)} %copy-done.1, s32[3]{0:T(128)S(1)} %collective-permute-done.1.recv_starts_ref, bf16[6,512,128]{2,1,0:T(8,128)(2,1)S(1)} %get-tuple-element.44.refs_0_, f32[6,512,128]{2,1,0:T(8,128)S(1)} %get-tuple-element.51.refs_1_, f32[6,512,128]{2,1,0:T(8,128)S(1)} %get-tuple-element.52.refs_2_, ...), custom_call_target="tpu_custom_call" | custom-call | flops 2000000000 | bytes 8388608 | tf_op jit(solution)/shard_map/pallas_call | solution.py:278
  39.1 0.0 slice-start.1
  39.1 0.1 collective-permute-start.8
  39.2 1.6 %collective-permute-start.9 = (bf16[384,512]{1,0:T(8,128)(2,1)S(1)}, bf16[384,512]{1,0:T(8,128)(2,1)S(1)}, u32[]{:S(2)}, u32[]{:S(2)}) collective-permute-start(bf16[384,512]{1,0:T(8,128)(2,1)S(1)} %shard_map.62), channel_id=1, source_target_pairs={{0,3},{1,2},{2,1},{3,0},{4,7},{5,6},{6,5},{7,4},{8,11},{9,10},{10,... | collective-permute-start | bytes 1179656 | tf_op jit(solution)/shard_map/ppermute | solution.py:35
  40.9 0.0 collective-permute-done.10.window_ref.refs_0_
  40.9 0.1 collective-permute-start.11
  40.9 0.1 shard_map.64
  41.0 1.7 %collective-permute-start.13 = (bf16[512,768]{1,0:T(8,128)(2,1)S(1)}, bf16[512,768]{1,0:T(8,128)(2,1)S(1)}, u32[]{:S(2)}, u32[]{:S(2)}) collective-permute-start(bf16[512,768]{1,0:T(8,128)(2,1)S(1)} %shard_map.64), channel_id=1, source_target_pairs={{0,8},{2,10},{4,12},{6,14},{8,0},{10,2},{12,4},{14,6},{16,24},{18,... | collective-permute-start | bytes 2359304 | tf_op jit(solution)/shard_map/ppermute | solution.py:29
  42.7 2.9 %shard_map.61 = bf16[384,512]{1,0:T(8,128)(2,1)S(1)} custom-call(s32[3]{0:T(128)S(1)} %copy-done.1, s32[3]{0:T(128)S(1)} %collective-permute-done.1.recv_starts_ref, bf16[6,512,128]{2,1,0:T(8,128)(2,1)S(1)} %get-tuple-element.44.refs_0_, f32[6,512,128]{2,1,0:T(8,128)S(1)} %get-tuple-element.51.refs_1_, f32[6,512,128]{2,1,0:T(8,128)S(1)} %get-tuple-element.52.refs_2_, ...), custom_call_target="tpu_custom_call" | custom-call | flops 2000000000 | bytes 8388608 | tf_op jit(solution)/shard_map/pallas_call | solution.py:278
  45.6 0.6 collective-permute-start.12
  46.2 0.0 collective-permute-done.8
  46.2 0.0 slice-done
  46.2 0.0 slice-done.1
  46.2 1.2 %fusion = f32[384,2048]{1,0:T(8,128)S(1)} fusion(bf16[384,512]{1,0:T(8,128)(2,1)S(1)} %collective-permute-done.8, bf16[1024,4096]{1,0:T(8,128)(2,1)S(1)} %bitcast.3, s32[]{:T(128)S(6)} %mul.29, s32[]{:T(128)S(6)} %mul.28), kind=kOutput, calls=%fused_computation.1 | convolution fusion | flops 805306368 | bytes 5636104 | tf_op jit(solution)/shard_map/dot_general | solution.py:338
  47.5 1.4 %add_convert_fusion.given_ref = bf16[384,2048]{1,0:T(8,128)(2,1)S(1)} fusion(f32[384,2048]{1,0:T(8,128)S(1)} %fusion, bf16[384,512]{1,0:T(8,128)(2,1)S(1)} %shard_map.61, bf16[1024,4096]{1,0:T(8,128)(2,1)S(1)} %bitcast.3, s32[]{:T(128)S(6)} %mul.25, s32[]{:T(128)S(6)} %mul.28), kind=kOutput, calls=%fused_computation | convolution fusion | flops 806879232 | bytes 7208968 | tf_op jit(solution)/shard_map/dot_general | solution.py:338
  48.8 10.3 %collective-permute-done.12.heads_ref = bf16[384,512]{1,0:T(8,128)(2,1)S(1)} collective-permute-done((bf16[384,512]{1,0:T(8,128)(2,1)S(1)}, bf16[384,512]{1,0:T(8,128)(2,1)S(1)}, u32[]{:S(2)}, u32[]{:S(2)}) %collective-permute-start.12) | collective-permute-done | bytes 393248 | tf_op jit(solution)/shard_map/ppermute | solution.py:35
  59.1 0.0 collective-permute-done.9.heads_ref
  59.1 1.8 %collective-permute-done.13.refs_1_ = bf16[512,768]{1,0:T(8,128)(2,1)S(1)} collective-permute-done((bf16[512,768]{1,0:T(8,128)(2,1)S(1)}, bf16[512,768]{1,0:T(8,128)(2,1)S(1)}, u32[]{:S(2)}, u32[]{:S(2)}) %collective-permute-start.13) | collective-permute-done | bytes 786464 | tf_op jit(solution)/shard_map/ppermute | solution.py:29
  60.9 0.0 collective-permute-start.14
  60.9 0.0 collective-permute-done.11.refs_0_
  60.9 0.8 %shard_map.63.given_ref = f32[384,2048]{1,0:T(8,128)S(1)} custom-call(bf16[384,2048]{1,0:T(8,128)(2,1)S(1)} %add_convert_fusion.given_ref, bf16[384,512]{1,0:T(8,128)(2,1)S(1)} %collective-permute-done.9.heads_ref, bf16[512,1280]{1,0:T(8,128)(2,1)S(1)} %collective-permute-done.11.refs_0_), custom_call_target="tpu_custom_call" | custom-call | flops 805306368 | bytes 4194304 | tf_op jit(solution)/shard_map/pallas_call | solution.py:112
  61.8 1.2 %shard_map.65.given_ref = f32[384,2048]{1,0:T(8,128)S(1)} custom-call(f32[384,2048]{1,0:T(8,128)S(1)} %shard_map.63.given_ref, bf16[384,512]{1,0:T(8,128)(2,1)S(1)} %collective-permute-done.12.heads_ref, bf16[512,1280]{1,0:T(8,128)(2,1)S(1)} %collective-permute-done.10.window_ref.refs_0_, bf16[512,768]{1,0:T(8,128)(2,1)S(1)} %collective-permute-done.13.refs_1_), custom_call_target="tpu_custom_call" | custom-call | flops 805306368 | bytes 4194304 | tf_op jit(solution)/shard_map/pallas_call | solution.py:112
  62.9 0.3 collective-permute-done.14.refs_0_
  63.2 1.7 %shard_map.66 = bf16[384,2048]{1,0:T(8,128)(2,1)} custom-call(f32[384,2048]{1,0:T(8,128)S(1)} %shard_map.65.given_ref, bf16[384,512]{1,0:T(8,128)(2,1)S(1)} %collective-permute-done.9.heads_ref, bf16[512,768]{1,0:T(8,128)(2,1)S(1)} %collective-permute-done.14.refs_0_), custom_call_target="tpu_custom_call" | custom-call | flops 805306368 | bytes 4194304 | tf_op jit(solution)/shard_map/pallas_call | solution.py:112
  (6 shorter events, 0.1 us)
Async XLA Ops:
  0.0 5.3 %collective-permute-start.2 = (bf16[384,1024]{1,0:T(8,128)(2,1)}, bf16[384,1024]{1,0:T(8,128)(2,1)S(1)}, u32[]{:S(2)}, u32[]{:S(2)}) collective-permute-start(bf16[384,1024]{1,0:T(8,128)(2,1)} %refs_0_.1), channel_id=1, source_target_pairs={{0,2},{2,0},{4,6},{6,4},{8,10},{10,8},{12,14},{14,12},{16,18},{18,... | collective-permute-start | bytes 2359304 | tf_op jit(solution)/shard_map/ppermute | solution.py:29
  1.3 7.7 %copy-start = (bf16[384,1024]{1,0:T(8,128)(2,1)S(1)}, bf16[384,1024]{1,0:T(8,128)(2,1)}, u32[]{:S(2)}) copy-start(bf16[384,1024]{1,0:T(8,128)(2,1)} %refs_0_.1) | copy-start | bytes 2359300
  1.3 7.7 %copy-start.1 = (s32[3]{0:T(128)S(1)}, s32[3]{0:T(128)}, u32[]{:S(2)}) copy-start(s32[3]{0:T(128)} %starts_ref.9) | copy-start | bytes 40
  1.4 2.3 %collective-permute-start = (bf16[384,256]{1,0:T(8,128)(2,1)S(1)}, bf16[384,256]{1,0:T(8,128)(2,1)S(1)}, u32[]{:S(2)}, u32[]{:S(2)}) collective-permute-start(bf16[384,256]{1,0:T(8,128)(2,1)S(1)} %pad_maximum_fusion), channel_id=1, source_target_pairs={{0,2},{2,0},{4,6},{6,4},{8,10},{10,8},{12,14},{14,12},{16,18},{18,... | collective-permute-start | bytes 589832 | tf_op jit(solution)/shard_map/ppermute | solution.py:29
  1.9 1.7 %collective-permute-start.1 = (s32[3]{0:T(128)}, s32[3]{0:T(128)S(1)}, u32[]{:S(2)}, u32[]{:S(2)}) collective-permute-start(s32[3]{0:T(128)} %starts_ref.9), channel_id=1, source_target_pairs={{0,2},{2,0},{4,6},{6,4},{8,10},{10,8},{12,14},{14,12},{16,18},{18,... | collective-permute-start | bytes 44 | tf_op jit(solution)/shard_map/ppermute | solution.py:29
  2.0 10.7 %collective-permute-start.3 = (bf16[384,256]{1,0:T(8,128)(2,1)S(1)}, bf16[384,256]{1,0:T(8,128)(2,1)S(1)}, u32[]{:S(2)}, u32[]{:S(2)}) collective-permute-start(bf16[384,256]{1,0:T(8,128)(2,1)S(1)} %pad_maximum_fusion.1.first_ref), channel_id=1, source_target_pairs={{0,8},{2,10},{4,12},{6,14},{8,16},{10,18},{12,20},{14,22},{16,24},... | collective-permute-start | bytes 589832 | tf_op jit(solution)/shard_map/ppermute | solution.py:20
  3.7 11.7 %collective-permute-start.4 = (bf16[384,256]{1,0:T(8,128)(2,1)S(1)}, bf16[384,256]{1,0:T(8,128)(2,1)S(1)}, u32[]{:S(2)}, u32[]{:S(2)}) collective-permute-start(bf16[384,256]{1,0:T(8,128)(2,1)S(1)} %collective-permute-done.second_ref), channel_id=1, source_target_pairs={{0,8},{2,10},{4,12},{6,14},{8,16},{10,18},{12,20},{14,22},{16,24},... | collective-permute-start | bytes 589832 | tf_op jit(solution)/shard_map/ppermute | solution.py:20
  7.5 33.4 %collective-permute-start.10 = (bf16[512,1280]{1,0:T(8,128)(2,1)S(1)}, bf16[512,1280]{1,0:T(8,128)(2,1)S(1)}, u32[]{:S(2)}, u32[]{:S(2)}) collective-permute-start(bf16[512,1280]{1,0:T(8,128)(2,1)S(1)} %dynamic_slice.23), channel_id=1, source_target_pairs={{0,1},{1,0},{2,3},{3,2},{4,5},{5,4},{6,7},{7,6},{8,9},{9,8},{10,11... | collective-permute-start | bytes 3932168 | tf_op jit(solution)/shard_map/ppermute | solution.py:35
  15.4 9.8 %collective-permute-start.6 = (bf16[768,256]{1,0:T(8,128)(2,1)S(1)}, bf16[768,256]{1,0:T(8,128)(2,1)S(1)}, u32[]{:S(2)}, u32[]{:S(2)}) collective-permute-start(bf16[768,256]{1,0:T(8,128)(2,1)S(1)} %shard_map.57.refs_3_), channel_id=1, source_target_pairs={{0,8},{2,10},{4,12},{6,14},{8,16},{10,18},{12,20},{14,22},{16,24},... | collective-permute-start | bytes 1179656 | tf_op jit(solution)/shard_map/ppermute | solution.py:25
  17.1 11.2 %collective-permute-start.5 = (bf16[768,256]{1,0:T(8,128)(2,1)S(1)}, bf16[768,256]{1,0:T(8,128)(2,1)S(1)}, u32[]{:S(2)}, u32[]{:S(2)}) collective-permute-start(bf16[768,256]{1,0:T(8,128)(2,1)S(1)} %shard_map.57.refs_3_), channel_id=1, source_target_pairs={{0,4},{2,6},{4,0},{6,2},{8,12},{10,14},{12,8},{14,10},{16,20},{18,... | collective-permute-start | bytes 1179656 | tf_op jit(solution)/shard_map/ppermute | solution.py:29
  25.3 10.7 %collective-permute-start.7 = (bf16[768,256]{1,0:T(8,128)(2,1)S(1)}, bf16[768,256]{1,0:T(8,128)(2,1)S(1)}, u32[]{:S(2)}, u32[]{:S(2)}) collective-permute-start(bf16[768,256]{1,0:T(8,128)(2,1)S(1)} %shard_map.60), channel_id=1, source_target_pairs={{0,4},{2,6},{4,0},{6,2},{8,12},{10,14},{12,8},{14,10},{16,20},{18,... | collective-permute-start | bytes 1179656 | tf_op jit(solution)/shard_map/ppermute | solution.py:29
  36.0 10.2 %slice-start = ((s8[8388608]{0:T(1024)(128)(4,1)}), s8[4194304]{0:T(1024)(128)(4,1)S(1)}, s32[]{:S(2)}) async-start(s8[8388608]{0:T(1024)(128)(4,1)} %bitcast.2), calls=%async_computation | async-start | bytes 8388608
  39.1 7.1 %slice-start.1 = ((s8[8388608]{0:T(1024)(128)(4,1)}), s8[4194304]{0:T(1024)(128)(4,1)S(1)}, s32[]{:S(2)}) async-start(s8[8388608]{0:T(1024)(128)(4,1)} %bitcast.2), calls=%async_computation.1 | async-start | bytes 8388608
  39.1 7.1 %collective-permute-start.8 = (bf16[384,512]{1,0:T(8,128)(2,1)S(1)}, bf16[384,512]{1,0:T(8,128)(2,1)S(1)}, u32[]{:S(2)}, u32[]{:S(2)}) collective-permute-start(bf16[384,512]{1,0:T(8,128)(2,1)S(1)} %shard_map.62), channel_id=1, source_target_pairs={{0,2},{2,0},{4,6},{6,4},{8,10},{10,8},{12,14},{14,12},{16,18},{18,... | collective-permute-start | bytes 1179656 | tf_op jit(solution)/shard_map/ppermute | solution.py:29
  39.2 19.9 %collective-permute-start.9 = (bf16[384,512]{1,0:T(8,128)(2,1)S(1)}, bf16[384,512]{1,0:T(8,128)(2,1)S(1)}, u32[]{:S(2)}, u32[]{:S(2)}) collective-permute-start(bf16[384,512]{1,0:T(8,128)(2,1)S(1)} %shard_map.62), channel_id=1, source_target_pairs={{0,3},{1,2},{2,1},{3,0},{4,7},{5,6},{6,5},{7,4},{8,11},{9,10},{10,... | collective-permute-start | bytes 1179656 | tf_op jit(solution)/shard_map/ppermute | solution.py:35
  40.9 20.1 %collective-permute-start.11 = (bf16[512,1280]{1,0:T(8,128)(2,1)S(1)}, bf16[512,1280]{1,0:T(8,128)(2,1)S(1)}, u32[]{:S(2)}, u32[]{:S(2)}) collective-permute-start(bf16[512,1280]{1,0:T(8,128)(2,1)S(1)} %collective-permute-done.10.window_ref.refs_0_), channel_id=1, source_target_pairs={{0,2},{2,0},{4,6},{6,4},{8,10},{10,8},{12,14},{14,12},{16,18},{18,... | collective-permute-start | bytes 3932168 | tf_op jit(solution)/shard_map/ppermute | solution.py:29
  41.0 20.0 %collective-permute-start.13 = (bf16[512,768]{1,0:T(8,128)(2,1)S(1)}, bf16[512,768]{1,0:T(8,128)(2,1)S(1)}, u32[]{:S(2)}, u32[]{:S(2)}) collective-permute-start(bf16[512,768]{1,0:T(8,128)(2,1)S(1)} %shard_map.64), channel_id=1, source_target_pairs={{0,8},{2,10},{4,12},{6,14},{8,0},{10,2},{12,4},{14,6},{16,24},{18,... | collective-permute-start | bytes 2359304 | tf_op jit(solution)/shard_map/ppermute | solution.py:29
  45.6 13.5 %collective-permute-start.12 = (bf16[384,512]{1,0:T(8,128)(2,1)S(1)}, bf16[384,512]{1,0:T(8,128)(2,1)S(1)}, u32[]{:S(2)}, u32[]{:S(2)}) collective-permute-start(bf16[384,512]{1,0:T(8,128)(2,1)S(1)} %shard_map.61), channel_id=1, source_target_pairs={{0,1},{1,0},{2,3},{3,2},{4,5},{5,4},{6,7},{7,6},{8,9},{9,8},{10,11... | collective-permute-start | bytes 1179656 | tf_op jit(solution)/shard_map/ppermute | solution.py:35
  60.9 2.3 %collective-permute-start.14 = (bf16[512,768]{1,0:T(8,128)(2,1)S(1)}, bf16[512,768]{1,0:T(8,128)(2,1)S(1)}, u32[]{:S(2)}, u32[]{:S(2)}) collective-permute-start(bf16[512,768]{1,0:T(8,128)(2,1)S(1)} %collective-permute-done.13.refs_1_), channel_id=1, source_target_pairs={{0,2},{2,0},{4,6},{6,4},{8,10},{10,8},{12,14},{14,12},{16,18},{18,... | collective-permute-start | bytes 2359304 | tf_op jit(solution)/shard_map/ppermute | solution.py:29

commit v18 on v17

--- a/solution.py
+++ b/solution.py
@@ -304,11 +304,13 @@
     def cut(x, start, size):
         return lax.dynamic_slice(x, start, size, allow_negative_indices=False)
 
-    def group_of(n):
+    def group_of(n, *both):
         size = (tok, HEAD_SIZE)
-        return jnp.concatenate([cut(keys, (0, lanes[n]), size), cut(values, (0, lanes[n]), size)], 1)
-
-    mine, theirs = group_of(0), group_of(1)
+        return jnp.concatenate([cut(x, (0, lanes[n]), size) for x in both], 1)
+
+    mine = group_of(0, keys, values)
+    _, *later = lax.optimization_barrier((mine, keys, values))
+    theirs = group_of(1, *later)
     recv, recv_starts = lax.optimization_barrier((swap(theirs, 1), swap(block_start, 1)))
     one_behind = [rotate(mine, 4), rotate(recv, 4)]
     q_recv = swap(queries, 1)

time: 65.7 us -> 67 us (1.020)
  local copies, waits for them, and re-layouts: 3.46 us -> 5.36 us
  waiting for transfers between devices: 30.8 us -> 29.5 us
    dynamic_slice x2 -> x4, local copies, waits for them, and re-layouts: 3.44 us -> 5.34 us  [cut(): return lax.dynamic_slice(x, start, size, allow_negative_indices=False)]
    ppermute x2, waiting for transfers between devices: 2.66 us -> 1.04 us  [rotate(): return lax.ppermute(x, 'ctx', [(i, (i + distance) % n) for i in range(n)])]
    ppermute x1, starting transfers between devices: 1.66 us -> 2.48 us  [shift(): lax.ppermute(x, 'ctx', [(i, i + distance) for i in range(n - distance)])]
  transfers between devices with their start and end apart: 15 -> 15, of which waited for: 7 -> 8; matrix products, arithmetic and copies ran while one was open for 9% -> 12% of each run, Pallas kernels for 21% -> 21%
where the time goes in v18:
time: 67 us; the launch traced here: 66.2 us
  waiting for transfers between devices  29.5 us (44%)
  Pallas kernels  15.3 us (23%)
  starting transfers between devices  13 us (19%)
  local copies, waits for them, and re-layouts  5.36 us (8%)
  matrix products  2.6 us (4%)
    pallas_call x5, Pallas kernels, attention_call(): pl.pallas_call(functools.partial(attention_kernel, stage, distances, n_he...  11.5 us
    ppermute x9, waiting for transfers between devices, swap(): lax.ppermute(x, 'ctx', [(i, i ^ mask) for i in range(lax.axis_size('ctx'))])  11.4 us
    ppermute x3, waiting for transfers between devices, cross(): return lax.ppermute(x, ('ctx', 'head'), route)  10.3 us
    ppermute x1, waiting for transfers between devices, shift(): lax.ppermute(x, 'ctx', [(i, i + distance) for i in range(n - distance)])  6.68 us
    dynamic_slice x4, local copies, waits for them, and re-layouts, cut(): return lax.dynamic_slice(x, start, size, allow_negative_indices=False)  5.34 us
    ppermute x3, starting transfers between devices, cross(): return lax.ppermute(x, ('ctx', 'head'), route)  3.94 us
    pallas_call x3, Pallas kernels, project(): pl.pallas_call(functools.partial(project_kernel, final, wide, window is n...  3.64 us
    ppermute x9, starting transfers between devices, swap(): lax.ppermute(x, 'ctx', [(i, i ^ mask) for i in range(lax.axis_size('ctx'))])  3.46 us
  transfers between devices with their start and end apart: 15, of which 8 were waited for; matrix products, arithmetic and copies ran while one was open for 12% of the time, Pallas kernels for 21%

profile of v18, /device:TPU:2, one launch (start us, length us, event | category | flops | bytes accessed | tf_op | source)
XLA Modules:
  0.0 66.2 jit_solution(5949433573696062739)
XLA Ops:
  0.0 0.0 collective-permute-start.2
  0.0 1.0 %constant_dynamic-slice_fusion.3 = bf16[384,128]{1,0:T(8,128)(2,1)S(1)} fusion(bf16[384,256]{1,0:T(8,128)(2,1)} %param.6, s32[]{:T(128)S(6)} %mul.23), kind=kLoop, calls=%fused_computation.9 | loop fusion | bytes 196612 | tf_op jit(solution)/shard_map/dynamic_slice | solution.py:305
  1.0 1.0 %constant_dynamic-slice_fusion.2 = bf16[384,128]{1,0:T(8,128)(2,1)S(1)} fusion(bf16[384,256]{1,0:T(8,128)(2,1)} %param.7, s32[]{:T(128)S(6)} %mul.23), kind=kLoop, calls=%fused_computation.8 | loop fusion | bytes 196612 | tf_op jit(solution)/shard_map/dynamic_slice | solution.py:305
  2.1 0.0 copy-start
  2.1 0.0 copy-start.1
  2.1 1.1 %constant_dynamic-slice_fusion = (bf16[384,128]{1,0:T(8,128)(2,1)S(1)}, bf16[384,128]{1,0:T(8,128)(2,1)S(1)}) fusion(bf16[384,256]{1,0:T(8,128)(2,1)} %param.7, s32[]{:T(128)S(6)} %mul.24, bf16[384,256]{1,0:T(8,128)(2,1)} %param.6), kind=kLoop, calls=%fused_computation.6 | loop fusion | bytes 393220 | tf_op jit(solution)/shard_map/dynamic_slice | solution.py:305
  3.3 0.6 collective-permute-start
  3.9 1.6 %collective-permute-start.3 = (bf16[384,256]{1,0:T(8,128)(2,1)S(1)}, bf16[384,256]{1,0:T(8,128)(2,1)S(1)}, u32[]{:S(2)}, u32[]{:S(2)}) collective-permute-start(bf16[384,256]{1,0:T(8,128)(2,1)S(1)} %pad_maximum_fusion.first_ref), channel_id=1, source_target_pairs={{0,8},{2,10},{4,12},{6,14},{8,16},{10,18},{12,20},{14,22},{16,24},... | collective-permute-start | bytes 589832 | tf_op jit(solution)/shard_map/ppermute | solution.py:20
  5.5 0.0 collective-permute-start.1
  5.5 1.3 %collective-permute-done.1.recv_starts_ref = s32[3]{0:T(128)S(1)} collective-permute-done((s32[3]{0:T(128)}, s32[3]{0:T(128)S(1)}, u32[]{:S(2)}, u32[]{:S(2)}) %collective-permute-start.1) | collective-permute-done | bytes 44 | tf_op jit(solution)/shard_map/ppermute | solution.py:29
  6.7 0.0 collective-permute-done.second_ref
  6.7 1.6 %collective-permute-start.4 = (bf16[384,256]{1,0:T(8,128)(2,1)S(1)}, bf16[384,256]{1,0:T(8,128)(2,1)S(1)}, u32[]{:S(2)}, u32[]{:S(2)}) collective-permute-start(bf16[384,256]{1,0:T(8,128)(2,1)S(1)} %collective-permute-done.second_ref), channel_id=1, source_target_pairs={{0,8},{2,10},{4,12},{6,14},{8,16},{10,18},{12,20},{14,22},{16,24},... | collective-permute-start | bytes 589832 | tf_op jit(solution)/shard_map/ppermute | solution.py:20
  8.3 0.0 collective-permute-done.2.refs_1_
  8.3 2.1 %dynamic_slice.25 = bf16[512,1280]{1,0:T(8,128)(2,1)S(1)} dynamic-slice(bf16[1024,4096]{1,0:T(8,128)(2,1)} %param.9, s32[]{:T(128)S(6)} %mul.25, s32[]{:T(128)S(6)} %add.16), dynamic_slice_sizes={512,1280} | dynamic-slice | bytes 2621444 | tf_op jit(solution)/shard_map/dynamic_slice | solution.py:305
  10.5 1.6 %collective-permute-start.10 = (bf16[512,1280]{1,0:T(8,128)(2,1)S(1)}, bf16[512,1280]{1,0:T(8,128)(2,1)S(1)}, u32[]{:S(2)}, u32[]{:S(2)}) collective-permute-start(bf16[512,1280]{1,0:T(8,128)(2,1)S(1)} %dynamic_slice.25), channel_id=1, source_target_pairs={{0,1},{1,0},{2,3},{3,2},{4,5},{5,4},{6,7},{7,6},{8,9},{9,8},{10,11... | collective-permute-start | bytes 3932168 | tf_op jit(solution)/shard_map/ppermute | solution.py:35
  12.1 0.0 copy-done
  12.1 0.0 copy-done.1
  12.1 3.7 %shard_map.56 = (bf16[6,512,128]{2,1,0:T(8,128)(2,1)S(1)}, f32[6,512,128]{2,1,0:T(8,128)S(1)}, f32[6,512,128]{2,1,0:T(8,128)S(1)}) custom-call(s32[3]{0:T(128)S(1)} %copy-done.1, s32[3]{0:T(128)S(1)} %collective-permute-done.1.recv_starts_ref, bf16[384,1024]{1,0:T(8,128)(2,1)S(1)} %copy-done, bf16[384,1024]{1,0:T(8,128)(2,1)S(1)} %collective-permute-done.2.refs_1_, ...), custom_call_target="tpu_custom_call" | custom-call | flops 5000000000 | bytes 8388608 | tf_op jit(solution)/shard_map/pallas_call | solution.py:278
  15.8 0.0 collective-permute-done.3.first_ref
  15.8 1.0 %collective-permute-done.4.second_ref = bf16[384,256]{1,0:T(8,128)(2,1)S(1)} collective-permute-done((bf16[384,256]{1,0:T(8,128)(2,1)S(1)}, bf16[384,256]{1,0:T(8,128)(2,1)S(1)}, u32[]{:S(2)}, u32[]{:S(2)}) %collective-permute-start.4) | collective-permute-done | bytes 196640 | tf_op jit(solution)/shard_map/ppermute | solution.py:20
  16.9 2.5 %collective-permute-start.6 = (bf16[768,256]{1,0:T(8,128)(2,1)S(1)}, bf16[768,256]{1,0:T(8,128)(2,1)S(1)}, u32[]{:S(2)}, u32[]{:S(2)}) collective-permute-start(bf16[768,256]{1,0:T(8,128)(2,1)S(1)} %shard_map.57.refs_3_), channel_id=1, source_target_pairs={{0,8},{2,10},{4,12},{6,14},{8,16},{10,18},{12,20},{14,22},{16,24},... | collective-permute-start | bytes 1179656 | tf_op jit(solution)/shard_map/ppermute | solution.py:25
  19.4 0.6 collective-permute-start.5
  20.0 0.8 %shard_map.58 = (f32[6,512,128]{2,1,0:T(8,128)S(1)}, f32[6,512,128]{2,1,0:T(8,128)S(1)}) custom-call(s32[3]{0:T(128)S(1)} %copy-done.1, s32[3]{0:T(128)S(1)} %collective-permute-done.1.recv_starts_ref, bf16[6,512,128]{2,1,0:T(8,128)(2,1)S(1)} %get-tuple-element.48.refs_0_, f32[6,512,128]{2,1,0:T(8,128)S(1)} %get-tuple-element.49.refs_1_, ...), custom_call_target="tpu_custom_call" | custom-call | flops 2100000000 | bytes 8388608 | tf_op jit(solution)/shard_map/pallas_call | solution.py:278
  20.8 6.7 %collective-permute-done.6.refs_4_.odd_ref = bf16[768,256]{1,0:T(8,128)(2,1)S(1)} collective-permute-done((bf16[768,256]{1,0:T(8,128)(2,1)S(1)}, bf16[768,256]{1,0:T(8,128)(2,1)S(1)}, u32[]{:S(2)}, u32[]{:S(2)}) %collective-permute-start.6) | collective-permute-done | bytes 393248 | tf_op jit(solution)/shard_map/ppermute | solution.py:25
  27.5 0.6 collective-permute-start.7
  28.1 2.5 %collective-permute-done.5.refs_3_ = bf16[768,256]{1,0:T(8,128)(2,1)S(1)} collective-permute-done((bf16[768,256]{1,0:T(8,128)(2,1)S(1)}, bf16[768,256]{1,0:T(8,128)(2,1)S(1)}, u32[]{:S(2)}, u32[]{:S(2)}) %collective-permute-start.5) | collective-permute-done | bytes 393248 | tf_op jit(solution)/shard_map/ppermute | solution.py:29
  30.6 0.9 %shard_map.59 = (f32[6,512,128]{2,1,0:T(8,128)S(1)}, f32[6,512,128]{2,1,0:T(8,128)S(1)}) custom-call(s32[3]{0:T(128)S(1)} %copy-done.1, s32[3]{0:T(128)S(1)} %collective-permute-done.1.recv_starts_ref, bf16[6,512,128]{2,1,0:T(8,128)(2,1)S(1)} %get-tuple-element.48.refs_0_, f32[6,512,128]{2,1,0:T(8,128)S(1)} %get-tuple-element.53.refs_1_, ...), custom_call_target="tpu_custom_call" | custom-call | flops 4000000000 | bytes 8388608 | tf_op jit(solution)/shard_map/pallas_call | solution.py:278
  31.6 6.7 %collective-permute-done.7.refs_3_ = bf16[768,256]{1,0:T(8,128)(2,1)S(1)} collective-permute-done((bf16[768,256]{1,0:T(8,128)(2,1)S(1)}, bf16[768,256]{1,0:T(8,128)(2,1)S(1)}, u32[]{:S(2)}, u32[]{:S(2)}) %collective-permute-start.7) | collective-permute-done | bytes 393248 | tf_op jit(solution)/shard_map/ppermute | solution.py:29
  38.2 0.0 slice-start
  38.2 3.1 %shard_map.62 = bf16[384,512]{1,0:T(8,128)(2,1)S(1)} custom-call(s32[3]{0:T(128)S(1)} %copy-done.1, s32[3]{0:T(128)S(1)} %collective-permute-done.1.recv_starts_ref, bf16[6,512,128]{2,1,0:T(8,128)(2,1)S(1)} %get-tuple-element.48.refs_0_, f32[6,512,128]{2,1,0:T(8,128)S(1)} %get-tuple-element.55.refs_1_, f32[6,512,128]{2,1,0:T(8,128)S(1)} %get-tuple-element.56.refs_2_, ...), custom_call_target="tpu_custom_call" | custom-call | flops 2000000000 | bytes 8388608 | tf_op jit(solution)/shard_map/pallas_call | solution.py:278
  41.4 0.0 slice-start.1
  41.4 0.1 collective-permute-start.8
  41.4 0.6 collective-permute-start.9
  42.0 0.0 collective-permute-done.10.window_ref.refs_0_
  42.0 0.1 collective-permute-start.11
  42.1 0.1 shard_map.64
  42.1 1.5 %collective-permute-start.13 = (bf16[512,768]{1,0:T(8,128)(2,1)S(1)}, bf16[512,768]{1,0:T(8,128)(2,1)S(1)}, u32[]{:S(2)}, u32[]{:S(2)}) collective-permute-start(bf16[512,768]{1,0:T(8,128)(2,1)S(1)} %shard_map.64), channel_id=1, source_target_pairs={{0,8},{2,10},{4,12},{6,14},{8,0},{10,2},{12,4},{14,6},{16,24},{18,... | collective-permute-start | bytes 2359304 | tf_op jit(solution)/shard_map/ppermute | solution.py:29
  43.7 2.9 %shard_map.61 = bf16[384,512]{1,0:T(8,128)(2,1)S(1)} custom-call(s32[3]{0:T(128)S(1)} %copy-done.1, s32[3]{0:T(128)S(1)} %collective-permute-done.1.recv_starts_ref, bf16[6,512,128]{2,1,0:T(8,128)(2,1)S(1)} %get-tuple-element.48.refs_0_, f32[6,512,128]{2,1,0:T(8,128)S(1)} %get-tuple-element.55.refs_1_, f32[6,512,128]{2,1,0:T(8,128)S(1)} %get-tuple-element.56.refs_2_, ...), custom_call_target="tpu_custom_call" | custom-call | flops 2000000000 | bytes 8388608 | tf_op jit(solution)/shard_map/pallas_call | solution.py:278
  46.6 1.8 %collective-permute-start.12 = (bf16[384,512]{1,0:T(8,128)(2,1)S(1)}, bf16[384,512]{1,0:T(8,128)(2,1)S(1)}, u32[]{:S(2)}, u32[]{:S(2)}) collective-permute-start(bf16[384,512]{1,0:T(8,128)(2,1)S(1)} %shard_map.61), channel_id=1, source_target_pairs={{0,1},{1,0},{2,3},{3,2},{4,5},{5,4},{6,7},{7,6},{8,9},{9,8},{10,11... | collective-permute-start | bytes 1179656 | tf_op jit(solution)/shard_map/ppermute | solution.py:35
  48.4 0.0 collective-permute-done.8
  48.4 0.0 slice-done
  48.4 0.0 slice-done.1
  48.4 1.2 %fusion = f32[384,2048]{1,0:T(8,128)S(1)} fusion(bf16[384,512]{1,0:T(8,128)(2,1)S(1)} %collective-permute-done.8, bf16[1024,4096]{1,0:T(8,128)(2,1)S(1)} %bitcast.3, s32[]{:T(128)S(6)} %mul.29, s32[]{:T(128)S(6)} %mul.28), kind=kOutput, calls=%fused_computation.1 | convolution fusion | flops 805306368 | bytes 5636104 | tf_op jit(solution)/shard_map/dot_general | solution.py:340
  49.7 1.4 %add_convert_fusion.given_ref = bf16[384,2048]{1,0:T(8,128)(2,1)S(1)} fusion(f32[384,2048]{1,0:T(8,128)S(1)} %fusion, bf16[384,512]{1,0:T(8,128)(2,1)S(1)} %shard_map.61, bf16[1024,4096]{1,0:T(8,128)(2,1)S(1)} %bitcast.3, s32[]{:T(128)S(6)} %mul.25, s32[]{:T(128)S(6)} %mul.28), kind=kOutput, calls=%fused_computation | convolution fusion | flops 806879232 | bytes 7208968 | tf_op jit(solution)/shard_map/dot_general | solution.py:340
  51.0 10.3 %collective-permute-done.12.heads_ref = bf16[384,512]{1,0:T(8,128)(2,1)S(1)} collective-permute-done((bf16[384,512]{1,0:T(8,128)(2,1)S(1)}, bf16[384,512]{1,0:T(8,128)(2,1)S(1)}, u32[]{:S(2)}, u32[]{:S(2)}) %collective-permute-start.12) | collective-permute-done | bytes 393248 | tf_op jit(solution)/shard_map/ppermute | solution.py:35
  61.4 0.0 collective-permute-done.9.heads_ref
  61.4 0.7 %collective-permute-done.13.refs_1_ = bf16[512,768]{1,0:T(8,128)(2,1)S(1)} collective-permute-done((bf16[512,768]{1,0:T(8,128)(2,1)S(1)}, bf16[512,768]{1,0:T(8,128)(2,1)S(1)}, u32[]{:S(2)}, u32[]{:S(2)}) %collective-permute-start.13) | collective-permute-done | bytes 786464 | tf_op jit(solution)/shard_map/ppermute | solution.py:29
  62.1 0.0 collective-permute-start.14
  62.1 0.0 collective-permute-done.11.refs_0_
  62.1 0.8 %shard_map.63.given_ref = f32[384,2048]{1,0:T(8,128)S(1)} custom-call(bf16[384,2048]{1,0:T(8,128)(2,1)S(1)} %add_convert_fusion.given_ref, bf16[384,512]{1,0:T(8,128)(2,1)S(1)} %collective-permute-done.9.heads_ref, bf16[512,1280]{1,0:T(8,128)(2,1)S(1)} %collective-permute-done.11.refs_0_), custom_call_target="tpu_custom_call" | custom-call | flops 805306368 | bytes 4194304 | tf_op jit(solution)/shard_map/pallas_call | solution.py:112
  63.0 1.2 %shard_map.65.given_ref = f32[384,2048]{1,0:T(8,128)S(1)} custom-call(f32[384,2048]{1,0:T(8,128)S(1)} %shard_map.63.given_ref, bf16[384,512]{1,0:T(8,128)(2,1)S(1)} %collective-permute-done.12.heads_ref, bf16[512,1280]{1,0:T(8,128)(2,1)S(1)} %collective-permute-done.10.window_ref.refs_0_, bf16[512,768]{1,0:T(8,128)(2,1)S(1)} %collective-permute-done.13.refs_1_), custom_call_target="tpu_custom_call" | custom-call | flops 805306368 | bytes 4194304 | tf_op jit(solution)/shard_map/pallas_call | solution.py:112
  64.1 0.3 collective-permute-done.14.refs_0_
  64.4 1.7 %shard_map.66 = bf16[384,2048]{1,0:T(8,128)(2,1)} custom-call(f32[384,2048]{1,0:T(8,128)S(1)} %shard_map.65.given_ref, bf16[384,512]{1,0:T(8,128)(2,1)S(1)} %collective-permute-done.9.heads_ref, bf16[512,768]{1,0:T(8,128)(2,1)S(1)} %collective-permute-done.14.refs_0_), custom_call_target="tpu_custom_call" | custom-call | flops 805306368 | bytes 4194304 | tf_op jit(solution)/shard_map/pallas_call | solution.py:112
  (6 shorter events, 0.1 us)
Async XLA Ops:
  0.0 8.3 %collective-permute-start.2 = (bf16[384,1024]{1,0:T(8,128)(2,1)}, bf16[384,1024]{1,0:T(8,128)(2,1)S(1)}, u32[]{:S(2)}, u32[]{:S(2)}) collective-permute-start(bf16[384,1024]{1,0:T(8,128)(2,1)} %refs_0_.1), channel_id=1, source_target_pairs={{0,2},{2,0},{4,6},{6,4},{8,10},{10,8},{12,14},{14,12},{16,18},{18,... | collective-permute-start | bytes 2359304 | tf_op jit(solution)/shard_map/ppermute | solution.py:29
  2.1 10.0 %copy-start = (bf16[384,1024]{1,0:T(8,128)(2,1)S(1)}, bf16[384,1024]{1,0:T(8,128)(2,1)}, u32[]{:S(2)}) copy-start(bf16[384,1024]{1,0:T(8,128)(2,1)} %refs_0_.1) | copy-start | bytes 2359300
  2.1 10.0 %copy-start.1 = (s32[3]{0:T(128)S(1)}, s32[3]{0:T(128)}, u32[]{:S(2)}) copy-start(s32[3]{0:T(128)} %starts_ref.9) | copy-start | bytes 40
  3.3 3.4 %collective-permute-start = (bf16[384,256]{1,0:T(8,128)(2,1)S(1)}, bf16[384,256]{1,0:T(8,128)(2,1)S(1)}, u32[]{:S(2)}, u32[]{:S(2)}) collective-permute-start(bf16[384,256]{1,0:T(8,128)(2,1)S(1)} %pad_maximum_fusion.1), channel_id=1, source_target_pairs={{0,2},{2,0},{4,6},{6,4},{8,10},{10,8},{12,14},{14,12},{16,18},{18,... | collective-permute-start | bytes 589832 | tf_op jit(solution)/shard_map/ppermute | solution.py:29
  3.9 11.9 %collective-permute-start.3 = (bf16[384,256]{1,0:T(8,128)(2,1)S(1)}, bf16[384,256]{1,0:T(8,128)(2,1)S(1)}, u32[]{:S(2)}, u32[]{:S(2)}) collective-permute-start(bf16[384,256]{1,0:T(8,128)(2,1)S(1)} %pad_maximum_fusion.first_ref), channel_id=1, source_target_pairs={{0,8},{2,10},{4,12},{6,14},{8,16},{10,18},{12,20},{14,22},{16,24},... | collective-permute-start | bytes 589832 | tf_op jit(solution)/shard_map/ppermute | solution.py:20
  5.5 1.3 %collective-permute-start.1 = (s32[3]{0:T(128)}, s32[3]{0:T(128)S(1)}, u32[]{:S(2)}, u32[]{:S(2)}) collective-permute-start(s32[3]{0:T(128)} %starts_ref.9), channel_id=1, source_target_pairs={{0,2},{2,0},{4,6},{6,4},{8,10},{10,8},{12,14},{14,12},{16,18},{18,... | collective-permute-start | bytes 44 | tf_op jit(solution)/shard_map/ppermute | solution.py:29
  6.7 10.1 %collective-permute-start.4 = (bf16[384,256]{1,0:T(8,128)(2,1)S(1)}, bf16[384,256]{1,0:T(8,128)(2,1)S(1)}, u32[]{:S(2)}, u32[]{:S(2)}) collective-permute-start(bf16[384,256]{1,0:T(8,128)(2,1)S(1)} %collective-permute-done.second_ref), channel_id=1, source_target_pairs={{0,8},{2,10},{4,12},{6,14},{8,16},{10,18},{12,20},{14,22},{16,24},... | collective-permute-start | bytes 589832 | tf_op jit(solution)/shard_map/ppermute | solution.py:20
  10.5 31.5 %collective-permute-start.10 = (bf16[512,1280]{1,0:T(8,128)(2,1)S(1)}, bf16[512,1280]{1,0:T(8,128)(2,1)S(1)}, u32[]{:S(2)}, u32[]{:S(2)}) collective-permute-start(bf16[512,1280]{1,0:T(8,128)(2,1)S(1)} %dynamic_slice.25), channel_id=1, source_target_pairs={{0,1},{1,0},{2,3},{3,2},{4,5},{5,4},{6,7},{7,6},{8,9},{9,8},{10,11... | collective-permute-start | bytes 3932168 | tf_op jit(solution)/shard_map/ppermute | solution.py:35
  16.9 10.6 %collective-permute-start.6 = (bf16[768,256]{1,0:T(8,128)(2,1)S(1)}, bf16[768,256]{1,0:T(8,128)(2,1)S(1)}, u32[]{:S(2)}, u32[]{:S(2)}) collective-permute-start(bf16[768,256]{1,0:T(8,128)(2,1)S(1)} %shard_map.57.refs_3_), channel_id=1, source_target_pairs={{0,8},{2,10},{4,12},{6,14},{8,16},{10,18},{12,20},{14,22},{16,24},... | collective-permute-start | bytes 1179656 | tf_op jit(solution)/shard_map/ppermute | solution.py:25
  19.4 11.3 %collective-permute-start.5 = (bf16[768,256]{1,0:T(8,128)(2,1)S(1)}, bf16[768,256]{1,0:T(8,128)(2,1)S(1)}, u32[]{:S(2)}, u32[]{:S(2)}) collective-permute-start(bf16[768,256]{1,0:T(8,128)(2,1)S(1)} %shard_map.57.refs_3_), channel_id=1, source_target_pairs={{0,4},{2,6},{4,0},{6,2},{8,12},{10,14},{12,8},{14,10},{16,20},{18,... | collective-permute-start | bytes 1179656 | tf_op jit(solution)/shard_map/ppermute | solution.py:29
  27.5 10.7 %collective-permute-start.7 = (bf16[768,256]{1,0:T(8,128)(2,1)S(1)}, bf16[768,256]{1,0:T(8,128)(2,1)S(1)}, u32[]{:S(2)}, u32[]{:S(2)}) collective-permute-start(bf16[768,256]{1,0:T(8,128)(2,1)S(1)} %shard_map.60), channel_id=1, source_target_pairs={{0,4},{2,6},{4,0},{6,2},{8,12},{10,14},{12,8},{14,10},{16,20},{18,... | collective-permute-start | bytes 1179656 | tf_op jit(solution)/shard_map/ppermute | solution.py:29
  38.2 10.2 %slice-start = ((s8[8388608]{0:T(1024)(128)(4,1)}), s8[4194304]{0:T(1024)(128)(4,1)S(1)}, s32[]{:S(2)}) async-start(s8[8388608]{0:T(1024)(128)(4,1)} %bitcast.2), calls=%async_computation | async-start | bytes 8388608
  41.4 7.1 %slice-start.1 = ((s8[8388608]{0:T(1024)(128)(4,1)}), s8[4194304]{0:T(1024)(128)(4,1)S(1)}, s32[]{:S(2)}) async-start(s8[8388608]{0:T(1024)(128)(4,1)} %bitcast.2), calls=%async_computation.1 | async-start | bytes 8388608
  41.4 7.0 %collective-permute-start.8 = (bf16[384,512]{1,0:T(8,128)(2,1)S(1)}, bf16[384,512]{1,0:T(8,128)(2,1)S(1)}, u32[]{:S(2)}, u32[]{:S(2)}) collective-permute-start(bf16[384,512]{1,0:T(8,128)(2,1)S(1)} %shard_map.62), channel_id=1, source_target_pairs={{0,2},{2,0},{4,6},{6,4},{8,10},{10,8},{12,14},{14,12},{16,18},{18,... | collective-permute-start | bytes 1179656 | tf_op jit(solution)/shard_map/ppermute | solution.py:29
  41.4 19.9 %collective-permute-start.9 = (bf16[384,512]{1,0:T(8,128)(2,1)S(1)}, bf16[384,512]{1,0:T(8,128)(2,1)S(1)}, u32[]{:S(2)}, u32[]{:S(2)}) collective-permute-start(bf16[384,512]{1,0:T(8,128)(2,1)S(1)} %shard_map.62), channel_id=1, source_target_pairs={{0,3},{1,2},{2,1},{3,0},{4,7},{5,6},{6,5},{7,4},{8,11},{9,10},{10,... | collective-permute-start | bytes 1179656 | tf_op jit(solution)/shard_map/ppermute | solution.py:35
  42.0 20.1 %collective-permute-start.11 = (bf16[512,1280]{1,0:T(8,128)(2,1)S(1)}, bf16[512,1280]{1,0:T(8,128)(2,1)S(1)}, u32[]{:S(2)}, u32[]{:S(2)}) collective-permute-start(bf16[512,1280]{1,0:T(8,128)(2,1)S(1)} %collective-permute-done.10.window_ref.refs_0_), channel_id=1, source_target_pairs={{0,2},{2,0},{4,6},{6,4},{8,10},{10,8},{12,14},{14,12},{16,18},{18,... | collective-permute-start | bytes 3932168 | tf_op jit(solution)/shard_map/ppermute | solution.py:29
  42.1 20.0 %collective-permute-start.13 = (bf16[512,768]{1,0:T(8,128)(2,1)S(1)}, bf16[512,768]{1,0:T(8,128)(2,1)S(1)}, u32[]{:S(2)}, u32[]{:S(2)}) collective-permute-start(bf16[512,768]{1,0:T(8,128)(2,1)S(1)} %shard_map.64), channel_id=1, source_target_pairs={{0,8},{2,10},{4,12},{6,14},{8,0},{10,2},{12,4},{14,6},{16,24},{18,... | collective-permute-start | bytes 2359304 | tf_op jit(solution)/shard_map/ppermute | solution.py:29
  46.6 14.7 %collective-permute-start.12 = (bf16[384,512]{1,0:T(8,128)(2,1)S(1)}, bf16[384,512]{1,0:T(8,128)(2,1)S(1)}, u32[]{:S(2)}, u32[]{:S(2)}) collective-permute-start(bf16[384,512]{1,0:T(8,128)(2,1)S(1)} %shard_map.61), channel_id=1, source_target_pairs={{0,1},{1,0},{2,3},{3,2},{4,5},{5,4},{6,7},{7,6},{8,9},{9,8},{10,11... | collective-permute-start | bytes 1179656 | tf_op jit(solution)/shard_map/ppermute | solution.py:35
  62.1 2.3 %collective-permute-start.14 = (bf16[512,768]{1,0:T(8,128)(2,1)S(1)}, bf16[512,768]{1,0:T(8,128)(2,1)S(1)}, u32[]{:S(2)}, u32[]{:S(2)}) collective-permute-start(bf16[512,768]{1,0:T(8,128)(2,1)S(1)} %collective-permute-done.13.refs_1_), channel_id=1, source_target_pairs={{0,2},{2,0},{4,6},{6,4},{8,10},{10,8},{12,14},{14,12},{16,18},{18,... | collective-permute-start | bytes 2359304 | tf_op jit(solution)/shard_map/ppermute | solution.py:29
